TPU v7x, 32 devices: a whole 2x2x4 slice. The times are simulated.
32 devices in a mesh: rep: 2 (over y), grp: 2 (over core), ep: 8 (over z, x).
Axes of the slice: x: 2, y: 2, z: 4, core: 2. Of those that a mesh axis runs over, the one named last changes fastest.
Arguments:
- tokens: bfloat16 [4096, 2048], P(('rep', 'grp', 'ep')), parts along dimension 0, may hold values from -6 to 6
- cotangent: bfloat16 [4096, 2048], P(('rep', 'grp', 'ep')), parts along dimension 0, may hold values from -6 to 6
- routes: int32 [4096, 4], P(('rep', 'grp', 'ep')), parts along dimension 0, may hold values from 0 to 15, all different within a row; in each aligned block of 128 rows (0 to 127, 128 to 255, ...) at most 48 rows name the same one
- gates: bfloat16 [4096, 4], P(('rep', 'grp', 'ep')), parts along dimension 0, may hold values from 0.049804688 to 1
- w_gate: bfloat16 [16, 2048, 768], P(('grp', 'ep')), may hold values from -0.125 to 0.125
- w_up: bfloat16 [16, 2048, 768], P(('grp', 'ep')), may hold values from -0.125 to 0.125
- w_down: bfloat16 [16, 768, 2048], P(('grp', 'ep')), may hold values from -0.21875 to 0.21875
Outputs:
- mixed: bfloat16 [4096, 2048], P(('rep', 'grp', 'ep')), parts along dimension 0
- d_tokens: bfloat16 [4096, 2048], P(('rep', 'grp', 'ep')), parts along dimension 0
- d_gates: float32 [4096, 4], P(('rep', 'grp', 'ep')), parts along dimension 0
There are 2 independent parts, one for each index of `rep`. A program takes and returns all parts, laid end to end along the dimension named above; an argument that names none is the same for every part. Nothing has to cross between parts.
Inputs may be any that keep to these rules, and one draw needn't show every extreme that they name: `routes`: each row names 4 different experts; of the 128 rows of one device at most 48 name one expert, a bound that some block reaches of them.
All inputs are finite; a program needn't handle non-finite values.
Results may differ from a plain program's by a relative error of at most 0.0058.
Values may be sent and summed in bfloat16 or wider, within the bound.
No kernel may reach another device: no remote copies, remote signals or barrier semaphores. Data moves between devices by JAX's collectives and lax.ppermute only.
A program may use at most 128 MiB of HBM per device.

v0:
```python
import jax
import jax.numpy as jnp
from jax import lax
from jax.sharding import PartitionSpec as P


def expert_pass(rows_in, rows_grad, gate_mat, up_mat, down_mat):
    pre_gate = jnp.dot(rows_in, gate_mat, preferred_element_type=jnp.float32)
    pre_up = jnp.dot(rows_in, up_mat, preferred_element_type=jnp.float32)
    activated = jax.nn.silu(pre_gate)
    hidden = (activated * pre_up).astype(jnp.bfloat16)
    outputs = jnp.dot(hidden, down_mat, preferred_element_type=jnp.float32).astype(jnp.bfloat16)
    d_hidden = lax.dot_general(
        rows_grad, down_mat, (((1,), (1,)), ((), ())), preferred_element_type=jnp.float32
    )
    sigma = jax.nn.sigmoid(pre_gate)
    d_pre_gate = (d_hidden * pre_up * sigma * (1.0 + pre_gate * (1.0 - sigma))).astype(jnp.bfloat16)
    d_pre_up = (d_hidden * activated).astype(jnp.bfloat16)
    both_pre = jnp.concatenate([d_pre_gate, d_pre_up], axis=1)
    both_mats = jnp.concatenate([gate_mat, up_mat], axis=1)
    d_copy = lax.dot_general(
        both_pre, both_mats, (((1,), (1,)), ((), ())), preferred_element_type=jnp.float32
    )
    return (outputs, d_copy.astype(jnp.bfloat16))


def run_items(pieces, gate_mat, up_mat, down_mat):
    rows_in, rows_grad = pieces
    lead_shape = rows_in.shape[:2]
    width = rows_in.shape[2]
    outputs, d_copy = expert_pass(
        rows_in.reshape(-1, width), rows_grad.reshape(-1, width), gate_mat, up_mat, down_mat
    )
    return (outputs.reshape(lead_shape + (width,)), d_copy.reshape(lead_shape + (width,)))


def ranks_of(chosen_hot):
    running = jnp.cumsum(chosen_hot, axis=-2)
    return jnp.sum(chosen_hot * running, axis=-1) - 1


def body(tokens, cotangent, routes, gates, w_gate, w_up, w_down):
    token_count = tokens.shape[0]
    width = tokens.shape[1]
    top_count = routes.shape[1]
    copy_count = token_count * top_count
    gate_mat = w_gate[0]
    up_mat = w_up[0]
    down_mat = w_down[0]
    expert_count = lax.axis_size(("grp", "ep"))
    capacity = max(2, 3 * token_count * top_count // (2 * expert_count))
    flat_experts = routes.reshape(-1)
    chosen_hot = (
        flat_experts[:, None] == jnp.arange(expert_count, dtype=jnp.int32)[None, :]
    ).astype(jnp.int32)
    slot_of = flat_experts * capacity + ranks_of(chosen_hot)
    token_of = jnp.arange(copy_count, dtype=jnp.int32) // top_count
    slot_token = jnp.zeros((expert_count * capacity,), jnp.int32).at[slot_of].set(token_of)
    slot_live = jnp.zeros((expert_count * capacity,), jnp.bool_).at[slot_of].set(True)
    send_in = jnp.where(
        slot_live[:, None], tokens[slot_token], jnp.zeros((), tokens.dtype)
    ).reshape(expert_count, capacity, width)
    send_grad = jnp.where(
        slot_live[:, None], cotangent[slot_token], jnp.zeros((), cotangent.dtype)
    ).reshape(expert_count, capacity, width)
    outputs, d_copy = run_items(
        (
            lax.all_to_all(send_in, ("grp", "ep"), split_axis=0, concat_axis=0, tiled=True),
            lax.all_to_all(send_grad, ("grp", "ep"), split_axis=0, concat_axis=0, tiled=True),
        ),
        gate_mat,
        up_mat,
        down_mat,
    )
    back_out = lax.all_to_all(outputs, ("grp", "ep"), split_axis=0, concat_axis=0, tiled=True)
    back_grad = lax.all_to_all(d_copy, ("grp", "ep"), split_axis=0, concat_axis=0, tiled=True)
    copy_out = back_out.reshape(-1, width)[slot_of].reshape(token_count, top_count, width)
    copy_grad = back_grad.reshape(-1, width)[slot_of].reshape(token_count, top_count, width)
    weight = gates.astype(jnp.float32)
    mixed = jnp.sum(weight[:, :, None] * copy_out.astype(jnp.float32), axis=1)
    d_tokens = jnp.sum(weight[:, :, None] * copy_grad.astype(jnp.float32), axis=1)
    d_gates = jnp.einsum("tkd,td->tk", copy_out, cotangent, preferred_element_type=jnp.float32)
    return (mixed.astype(jnp.bfloat16), d_tokens.astype(jnp.bfloat16), d_gates)


def solution(mesh):
    return jax.shard_map(
        body,
        mesh=mesh,
        in_specs=(
            P(("rep", "grp", "ep"), None),
            P(("rep", "grp", "ep"), None),
            P(("rep", "grp", "ep"), None),
            P(("rep", "grp", "ep"), None),
            P(("grp", "ep"), None, None),
            P(("grp", "ep"), None, None),
            P(("grp", "ep"), None, None),
        ),
        out_specs=(
            P(("rep", "grp", "ep"), None),
            P(("rep", "grp", "ep"), None),
            P(("rep", "grp", "ep"), None),
        ),
        check_vma=False,
    )
```

profile of v0, /device:TPU:0, one launch (start us, length us, event | category | flops | bytes accessed | tf_op | source)
XLA Modules:
  0.0 373.5 jit_solution(6299424062845302771)
XLA Ops:
  0.6 0.0 copy-start
  0.6 0.9 copy.13
  1.6 0.1 eq.29
  1.7 0.1 eq.25
  1.8 0.7 broadcast_multiply_fusion
  2.5 1.2 reduce-window.6
  3.7 0.2 slice_reduce_fusion
  3.9 0.1 fusion.18
  4.0 0.1 copy.12
  4.1 0.1 mul.58
  4.3 2.4 scatter_custom_fusion.1
  6.7 8.3 %gather_fusion.2 = bf16[768,2048]{1,0:T(8,128)(2,1)} fusion(bf16[128,2048]{1,0:T(8,128)(2,1)} %param.8, s32[1024]{0:T(1024)S(1)} %pad_clamp_fusion.1), kind=kCustom, calls=%fused_computation.2 | custom fusion | bytes 6294528 | tf_op jit(solution)/shard_map/gather | solution.py:64
  15.0 8.2 %gather_fusion = bf16[768,2048]{1,0:T(8,128)(2,1)} fusion(bf16[128,2048]{1,0:T(8,128)(2,1)} %param.7, s32[1024]{0:T(1024)S(1)} %pad_clamp_fusion.1), kind=kCustom, calls=%fused_computation | custom fusion | bytes 6294528 | tf_op jit(solution)/shard_map/gather | solution.py:61
  23.3 2.4 scatter_custom_fusion
  25.7 0.1 broadcast_in_dim.39
  25.8 4.3 %broadcast_select_fusion.1 = (bf16[16,48,2048]{2,1,0:T(8,128)(2,1)S(1)}, bf16[16,48,2048]{2,1,0:T(8,128)(2,1)}) fusion(bf16[16,48,2048]{2,1,0:T(8,128)(2,1)} %bitcast.46, pred[16,48]{1,0:T(8,128)(4,1)S(1)} %broadcast_in_dim.39, bf16[16,48,2048]{2,1,0:T(8,128)(2,1)} %bitcast.45), kind=kLoop, calls=%fused_computation.18 | loop fusion | flops 3145728 | bytes 12583680 | tf_op jit(solution)/shard_map/jit(_where)/select_n | solution.py:60
  30.1 79.2 %all_to_all.20 = bf16[16,48,2048]{2,1,0:T(8,128)(2,1)} all-to-all(bf16[16,48,2048]{2,1,0:T(8,128)(2,1)S(1)} %get-tuple-element.7), channel_id=1, replica_groups=mesh['rep'=2,'grp'=2,'ep'=8] {'grp','ep'}, dimensions={0} | all-to-all | bytes 6291456 | tf_op jit(solution)/shard_map/all_to_all | solution.py:68
  109.3 4.7 %all-to-all-start.2 = ((bf16[16,48,2048]{2,1,0:T(8,128)(2,1)}), bf16[16,48,2048]{2,1,0:T(8,128)(2,1)}, u32[]{:S(2)}, u32[]{:S(2)}) async-start(bf16[16,48,2048]{2,1,0:T(8,128)(2,1)} %get-tuple-element.8), calls=%async_computation.2 | async-start | bytes 6291456 | tf_op jit(solution)/shard_map/all_to_all | solution.py:69
  114.0 6.9 %fusion.28 = f32[768,768]{0,1:T(8,128)} fusion(bf16[768,2048]{1,0:T(8,128)(2,1)} %bitcast.47, bf16[1,2048,768]{2,1,0:T(8,128)(2,1)} %param.12), kind=kOutput, calls=%fused_computation.55 | convolution fusion | flops 2415919104 | bytes 8650752 | tf_op jit(solution)/shard_map/dot_general | solution.py:9
  120.9 61.6 %all-to-all-done.2 = bf16[16,48,2048]{2,1,0:T(8,128)(2,1)} async-done(((bf16[16,48,2048]{2,1,0:T(8,128)(2,1)}), bf16[16,48,2048]{2,1,0:T(8,128)(2,1)}, u32[]{:S(2)}, u32[]{:S(2)}) %all-to-all-start.2) | async-done | bytes 3145760 | tf_op jit(solution)/shard_map/all_to_all | solution.py:69
  182.5 0.0 copy-done
  182.5 0.0 copy-start.1
  182.5 0.0 copy-start.3
  182.5 0.0 copy-start.4
  182.5 4.7 %fusion.7 = f32[768,768]{0,1:T(8,128)S(1)} fusion(bf16[768,2048]{1,0:T(8,128)(2,1)} %bitcast.11, bf16[1,768,2048]{2,1,0:T(8,128)(2,1)S(1)} %copy-done), kind=kOutput, calls=%fused_computation.14 | convolution fusion | flops 2415919104 | bytes 8650752 | tf_op jit(solution)/shard_map/dot_general | solution.py:13
  187.2 0.0 copy-done.1
  187.2 0.0 copy-done.3
  187.2 0.0 copy-done.4
  187.2 5.1 %multiply_convert_fusion.1 = (bf16[768,768]{0,1:T(8,128)(2,1)}, bf16[768,768]{0,1:T(8,128)(2,1)}, f32[768,768]{0,1:T(8,128)S(1)}) fusion(f32[768,768]{0,1:T(8,128)S(1)} %fusion.7, f32[768,768]{0,1:T(8,128)S(1)} %copy-done.4, bf16[768,2048]{1,0:T(8,128)(2,1)S(1)} %bitcast.48, bf16[1,2048,768]{2,1,0:T(8,128)(2,1)S(1)} %copy-done.3), kind=kOutput, calls=%fused_computation.23 | convolution fusion | flops 2423586816 | bytes 15728640 | tf_op jit(solution)/shard_map/dot_general | solution.py:8
  192.3 4.2 %convolution_convert_fusion = bf16[768,2048]{1,0:T(8,128)(2,1)} fusion(bf16[1,768,2048]{2,1,0:T(8,128)(2,1)S(1)} %copy-done, f32[768,768]{0,1:T(8,128)S(1)} %copy-done.4, f32[768,768]{0,1:T(8,128)S(1)} %get-tuple-element.9), kind=kOutput, calls=%fused_computation.12 | convolution fusion | flops 2421030912 | bytes 11010048 | tf_op jit(solution)/shard_map/dot_general | solution.py:12
  196.6 6.5 %all-to-all-start.1 = ((bf16[16,48,2048]{2,1,0:T(8,128)(2,1)}), bf16[16,48,2048]{2,1,0:T(8,128)(2,1)}, u32[]{:S(2)}, u32[]{:S(2)}) async-start(bf16[16,48,2048]{2,1,0:T(8,128)(2,1)} %bitcast.50), calls=%async_computation.1 | async-start | bytes 6291456 | tf_op jit(solution)/shard_map/all_to_all | solution.py:75
  203.1 9.1 %fusion.4 = bf16[768,2048]{1,0:T(8,128)(2,1)} fusion(bf16[2048,768]{1,0:T(8,128)(2,1)} %bitcast.56, bf16[2048,768]{1,0:T(8,128)(2,1)} %bitcast.57, bf16[768,768]{0,1:T(8,128)(2,1)} %get-tuple-element.6, bf16[768,768]{0,1:T(8,128)(2,1)} %get-tuple-element.5), kind=kOutput, calls=%fused_computation.13 | convolution fusion | flops 4850712576 | bytes 11796480 | tf_op jit(solution)/shard_map/dot_general | solution.py:21
  212.2 59.6 %all-to-all-done.1 = bf16[16,48,2048]{2,1,0:T(8,128)(2,1)} async-done(((bf16[16,48,2048]{2,1,0:T(8,128)(2,1)}), bf16[16,48,2048]{2,1,0:T(8,128)(2,1)}, u32[]{:S(2)}, u32[]{:S(2)}) %all-to-all-start.1) | async-done | bytes 3145760 | tf_op jit(solution)/shard_map/all_to_all | solution.py:75
  271.8 0.0 copy-start.2
  271.8 6.6 %all-to-all-start.3 = ((bf16[16,48,2048]{2,1,0:T(8,128)(2,1)}), bf16[16,48,2048]{2,1,0:T(8,128)(2,1)}, u32[]{:S(2)}, u32[]{:S(2)}) async-start(bf16[16,48,2048]{2,1,0:T(8,128)(2,1)} %bitcast.49), calls=%async_computation.3 | async-start | bytes 6291456 | tf_op jit(solution)/shard_map/all_to_all | solution.py:76
  278.4 0.0 copy-done.2
  278.4 0.1 copy.11
  278.5 7.5 %gather_fusion.1 = bf16[512,2048]{1,0:T(8,128)(2,1)} fusion(bf16[768,2048]{1,0:T(8,128)(2,1)} %bitcast.9, s32[1024]{0:T(1024)S(1)} %pad_clamp_fusion), kind=kCustom, calls=%fused_computation.1 | custom fusion | bytes 4196352 | tf_op jit(solution)/shard_map/gather | solution.py:77
  286.1 4.1 %reshape.100 = bf16[128,4,2048]{2,1,0:T(4,128)(2,1)} reshape(bf16[512,2048]{1,0:T(8,128)(2,1)} %gather_fusion.1) | data formatting | bytes 4194304 | tf_op jit(solution)/shard_map/reshape | solution.py:77
  290.2 57.0 %all-to-all-done.3 = bf16[16,48,2048]{2,1,0:T(8,128)(2,1)} async-done(((bf16[16,48,2048]{2,1,0:T(8,128)(2,1)}), bf16[16,48,2048]{2,1,0:T(8,128)(2,1)}, u32[]{:S(2)}, u32[]{:S(2)}) %all-to-all-start.3) | async-done | bytes 3145760 | tf_op jit(solution)/shard_map/all_to_all | solution.py:76
  347.1 7.5 %gather_fusion.3 = bf16[512,2048]{1,0:T(8,128)(2,1)} fusion(bf16[768,2048]{1,0:T(8,128)(2,1)} %bitcast.13, s32[1024]{0:T(1024)S(1)} %pad_clamp_fusion), kind=kCustom, calls=%fused_computation.3 | custom fusion | bytes 4196352 | tf_op jit(solution)/shard_map/gather | solution.py:78
  354.7 4.8 %reshape.104 = f32[128,4,2048]{2,1,0:T(4,128)} reshape(bf16[512,2048]{1,0:T(8,128)(2,1)} %gather_fusion.3) | data formatting | bytes 6291456 | tf_op jit(solution)/shard_map/convert_element_type | solution.py:81
  359.4 4.5 %fusion.14 = f32[128,1,4]{2,1,0:T(1,128)S(1)} fusion(bf16[128,4,2048]{2,1,0:T(4,128)(2,1)} %reshape.100, bf16[128,2048,1]{1,0,2:T(8,128)(2,1)} %bitcast.44), kind=kOutput, calls=%fused_computation.27 | convolution fusion | flops 2097152 | bytes 2623488 | tf_op jit(solution)/shard_map/tkd,td->tk/dot_general | solution.py:82
  363.9 0.7 copy.17
  364.6 8.9 %multiply_reduce_fusion = (bf16[128,2048]{1,0:T(8,128)(2,1)}, bf16[128,2048]{1,0:T(8,128)(2,1)}) fusion(f32[128,4,2048]{2,1,0:T(4,128)} %reshape.104, f32[128,4]{1,0:T(8,128)S(1)} %copy.11, bf16[128,4,2048]{2,1,0:T(4,128)(2,1)} %reshape.100), kind=kLoop, calls=%fused_computation.10 | loop fusion | flops 4718592 | bytes 7342080 | tf_op jit(solution)/shard_map/reduce_sum | solution.py:81
  (10 shorter events, 0.1 us)
Async XLA Ops:
  0.6 181.8 %copy-start = (bf16[1,768,2048]{2,1,0:T(8,128)(2,1)S(1)}, bf16[1,768,2048]{2,1,0:T(8,128)(2,1)}, u32[]{:S(2)}) copy-start(bf16[1,768,2048]{2,1,0:T(8,128)(2,1)} %param.13) | copy-start | bytes 9437188
  109.3 73.1 %all-to-all-start.2 = ((bf16[16,48,2048]{2,1,0:T(8,128)(2,1)}), bf16[16,48,2048]{2,1,0:T(8,128)(2,1)}, u32[]{:S(2)}, u32[]{:S(2)}) async-start(bf16[16,48,2048]{2,1,0:T(8,128)(2,1)} %get-tuple-element.8), calls=%async_computation.2 | async-start | bytes 6291456 | tf_op jit(solution)/shard_map/all_to_all | solution.py:69
  182.5 4.7 %copy-start.1 = (bf16[16,48,2048]{2,1,0:T(8,128)(2,1)S(1)}, bf16[16,48,2048]{2,1,0:T(8,128)(2,1)}, u32[]{:S(2)}) copy-start(bf16[16,48,2048]{2,1,0:T(8,128)(2,1)} %all_to_all.20) | copy-start | bytes 9437188
  182.5 4.7 %copy-start.3 = (bf16[1,2048,768]{2,1,0:T(8,128)(2,1)S(1)}, bf16[1,2048,768]{2,1,0:T(8,128)(2,1)}, u32[]{:S(2)}) copy-start(bf16[1,2048,768]{2,1,0:T(8,128)(2,1)} %param.11) | copy-start | bytes 9437188
  182.5 4.7 %copy-start.4 = (f32[768,768]{0,1:T(8,128)S(1)}, f32[768,768]{0,1:T(8,128)}, u32[]{:S(2)}) copy-start(f32[768,768]{0,1:T(8,128)} %fusion.28) | copy-start | bytes 7077892
  196.6 75.2 %all-to-all-start.1 = ((bf16[16,48,2048]{2,1,0:T(8,128)(2,1)}), bf16[16,48,2048]{2,1,0:T(8,128)(2,1)}, u32[]{:S(2)}, u32[]{:S(2)}) async-start(bf16[16,48,2048]{2,1,0:T(8,128)(2,1)} %bitcast.50), calls=%async_computation.1 | async-start | bytes 6291456 | tf_op jit(solution)/shard_map/all_to_all | solution.py:75
  271.8 6.6 %copy-start.2 = (bf16[128,4]{0,1:T(4,128)(2,1)S(1)}, bf16[128,4]{0,1:T(4,128)(2,1)}, u32[]{:S(2)}) copy-start(bf16[128,4]{0,1:T(4,128)(2,1)} %param.10) | copy-start | bytes 3076
  271.8 75.3 %all-to-all-start.3 = ((bf16[16,48,2048]{2,1,0:T(8,128)(2,1)}), bf16[16,48,2048]{2,1,0:T(8,128)(2,1)}, u32[]{:S(2)}, u32[]{:S(2)}) async-start(bf16[16,48,2048]{2,1,0:T(8,128)(2,1)} %bitcast.49), calls=%async_computation.3 | async-start | bytes 6291456 | tf_op jit(solution)/shard_map/all_to_all | solution.py:76
where the time goes:
time: 375 us; the launch traced here: 373 us
  waiting for transfers between devices  178 us (47%)
  blocking collectives  79.2 us (21%)
  local copies, waits for them, and re-layouts  47.8 us (13%)
  matrix products  34.6 us (9%)
  starting transfers between devices  17.7 us (5%)
  other arithmetic  15.2 us (4%)
    all_to_all x1, blocking collectives, body(): lax.all_to_all(send_in, ('grp', 'ep'), split_axis=0, concat_axis=0, tiled...  79.2 us
    all_to_all x1, waiting for transfers between devices, body(): lax.all_to_all(send_grad, ('grp', 'ep'), split_axis=0, concat_axis=0, til...  61.6 us
    all_to_all x1, waiting for transfers between devices, body(): lax.all_to_all(outputs, ('grp', 'ep'), split_axis=0, concat_axis=0, tiled...  59.6 us
    all_to_all x1, waiting for transfers between devices, body(): lax.all_to_all(d_copy, ('grp', 'ep'), split_axis=0, concat_axis=0, tiled=...  57 us
    dot_general x1, matrix products, expert_pass(): lax.dot_general(both_pre, both_mats, (((1,), (1,)), ((), ())), preferred_...  9.13 us
    reduce_sum x1, other arithmetic, body(): jnp.sum(weight[:, :, None] * copy_grad.astype(jnp.float32), axis=1)  8.9 us
    gather x1, local copies, waits for them, and re-layouts, body(): cotangent[slot_token]  8.3 us
    gather x1, local copies, waits for them, and re-layouts, body(): tokens[slot_token]  8.24 us
  transfers between devices with their start and end apart: 3, of which 3 were waited for; matrix products, arithmetic and copies ran while one was open for 7% of the time, Pallas kernels for 0%

commit v1 on v0

--- a/solution.py
+++ b/solution.py
@@ -39,7 +39,7 @@
     return jnp.sum(chosen_hot * running, axis=-1) - 1
 
 
-def body(tokens, cotangent, routes, gates, w_gate, w_up, w_down):
+def body_exchange(tokens, cotangent, routes, gates, w_gate, w_up, w_down):
     token_count = tokens.shape[0]
     width = tokens.shape[1]
     top_count = routes.shape[1]
@@ -83,9 +83,153 @@
     return (mixed.astype(jnp.bfloat16), d_tokens.astype(jnp.bfloat16), d_gates)
 
 
+def ring_order(count):
+    return list(range(0, count, 2)) + list(range(count - 1, 0, -2))
+
+
+def ring_shift(array, count, step):
+    order = ring_order(count)
+    pairs = [(order[i], order[(i + step) % count]) for i in range(count)]
+    return lax.ppermute(array, "ep", pairs)
+
+
+def ring_gather(shard, count, far_step):
+    held = {0: shard}
+    for step in (far_step, -far_step):
+        hops = count // 2 if step == far_step else (count - 1) // 2
+        moving = shard
+        for hop in range(1, hops + 1):
+            moving = ring_shift(moving, count, step)
+            held[(-step * hop) % count] = moving
+    return [held[place] for place in range(count)]
+
+
+def ring_reduce(share_of, count, far_step):
+    arrived = []
+    for step in (far_step, -far_step):
+        hops = count // 2 if step == far_step else (count - 1) // 2
+        moving = None
+        for hop in range(hops, 0, -1):
+            moving = ring_shift(share_of((step * hop) % count, moving), count, step)
+        arrived.append(moving)
+    total = share_of(0, arrived[0], arrived[1])
+    return total
+
+
+def swap_cores(array):
+    return lax.ppermute(array, "grp", [(0, 1), (1, 0)])
+
+
+def body_ring(tokens, cotangent, routes, gates, w_gate, w_up, w_down):
+    token_count = tokens.shape[0]
+    width = tokens.shape[1]
+    top_count = routes.shape[1]
+    chips = lax.axis_size("ep")
+    expert_count = lax.axis_size(("grp", "ep"))
+    capacity = max(2, 3 * token_count * top_count // (2 * expert_count))
+    f32, bf16 = jnp.float32, jnp.bfloat16
+
+    in_shards = ring_gather(tokens, chips, 1)
+    grad_shards = ring_gather(cotangent, chips, -1)
+    gate_mats = (w_gate[0], swap_cores(w_gate[0]))
+    up_mats = (w_up[0], swap_cores(w_up[0]))
+    down_mats = (w_down[0], swap_cores(w_down[0]))
+
+    core = lax.axis_index("grp")
+    chip = lax.axis_index("ep")
+    order = jnp.array(ring_order(chips), jnp.int32)
+    place = jnp.argmax(order == chip).astype(jnp.int32)
+    sources = order[(place + jnp.arange(chips, dtype=jnp.int32)) % chips]
+    table = jnp.concatenate([routes.astype(f32), gates.astype(f32)], axis=1).T
+    tables = lax.all_gather(table, "ep", axis=0)[sources]
+    named = tables[:, :top_count].astype(jnp.int32)
+    weights = tables[:, top_count:]
+    mine = jnp.stack([core * chips + chip, (1 - core) * chips + chip])
+    hits = named[:, None] == mine[None, :, None, None]
+    weight = jnp.sum(jnp.where(hits, weights[:, None], 0.0), axis=2)
+    hit = jnp.any(hits, axis=2)
+    before = (
+        jnp.arange(token_count)[:, None] <= jnp.arange(token_count)[None, :]
+    ).astype(bf16)
+    rank = jnp.dot(
+        hit.astype(bf16).reshape(-1, token_count), before, preferred_element_type=f32
+    ).reshape(hit.shape).astype(jnp.int32) - 1
+    slots = jnp.arange(capacity, dtype=jnp.int32)
+    picks = hit[:, :, None, :] & (rank[:, :, None, :] == slots[None, None, :, None])
+    rows_per = 2 * capacity
+    pick = picks.astype(bf16).reshape(chips, rows_per, token_count)
+    spread = jnp.where(picks, weight[:, :, None, :], 0.0).astype(bf16).reshape(
+        chips, rows_per, token_count
+    )
+
+    def gather_rows(shards):
+        parts = [
+            jnp.dot(pick[s], shards[s], preferred_element_type=f32).astype(bf16)
+            for s in range(chips)
+        ]
+        stacked = jnp.stack(parts).reshape(chips, 2, capacity, width)
+        return [stacked[:, e].reshape(chips * capacity, width) for e in range(2)]
+
+    def scatter_rows(outputs):
+        blocks = [o.reshape(chips, capacity, width) for o in outputs]
+
+        def share_of(s, *partials):
+            block = jnp.concatenate([b[s] for b in blocks], axis=0)
+            total = lax.dot_general(
+                spread[s], block, (((0,), (0,)), ((), ())), preferred_element_type=f32
+            )
+            for partial in partials:
+                if partial is not None:
+                    total = total + partial.astype(f32)
+            return total.astype(bf16)
+
+        return share_of
+
+    rows_in = gather_rows(in_shards)
+    pre_gate = [jnp.dot(rows_in[e], gate_mats[e], preferred_element_type=f32) for e in range(2)]
+    pre_up = [jnp.dot(rows_in[e], up_mats[e], preferred_element_type=f32) for e in range(2)]
+    activated = [jax.nn.silu(v) for v in pre_gate]
+    hidden = [(activated[e] * pre_up[e]).astype(bf16) for e in range(2)]
+    outputs = [
+        jnp.dot(hidden[e], down_mats[e], preferred_element_type=f32).astype(bf16)
+        for e in range(2)
+    ]
+    mixed = ring_reduce(scatter_rows(outputs), chips, 1)
+
+    rows_grad = gather_rows(grad_shards)
+    last = (((1,), (1,)), ((), ()))
+    d_copies = []
+    inner = []
+    for e in range(2):
+        d_hidden = lax.dot_general(rows_grad[e], down_mats[e], last, preferred_element_type=f32)
+        sigma = jax.nn.sigmoid(pre_gate[e])
+        d_pre_gate = (d_hidden * pre_up[e] * sigma * (1.0 + pre_gate[e] * (1.0 - sigma))).astype(bf16)
+        d_pre_up = (d_hidden * activated[e]).astype(bf16)
+        d_copy = lax.dot_general(d_pre_gate, gate_mats[e], last, preferred_element_type=f32)
+        d_copy = d_copy + lax.dot_general(d_pre_up, up_mats[e], last, preferred_element_type=f32)
+        d_copies.append(d_copy.astype(bf16))
+        inner.append(
+            jnp.sum(rows_grad[e].astype(f32) * outputs[e].astype(f32), axis=1).reshape(
+                chips, capacity
+            )
+        )
+    d_tokens = ring_reduce(scatter_rows(d_copies), chips, -1)
+
+    inner = jnp.stack(inner, axis=1)
+    per_token = jnp.sum(jnp.where(picks, inner[:, :, :, None], 0.0), axis=2)
+    by_chip = jnp.zeros_like(per_token).at[sources].set(per_token)
+    returned = lax.all_to_all(by_chip, "ep", split_axis=0, concat_axis=0, tiled=True)
+    chip_ids = jnp.arange(chips, dtype=jnp.int32)
+    served = jnp.stack([core * chips + chip_ids, (1 - core) * chips + chip_ids], axis=1)
+    chosen = routes.T[None, None] == served[:, :, None, None]
+    d_gates = jnp.sum(jnp.where(chosen, returned[:, :, None, :], 0.0), axis=(0, 1)).T
+    return (mixed, d_tokens, d_gates)
+
+
 def solution(mesh):
+    plan = body_ring if mesh.shape["ep"] <= 8 and mesh.shape["grp"] == 2 else body_exchange
     return jax.shard_map(
-        body,
+        plan,
         mesh=mesh,
         in_specs=(
             P(("rep", "grp", "ep"), None),

time: 375 us -> 274 us (0.73)
  waiting for transfers between devices: 178 us -> 107 us
  blocking collectives: 79.2 us -> 42.8 us
  local copies, waits for them, and re-layouts: 47.8 us -> 14.1 us
  matrix products: 34.6 us -> 66.8 us
  starting transfers between devices: 17.7 us -> 31.2 us
  other arithmetic: 15.2 us -> 9.09 us
    all_to_all x3 -> x1, waiting for transfers between devices: 178 us -> 0.01 us  [body_ring(): lax.all_to_all(by_chip, 'ep', split_axis=0, concat_axis=0, tiled=True)]
    ppermute x0 -> x31, waiting for transfers between devices: none -> 107 us  [the longest x28 107 us: ring_shift(): return lax.ppermute(array, 'ep', pairs)]
    all_to_all x1 -> x0, blocking collectives: 79.2 us -> none  [body(): lax.all_to_all(send_in, ('grp', 'ep'), split_axis=0, concat_axis=0, tiled...]
    all_gather x0 -> x1, blocking collectives: none -> 42.8 us  [body_ring(): tables = lax.all_gather(table, 'ep', axis=0)[sources]]
    dot_general x6 -> x45, matrix products: 34.6 us -> 66.8 us  [the longest x16 19.7 us: share_of(): lax.dot_general(spread[s], block, (((0,), (0,)), ((), ())), preferred_ele...]
    gather x4 -> x2, local copies, waits for them, and re-layouts: 31.6 us -> 1.85 us  [the longest x1 1.29 us: body_ring(): sources = order[(place + jnp.arange(chips, dtype=jnp.int32)) % chips]]
    ppermute x0 -> x31, starting transfers between devices: none -> 28 us  [the longest x28 27.9 us: ring_shift(): return lax.ppermute(array, 'ep', pairs)]
    all_to_all x3 -> x1, starting transfers between devices: 17.7 us -> 3.28 us  [body_ring(): lax.all_to_all(by_chip, 'ep', split_axis=0, concat_axis=0, tiled=True)]
  transfers between devices with their start and end apart: 3 -> 32, of which waited for: 3 -> 14; matrix products, arithmetic and copies ran while one was open for 7% -> 24% of each run, Pallas kernels for 0% -> 0%
where the time goes in v1:
time: 274 us; the launch traced here: 273 us
  waiting for transfers between devices  107 us (39%)
  matrix products  66.8 us (24%)
  blocking collectives  42.8 us (16%)
  starting transfers between devices  31.2 us (11%)
  local copies, waits for them, and re-layouts  14.1 us (5%)
  other arithmetic  9.09 us (3%)
    ppermute x28, waiting for transfers between devices, ring_shift(): return lax.ppermute(array, 'ep', pairs)  107 us
    all_gather x1, blocking collectives, body_ring(): tables = lax.all_gather(table, 'ep', axis=0)[sources]  42.8 us
    ppermute x28, starting transfers between devices, ring_shift(): return lax.ppermute(array, 'ep', pairs)  27.9 us
    dot_general x16, matrix products, share_of(): lax.dot_general(spread[s], block, (((0,), (0,)), ((), ())), preferred_ele...  19.7 us
    dot_general x2, matrix products, body_ring(): lax.dot_general(d_pre_gate, gate_mats[e], last, preferred_element_type=f32)  7.26 us
    dot_general x2, matrix products, body_ring(): lax.dot_general(rows_grad[e], down_mats[e], last, preferred_element_type=...  7.24 us
    dot_general x2, matrix products, body_ring(): jnp.dot(rows_in[e], up_mats[e], preferred_element_type=f32)  7.17 us
    dot_general x2, matrix products, body_ring(): lax.dot_general(d_pre_up, up_mats[e], last, preferred_element_type=f32)  6.94 us
  transfers between devices with their start and end apart: 32, of which 14 were waited for; matrix products, arithmetic and copies ran while one was open for 24% of the time, Pallas kernels for 0%

profile of v1, /device:TPU:0, one launch (start us, length us, event | category | flops | bytes accessed | tf_op | source)
XLA Modules:
  0.0 272.6 jit_solution(2762753449166359106)
XLA Ops:
  0.6 3.1 %collective-permute-start.3 = (bf16[128,2048]{1,0:T(8,128)(2,1)}, bf16[128,2048]{1,0:T(8,128)(2,1)S(1)}, u32[]{:S(2)}, u32[]{:S(2)}) collective-permute-start(bf16[128,2048]{1,0:T(8,128)(2,1)} %param.8), channel_id=1, source_target_pairs={{0,2},{2,4},{4,6},{6,7},{7,5},{5,3},{3,1},{1,0},{8,10},{10,12},{12... | collective-permute-start | bytes 1572872 | tf_op jit(solution)/shard_map/ppermute | solution.py:93
  3.7 2.0 collective-permute-start.21
  11.0 42.8 %all-gather = f32[64,128]{1,0:T(8,128)S(1)} all-gather(f32[8,128]{1,0:T(8,128)S(1)} %maximum_bitcast_fusion), channel_id=2, replica_groups=mesh['rep'=2,'grp'=2,'ep'=8] {'ep'}, dimensions={0}, use_global_device_ids=true | all-gather | bytes 36864 | tf_op jit(solution)/shard_map/all_gather | solution.py:144
  58.5 2.1 collective-permute-start.1
  61.3 11.6 %collective-permute-done.1 = bf16[128,2048]{1,0:T(8,128)(2,1)S(1)} collective-permute-done((bf16[128,2048]{1,0:T(8,128)(2,1)S(1)}, bf16[128,2048]{1,0:T(8,128)(2,1)S(1)}, u32[]{:S(2)}, u32[]{:S(2)}) %collective-permute-start.1) | collective-permute-done | bytes 524320 | tf_op jit(solution)/shard_map/ppermute | solution.py:93
  72.9 1.7 collective-permute-start.18
  75.5 10.9 %collective-permute-done.18 = bf16[128,2048]{1,0:T(8,128)(2,1)S(1)} collective-permute-done((bf16[128,2048]{1,0:T(8,128)(2,1)S(1)}, bf16[128,2048]{1,0:T(8,128)(2,1)S(1)}, u32[]{:S(2)}, u32[]{:S(2)}) %collective-permute-start.18) | collective-permute-done | bytes 524320 | tf_op jit(solution)/shard_map/ppermute | solution.py:93
  86.5 1.4 collective-permute-start.2
  89.1 12.2 %collective-permute-done.2 = bf16[128,2048]{1,0:T(8,128)(2,1)S(1)} collective-permute-done((bf16[128,2048]{1,0:T(8,128)(2,1)S(1)}, bf16[128,2048]{1,0:T(8,128)(2,1)S(1)}, u32[]{:S(2)}, u32[]{:S(2)}) %collective-permute-start.2) | collective-permute-done | bytes 524320 | tf_op jit(solution)/shard_map/ppermute | solution.py:93
  101.7 8.7 %collective-permute-done.19 = bf16[128,2048]{1,0:T(8,128)(2,1)S(1)} collective-permute-done((bf16[128,2048]{1,0:T(8,128)(2,1)S(1)}, bf16[128,2048]{1,0:T(8,128)(2,1)S(1)}, u32[]{:S(2)}, u32[]{:S(2)}) %collective-permute-start.19) | collective-permute-done | bytes 524320 | tf_op jit(solution)/shard_map/ppermute | solution.py:93
  110.9 5.5 %collective-permute-done.23 = bf16[128,2048]{1,0:T(8,128)(2,1)S(1)} collective-permute-done((bf16[128,2048]{1,0:T(8,128)(2,1)S(1)}, bf16[128,2048]{1,0:T(8,128)(2,1)S(1)}, u32[]{:S(2)}, u32[]{:S(2)}) %collective-permute-start.23) | collective-permute-done | bytes 524320 | tf_op jit(solution)/shard_map/ppermute | solution.py:93
  116.4 1.4 collective-permute-start.20
  118.1 9.2 %collective-permute-done.6 = bf16[128,2048]{1,0:T(8,128)(2,1)S(1)} collective-permute-done((bf16[128,2048]{1,0:T(8,128)(2,1)S(1)}, bf16[128,2048]{1,0:T(8,128)(2,1)S(1)}, u32[]{:S(2)}, u32[]{:S(2)}) %collective-permute-start.6) | collective-permute-done | bytes 524320 | tf_op jit(solution)/shard_map/ppermute | solution.py:93
  127.7 1.5 fusion.118
  129.2 3.3 %fusion.109 = f32[384,768]{1,0:T(8,128)S(1)} fusion(bf16[384,2048]{1,0:T(8,128)(2,1)S(1)} %bitcast.168, bf16[1,2048,768]{2,1,0:T(8,128)(2,1)} %param.12), kind=kOutput, calls=%fused_computation.184 | convolution fusion | flops 1207959552 | bytes 5898240 | tf_op jit(solution)/shard_map/dot_general | solution.py:189
  133.3 3.9 %fusion.106 = f32[384,768]{1,0:T(8,128)S(1)} fusion(bf16[384,2048]{1,0:T(8,128)(2,1)S(1)} %bitcast.169, bf16[1,2048,768]{2,1,0:T(8,128)(2,1)} %param.13), kind=kOutput, calls=%fused_computation.181 | convolution fusion | flops 1207959552 | bytes 5898240 | tf_op jit(solution)/shard_map/dot_general | solution.py:190
  137.2 1.6 multiply_reduce_fusion.1
  138.9 3.9 %fusion.102 = f32[384,768]{1,0:T(8,128)S(1)} fusion(bf16[384,2048]{1,0:T(8,128)(2,1)} %bitcast.170, bf16[1,768,2048]{2,1,0:T(8,128)(2,1)} %param.14), kind=kOutput, calls=%fused_computation.177 | convolution fusion | flops 1207959552 | bytes 5898240 | tf_op jit(solution)/shard_map/dot_general | solution.py:204
  142.9 3.6 %fusion.3 = f32[384,2048]{1,0:T(8,128)S(1)} fusion(f32[384,768]{1,0:T(8,128)S(1)} %copy-done.35, f32[384,768]{1,0:T(8,128)S(1)} %fusion.102, f32[384,768]{1,0:T(8,128)S(1)} %copy-done.37, bf16[1,2048,768]{2,1,0:T(8,128)(2,1)} %param.12), kind=kOutput, calls=%fused_computation.53 | convolution fusion | flops 1210908672 | bytes 9830400 | tf_op jit(solution)/shard_map/dot_general | solution.py:208
  146.5 3.4 %add_convert_fusion.1 = bf16[384,2048]{1,0:T(8,128)(2,1)S(1)} fusion(f32[384,2048]{1,0:T(8,128)S(1)} %fusion.3, f32[384,768]{1,0:T(8,128)S(1)} %fusion.102, f32[384,768]{1,0:T(8,128)S(1)} %copy-done.35, bf16[1,2048,768]{2,1,0:T(8,128)(2,1)} %param.13), kind=kOutput, calls=%fused_computation.6 | convolution fusion | flops 1211301888 | bytes 10223616 | tf_op jit(solution)/shard_map/dot_general | solution.py:209
  151.7 3.3 %fusion.127 = f32[384,768]{1,0:T(8,128)S(1)} fusion(bf16[384,2048]{1,0:T(8,128)(2,1)S(1)} %bitcast.166, bf16[2048,768]{1,0:T(8,128)(2,1)} %collective-permute-done.8), kind=kOutput, calls=%fused_computation.202 | convolution fusion | flops 1207959552 | bytes 5898240 | tf_op jit(solution)/shard_map/dot_general | solution.py:190
  155.0 3.3 %fusion.126 = f32[384,768]{1,0:T(8,128)S(1)} fusion(bf16[384,2048]{1,0:T(8,128)(2,1)S(1)} %bitcast.167, bf16[2048,768]{1,0:T(8,128)(2,1)} %collective-permute-done.7), kind=kOutput, calls=%fused_computation.201 | convolution fusion | flops 1207959552 | bytes 5898240 | tf_op jit(solution)/shard_map/dot_general | solution.py:189
  158.3 3.3 %fusion.128 = f32[384,768]{1,0:T(8,128)S(1)} fusion(bf16[384,2048]{1,0:T(8,128)(2,1)S(1)} %bitcast.165, bf16[768,2048]{1,0:T(8,128)(2,1)} %collective-permute-done.9), kind=kOutput, calls=%fused_computation.203 | convolution fusion | flops 1207959552 | bytes 5898240 | tf_op jit(solution)/shard_map/dot_general | solution.py:204
  161.6 3.6 %fusion.4 = f32[384,2048]{1,0:T(8,128)S(1)} fusion(bf16[2048,768]{1,0:T(8,128)(2,1)} %collective-permute-done.8, f32[384,768]{1,0:T(8,128)S(1)} %fusion.128, f32[384,768]{1,0:T(8,128)S(1)} %fusion.126), kind=kOutput, calls=%fused_computation.54 | convolution fusion | flops 1209729024 | bytes 8650752 | tf_op jit(solution)/shard_map/dot_general | solution.py:209
  165.2 3.6 %add_convert_fusion = bf16[384,2048]{1,0:T(8,128)(2,1)S(1)} fusion(f32[384,2048]{1,0:T(8,128)S(1)} %fusion.4, bf16[2048,768]{1,0:T(8,128)(2,1)} %collective-permute-done.7, f32[384,768]{1,0:T(8,128)S(1)} %fusion.126, f32[384,768]{1,0:T(8,128)S(1)} %fusion.128, f32[384,768]{1,0:T(8,128)S(1)} %fusion.127), kind=kOutput, calls=%fused_computation.5 | convolution fusion | flops 1212481536 | bytes 11403264 | tf_op jit(solution)/shard_map/dot_general | solution.py:208
  170.0 5.1 %multiply_reduce_fusion = (f32[384]{0:T(512)}, bf16[384,2048]{1,0:T(8,128)(2,1)}) fusion(bf16[8,1,48,2048]{3,2,0,1:T(8,128)(2,1)S(1)} %get-tuple-element.6, bf16[768,2048]{1,0:T(8,128)(2,1)} %collective-permute-done.9, f32[384,768]{1,0:T(8,128)S(1)} %fusion.127, f32[384,768]{1,0:T(8,128)S(1)} %fusion.126), kind=kOutput, calls=%fused_computation.3 | convolution fusion | flops 1213660800 | bytes 8652288 | tf_op jit(solution)/shard_map/dot_general | solution.py:194
  175.1 1.5 stack_reshape.7
  178.6 2.0 scatter_fusion
  180.7 3.3 %all-to-all-start = ((f32[8,2,128]{2,1,0:T(2,128)}), f32[8,2,128]{2,1,0:T(2,128)S(1)}, u32[]{:S(2)}, u32[]{:S(2)}) async-start(f32[8,2,128]{2,1,0:T(2,128)} %scatter_fusion), calls=%async_computation | async-start | bytes 16384 | tf_op jit(solution)/shard_map/all_to_all | solution.py:221
  183.9 2.1 convolution_convert_fusion.3
  186.0 1.9 collective-permute-start.24
  187.9 2.1 convolution_convert_fusion.2
  192.4 1.9 collective-permute-start.10
  203.5 1.7 collective-permute-done.28
  205.2 1.6 add_convert_fusion.4
  208.6 1.8 collective-permute-start.25
  210.3 6.1 %collective-permute-done.10 = bf16[128,2048]{1,0:T(8,128)(2,1)} collective-permute-done((bf16[128,2048]{1,0:T(8,128)(2,1)}, bf16[128,2048]{1,0:T(8,128)(2,1)}, u32[]{:S(2)}, u32[]{:S(2)}) %collective-permute-start.10) | collective-permute-done | bytes 524320 | tf_op jit(solution)/shard_map/ppermute | solution.py:93
  218.0 1.4 add_convert_fusion.10
  219.5 2.0 collective-permute-start.15
  221.4 6.2 %collective-permute-done.29 = bf16[128,2048]{1,0:T(8,128)(2,1)S(1)} collective-permute-done((bf16[128,2048]{1,0:T(8,128)(2,1)S(1)}, bf16[128,2048]{1,0:T(8,128)(2,1)S(1)}, u32[]{:S(2)}, u32[]{:S(2)}) %collective-permute-start.29) | collective-permute-done | bytes 524320 | tf_op jit(solution)/shard_map/ppermute | solution.py:93
  228.0 2.0 collective-permute-start.26
  230.0 8.8 %collective-permute-done.11 = bf16[128,2048]{1,0:T(8,128)(2,1)S(1)} collective-permute-done((bf16[128,2048]{1,0:T(8,128)(2,1)S(1)}, bf16[128,2048]{1,0:T(8,128)(2,1)S(1)}, u32[]{:S(2)}, u32[]{:S(2)}) %collective-permute-start.11) | collective-permute-done | bytes 524320 | tf_op jit(solution)/shard_map/ppermute | solution.py:93
  239.2 2.0 collective-permute-start.16
  241.2 4.8 %collective-permute-done.26 = bf16[128,2048]{1,0:T(8,128)(2,1)S(1)} collective-permute-done((bf16[128,2048]{1,0:T(8,128)(2,1)S(1)}, bf16[128,2048]{1,0:T(8,128)(2,1)S(1)}, u32[]{:S(2)}, u32[]{:S(2)}) %collective-permute-start.26) | collective-permute-done | bytes 524320 | tf_op jit(solution)/shard_map/ppermute | solution.py:93
  246.1 2.0 collective-permute-start.27
  248.1 11.3 %collective-permute-done.12 = bf16[128,2048]{1,0:T(8,128)(2,1)S(1)} collective-permute-done((bf16[128,2048]{1,0:T(8,128)(2,1)S(1)}, bf16[128,2048]{1,0:T(8,128)(2,1)S(1)}, u32[]{:S(2)}, u32[]{:S(2)}) %collective-permute-start.12) | collective-permute-done | bytes 524320 | tf_op jit(solution)/shard_map/ppermute | solution.py:93
  260.6 6.6 %collective-permute-done.27 = bf16[128,2048]{1,0:T(8,128)(2,1)S(1)} collective-permute-done((bf16[128,2048]{1,0:T(8,128)(2,1)S(1)}, bf16[128,2048]{1,0:T(8,128)(2,1)S(1)}, u32[]{:S(2)}, u32[]{:S(2)}) %collective-permute-start.27) | collective-permute-done | bytes 524320 | tf_op jit(solution)/shard_map/ppermute | solution.py:93
  268.2 3.4 %collective-permute-done.13 = bf16[128,2048]{1,0:T(8,128)(2,1)S(1)} collective-permute-done((bf16[128,2048]{1,0:T(8,128)(2,1)S(1)}, bf16[128,2048]{1,0:T(8,128)(2,1)S(1)}, u32[]{:S(2)}, u32[]{:S(2)}) %collective-permute-start.13) | collective-permute-done | bytes 524320 | tf_op jit(solution)/shard_map/ppermute | solution.py:93
  (200 shorter events, 38.7 us)
Async XLA Ops:
  0.6 55.4 %copy-start.20 = (bf16[128,2048]{1,0:T(8,128)(2,1)S(1)}, bf16[128,2048]{1,0:T(8,128)(2,1)}, u32[]{:S(2)}) copy-start(bf16[128,2048]{1,0:T(8,128)(2,1)} %param.8) | copy-start | bytes 1572868
  0.6 57.2 %collective-permute-start.3 = (bf16[128,2048]{1,0:T(8,128)(2,1)}, bf16[128,2048]{1,0:T(8,128)(2,1)S(1)}, u32[]{:S(2)}, u32[]{:S(2)}) collective-permute-start(bf16[128,2048]{1,0:T(8,128)(2,1)} %param.8), channel_id=1, source_target_pairs={{0,2},{2,4},{4,6},{6,7},{7,5},{5,3},{3,1},{1,0},{8,10},{10,12},{12... | collective-permute-start | bytes 1572872 | tf_op jit(solution)/shard_map/ppermute | solution.py:93
  3.7 54.4 %collective-permute-start = (bf16[128,2048]{1,0:T(8,128)(2,1)}, bf16[128,2048]{1,0:T(8,128)(2,1)S(1)}, u32[]{:S(2)}, u32[]{:S(2)}) collective-permute-start(bf16[128,2048]{1,0:T(8,128)(2,1)} %param.8), channel_id=1, source_target_pairs={{0,1},{2,0},{4,2},{6,4},{7,6},{5,7},{3,5},{1,3},{8,9},{10,8},{12,1... | collective-permute-start | bytes 1572872 | tf_op jit(solution)/shard_map/ppermute | solution.py:93
  3.7 54.8 %collective-permute-start.21 = (bf16[128,2048]{1,0:T(8,128)(2,1)}, bf16[128,2048]{1,0:T(8,128)(2,1)S(1)}, u32[]{:S(2)}, u32[]{:S(2)}) collective-permute-start(bf16[128,2048]{1,0:T(8,128)(2,1)} %param.9), channel_id=1, source_target_pairs={{0,2},{2,4},{4,6},{6,7},{7,5},{5,3},{3,1},{1,0},{8,10},{10,12},{12... | collective-permute-start | bytes 1572872 | tf_op jit(solution)/shard_map/ppermute | solution.py:93
  5.7 55.1 %collective-permute-start.17 = (bf16[128,2048]{1,0:T(8,128)(2,1)}, bf16[128,2048]{1,0:T(8,128)(2,1)S(1)}, u32[]{:S(2)}, u32[]{:S(2)}) collective-permute-start(bf16[128,2048]{1,0:T(8,128)(2,1)} %param.9), channel_id=1, source_target_pairs={{0,1},{2,0},{4,2},{6,4},{7,6},{5,7},{3,5},{1,3},{8,9},{10,8},{12,1... | collective-permute-start | bytes 1572872 | tf_op jit(solution)/shard_map/ppermute | solution.py:93
  5.7 152.5 %collective-permute-start.9 = (bf16[768,2048]{1,0:T(8,128)(2,1)}, bf16[768,2048]{1,0:T(8,128)(2,1)}, u32[]{:S(2)}, u32[]{:S(2)}) collective-permute-start(bf16[768,2048]{1,0:T(8,128)(2,1)} %bitcast.206), channel_id=1, source_target_pairs={{0,8},{8,0},{1,9},{9,1},{2,10},{10,2},{3,11},{11,3},{4,12},{12,4},... | collective-permute-start | bytes 9437192 | tf_op jit(solution)/shard_map/ppermute | solution.py:120
  57.9 93.1 %collective-permute-start.8 = (bf16[2048,768]{1,0:T(8,128)(2,1)}, bf16[2048,768]{1,0:T(8,128)(2,1)}, u32[]{:S(2)}, u32[]{:S(2)}) collective-permute-start(bf16[2048,768]{1,0:T(8,128)(2,1)} %bitcast.27), channel_id=1, source_target_pairs={{0,8},{8,0},{1,9},{9,1},{2,10},{10,2},{3,11},{11,3},{4,12},{12,4},... | collective-permute-start | bytes 9437192 | tf_op jit(solution)/shard_map/ppermute | solution.py:120
  58.2 16.8 %collective-permute-start.4 = (bf16[128,2048]{1,0:T(8,128)(2,1)S(1)}, bf16[128,2048]{1,0:T(8,128)(2,1)S(1)}, u32[]{:S(2)}, u32[]{:S(2)}) collective-permute-start(bf16[128,2048]{1,0:T(8,128)(2,1)S(1)} %collective-permute-done.3), channel_id=1, source_target_pairs={{0,2},{2,4},{4,6},{6,7},{7,5},{5,3},{3,1},{1,0},{8,10},{10,12},{12... | collective-permute-start | bytes 1572872 | tf_op jit(solution)/shard_map/ppermute | solution.py:93
  58.5 14.4 %collective-permute-start.1 = (bf16[128,2048]{1,0:T(8,128)(2,1)S(1)}, bf16[128,2048]{1,0:T(8,128)(2,1)S(1)}, u32[]{:S(2)}, u32[]{:S(2)}) collective-permute-start(bf16[128,2048]{1,0:T(8,128)(2,1)S(1)} %collective-permute-done), channel_id=1, source_target_pairs={{0,1},{2,0},{4,2},{6,4},{7,6},{5,7},{3,5},{1,3},{8,9},{10,8},{12,1... | collective-permute-start | bytes 1572872 | tf_op jit(solution)/shard_map/ppermute | solution.py:93
  61.2 27.0 %collective-permute-start.22 = (bf16[128,2048]{1,0:T(8,128)(2,1)S(1)}, bf16[128,2048]{1,0:T(8,128)(2,1)S(1)}, u32[]{:S(2)}, u32[]{:S(2)}) collective-permute-start(bf16[128,2048]{1,0:T(8,128)(2,1)S(1)} %collective-permute-done.21), channel_id=1, source_target_pairs={{0,2},{2,4},{4,6},{6,7},{7,5},{5,3},{3,1},{1,0},{8,10},{10,12},{12... | collective-permute-start | bytes 1572872 | tf_op jit(solution)/shard_map/ppermute | solution.py:93
  72.9 13.6 %collective-permute-start.18 = (bf16[128,2048]{1,0:T(8,128)(2,1)S(1)}, bf16[128,2048]{1,0:T(8,128)(2,1)S(1)}, u32[]{:S(2)}, u32[]{:S(2)}) collective-permute-start(bf16[128,2048]{1,0:T(8,128)(2,1)S(1)} %collective-permute-done.17), channel_id=1, source_target_pairs={{0,1},{2,0},{4,2},{6,4},{7,6},{5,7},{3,5},{1,3},{8,9},{10,8},{12,1... | collective-permute-start | bytes 1572872 | tf_op jit(solution)/shard_map/ppermute | solution.py:93
  74.9 26.7 %collective-permute-start.5 = (bf16[128,2048]{1,0:T(8,128)(2,1)S(1)}, bf16[128,2048]{1,0:T(8,128)(2,1)S(1)}, u32[]{:S(2)}, u32[]{:S(2)}) collective-permute-start(bf16[128,2048]{1,0:T(8,128)(2,1)S(1)} %collective-permute-done.4), channel_id=1, source_target_pairs={{0,2},{2,4},{4,6},{6,7},{7,5},{5,3},{3,1},{1,0},{8,10},{10,12},{12... | collective-permute-start | bytes 1572872 | tf_op jit(solution)/shard_map/ppermute | solution.py:93
  86.5 14.9 %collective-permute-start.2 = (bf16[128,2048]{1,0:T(8,128)(2,1)S(1)}, bf16[128,2048]{1,0:T(8,128)(2,1)S(1)}, u32[]{:S(2)}, u32[]{:S(2)}) collective-permute-start(bf16[128,2048]{1,0:T(8,128)(2,1)S(1)} %collective-permute-done.1), channel_id=1, source_target_pairs={{0,1},{2,0},{4,2},{6,4},{7,6},{5,7},{3,5},{1,3},{8,9},{10,8},{12,1... | collective-permute-start | bytes 1572872 | tf_op jit(solution)/shard_map/ppermute | solution.py:93
  88.2 22.2 %collective-permute-start.19 = (bf16[128,2048]{1,0:T(8,128)(2,1)S(1)}, bf16[128,2048]{1,0:T(8,128)(2,1)S(1)}, u32[]{:S(2)}, u32[]{:S(2)}) collective-permute-start(bf16[128,2048]{1,0:T(8,128)(2,1)S(1)} %collective-permute-done.18), channel_id=1, source_target_pairs={{0,1},{2,0},{4,2},{6,4},{7,6},{5,7},{3,5},{1,3},{8,9},{10,8},{12,1... | collective-permute-start | bytes 1572872 | tf_op jit(solution)/shard_map/ppermute | solution.py:93
  101.3 53.7 %collective-permute-start.7 = (bf16[2048,768]{1,0:T(8,128)(2,1)}, bf16[2048,768]{1,0:T(8,128)(2,1)}, u32[]{:S(2)}, u32[]{:S(2)}) collective-permute-start(bf16[2048,768]{1,0:T(8,128)(2,1)} %bitcast.26), channel_id=1, source_target_pairs={{0,8},{8,0},{1,9},{9,1},{2,10},{10,2},{3,11},{11,3},{4,12},{12,4},... | collective-permute-start | bytes 9437192 | tf_op jit(solution)/shard_map/ppermute | solution.py:120
  101.6 14.8 %collective-permute-start.23 = (bf16[128,2048]{1,0:T(8,128)(2,1)S(1)}, bf16[128,2048]{1,0:T(8,128)(2,1)S(1)}, u32[]{:S(2)}, u32[]{:S(2)}) collective-permute-start(bf16[128,2048]{1,0:T(8,128)(2,1)S(1)} %collective-permute-done.22), channel_id=1, source_target_pairs={{0,2},{2,4},{4,6},{6,7},{7,5},{5,3},{3,1},{1,0},{8,10},{10,12},{12... | collective-permute-start | bytes 1572872 | tf_op jit(solution)/shard_map/ppermute | solution.py:93
  110.4 16.9 %collective-permute-start.6 = (bf16[128,2048]{1,0:T(8,128)(2,1)S(1)}, bf16[128,2048]{1,0:T(8,128)(2,1)S(1)}, u32[]{:S(2)}, u32[]{:S(2)}) collective-permute-start(bf16[128,2048]{1,0:T(8,128)(2,1)S(1)} %collective-permute-done.5), channel_id=1, source_target_pairs={{0,2},{2,4},{4,6},{6,7},{7,5},{5,3},{3,1},{1,0},{8,10},{10,12},{12... | collective-permute-start | bytes 1572872 | tf_op jit(solution)/shard_map/ppermute | solution.py:93
  116.4 16.1 %collective-permute-start.20 = (bf16[128,2048]{1,0:T(8,128)(2,1)S(1)}, bf16[128,2048]{1,0:T(8,128)(2,1)S(1)}, u32[]{:S(2)}, u32[]{:S(2)}) collective-permute-start(bf16[128,2048]{1,0:T(8,128)(2,1)S(1)} %collective-permute-done.19), channel_id=1, source_target_pairs={{0,1},{2,0},{4,2},{6,4},{7,6},{5,7},{3,5},{1,3},{8,9},{10,8},{12,1... | collective-permute-start | bytes 1572872 | tf_op jit(solution)/shard_map/ppermute | solution.py:93
  132.5 4.7 %copy-start.34 = (f32[384,768]{1,0:T(8,128)}, f32[384,768]{1,0:T(8,128)S(1)}, u32[]{:S(2)}) copy-start(f32[384,768]{1,0:T(8,128)S(1)} %fusion.109) | copy-start | bytes 3538948
  175.1 15.0 %copy-start.6 = (bf16[384,2048]{1,0:T(8,128)(2,1)S(1)}, bf16[384,2048]{1,0:T(8,128)(2,1)}, u32[]{:S(2)}) copy-start(bf16[384,2048]{1,0:T(8,128)(2,1)} %get-tuple-element.60) | copy-start | bytes 4718596
  180.7 22.8 %all-to-all-start = ((f32[8,2,128]{2,1,0:T(2,128)}), f32[8,2,128]{2,1,0:T(2,128)S(1)}, u32[]{:S(2)}, u32[]{:S(2)}) async-start(f32[8,2,128]{2,1,0:T(2,128)} %scatter_fusion), calls=%async_computation | async-start | bytes 16384 | tf_op jit(solution)/shard_map/all_to_all | solution.py:221
  186.0 21.1 %collective-permute-start.24 = (bf16[128,2048]{1,0:T(8,128)(2,1)}, bf16[128,2048]{1,0:T(8,128)(2,1)}, u32[]{:S(2)}, u32[]{:S(2)}) collective-permute-start(bf16[128,2048]{1,0:T(8,128)(2,1)} %convolution_convert_fusion.3), channel_id=1, source_target_pairs={{0,1},{2,0},{4,2},{6,4},{7,6},{5,7},{3,5},{1,3},{8,9},{10,8},{12,1... | collective-permute-start | bytes 1572872 | tf_op jit(solution)/shard_map/ppermute | solution.py:93
  190.0 15.2 %collective-permute-start.28 = (bf16[128,2048]{1,0:T(8,128)(2,1)}, bf16[128,2048]{1,0:T(8,128)(2,1)}, u32[]{:S(2)}, u32[]{:S(2)}) collective-permute-start(bf16[128,2048]{1,0:T(8,128)(2,1)} %convolution_convert_fusion.2), channel_id=1, source_target_pairs={{0,2},{2,4},{4,6},{6,7},{7,5},{5,3},{3,1},{1,0},{8,10},{10,12},{12... | collective-permute-start | bytes 1572872 | tf_op jit(solution)/shard_map/ppermute | solution.py:93
  191.3 4.3 %copy-start.19 = (bf16[48,2048]{1,0:T(8,128)(2,1)S(1)}, bf16[48,2048]{1,0:T(8,128)(2,1)}, u32[]{:S(2)}) copy-start(bf16[48,2048]{1,0:T(8,128)(2,1)} %get-tuple-element.23) | copy-start | bytes 589828
  191.3 4.3 %copy-start.28 = (bf16[1,2,48,128]{3,2,1,0:T(8,128)(2,1)S(1)}, bf16[1,2,48,128]{3,2,1,0:T(8,128)(2,1)}, u32[]{:S(2)}) copy-start(bf16[1,2,48,128]{3,2,1,0:T(8,128)(2,1)} %get-tuple-element.44) | copy-start | bytes 73732
  192.4 24.1 %collective-permute-start.10 = (bf16[128,2048]{1,0:T(8,128)(2,1)}, bf16[128,2048]{1,0:T(8,128)(2,1)}, u32[]{:S(2)}, u32[]{:S(2)}) collective-permute-start(bf16[128,2048]{1,0:T(8,128)(2,1)} %convolution_convert_fusion.5), channel_id=1, source_target_pairs={{0,2},{2,4},{4,6},{6,7},{7,5},{5,3},{3,1},{1,0},{8,10},{10,12},{12... | collective-permute-start | bytes 1572872 | tf_op jit(solution)/shard_map/ppermute | solution.py:93
  195.4 22.6 %collective-permute-start.14 = (bf16[128,2048]{1,0:T(8,128)(2,1)}, bf16[128,2048]{1,0:T(8,128)(2,1)}, u32[]{:S(2)}, u32[]{:S(2)}) collective-permute-start(bf16[128,2048]{1,0:T(8,128)(2,1)} %convolution_convert_fusion.4), channel_id=1, source_target_pairs={{0,1},{2,0},{4,2},{6,4},{7,6},{5,7},{3,5},{1,3},{8,9},{10,8},{12,1... | collective-permute-start | bytes 1572872 | tf_op jit(solution)/shard_map/ppermute | solution.py:93
  203.5 13.0 %copy-start.8 = (bf16[48,2048]{1,0:T(8,128)(2,1)S(1)}, bf16[48,2048]{1,0:T(8,128)(2,1)}, u32[]{:S(2)}) copy-start(bf16[48,2048]{1,0:T(8,128)(2,1)} %get-tuple-element.25) | copy-start | bytes 589828
  203.5 13.0 %copy-start.9 = (bf16[48,2048]{1,0:T(8,128)(2,1)S(1)}, bf16[48,2048]{1,0:T(8,128)(2,1)}, u32[]{:S(2)}) copy-start(bf16[48,2048]{1,0:T(8,128)(2,1)} %get-tuple-element.70) | copy-start | bytes 589828
  203.5 13.0 %copy-start.23 = (bf16[1,2,48,128]{3,2,1,0:T(8,128)(2,1)S(1)}, bf16[1,2,48,128]{3,2,1,0:T(8,128)(2,1)}, u32[]{:S(2)}) copy-start(bf16[1,2,48,128]{3,2,1,0:T(8,128)(2,1)} %get-tuple-element.41) | copy-start | bytes 73732
  206.8 11.2 %copy-start.22 = (bf16[1,2,48,128]{3,2,1,0:T(8,128)(2,1)S(1)}, bf16[1,2,48,128]{3,2,1,0:T(8,128)(2,1)}, u32[]{:S(2)}) copy-start(bf16[1,2,48,128]{3,2,1,0:T(8,128)(2,1)} %get-tuple-element.43) | copy-start | bytes 73732
  206.8 20.8 %collective-permute-start.29 = (bf16[128,2048]{1,0:T(8,128)(2,1)S(1)}, bf16[128,2048]{1,0:T(8,128)(2,1)S(1)}, u32[]{:S(2)}, u32[]{:S(2)}) collective-permute-start(bf16[128,2048]{1,0:T(8,128)(2,1)S(1)} %add_convert_fusion.4), channel_id=1, source_target_pairs={{0,2},{2,4},{4,6},{6,7},{7,5},{5,3},{3,1},{1,0},{8,10},{10,12},{12... | collective-permute-start | bytes 1572872 | tf_op jit(solution)/shard_map/ppermute | solution.py:93
  208.5 19.0 %copy-start.3 = (f32[128,2048]{1,0:T(8,128)S(1)}, f32[128,2048]{1,0:T(8,128)}, u32[]{:S(2)}) copy-start(f32[128,2048]{1,0:T(8,128)} %fusion.62) | copy-start | bytes 3145732
  208.6 19.3 %collective-permute-start.25 = (bf16[128,2048]{1,0:T(8,128)(2,1)S(1)}, bf16[128,2048]{1,0:T(8,128)(2,1)S(1)}, u32[]{:S(2)}, u32[]{:S(2)}) collective-permute-start(bf16[128,2048]{1,0:T(8,128)(2,1)S(1)} %add_convert_fusion.7), channel_id=1, source_target_pairs={{0,1},{2,0},{4,2},{6,4},{7,6},{5,7},{3,5},{1,3},{8,9},{10,8},{12,1... | collective-permute-start | bytes 1572872 | tf_op jit(solution)/shard_map/ppermute | solution.py:93
  217.8 21.0 %collective-permute-start.11 = (bf16[128,2048]{1,0:T(8,128)(2,1)S(1)}, bf16[128,2048]{1,0:T(8,128)(2,1)S(1)}, u32[]{:S(2)}, u32[]{:S(2)}) collective-permute-start(bf16[128,2048]{1,0:T(8,128)(2,1)S(1)} %add_convert_fusion.13), channel_id=1, source_target_pairs={{0,2},{2,4},{4,6},{6,7},{7,5},{5,3},{3,1},{1,0},{8,10},{10,12},{12... | collective-permute-start | bytes 1572872 | tf_op jit(solution)/shard_map/ppermute | solution.py:93
  218.0 9.9 %copy-start.4 = (f32[128,2048]{1,0:T(8,128)S(1)}, f32[128,2048]{1,0:T(8,128)}, u32[]{:S(2)}) copy-start(f32[128,2048]{1,0:T(8,128)} %fusion.49) | copy-start | bytes 3145732
  219.5 19.6 %collective-permute-start.15 = (bf16[128,2048]{1,0:T(8,128)(2,1)S(1)}, bf16[128,2048]{1,0:T(8,128)(2,1)S(1)}, u32[]{:S(2)}, u32[]{:S(2)}) collective-permute-start(bf16[128,2048]{1,0:T(8,128)(2,1)S(1)} %add_convert_fusion.10), channel_id=1, source_target_pairs={{0,1},{2,0},{4,2},{6,4},{7,6},{5,7},{3,5},{1,3},{8,9},{10,8},{12,1... | collective-permute-start | bytes 1572872 | tf_op jit(solution)/shard_map/ppermute | solution.py:93
  227.7 11.1 %copy-start.2 = (f32[128,2048]{1,0:T(8,128)S(1)}, f32[128,2048]{1,0:T(8,128)}, u32[]{:S(2)}) copy-start(f32[128,2048]{1,0:T(8,128)} %fusion.15) | copy-start | bytes 3145732
  227.7 32.9 %collective-permute-start.30 = (bf16[128,2048]{1,0:T(8,128)(2,1)S(1)}, bf16[128,2048]{1,0:T(8,128)(2,1)S(1)}, u32[]{:S(2)}, u32[]{:S(2)}) collective-permute-start(bf16[128,2048]{1,0:T(8,128)(2,1)S(1)} %add_convert_fusion.3), channel_id=1, source_target_pairs={{0,2},{2,4},{4,6},{6,7},{7,5},{5,3},{3,1},{1,0},{8,10},{10,12},{12... | collective-permute-start | bytes 1572872 | tf_op jit(solution)/shard_map/ppermute | solution.py:93
  228.0 11.1 %copy-start.1 = (f32[128,2048]{1,0:T(8,128)S(1)}, f32[128,2048]{1,0:T(8,128)}, u32[]{:S(2)}) copy-start(f32[128,2048]{1,0:T(8,128)} %fusion.28) | copy-start | bytes 3145732
  228.0 18.0 %collective-permute-start.26 = (bf16[128,2048]{1,0:T(8,128)(2,1)S(1)}, bf16[128,2048]{1,0:T(8,128)(2,1)S(1)}, u32[]{:S(2)}, u32[]{:S(2)}) collective-permute-start(bf16[128,2048]{1,0:T(8,128)(2,1)S(1)} %add_convert_fusion.6), channel_id=1, source_target_pairs={{0,1},{2,0},{4,2},{6,4},{7,6},{5,7},{3,5},{1,3},{8,9},{10,8},{12,1... | collective-permute-start | bytes 1572872 | tf_op jit(solution)/shard_map/ppermute | solution.py:93
  238.9 7.1 %copy-start = (f32[128,2048]{1,0:T(8,128)S(1)}, f32[128,2048]{1,0:T(8,128)}, u32[]{:S(2)}) copy-start(f32[128,2048]{1,0:T(8,128)} %fusion.45) | copy-start | bytes 3145732
  238.9 20.5 %collective-permute-start.12 = (bf16[128,2048]{1,0:T(8,128)(2,1)S(1)}, bf16[128,2048]{1,0:T(8,128)(2,1)S(1)}, u32[]{:S(2)}, u32[]{:S(2)}) collective-permute-start(bf16[128,2048]{1,0:T(8,128)(2,1)S(1)} %add_convert_fusion.12), channel_id=1, source_target_pairs={{0,2},{2,4},{4,6},{6,7},{7,5},{5,3},{3,1},{1,0},{8,10},{10,12},{12... | collective-permute-start | bytes 1572872 | tf_op jit(solution)/shard_map/ppermute | solution.py:93
  239.2 29.0 %collective-permute-start.16 = (bf16[128,2048]{1,0:T(8,128)(2,1)S(1)}, bf16[128,2048]{1,0:T(8,128)(2,1)S(1)}, u32[]{:S(2)}, u32[]{:S(2)}) collective-permute-start(bf16[128,2048]{1,0:T(8,128)(2,1)S(1)} %add_convert_fusion.9), channel_id=1, source_target_pairs={{0,1},{2,0},{4,2},{6,4},{7,6},{5,7},{3,5},{1,3},{8,9},{10,8},{12,1... | collective-permute-start | bytes 1572872 | tf_op jit(solution)/shard_map/ppermute | solution.py:93
  246.1 13.9 %copy-start.30 = (s32[128,4]{0,1:T(4,128)S(1)}, s32[128,4]{0,1:T(4,128)}, u32[]{:S(2)}) copy-start(s32[128,4]{0,1:T(4,128)} %param.10) | copy-start | bytes 6148
  246.1 13.9 %copy-start.31 = (s32[8,2]{0,1:T(2,128)S(1)}, s32[8,2]{0,1:T(2,128)}, u32[]{:S(2)}) copy-start(s32[8,2]{0,1:T(2,128)} %pad_add_fusion) | copy-start | bytes 196
  246.1 21.1 %collective-permute-start.27 = (bf16[128,2048]{1,0:T(8,128)(2,1)S(1)}, bf16[128,2048]{1,0:T(8,128)(2,1)S(1)}, u32[]{:S(2)}, u32[]{:S(2)}) collective-permute-start(bf16[128,2048]{1,0:T(8,128)(2,1)S(1)} %add_convert_fusion.5), channel_id=1, source_target_pairs={{0,1},{2,0},{4,2},{6,4},{7,6},{5,7},{3,5},{1,3},{8,9},{10,8},{12,1... | collective-permute-start | bytes 1572872 | tf_op jit(solution)/shard_map/ppermute | solution.py:93
  259.5 12.1 %collective-permute-start.13 = (bf16[128,2048]{1,0:T(8,128)(2,1)S(1)}, bf16[128,2048]{1,0:T(8,128)(2,1)S(1)}, u32[]{:S(2)}, u32[]{:S(2)}) collective-permute-start(bf16[128,2048]{1,0:T(8,128)(2,1)S(1)} %add_convert_fusion.11), channel_id=1, source_target_pairs={{0,2},{2,4},{4,6},{6,7},{7,5},{5,3},{3,1},{1,0},{8,10},{10,12},{12... | collective-permute-start | bytes 1572872 | tf_op jit(solution)/shard_map/ppermute | solution.py:93
  (22 other events, 55.0 us)

commit v2 on v1

--- a/solution.py
+++ b/solution.py
@@ -1,6 +1,8 @@
 import jax
 import jax.numpy as jnp
 from jax import lax
+from jax.experimental import pallas as pl
+from jax.experimental.pallas import tpu as pltpu
 from jax.sharding import PartitionSpec as P
 
 
@@ -104,16 +106,249 @@
     return [held[place] for place in range(count)]
 
 
-def ring_reduce(share_of, count, far_step):
+def after(array, *others):
+    for other in others:
+        array = array + other[:1, :1] * 0
+    return array
+
+
+def ring_reduce(share_of, count, far_step, first=(), seen=None):
     arrived = []
     for step in (far_step, -far_step):
         hops = count // 2 if step == far_step else (count - 1) // 2
         moving = None
         for hop in range(hops, 0, -1):
-            moving = ring_shift(share_of((step * hop) % count, moving), count, step)
+            share = share_of((step * hop) % count, moving)
+            if moving is None:
+                share = after(share, *first)
+            moving = ring_shift(share, count, step)
+            if seen is not None and hop == max(1, hops - 1):
+                seen.append(moving)
         arrived.append(moving)
     total = share_of(0, arrived[0], arrived[1])
     return total
+
+
+VMEM_LIMIT = 48 * 1024 * 1024
+LAST = (((1,), (1,)), ((), ()))
+
+
+def cut(size, most):
+    return max(w for w in range(128, most + 1, 128) if size % w == 0)
+
+
+def call_kernel(kernel, operands, kinds, outs, scratch, flops):
+    spaces = {"any": pl.ANY, "vmem": pltpu.VMEM}
+    return pl.pallas_call(
+        kernel,
+        out_shape=outs,
+        in_specs=[pl.BlockSpec(memory_space=spaces[k]) for k in kinds],
+        out_specs=[pl.BlockSpec(memory_space=pltpu.VMEM) for _ in outs],
+        scratch_shapes=scratch,
+        compiler_params=pltpu.CompilerParams(vmem_limit_bytes=VMEM_LIMIT),
+        cost_estimate=pl.CostEstimate(flops=flops, bytes_accessed=1 << 20, transcendentals=0),
+    )(*operands)
+
+
+def pack_rows(parts, packed):
+    half = parts[0].shape[0] // 2
+    for e in range(2):
+        for s, part in enumerate(parts):
+            packed[e, s * half : (s + 1) * half, :] = part[e * half : (e + 1) * half, :]
+
+
+def run_hidden(parts, gate_mats, up_mats):
+    count, rows, width = len(parts), parts[0].shape[0], parts[0].shape[1]
+    units = gate_mats[0].shape[1]
+    total = count * rows // 2
+    tile = cut(units, 256)
+    tiles = units // tile
+
+    def kernel(*refs):
+        part_refs, mats = refs[:count], refs[count : count + 4]
+        hidden_ref, slope_ref, act_ref, packed, held, sems = refs[count + 4 :]
+        copies = {}
+        for e in range(2):
+            for n in range(tiles):
+                for m in range(2):
+                    copies[e, n, m] = pltpu.make_async_copy(
+                        mats[2 * m + e].at[:, n * tile : (n + 1) * tile],
+                        held.at[e, n, m],
+                        sems.at[e, n, m],
+                    )
+                    copies[e, n, m].start()
+        pack_rows(part_refs, packed)
+        for e in range(2):
+            for n in range(tiles):
+                span = slice(n * tile, (n + 1) * tile)
+                copies[e, n, 0].wait()
+                gate = jnp.dot(packed[e], held[e, n, 0], preferred_element_type=jnp.float32)
+                copies[e, n, 1].wait()
+                up = jnp.dot(packed[e], held[e, n, 1], preferred_element_type=jnp.float32)
+                sigma = 1.0 / (1.0 + jnp.exp(-gate))
+                act = gate * sigma
+                hidden_ref[e, :, span] = (act * up).astype(jnp.bfloat16)
+                slope_ref[e, :, span] = up * sigma * (1.0 + gate * (1.0 - sigma))
+                act_ref[e, :, span] = act
+
+    return call_kernel(
+        kernel,
+        [*parts, *gate_mats, *up_mats],
+        ["vmem"] * count + ["any"] * 4,
+        [
+            jax.ShapeDtypeStruct((2, total, units), jnp.bfloat16),
+            jax.ShapeDtypeStruct((2, total, units), jnp.float32),
+            jax.ShapeDtypeStruct((2, total, units), jnp.float32),
+        ],
+        [
+            pltpu.VMEM((2, total, width), jnp.bfloat16),
+            pltpu.VMEM((2, tiles, 2, width, tile), jnp.bfloat16),
+            pltpu.SemaphoreType.DMA((2, tiles, 2)),
+        ],
+        8 * total * width * units,
+    )
+
+
+def run_down(hidden, down_mats, count):
+    _, total, units = hidden.shape
+    width = down_mats[0].shape[1]
+    half = total // count
+    tile = cut(width, 512)
+    tiles = width // tile
+
+    def kernel(hidden_ref, own_ref, other_ref, out_ref, held, sems):
+        copies = {}
+        for e, mat in enumerate((own_ref, other_ref)):
+            for n in range(tiles):
+                copies[e, n] = pltpu.make_async_copy(
+                    mat.at[:, n * tile : (n + 1) * tile], held.at[e, n], sems.at[e, n]
+                )
+                copies[e, n].start()
+        for e in range(2):
+            for n in range(tiles):
+                copies[e, n].wait()
+                out = jnp.dot(hidden_ref[e], held[e, n], preferred_element_type=jnp.float32)
+                out_ref[:, e * half : (e + 1) * half, n * tile : (n + 1) * tile] = (
+                    out.astype(jnp.bfloat16).reshape(count, half, tile)
+                )
+
+    return call_kernel(
+        kernel,
+        [hidden, *down_mats],
+        ["vmem", "any", "any"],
+        [jax.ShapeDtypeStruct((count, 2 * half, width), jnp.bfloat16)],
+        [
+            pltpu.VMEM((2, tiles, units, tile), jnp.bfloat16),
+            pltpu.SemaphoreType.DMA((2, tiles)),
+        ],
+        4 * total * width * units,
+    )[0]
+
+
+def run_d_hidden(parts, outputs, pick, slope, activated, down_mats):
+    count, rows, width = len(parts), parts[0].shape[0], parts[0].shape[1]
+    half = rows // 2
+    _, total, units = slope.shape
+    tile = cut(units, 256)
+    tiles = units // tile
+    tokens = pick.shape[2]
+
+    def kernel(*refs):
+        part_refs = refs[:count]
+        out_ref, pick_ref, slope_ref, act_ref, own_ref, other_ref = refs[count : count + 6]
+        d_gate_ref, d_up_ref, token_ref, packed, held, sems = refs[count + 6 :]
+        copies = {}
+        for e, mat in enumerate((own_ref, other_ref)):
+            for n in range(tiles):
+                copies[e, n] = pltpu.make_async_copy(
+                    mat.at[n * tile : (n + 1) * tile, :], held.at[e, n], sems.at[e, n]
+                )
+                copies[e, n].start()
+        pack_rows(part_refs, packed)
+        for e in range(2):
+            for n in range(tiles):
+                span = slice(n * tile, (n + 1) * tile)
+                copies[e, n].wait()
+                d_hidden = lax.dot_general(
+                    packed[e], held[e, n], LAST, preferred_element_type=jnp.float32
+                )
+                d_gate_ref[e, :, span] = (d_hidden * slope_ref[e, :, span]).astype(jnp.bfloat16)
+                d_up_ref[e, :, span] = (d_hidden * act_ref[e, :, span]).astype(jnp.bfloat16)
+        for s in range(count):
+            inner = jnp.sum(
+                part_refs[s][...].astype(jnp.float32) * out_ref[s].astype(jnp.float32),
+                axis=1,
+                keepdims=True,
+            )
+            spread = pick_ref[s].astype(jnp.float32) * inner
+            for e in range(2):
+                token_ref[s, e : e + 1, :] = jnp.sum(
+                    spread[e * half : (e + 1) * half], axis=0, keepdims=True
+                )
+
+    return call_kernel(
+        kernel,
+        [*parts, outputs, pick, slope, activated, *down_mats],
+        ["vmem"] * (count + 4) + ["any"] * 2,
+        [
+            jax.ShapeDtypeStruct((2, total, units), jnp.bfloat16),
+            jax.ShapeDtypeStruct((2, total, units), jnp.bfloat16),
+            jax.ShapeDtypeStruct((count, 2, tokens), jnp.float32),
+        ],
+        [
+            pltpu.VMEM((2, total, width), jnp.bfloat16),
+            pltpu.VMEM((2, tiles, tile, width), jnp.bfloat16),
+            pltpu.SemaphoreType.DMA((2, tiles)),
+        ],
+        4 * total * width * units,
+    )
+
+
+def run_d_copy(d_pre_gate, d_pre_up, gate_mats, up_mats, count):
+    _, total, units = d_pre_gate.shape
+    width = gate_mats[0].shape[0]
+    half = total // count
+    tile = cut(width, 512)
+    tiles = width // tile
+
+    def kernel(d_gate_ref, d_up_ref, *refs):
+        mats = refs[:4]
+        out_ref, held, sems = refs[4:]
+        copies = {}
+        for e in range(2):
+            for n in range(tiles):
+                for m in range(2):
+                    copies[e, n, m] = pltpu.make_async_copy(
+                        mats[2 * m + e].at[n * tile : (n + 1) * tile, :],
+                        held.at[e, n, m],
+                        sems.at[e, n, m],
+                    )
+                    copies[e, n, m].start()
+        for e in range(2):
+            for n in range(tiles):
+                copies[e, n, 0].wait()
+                out = lax.dot_general(
+                    d_gate_ref[e], held[e, n, 0], LAST, preferred_element_type=jnp.float32
+                )
+                copies[e, n, 1].wait()
+                out = out + lax.dot_general(
+                    d_up_ref[e], held[e, n, 1], LAST, preferred_element_type=jnp.float32
+                )
+                out_ref[:, e * half : (e + 1) * half, n * tile : (n + 1) * tile] = (
+                    out.astype(jnp.bfloat16).reshape(count, half, tile)
+                )
+
+    return call_kernel(
+        kernel,
+        [d_pre_gate, d_pre_up, *gate_mats, *up_mats],
+        ["vmem", "vmem"] + ["any"] * 4,
+        [jax.ShapeDtypeStruct((count, 2 * half, width), jnp.bfloat16)],
+        [
+            pltpu.VMEM((2, tiles, 2, tile, units), jnp.bfloat16),
+            pltpu.SemaphoreType.DMA((2, tiles, 2)),
+        ],
+        8 * total * width * units,
+    )[0]
 
 
 def swap_cores(array):
@@ -130,7 +365,10 @@
     f32, bf16 = jnp.float32, jnp.bfloat16
 
     in_shards = ring_gather(tokens, chips, 1)
-    grad_shards = ring_gather(cotangent, chips, -1)
+    late = min(2, (chips - 1) // 2)
+    grad_shards = ring_gather(
+        after(cotangent, in_shards[-late % chips], in_shards[late]), chips, -1
+    )
     gate_mats = (w_gate[0], swap_cores(w_gate[0]))
     up_mats = (w_up[0], swap_cores(w_up[0]))
     down_mats = (w_down[0], swap_cores(w_down[0]))
@@ -141,7 +379,8 @@
     place = jnp.argmax(order == chip).astype(jnp.int32)
     sources = order[(place + jnp.arange(chips, dtype=jnp.int32)) % chips]
     table = jnp.concatenate([routes.astype(f32), gates.astype(f32)], axis=1).T
-    tables = lax.all_gather(table, "ep", axis=0)[sources]
+    copies = jnp.broadcast_to(table[None], (chips,) + table.shape)
+    tables = lax.all_to_all(copies, "ep", split_axis=0, concat_axis=0, tiled=True)[sources]
     named = tables[:, :top_count].astype(jnp.int32)
     weights = tables[:, top_count:]
     mine = jnp.stack([core * chips + chip, (1 - core) * chips + chip])
@@ -163,20 +402,15 @@
     )
 
     def gather_rows(shards):
-        parts = [
+        return [
             jnp.dot(pick[s], shards[s], preferred_element_type=f32).astype(bf16)
             for s in range(chips)
         ]
-        stacked = jnp.stack(parts).reshape(chips, 2, capacity, width)
-        return [stacked[:, e].reshape(chips * capacity, width) for e in range(2)]
-
-    def scatter_rows(outputs):
-        blocks = [o.reshape(chips, capacity, width) for o in outputs]
-
+
+    def scatter_rows(blocks):
         def share_of(s, *partials):
-            block = jnp.concatenate([b[s] for b in blocks], axis=0)
             total = lax.dot_general(
-                spread[s], block, (((0,), (0,)), ((), ())), preferred_element_type=f32
+                spread[s], blocks[s], (((0,), (0,)), ((), ())), preferred_element_type=f32
             )
             for partial in partials:
                 if partial is not None:
@@ -186,37 +420,18 @@
         return share_of
 
     rows_in = gather_rows(in_shards)
-    pre_gate = [jnp.dot(rows_in[e], gate_mats[e], preferred_element_type=f32) for e in range(2)]
-    pre_up = [jnp.dot(rows_in[e], up_mats[e], preferred_element_type=f32) for e in range(2)]
-    activated = [jax.nn.silu(v) for v in pre_gate]
-    hidden = [(activated[e] * pre_up[e]).astype(bf16) for e in range(2)]
-    outputs = [
-        jnp.dot(hidden[e], down_mats[e], preferred_element_type=f32).astype(bf16)
-        for e in range(2)
-    ]
-    mixed = ring_reduce(scatter_rows(outputs), chips, 1)
+    hidden, slope, activated = run_hidden(rows_in, gate_mats, up_mats)
+    outputs = run_down(hidden, down_mats, chips)
+    seen = []
+    mixed = ring_reduce(scatter_rows(outputs), chips, 1, seen=seen)
 
     rows_grad = gather_rows(grad_shards)
-    last = (((1,), (1,)), ((), ()))
-    d_copies = []
-    inner = []
-    for e in range(2):
-        d_hidden = lax.dot_general(rows_grad[e], down_mats[e], last, preferred_element_type=f32)
-        sigma = jax.nn.sigmoid(pre_gate[e])
-        d_pre_gate = (d_hidden * pre_up[e] * sigma * (1.0 + pre_gate[e] * (1.0 - sigma))).astype(bf16)
-        d_pre_up = (d_hidden * activated[e]).astype(bf16)
-        d_copy = lax.dot_general(d_pre_gate, gate_mats[e], last, preferred_element_type=f32)
-        d_copy = d_copy + lax.dot_general(d_pre_up, up_mats[e], last, preferred_element_type=f32)
-        d_copies.append(d_copy.astype(bf16))
-        inner.append(
-            jnp.sum(rows_grad[e].astype(f32) * outputs[e].astype(f32), axis=1).reshape(
-                chips, capacity
-            )
-        )
-    d_tokens = ring_reduce(scatter_rows(d_copies), chips, -1)
-
-    inner = jnp.stack(inner, axis=1)
-    per_token = jnp.sum(jnp.where(picks, inner[:, :, :, None], 0.0), axis=2)
+    d_pre_gate, d_pre_up, per_token = run_d_hidden(
+        rows_grad, outputs, pick, slope, activated, down_mats
+    )
+    d_copies = run_d_copy(d_pre_gate, d_pre_up, gate_mats, up_mats, chips)
+    d_tokens = ring_reduce(scatter_rows(d_copies), chips, -1, first=seen)
+
     by_chip = jnp.zeros_like(per_token).at[sources].set(per_token)
     returned = lax.all_to_all(by_chip, "ep", split_axis=0, concat_axis=0, tiled=True)
     chip_ids = jnp.arange(chips, dtype=jnp.int32)

time: 274 us -> 216 us (0.79)
  matrix products: 66.8 us -> 19.9 us
  blocking collectives: 42.8 us -> 0 us
  Pallas kernels: 0 us -> 39.7 us
  waiting for transfers between devices: 107 us -> 92.9 us
  starting transfers between devices: 31.2 us -> 44 us
  local copies, waits for them, and re-layouts: 14.1 us -> 8.79 us
  other arithmetic: 9.09 us -> 4.61 us
  between operations: 1.56 us -> 5.22 us
    dot_general x28 -> x16, matrix products: 61.5 us -> 12.5 us  [share_of(): lax.dot_general(spread[s], blocks[s], (((0,), (0,)), ((), ())), preferred...]
    all_gather x1 -> x0, blocking collectives: 42.8 us -> none  [body_ring(): tables = lax.all_gather(table, 'ep', axis=0)[sources]]
    pallas_call x0 -> x4, Pallas kernels: none -> 39.7 us  [call_kernel(): pl.pallas_call(kernel, out_shape=outs, in_specs=[pl.BlockSpec(memory_spac...]
    ppermute x28, waiting for transfers between devices: 107 us -> 82.7 us  [ring_shift(): return lax.ppermute(array, 'ep', pairs)]
    all_to_all x1, waiting for transfers between devices: 0.01 us -> 6.44 us  [body_ring(): lax.all_to_all(by_chip, 'ep', split_axis=0, concat_axis=0, tiled=True)]
    all_to_all x0 -> x1, starting transfers between devices: none -> 6.25 us  [body_ring(): lax.all_to_all(copies, 'ep', split_axis=0, concat_axis=0, tiled=True)]
    ppermute x28, starting transfers between devices: 27.9 us -> 33.8 us  [ring_shift(): return lax.ppermute(array, 'ep', pairs)]
    all_to_all x0 -> x1, waiting for transfers between devices: none -> 3.75 us  [body_ring(): lax.all_to_all(copies, 'ep', split_axis=0, concat_axis=0, tiled=True)]
  transfers between devices with their start and end apart: 32 -> 33, of which waited for: 14 -> 16; matrix products, arithmetic and copies ran while one was open for 24% -> 13% of each run, Pallas kernels for 0% -> 18%
where the time goes in v2:
time: 216 us; the launch traced here: 215 us
  waiting for transfers between devices  92.9 us (43%)
  starting transfers between devices  44 us (20%)
  Pallas kernels  39.7 us (18%)
  matrix products  19.9 us (9%)
  local copies, waits for them, and re-layouts  8.79 us (4%)
  between operations  5.22 us (2%)
  other arithmetic  4.61 us (2%)
    ppermute x28, waiting for transfers between devices, ring_shift(): return lax.ppermute(array, 'ep', pairs)  82.7 us
    pallas_call x4, Pallas kernels, call_kernel(): pl.pallas_call(kernel, out_shape=outs, in_specs=[pl.BlockSpec(memory_spac...  39.7 us
    ppermute x28, starting transfers between devices, ring_shift(): return lax.ppermute(array, 'ep', pairs)  33.8 us
    dot_general x16, matrix products, share_of(): lax.dot_general(spread[s], blocks[s], (((0,), (0,)), ((), ())), preferred...  12.5 us
    dot_general x16, matrix products, gather_rows(): jnp.dot(pick[s], shards[s], preferred_element_type=f32).astype(bf16)  7.26 us
    all_to_all x1, waiting for transfers between devices, body_ring(): lax.all_to_all(by_chip, 'ep', split_axis=0, concat_axis=0, tiled=True)  6.44 us
    all_to_all x1, starting transfers between devices, body_ring(): lax.all_to_all(copies, 'ep', split_axis=0, concat_axis=0, tiled=True)  6.25 us
  transfers between devices with their start and end apart: 33, of which 16 were waited for; matrix products, arithmetic and copies ran while one was open for 13% of the time, Pallas kernels for 18%

profile of v2, /device:TPU:0, one launch (start us, length us, event | category | flops | bytes accessed | tf_op | source)
XLA Modules:
  0.0 215.1 jit_solution(3741641380676701696)
XLA Ops:
  0.6 3.1 %collective-permute-start.3 = (bf16[128,2048]{1,0:T(8,128)(2,1)}, bf16[128,2048]{1,0:T(8,128)(2,1)}, u32[]{:S(2)}, u32[]{:S(2)}) collective-permute-start(bf16[128,2048]{1,0:T(8,128)(2,1)} %param.8), channel_id=1, source_target_pairs={{0,2},{2,4},{4,6},{6,7},{7,5},{5,3},{3,1},{1,0},{8,10},{10,12},{12... | collective-permute-start | bytes 1572872 | tf_op jit(solution)/shard_map/ppermute | solution.py:95
  5.7 6.3 %all-to-all-start = ((f32[8,8,128]{2,1,0:T(8,128)}), f32[8,8,128]{2,1,0:T(8,128)S(1)}, u32[]{:S(2)}, u32[]{:S(2)}) async-start(f32[8,8,128]{2,1,0:T(8,128)} %broadcast_in_dim.34), calls=%async_computation | async-start | bytes 65536 | tf_op jit(solution)/shard_map/all_to_all | solution.py:383
  12.5 1.3 compare_reduce_fusion.1
  14.5 1.3 gather_fusion
  16.0 3.7 %all-to-all-done = f32[8,8,128]{2,1,0:T(8,128)S(1)} async-done(((f32[8,8,128]{2,1,0:T(8,128)}), f32[8,8,128]{2,1,0:T(8,128)S(1)}, u32[]{:S(2)}, u32[]{:S(2)}) %all-to-all-start) | async-done | bytes 32800 | tf_op jit(solution)/shard_map/all_to_all | solution.py:383
  20.8 1.3 convolution_convert_fusion.19.refs_0_
  22.9 1.4 collective-permute-start.1
  24.5 1.3 convolution_convert_fusion.12.refs_7_
  25.8 8.7 %collective-permute-done.4 = bf16[128,2048]{1,0:T(8,128)(2,1)S(1)} collective-permute-done((bf16[128,2048]{1,0:T(8,128)(2,1)}, bf16[128,2048]{1,0:T(8,128)(2,1)S(1)}, u32[]{:S(2)}, u32[]{:S(2)}) %collective-permute-start.4) | collective-permute-done | bytes 524320 | tf_op jit(solution)/shard_map/ppermute | solution.py:95
  35.2 1.3 convolution_convert_fusion.18.refs_1_
  38.9 1.4 collective-permute-start.2
  40.3 5.4 %collective-permute-done.5 = bf16[128,2048]{1,0:T(8,128)(2,1)S(1)} collective-permute-done((bf16[128,2048]{1,0:T(8,128)(2,1)S(1)}, bf16[128,2048]{1,0:T(8,128)(2,1)S(1)}, u32[]{:S(2)}, u32[]{:S(2)}) %collective-permute-start.5) | collective-permute-done | bytes 524320 | tf_op jit(solution)/shard_map/ppermute | solution.py:95
  45.8 1.3 collective-permute-start.17
  47.3 6.5 %collective-permute-done.2 = bf16[128,2048]{1,0:T(8,128)(2,1)S(1)} collective-permute-done((bf16[128,2048]{1,0:T(8,128)(2,1)S(1)}, bf16[128,2048]{1,0:T(8,128)(2,1)S(1)}, u32[]{:S(2)}, u32[]{:S(2)}) %collective-permute-start.2) | collective-permute-done | bytes 524320 | tf_op jit(solution)/shard_map/ppermute | solution.py:95
  53.8 1.2 collective-permute-start.21
  55.5 6.2 %collective-permute-done.17 = bf16[128,2048]{1,0:T(8,128)(2,1)S(1)} collective-permute-done((bf16[128,2048]{1,0:T(8,128)(2,1)S(1)}, bf16[128,2048]{1,0:T(8,128)(2,1)S(1)}, u32[]{:S(2)}, u32[]{:S(2)}) %collective-permute-start.17) | collective-permute-done | bytes 524320 | tf_op jit(solution)/shard_map/ppermute | solution.py:95
  61.7 1.9 collective-permute-start.18
  66.0 6.5 %collective-permute-done.18 = bf16[128,2048]{1,0:T(8,128)(2,1)S(1)} collective-permute-done((bf16[128,2048]{1,0:T(8,128)(2,1)S(1)}, bf16[128,2048]{1,0:T(8,128)(2,1)S(1)}, u32[]{:S(2)}, u32[]{:S(2)}) %collective-permute-start.18) | collective-permute-done | bytes 524320 | tf_op jit(solution)/shard_map/ppermute | solution.py:95
  72.5 2.2 %collective-permute-start.6 = (bf16[128,2048]{1,0:T(8,128)(2,1)S(1)}, bf16[128,2048]{1,0:T(8,128)(2,1)S(1)}, u32[]{:S(2)}, u32[]{:S(2)}) collective-permute-start(bf16[128,2048]{1,0:T(8,128)(2,1)S(1)} %collective-permute-done.5), channel_id=1, source_target_pairs={{0,2},{2,4},{4,6},{6,7},{7,5},{5,3},{3,1},{1,0},{8,10},{10,12},{12... | collective-permute-start | bytes 1572872 | tf_op jit(solution)/shard_map/ppermute | solution.py:95
  75.0 2.3 %collective-permute-done.22 = bf16[128,2048]{1,0:T(8,128)(2,1)S(1)} collective-permute-done((bf16[128,2048]{1,0:T(8,128)(2,1)S(1)}, bf16[128,2048]{1,0:T(8,128)(2,1)S(1)}, u32[]{:S(2)}, u32[]{:S(2)}) %collective-permute-start.22) | collective-permute-done | bytes 524320 | tf_op jit(solution)/shard_map/ppermute | solution.py:95
  77.3 2.2 %collective-permute-start.19 = (bf16[128,2048]{1,0:T(8,128)(2,1)S(1)}, bf16[128,2048]{1,0:T(8,128)(2,1)S(1)}, u32[]{:S(2)}, u32[]{:S(2)}) collective-permute-start(bf16[128,2048]{1,0:T(8,128)(2,1)S(1)} %collective-permute-done.18), channel_id=1, source_target_pairs={{0,1},{2,0},{4,2},{6,4},{7,6},{5,7},{3,5},{1,3},{8,9},{10,8},{12,1... | collective-permute-start | bytes 1572872 | tf_op jit(solution)/shard_map/ppermute | solution.py:95
  80.0 5.7 %collective-permute-done.6 = bf16[128,2048]{1,0:T(8,128)(2,1)S(1)} collective-permute-done((bf16[128,2048]{1,0:T(8,128)(2,1)S(1)}, bf16[128,2048]{1,0:T(8,128)(2,1)S(1)}, u32[]{:S(2)}, u32[]{:S(2)}) %collective-permute-start.6) | collective-permute-done | bytes 524320 | tf_op jit(solution)/shard_map/ppermute | solution.py:95
  85.7 1.1 collective-permute-start.23
  87.4 2.5 %collective-permute-start.20 = (bf16[128,2048]{1,0:T(8,128)(2,1)S(1)}, bf16[128,2048]{1,0:T(8,128)(2,1)S(1)}, u32[]{:S(2)}, u32[]{:S(2)}) collective-permute-start(bf16[128,2048]{1,0:T(8,128)(2,1)S(1)} %collective-permute-done.19), channel_id=1, source_target_pairs={{0,1},{2,0},{4,2},{6,4},{7,6},{5,7},{3,5},{1,3},{8,9},{10,8},{12,1... | collective-permute-start | bytes 1572872 | tf_op jit(solution)/shard_map/ppermute | solution.py:95
  90.2 15.0 %shard_map.103 = (bf16[2,384,768]{2,1,0:T(8,128)(2,1)S(1)}, f32[2,384,768]{2,1,0:T(8,128)}, f32[2,384,768]{2,1,0:T(8,128)}) custom-call(bf16[96,2048]{1,0:T(8,128)(2,1)S(1)} %convolution_convert_fusion.19.refs_0_, bf16[96,2048]{1,0:T(8,128)(2,1)S(1)} %convolution_convert_fusion.18.refs_1_, bf16[96,2048]{1,0:T(8,128)(2,1)S(1)} %convolution_convert_fusion.17.refs_2_, ...), custom_call_target="tpu_custom_call" | custom-call | flops 4831838208 | bytes 1048576 | tf_op jit(solution)/shard_map/pallas_call | solution.py:142
  105.2 1.7 copy-done.3
  106.9 5.0 %shard_map.104.refs_8_ = bf16[8,96,2048]{2,1,0:T(8,128)(2,1)S(1)} custom-call(bf16[2,384,768]{2,1,0:T(8,128)(2,1)S(1)} %get-tuple-element.11.hidden_ref, bf16[768,2048]{1,0:T(8,128)(2,1)} %bitcast.144, bf16[768,2048]{1,0:T(8,128)(2,1)} %copy-done.3), custom_call_target="tpu_custom_call" | custom-call | flops 2415919104 | bytes 1048576 | tf_op jit(solution)/shard_map/pallas_call | solution.py:142
  112.6 2.1 collective-permute-start.14
  115.2 9.7 %collective-permute-done.10 = bf16[128,2048]{1,0:T(8,128)(2,1)S(1)} collective-permute-done((bf16[128,2048]{1,0:T(8,128)(2,1)S(1)}, bf16[128,2048]{1,0:T(8,128)(2,1)S(1)}, u32[]{:S(2)}, u32[]{:S(2)}) %collective-permute-start.10) | collective-permute-done | bytes 524320 | tf_op jit(solution)/shard_map/ppermute | solution.py:95
  125.7 2.3 %collective-permute-start.15 = (bf16[128,2048]{1,0:T(8,128)(2,1)S(1)}, bf16[128,2048]{1,0:T(8,128)(2,1)S(1)}, u32[]{:S(2)}, u32[]{:S(2)}) collective-permute-start(bf16[128,2048]{1,0:T(8,128)(2,1)S(1)} %fusion.7), channel_id=1, source_target_pairs={{0,1},{2,0},{4,2},{6,4},{7,6},{5,7},{3,5},{1,3},{8,9},{10,8},{12,1... | collective-permute-start | bytes 1572872 | tf_op jit(solution)/shard_map/ppermute | solution.py:95
  127.9 11.2 %shard_map.105 = (bf16[2,384,768]{2,1,0:T(8,128)(2,1)S(1)}, bf16[2,384,768]{2,1,0:T(8,128)(2,1)S(1)}, f32[8,2,128]{2,1,0:T(2,128)S(1)}) custom-call(bf16[96,2048]{1,0:T(8,128)(2,1)S(1)} %convolution_convert_fusion.11.refs_0_, bf16[96,2048]{1,0:T(8,128)(2,1)S(1)} %convolution_convert_fusion.10.refs_1_, ...), custom_call_target="tpu_custom_call" | custom-call | flops 2415919104 | bytes 1048576 | tf_op jit(solution)/shard_map/pallas_call | solution.py:142
  139.1 8.6 %shard_map.106 = bf16[8,96,2048]{2,1,0:T(8,128)(2,1)S(1)} custom-call(bf16[2,384,768]{2,1,0:T(8,128)(2,1)S(1)} %get-tuple-element.14.d_gate_ref, bf16[2,384,768]{2,1,0:T(8,128)(2,1)S(1)} %get-tuple-element.15.d_up_ref, bf16[2048,768]{1,0:T(8,128)(2,1)} %bitcast.148, bf16[2048,768]{1,0:T(8,128)(2,1)} %collective-permute-done.7.refs_9_.refs_1_, ...), custom_call_target="tpu_custom_call" | custom-call | flops 4831838208 | bytes 1048576 | tf_op jit(solution)/shard_map/pallas_call | solution.py:142
  152.2 2.0 collective-permute-start.28
  154.2 11.5 %collective-permute-done.24 = bf16[128,2048]{1,0:T(8,128)(2,1)S(1)} collective-permute-done((bf16[128,2048]{1,0:T(8,128)(2,1)S(1)}, bf16[128,2048]{1,0:T(8,128)(2,1)S(1)}, u32[]{:S(2)}, u32[]{:S(2)}) %collective-permute-start.24) | collective-permute-done | bytes 524320 | tf_op jit(solution)/shard_map/ppermute | solution.py:95
  166.5 2.0 collective-permute-start.12
  169.4 11.6 %collective-permute-done.25 = bf16[128,2048]{1,0:T(8,128)(2,1)S(1)} collective-permute-done((bf16[128,2048]{1,0:T(8,128)(2,1)S(1)}, bf16[128,2048]{1,0:T(8,128)(2,1)S(1)}, u32[]{:S(2)}, u32[]{:S(2)}) %collective-permute-start.25) | collective-permute-done | bytes 524320 | tf_op jit(solution)/shard_map/ppermute | solution.py:95
  181.4 1.1 fusion.6
  182.5 1.1 fusion.3
  183.6 2.0 collective-permute-start.13
  185.7 7.0 %collective-permute-done.29 = bf16[128,2048]{1,0:T(8,128)(2,1)S(1)} collective-permute-done((bf16[128,2048]{1,0:T(8,128)(2,1)S(1)}, bf16[128,2048]{1,0:T(8,128)(2,1)S(1)}, u32[]{:S(2)}, u32[]{:S(2)}) %collective-permute-start.29) | collective-permute-done | bytes 524320 | tf_op jit(solution)/shard_map/ppermute | solution.py:95
  192.7 1.1 fusion.12
  193.8 2.0 collective-permute-start.30
  196.1 1.1 fusion.9
  198.0 1.8 scatter_fusion
  199.8 3.3 %all-to-all-start.1 = ((f32[8,2,128]{2,1,0:T(2,128)}), f32[8,2,128]{2,1,0:T(2,128)S(1)}, u32[]{:S(2)}, u32[]{:S(2)}) async-start(f32[8,2,128]{2,1,0:T(2,128)} %scatter_fusion), calls=%async_computation.1 | async-start | bytes 16384 | tf_op jit(solution)/shard_map/all_to_all | solution.py:436
  203.2 6.4 %all-to-all-done.1 = f32[8,2,128]{2,1,0:T(2,128)S(1)} async-done(((f32[8,2,128]{2,1,0:T(2,128)}), f32[8,2,128]{2,1,0:T(2,128)S(1)}, u32[]{:S(2)}, u32[]{:S(2)}) %all-to-all-start.1) | async-done | bytes 8224 | tf_op jit(solution)/shard_map/all_to_all | solution.py:436
  210.3 2.3 %fusion.2 = bf16[128,2048]{1,0:T(8,128)(2,1)} fusion(bf16[96,128]{1,0:T(8,128)(2,1)S(1)} %bitcast.152, bf16[128,2048]{1,0:T(8,128)(2,1)} %collective-permute-done.16, bf16[128,2048]{1,0:T(8,128)(2,1)} %collective-permute-done.13, bf16[8,96,2048]{2,1,0:T(8,128)(2,1)S(1)} %copy-done.1), kind=kOutput, calls=%fused_computation.17 | convolution fusion | flops 51642368 | bytes 1990656 | tf_op jit(solution)/shard_map/dot_general | solution.py:412
  212.6 2.5 %fusion.8 = bf16[128,2048]{1,0:T(8,128)(2,1)} fusion(bf16[96,128]{1,0:T(8,128)(2,1)S(1)} %bitcast.153, bf16[128,2048]{1,0:T(8,128)(2,1)} %collective-permute-done.30, bf16[128,2048]{1,0:T(8,128)(2,1)} %collective-permute-done.27, bf16[8,96,2048]{2,1,0:T(8,128)(2,1)} %copy-done.2), kind=kOutput, calls=%fused_computation.23 | convolution fusion | flops 51642368 | bytes 1990656 | tf_op jit(solution)/shard_map/dot_general | solution.py:412
  (105 shorter events, 19.3 us)
Async XLA Ops:
  0.6 21.5 %collective-permute-start.3 = (bf16[128,2048]{1,0:T(8,128)(2,1)}, bf16[128,2048]{1,0:T(8,128)(2,1)}, u32[]{:S(2)}, u32[]{:S(2)}) collective-permute-start(bf16[128,2048]{1,0:T(8,128)(2,1)} %param.8), channel_id=1, source_target_pairs={{0,2},{2,4},{4,6},{6,7},{7,5},{5,3},{3,1},{1,0},{8,10},{10,12},{12... | collective-permute-start | bytes 1572872 | tf_op jit(solution)/shard_map/ppermute | solution.py:95
  3.7 19.2 %collective-permute-start = (bf16[128,2048]{1,0:T(8,128)(2,1)}, bf16[128,2048]{1,0:T(8,128)(2,1)}, u32[]{:S(2)}, u32[]{:S(2)}) collective-permute-start(bf16[128,2048]{1,0:T(8,128)(2,1)} %param.8), channel_id=1, source_target_pairs={{0,1},{2,0},{4,2},{6,4},{7,6},{5,7},{3,5},{1,3},{8,9},{10,8},{12,1... | collective-permute-start | bytes 1572872 | tf_op jit(solution)/shard_map/ppermute | solution.py:95
  5.7 14.1 %all-to-all-start = ((f32[8,8,128]{2,1,0:T(8,128)}), f32[8,8,128]{2,1,0:T(8,128)S(1)}, u32[]{:S(2)}, u32[]{:S(2)}) async-start(f32[8,8,128]{2,1,0:T(8,128)} %broadcast_in_dim.34), calls=%async_computation | async-start | bytes 65536 | tf_op jit(solution)/shard_map/all_to_all | solution.py:383
  12.0 78.2 %collective-permute-start.7 = (bf16[2048,768]{1,0:T(8,128)(2,1)}, bf16[2048,768]{1,0:T(8,128)(2,1)}, u32[]{:S(2)}, u32[]{:S(2)}) collective-permute-start(bf16[2048,768]{1,0:T(8,128)(2,1)} %bitcast.146), channel_id=1, source_target_pairs={{0,8},{8,0},{1,9},{9,1},{2,10},{10,2},{3,11},{11,3},{4,12},{12,4},... | collective-permute-start | bytes 9437192 | tf_op jit(solution)/shard_map/ppermute | solution.py:355
  12.0 78.2 %collective-permute-start.8 = (bf16[2048,768]{1,0:T(8,128)(2,1)}, bf16[2048,768]{1,0:T(8,128)(2,1)}, u32[]{:S(2)}, u32[]{:S(2)}) collective-permute-start(bf16[2048,768]{1,0:T(8,128)(2,1)} %bitcast.149), channel_id=1, source_target_pairs={{0,8},{8,0},{1,9},{9,1},{2,10},{10,2},{3,11},{11,3},{4,12},{12,4},... | collective-permute-start | bytes 9437192 | tf_op jit(solution)/shard_map/ppermute | solution.py:355
  12.5 92.8 %collective-permute-start.9 = (bf16[768,2048]{1,0:T(8,128)(2,1)}, bf16[768,2048]{1,0:T(8,128)(2,1)S(1)}, u32[]{:S(2)}, u32[]{:S(2)}) collective-permute-start(bf16[768,2048]{1,0:T(8,128)(2,1)} %bitcast.143), channel_id=1, source_target_pairs={{0,8},{8,0},{1,9},{9,1},{2,10},{10,2},{3,11},{11,3},{4,12},{12,4},... | collective-permute-start | bytes 9437192 | tf_op jit(solution)/shard_map/ppermute | solution.py:355
  20.3 19.9 %copy-start.4 = (bf16[128,2048]{1,0:T(8,128)(2,1)S(1)}, bf16[128,2048]{1,0:T(8,128)(2,1)}, u32[]{:S(2)}) copy-start(bf16[128,2048]{1,0:T(8,128)(2,1)} %param.9) | copy-start | bytes 1572868
  22.1 12.4 %collective-permute-start.4 = (bf16[128,2048]{1,0:T(8,128)(2,1)}, bf16[128,2048]{1,0:T(8,128)(2,1)S(1)}, u32[]{:S(2)}, u32[]{:S(2)}) collective-permute-start(bf16[128,2048]{1,0:T(8,128)(2,1)} %collective-permute-done.3), channel_id=1, source_target_pairs={{0,2},{2,4},{4,6},{6,7},{7,5},{5,3},{3,1},{1,0},{8,10},{10,12},{12... | collective-permute-start | bytes 1572872 | tf_op jit(solution)/shard_map/ppermute | solution.py:95
  22.9 14.8 %collective-permute-start.1 = (bf16[128,2048]{1,0:T(8,128)(2,1)}, bf16[128,2048]{1,0:T(8,128)(2,1)S(1)}, u32[]{:S(2)}, u32[]{:S(2)}) collective-permute-start(bf16[128,2048]{1,0:T(8,128)(2,1)} %collective-permute-done), channel_id=1, source_target_pairs={{0,1},{2,0},{4,2},{6,4},{7,6},{5,7},{3,5},{1,3},{8,9},{10,8},{12,1... | collective-permute-start | bytes 1572872 | tf_op jit(solution)/shard_map/ppermute | solution.py:95
  34.5 11.2 %collective-permute-start.5 = (bf16[128,2048]{1,0:T(8,128)(2,1)S(1)}, bf16[128,2048]{1,0:T(8,128)(2,1)S(1)}, u32[]{:S(2)}, u32[]{:S(2)}) collective-permute-start(bf16[128,2048]{1,0:T(8,128)(2,1)S(1)} %collective-permute-done.4), channel_id=1, source_target_pairs={{0,2},{2,4},{4,6},{6,7},{7,5},{5,3},{3,1},{1,0},{8,10},{10,12},{12... | collective-permute-start | bytes 1572872 | tf_op jit(solution)/shard_map/ppermute | solution.py:95
  38.9 14.9 %collective-permute-start.2 = (bf16[128,2048]{1,0:T(8,128)(2,1)S(1)}, bf16[128,2048]{1,0:T(8,128)(2,1)S(1)}, u32[]{:S(2)}, u32[]{:S(2)}) collective-permute-start(bf16[128,2048]{1,0:T(8,128)(2,1)S(1)} %collective-permute-done.1), channel_id=1, source_target_pairs={{0,1},{2,0},{4,2},{6,4},{7,6},{5,7},{3,5},{1,3},{8,9},{10,8},{12,1... | collective-permute-start | bytes 1572872 | tf_op jit(solution)/shard_map/ppermute | solution.py:95
  45.8 15.9 %collective-permute-start.17 = (bf16[128,2048]{1,0:T(8,128)(2,1)S(1)}, bf16[128,2048]{1,0:T(8,128)(2,1)S(1)}, u32[]{:S(2)}, u32[]{:S(2)}) collective-permute-start(bf16[128,2048]{1,0:T(8,128)(2,1)S(1)} %add_add_fusion), channel_id=1, source_target_pairs={{0,1},{2,0},{4,2},{6,4},{7,6},{5,7},{3,5},{1,3},{8,9},{10,8},{12,1... | collective-permute-start | bytes 1572872 | tf_op jit(solution)/shard_map/ppermute | solution.py:95
  53.8 10.9 %collective-permute-start.21 = (bf16[128,2048]{1,0:T(8,128)(2,1)S(1)}, bf16[128,2048]{1,0:T(8,128)(2,1)S(1)}, u32[]{:S(2)}, u32[]{:S(2)}) collective-permute-start(bf16[128,2048]{1,0:T(8,128)(2,1)S(1)} %add_add_fusion), channel_id=1, source_target_pairs={{0,2},{2,4},{4,6},{6,7},{7,5},{5,3},{3,1},{1,0},{8,10},{10,12},{12... | collective-permute-start | bytes 1572872 | tf_op jit(solution)/shard_map/ppermute | solution.py:95
  61.7 10.8 %collective-permute-start.18 = (bf16[128,2048]{1,0:T(8,128)(2,1)S(1)}, bf16[128,2048]{1,0:T(8,128)(2,1)S(1)}, u32[]{:S(2)}, u32[]{:S(2)}) collective-permute-start(bf16[128,2048]{1,0:T(8,128)(2,1)S(1)} %collective-permute-done.17), channel_id=1, source_target_pairs={{0,1},{2,0},{4,2},{6,4},{7,6},{5,7},{3,5},{1,3},{8,9},{10,8},{12,1... | collective-permute-start | bytes 1572872 | tf_op jit(solution)/shard_map/ppermute | solution.py:95
  64.7 12.5 %collective-permute-start.22 = (bf16[128,2048]{1,0:T(8,128)(2,1)S(1)}, bf16[128,2048]{1,0:T(8,128)(2,1)S(1)}, u32[]{:S(2)}, u32[]{:S(2)}) collective-permute-start(bf16[128,2048]{1,0:T(8,128)(2,1)S(1)} %collective-permute-done.21), channel_id=1, source_target_pairs={{0,2},{2,4},{4,6},{6,7},{7,5},{5,3},{3,1},{1,0},{8,10},{10,12},{12... | collective-permute-start | bytes 1572872 | tf_op jit(solution)/shard_map/ppermute | solution.py:95
  72.5 13.2 %collective-permute-start.6 = (bf16[128,2048]{1,0:T(8,128)(2,1)S(1)}, bf16[128,2048]{1,0:T(8,128)(2,1)S(1)}, u32[]{:S(2)}, u32[]{:S(2)}) collective-permute-start(bf16[128,2048]{1,0:T(8,128)(2,1)S(1)} %collective-permute-done.5), channel_id=1, source_target_pairs={{0,2},{2,4},{4,6},{6,7},{7,5},{5,3},{3,1},{1,0},{8,10},{10,12},{12... | collective-permute-start | bytes 1572872 | tf_op jit(solution)/shard_map/ppermute | solution.py:95
  77.3 10.1 %collective-permute-start.19 = (bf16[128,2048]{1,0:T(8,128)(2,1)S(1)}, bf16[128,2048]{1,0:T(8,128)(2,1)S(1)}, u32[]{:S(2)}, u32[]{:S(2)}) collective-permute-start(bf16[128,2048]{1,0:T(8,128)(2,1)S(1)} %collective-permute-done.18), channel_id=1, source_target_pairs={{0,1},{2,0},{4,2},{6,4},{7,6},{5,7},{3,5},{1,3},{8,9},{10,8},{12,1... | collective-permute-start | bytes 1572872 | tf_op jit(solution)/shard_map/ppermute | solution.py:95
  85.7 28.9 %collective-permute-start.23 = (bf16[128,2048]{1,0:T(8,128)(2,1)S(1)}, bf16[128,2048]{1,0:T(8,128)(2,1)S(1)}, u32[]{:S(2)}, u32[]{:S(2)}) collective-permute-start(bf16[128,2048]{1,0:T(8,128)(2,1)S(1)} %collective-permute-done.22), channel_id=1, source_target_pairs={{0,2},{2,4},{4,6},{6,7},{7,5},{5,3},{3,1},{1,0},{8,10},{10,12},{12... | collective-permute-start | bytes 1572872 | tf_op jit(solution)/shard_map/ppermute | solution.py:95
  87.4 27.5 %collective-permute-start.20 = (bf16[128,2048]{1,0:T(8,128)(2,1)S(1)}, bf16[128,2048]{1,0:T(8,128)(2,1)S(1)}, u32[]{:S(2)}, u32[]{:S(2)}) collective-permute-start(bf16[128,2048]{1,0:T(8,128)(2,1)S(1)} %collective-permute-done.19), channel_id=1, source_target_pairs={{0,1},{2,0},{4,2},{6,4},{7,6},{5,7},{3,5},{1,3},{8,9},{10,8},{12,1... | collective-permute-start | bytes 1572872 | tf_op jit(solution)/shard_map/ppermute | solution.py:95
  105.2 1.7 copy-start.3
  111.9 13.8 %copy-start = (bf16[8,96,2048]{2,1,0:T(8,128)(2,1)}, bf16[8,96,2048]{2,1,0:T(8,128)(2,1)S(1)}, u32[]{:S(2)}) copy-start(bf16[8,96,2048]{2,1,0:T(8,128)(2,1)S(1)} %shard_map.104.refs_8_) | copy-start | bytes 9437188
  112.2 12.7 %collective-permute-start.10 = (bf16[128,2048]{1,0:T(8,128)(2,1)S(1)}, bf16[128,2048]{1,0:T(8,128)(2,1)S(1)}, u32[]{:S(2)}, u32[]{:S(2)}) collective-permute-start(bf16[128,2048]{1,0:T(8,128)(2,1)S(1)} %convolution_convert_fusion.3), channel_id=1, source_target_pairs={{0,2},{2,4},{4,6},{6,7},{7,5},{5,3},{3,1},{1,0},{8,10},{10,12},{12... | collective-permute-start | bytes 1572872 | tf_op jit(solution)/shard_map/ppermute | solution.py:95
  112.6 12.7 %collective-permute-start.14 = (bf16[128,2048]{1,0:T(8,128)(2,1)S(1)}, bf16[128,2048]{1,0:T(8,128)(2,1)S(1)}, u32[]{:S(2)}, u32[]{:S(2)}) collective-permute-start(bf16[128,2048]{1,0:T(8,128)(2,1)S(1)} %convolution_convert_fusion.2), channel_id=1, source_target_pairs={{0,1},{2,0},{4,2},{6,4},{7,6},{5,7},{3,5},{1,3},{8,9},{10,8},{12,1... | collective-permute-start | bytes 1572872 | tf_op jit(solution)/shard_map/ppermute | solution.py:95
  125.2 22.4 %collective-permute-start.11 = (bf16[128,2048]{1,0:T(8,128)(2,1)S(1)}, bf16[128,2048]{1,0:T(8,128)(2,1)S(1)}, u32[]{:S(2)}, u32[]{:S(2)}) collective-permute-start(bf16[128,2048]{1,0:T(8,128)(2,1)S(1)} %fusion.5), channel_id=1, source_target_pairs={{0,2},{2,4},{4,6},{6,7},{7,5},{5,3},{3,1},{1,0},{8,10},{10,12},{12... | collective-permute-start | bytes 1572872 | tf_op jit(solution)/shard_map/ppermute | solution.py:95
  125.7 24.6 %collective-permute-start.15 = (bf16[128,2048]{1,0:T(8,128)(2,1)S(1)}, bf16[128,2048]{1,0:T(8,128)(2,1)S(1)}, u32[]{:S(2)}, u32[]{:S(2)}) collective-permute-start(bf16[128,2048]{1,0:T(8,128)(2,1)S(1)} %fusion.7), channel_id=1, source_target_pairs={{0,1},{2,0},{4,2},{6,4},{7,6},{5,7},{3,5},{1,3},{8,9},{10,8},{12,1... | collective-permute-start | bytes 1572872 | tf_op jit(solution)/shard_map/ppermute | solution.py:95
  147.7 48.5 %copy-start.2 = (bf16[8,96,2048]{2,1,0:T(8,128)(2,1)}, bf16[8,96,2048]{2,1,0:T(8,128)(2,1)S(1)}, u32[]{:S(2)}) copy-start(bf16[8,96,2048]{2,1,0:T(8,128)(2,1)S(1)} %shard_map.106) | copy-start | bytes 9437188
  147.7 18.5 %copy-start.1 = (bf16[8,96,2048]{2,1,0:T(8,128)(2,1)S(1)}, bf16[8,96,2048]{2,1,0:T(8,128)(2,1)}, u32[]{:S(2)}) copy-start(bf16[8,96,2048]{2,1,0:T(8,128)(2,1)} %copy-done) | copy-start | bytes 9437188
  151.8 14.0 %collective-permute-start.24 = (bf16[128,2048]{1,0:T(8,128)(2,1)S(1)}, bf16[128,2048]{1,0:T(8,128)(2,1)S(1)}, u32[]{:S(2)}, u32[]{:S(2)}) collective-permute-start(bf16[128,2048]{1,0:T(8,128)(2,1)S(1)} %fusion.15), channel_id=1, source_target_pairs={{0,1},{2,0},{4,2},{6,4},{7,6},{5,7},{3,5},{1,3},{8,9},{10,8},{12,1... | collective-permute-start | bytes 1572872 | tf_op jit(solution)/shard_map/ppermute | solution.py:95
  152.2 16.4 %collective-permute-start.28 = (bf16[128,2048]{1,0:T(8,128)(2,1)S(1)}, bf16[128,2048]{1,0:T(8,128)(2,1)S(1)}, u32[]{:S(2)}, u32[]{:S(2)}) collective-permute-start(bf16[128,2048]{1,0:T(8,128)(2,1)S(1)} %fusion.17), channel_id=1, source_target_pairs={{0,2},{2,4},{4,6},{6,7},{7,5},{5,3},{3,1},{1,0},{8,10},{10,12},{12... | collective-permute-start | bytes 1572872 | tf_op jit(solution)/shard_map/ppermute | solution.py:95
  166.1 14.9 %collective-permute-start.25 = (bf16[128,2048]{1,0:T(8,128)(2,1)S(1)}, bf16[128,2048]{1,0:T(8,128)(2,1)S(1)}, u32[]{:S(2)}, u32[]{:S(2)}) collective-permute-start(bf16[128,2048]{1,0:T(8,128)(2,1)S(1)} %fusion.11), channel_id=1, source_target_pairs={{0,1},{2,0},{4,2},{6,4},{7,6},{5,7},{3,5},{1,3},{8,9},{10,8},{12,1... | collective-permute-start | bytes 1572872 | tf_op jit(solution)/shard_map/ppermute | solution.py:95
  166.5 16.0 %collective-permute-start.12 = (bf16[128,2048]{1,0:T(8,128)(2,1)S(1)}, bf16[128,2048]{1,0:T(8,128)(2,1)S(1)}, u32[]{:S(2)}, u32[]{:S(2)}) collective-permute-start(bf16[128,2048]{1,0:T(8,128)(2,1)S(1)} %fusion.4), channel_id=1, source_target_pairs={{0,2},{2,4},{4,6},{6,7},{7,5},{5,3},{3,1},{1,0},{8,10},{10,12},{12... | collective-permute-start | bytes 1572872 | tf_op jit(solution)/shard_map/ppermute | solution.py:95
  168.9 23.8 %collective-permute-start.29 = (bf16[128,2048]{1,0:T(8,128)(2,1)S(1)}, bf16[128,2048]{1,0:T(8,128)(2,1)S(1)}, u32[]{:S(2)}, u32[]{:S(2)}) collective-permute-start(bf16[128,2048]{1,0:T(8,128)(2,1)S(1)} %fusion.13), channel_id=1, source_target_pairs={{0,2},{2,4},{4,6},{6,7},{7,5},{5,3},{3,1},{1,0},{8,10},{10,12},{12... | collective-permute-start | bytes 1572872 | tf_op jit(solution)/shard_map/ppermute | solution.py:95
  181.3 28.3 %copy-start.5 = (s32[128,4]{0,1:T(4,128)S(1)}, s32[128,4]{0,1:T(4,128)}, u32[]{:S(2)}) copy-start(s32[128,4]{0,1:T(4,128)} %param.10) | copy-start | bytes 6148
  181.3 14.8 %collective-permute-start.26 = (bf16[128,2048]{1,0:T(8,128)(2,1)S(1)}, bf16[128,2048]{1,0:T(8,128)(2,1)S(1)}, u32[]{:S(2)}, u32[]{:S(2)}) collective-permute-start(bf16[128,2048]{1,0:T(8,128)(2,1)S(1)} %fusion.10), channel_id=1, source_target_pairs={{0,1},{2,0},{4,2},{6,4},{7,6},{5,7},{3,5},{1,3},{8,9},{10,8},{12,1... | collective-permute-start | bytes 1572872 | tf_op jit(solution)/shard_map/ppermute | solution.py:95
  182.5 27.8 %collective-permute-start.16 = (bf16[128,2048]{1,0:T(8,128)(2,1)}, bf16[128,2048]{1,0:T(8,128)(2,1)}, u32[]{:S(2)}, u32[]{:S(2)}) collective-permute-start(bf16[128,2048]{1,0:T(8,128)(2,1)} %fusion.6), channel_id=1, source_target_pairs={{0,1},{2,0},{4,2},{6,4},{7,6},{5,7},{3,5},{1,3},{8,9},{10,8},{12,1... | collective-permute-start | bytes 1572872 | tf_op jit(solution)/shard_map/ppermute | solution.py:95
  183.6 26.7 %collective-permute-start.13 = (bf16[128,2048]{1,0:T(8,128)(2,1)}, bf16[128,2048]{1,0:T(8,128)(2,1)}, u32[]{:S(2)}, u32[]{:S(2)}) collective-permute-start(bf16[128,2048]{1,0:T(8,128)(2,1)} %fusion.3), channel_id=1, source_target_pairs={{0,2},{2,4},{4,6},{6,7},{7,5},{5,3},{3,1},{1,0},{8,10},{10,12},{12... | collective-permute-start | bytes 1572872 | tf_op jit(solution)/shard_map/ppermute | solution.py:95
  193.8 18.8 %collective-permute-start.30 = (bf16[128,2048]{1,0:T(8,128)(2,1)}, bf16[128,2048]{1,0:T(8,128)(2,1)}, u32[]{:S(2)}, u32[]{:S(2)}) collective-permute-start(bf16[128,2048]{1,0:T(8,128)(2,1)} %fusion.12), channel_id=1, source_target_pairs={{0,2},{2,4},{4,6},{6,7},{7,5},{5,3},{3,1},{1,0},{8,10},{10,12},{12... | collective-permute-start | bytes 1572872 | tf_op jit(solution)/shard_map/ppermute | solution.py:95
  197.3 15.4 %collective-permute-start.27 = (bf16[128,2048]{1,0:T(8,128)(2,1)}, bf16[128,2048]{1,0:T(8,128)(2,1)}, u32[]{:S(2)}, u32[]{:S(2)}) collective-permute-start(bf16[128,2048]{1,0:T(8,128)(2,1)} %fusion.9), channel_id=1, source_target_pairs={{0,1},{2,0},{4,2},{6,4},{7,6},{5,7},{3,5},{1,3},{8,9},{10,8},{12,1... | collective-permute-start | bytes 1572872 | tf_op jit(solution)/shard_map/ppermute | solution.py:95
  199.8 9.8 %all-to-all-start.1 = ((f32[8,2,128]{2,1,0:T(2,128)}), f32[8,2,128]{2,1,0:T(2,128)S(1)}, u32[]{:S(2)}, u32[]{:S(2)}) async-start(f32[8,2,128]{2,1,0:T(2,128)} %scatter_fusion), calls=%async_computation.1 | async-start | bytes 16384 | tf_op jit(solution)/shard_map/all_to_all | solution.py:436

commit v3 on v2

--- a/solution.py
+++ b/solution.py
@@ -95,38 +95,52 @@
     return lax.ppermute(array, "ep", pairs)
 
 
-def ring_gather(shard, count, far_step):
+def ring_gather(shard, count, far_step, behind={}):
     held = {0: shard}
+    latest = {}
     for step in (far_step, -far_step):
         hops = count // 2 if step == far_step else (count - 1) // 2
-        moving = shard
+        moving = held_back(shard, behind[step]) if step in behind else shard
         for hop in range(1, hops + 1):
             moving = ring_shift(moving, count, step)
             held[(-step * hop) % count] = moving
-    return [held[place] for place in range(count)]
+        latest[step] = (moving,)
+    return [held[place] for place in range(count)], latest
 
 
 def after(array, *others):
     for other in others:
-        array = array + other[:1, :1] * 0
+        array = array + other[(slice(0, 1),) * other.ndim].reshape((1,) * array.ndim).astype(array.dtype) * 0
     return array
 
 
-def ring_reduce(share_of, count, far_step, first=(), seen=None):
-    arrived = []
+def held_back(array, others):
+    def kernel(*refs):
+        pass
+
+    return pl.pallas_call(
+        kernel,
+        out_shape=jax.ShapeDtypeStruct(array.shape, array.dtype),
+        in_specs=[pl.BlockSpec(memory_space=pl.ANY) for _ in range(1 + len(others))],
+        out_specs=pl.BlockSpec(memory_space=pl.ANY),
+        input_output_aliases={0: 0},
+    )(array, *others)
+
+
+def ring_reduce(share_of, count, far_step, behind={}):
+    arrived = {}
     for step in (far_step, -far_step):
         hops = count // 2 if step == far_step else (count - 1) // 2
         moving = None
+        steps = []
         for hop in range(hops, 0, -1):
-            share = share_of((step * hop) % count, moving)
-            if moving is None:
-                share = after(share, *first)
+            waits = behind.get((step, hops - hop), ())
+            share = share_of((step * hop) % count, moving, waits)
             moving = ring_shift(share, count, step)
-            if seen is not None and hop == max(1, hops - 1):
-                seen.append(moving)
-        arrived.append(moving)
-    total = share_of(0, arrived[0], arrived[1])
-    return total
+            steps.append(moving)
+        arrived[step] = steps
+    total = share_of(0, arrived[far_step][-1], (arrived[-far_step][-1],), True)
+    return total, arrived
 
 
 VMEM_LIMIT = 48 * 1024 * 1024
@@ -137,10 +151,17 @@
     return max(w for w in range(128, most + 1, 128) if size % w == 0)
 
 
-def call_kernel(kernel, operands, kinds, outs, scratch, flops):
-    spaces = {"any": pl.ANY, "vmem": pltpu.VMEM}
+def call_kernel(kernel, operands, kinds, outs, scratch, flops, behind=()):
+    spaces = {"any": pl.ANY, "vmem": pltpu.VMEM, "smem": pltpu.SMEM}
+    count = len(operands)
+    operands = [*operands, *behind]
+    kinds = [*kinds, *["any" for _ in behind]]
+
+    def body(*refs):
+        kernel(*refs[:count], *refs[len(operands) :])
+
     return pl.pallas_call(
-        kernel,
+        body,
         out_shape=outs,
         in_specs=[pl.BlockSpec(memory_space=spaces[k]) for k in kinds],
         out_specs=[pl.BlockSpec(memory_space=pltpu.VMEM) for _ in outs],
@@ -157,6 +178,47 @@
             packed[e, s * half : (s + 1) * half, :] = part[e * half : (e + 1) * half, :]
 
 
+def source_at(distance, chip, count):
+    place = jnp.where(chip % 2 == 0, chip // 2, count - (chip + 1) // 2)
+    place = (place + distance) % count
+    return jnp.where(place < count // 2, 2 * place, 2 * (count - place) - 1)
+
+
+def run_routing(ids, tables, top_count, capacity):
+    count, _, tokens = tables.shape
+    f32, bf16 = jnp.float32, jnp.bfloat16
+
+    def kernel(ids_ref, table_ref, pick_ref, spread_ref):
+        core, chip = ids_ref[0], ids_ref[1]
+        first = lax.broadcasted_iota(jnp.int32, (tokens, tokens), 0)
+        second = lax.broadcasted_iota(jnp.int32, (tokens, tokens), 1)
+        before = (first <= second).astype(f32).astype(bf16)
+        slot = lax.broadcasted_iota(jnp.int32, (capacity, tokens), 0).astype(f32)
+        hits, weights = [], []
+        for s in range(count):
+            table = table_ref[source_at(s, chip, count)]
+            for e in range(2):
+                expert = jnp.where(core == e, chip, count + chip).astype(f32)
+                hit = (table[:top_count] == expert).astype(f32)
+                hits.append(jnp.sum(hit, axis=0, keepdims=True))
+                weights.append(
+                    jnp.sum(hit * table[top_count : 2 * top_count], axis=0, keepdims=True)
+                )
+        rank = jnp.dot(
+            jnp.concatenate(hits, axis=0).astype(bf16), before, preferred_element_type=f32
+        )
+        for s in range(count):
+            for e in range(2):
+                i = 2 * s + e
+                chosen = jnp.where(slot == rank[i : i + 1] - 1.0, hits[i], 0.0)
+                span = slice(e * capacity, (e + 1) * capacity)
+                pick_ref[s, span, :] = chosen.astype(bf16)
+                spread_ref[s, span, :] = (chosen * weights[i]).astype(bf16)
+
+    shape = jax.ShapeDtypeStruct((count, 2 * capacity, tokens), bf16)
+    return call_kernel(kernel, [ids, tables], ["smem", "vmem"], [shape, shape], [], 1 << 20)
+
+
 def run_hidden(parts, gate_mats, up_mats):
     count, rows, width = len(parts), parts[0].shape[0], parts[0].shape[1]
     units = gate_mats[0].shape[1]
@@ -169,22 +231,19 @@
         hidden_ref, slope_ref, act_ref, packed, held, sems = refs[count + 4 :]
         copies = {}
         for e in range(2):
-            for n in range(tiles):
-                for m in range(2):
-                    copies[e, n, m] = pltpu.make_async_copy(
-                        mats[2 * m + e].at[:, n * tile : (n + 1) * tile],
-                        held.at[e, n, m],
-                        sems.at[e, n, m],
-                    )
-                    copies[e, n, m].start()
+            for m in range(2):
+                copies[e, m] = pltpu.make_async_copy(
+                    mats[2 * m + e], held.at[e, m], sems.at[e, m]
+                )
+                copies[e, m].start()
         pack_rows(part_refs, packed)
         for e in range(2):
+            for m in range(2):
+                copies[e, m].wait()
             for n in range(tiles):
                 span = slice(n * tile, (n + 1) * tile)
-                copies[e, n, 0].wait()
-                gate = jnp.dot(packed[e], held[e, n, 0], preferred_element_type=jnp.float32)
-                copies[e, n, 1].wait()
-                up = jnp.dot(packed[e], held[e, n, 1], preferred_element_type=jnp.float32)
+                gate = jnp.dot(packed[e], held[e, 0, :, span], preferred_element_type=jnp.float32)
+                up = jnp.dot(packed[e], held[e, 1, :, span], preferred_element_type=jnp.float32)
                 sigma = 1.0 / (1.0 + jnp.exp(-gate))
                 act = gate * sigma
                 hidden_ref[e, :, span] = (act * up).astype(jnp.bfloat16)
@@ -202,8 +261,8 @@
         ],
         [
             pltpu.VMEM((2, total, width), jnp.bfloat16),
-            pltpu.VMEM((2, tiles, 2, width, tile), jnp.bfloat16),
-            pltpu.SemaphoreType.DMA((2, tiles, 2)),
+            pltpu.VMEM((2, 2, width, units), jnp.bfloat16),
+            pltpu.SemaphoreType.DMA((2, 2)),
         ],
         8 * total * width * units,
     )
@@ -219,15 +278,13 @@
     def kernel(hidden_ref, own_ref, other_ref, out_ref, held, sems):
         copies = {}
         for e, mat in enumerate((own_ref, other_ref)):
+            copies[e] = pltpu.make_async_copy(mat, held.at[e], sems.at[e])
+            copies[e].start()
+        for e in range(2):
+            copies[e].wait()
             for n in range(tiles):
-                copies[e, n] = pltpu.make_async_copy(
-                    mat.at[:, n * tile : (n + 1) * tile], held.at[e, n], sems.at[e, n]
-                )
-                copies[e, n].start()
-        for e in range(2):
-            for n in range(tiles):
-                copies[e, n].wait()
-                out = jnp.dot(hidden_ref[e], held[e, n], preferred_element_type=jnp.float32)
+                columns = held[e, :, n * tile : (n + 1) * tile]
+                out = jnp.dot(hidden_ref[e], columns, preferred_element_type=jnp.float32)
                 out_ref[:, e * half : (e + 1) * half, n * tile : (n + 1) * tile] = (
                     out.astype(jnp.bfloat16).reshape(count, half, tile)
                 )
@@ -238,14 +295,14 @@
         ["vmem", "any", "any"],
         [jax.ShapeDtypeStruct((count, 2 * half, width), jnp.bfloat16)],
         [
-            pltpu.VMEM((2, tiles, units, tile), jnp.bfloat16),
-            pltpu.SemaphoreType.DMA((2, tiles)),
+            pltpu.VMEM((2, units, width), jnp.bfloat16),
+            pltpu.SemaphoreType.DMA((2,)),
         ],
         4 * total * width * units,
     )[0]
 
 
-def run_d_hidden(parts, outputs, pick, slope, activated, down_mats):
+def run_d_hidden(ids, parts, outputs, pick, slope, activated, down_mats, behind):
     count, rows, width = len(parts), parts[0].shape[0], parts[0].shape[1]
     half = rows // 2
     _, total, units = slope.shape
@@ -254,6 +311,7 @@
     tokens = pick.shape[2]
 
     def kernel(*refs):
+        ids_ref, refs = refs[0], refs[1:]
         part_refs = refs[:count]
         out_ref, pick_ref, slope_ref, act_ref, own_ref, other_ref = refs[count : count + 6]
         d_gate_ref, d_up_ref, token_ref, packed, held, sems = refs[count + 6 :]
@@ -281,15 +339,16 @@
                 keepdims=True,
             )
             spread = pick_ref[s].astype(jnp.float32) * inner
-            for e in range(2):
-                token_ref[s, e : e + 1, :] = jnp.sum(
-                    spread[e * half : (e + 1) * half], axis=0, keepdims=True
-                )
+            sums = [
+                jnp.sum(spread[e * half : (e + 1) * half], axis=0, keepdims=True)
+                for e in range(2)
+            ]
+            token_ref[source_at(s, ids_ref[1], count)] = jnp.concatenate(sums, axis=0)
 
     return call_kernel(
         kernel,
-        [*parts, outputs, pick, slope, activated, *down_mats],
-        ["vmem"] * (count + 4) + ["any"] * 2,
+        [ids, *parts, outputs, pick, slope, activated, *down_mats],
+        ["smem"] + ["vmem"] * (count + 4) + ["any"] * 2,
         [
             jax.ShapeDtypeStruct((2, total, units), jnp.bfloat16),
             jax.ShapeDtypeStruct((2, total, units), jnp.bfloat16),
@@ -301,10 +360,11 @@
             pltpu.SemaphoreType.DMA((2, tiles)),
         ],
         4 * total * width * units,
-    )
-
-
-def run_d_copy(d_pre_gate, d_pre_up, gate_mats, up_mats, count):
+        behind,
+    )
+
+
+def run_d_copy(d_pre_gate, d_pre_up, gate_mats, up_mats, count, behind):
     _, total, units = d_pre_gate.shape
     width = gate_mats[0].shape[0]
     half = total // count
@@ -348,6 +408,7 @@
             pltpu.SemaphoreType.DMA((2, tiles, 2)),
         ],
         8 * total * width * units,
+        behind,
     )[0]
 
 
@@ -364,42 +425,20 @@
     capacity = max(2, 3 * token_count * top_count // (2 * expert_count))
     f32, bf16 = jnp.float32, jnp.bfloat16
 
-    in_shards = ring_gather(tokens, chips, 1)
-    late = min(2, (chips - 1) // 2)
-    grad_shards = ring_gather(
-        after(cotangent, in_shards[-late % chips], in_shards[late]), chips, -1
-    )
+    in_shards, in_latest = ring_gather(tokens, chips, 1)
+    grad_shards, grad_latest = ring_gather(cotangent, chips, -1, in_latest)
     gate_mats = (w_gate[0], swap_cores(w_gate[0]))
     up_mats = (w_up[0], swap_cores(w_up[0]))
     down_mats = (w_down[0], swap_cores(w_down[0]))
 
     core = lax.axis_index("grp")
     chip = lax.axis_index("ep")
-    order = jnp.array(ring_order(chips), jnp.int32)
-    place = jnp.argmax(order == chip).astype(jnp.int32)
-    sources = order[(place + jnp.arange(chips, dtype=jnp.int32)) % chips]
+    ids = jnp.stack([core, chip]).astype(jnp.int32)
     table = jnp.concatenate([routes.astype(f32), gates.astype(f32)], axis=1).T
+    table = after(table, in_shards[1], in_shards[-1])
     copies = jnp.broadcast_to(table[None], (chips,) + table.shape)
-    tables = lax.all_to_all(copies, "ep", split_axis=0, concat_axis=0, tiled=True)[sources]
-    named = tables[:, :top_count].astype(jnp.int32)
-    weights = tables[:, top_count:]
-    mine = jnp.stack([core * chips + chip, (1 - core) * chips + chip])
-    hits = named[:, None] == mine[None, :, None, None]
-    weight = jnp.sum(jnp.where(hits, weights[:, None], 0.0), axis=2)
-    hit = jnp.any(hits, axis=2)
-    before = (
-        jnp.arange(token_count)[:, None] <= jnp.arange(token_count)[None, :]
-    ).astype(bf16)
-    rank = jnp.dot(
-        hit.astype(bf16).reshape(-1, token_count), before, preferred_element_type=f32
-    ).reshape(hit.shape).astype(jnp.int32) - 1
-    slots = jnp.arange(capacity, dtype=jnp.int32)
-    picks = hit[:, :, None, :] & (rank[:, :, None, :] == slots[None, None, :, None])
-    rows_per = 2 * capacity
-    pick = picks.astype(bf16).reshape(chips, rows_per, token_count)
-    spread = jnp.where(picks, weight[:, :, None, :], 0.0).astype(bf16).reshape(
-        chips, rows_per, token_count
-    )
+    tables = lax.all_to_all(copies, "ep", split_axis=0, concat_axis=0, tiled=True)
+    pick, spread = run_routing(ids, tables, top_count, capacity)
 
     def gather_rows(shards):
         return [
@@ -408,32 +447,34 @@
         ]
 
     def scatter_rows(blocks):
-        def share_of(s, *partials):
+        def share_of(s, partial, waits=(), add_waits=False):
             total = lax.dot_general(
                 spread[s], blocks[s], (((0,), (0,)), ((), ())), preferred_element_type=f32
             )
-            for partial in partials:
-                if partial is not None:
-                    total = total + partial.astype(f32)
-            return total.astype(bf16)
+            if partial is not None:
+                total = total + partial.astype(f32)
+            if add_waits:
+                return (total + waits[0].astype(f32)).astype(bf16)
+            return after(total.astype(bf16), *waits)
 
         return share_of
 
     rows_in = gather_rows(in_shards)
     hidden, slope, activated = run_hidden(rows_in, gate_mats, up_mats)
     outputs = run_down(hidden, down_mats, chips)
-    seen = []
-    mixed = ring_reduce(scatter_rows(outputs), chips, 1, seen=seen)
+    behind = {(step, 0): grad_latest[step] for step in (1, -1)}
+    mixed, mixed_hops = ring_reduce(scatter_rows(outputs), chips, 1, behind)
 
     rows_grad = gather_rows(grad_shards)
+    hop_of = lambda hop: [mixed_hops[step][min(hop, len(mixed_hops[step]) - 1)] for step in (1, -1)]
     d_pre_gate, d_pre_up, per_token = run_d_hidden(
-        rows_grad, outputs, pick, slope, activated, down_mats
-    )
-    d_copies = run_d_copy(d_pre_gate, d_pre_up, gate_mats, up_mats, chips)
-    d_tokens = ring_reduce(scatter_rows(d_copies), chips, -1, first=seen)
-
-    by_chip = jnp.zeros_like(per_token).at[sources].set(per_token)
-    returned = lax.all_to_all(by_chip, "ep", split_axis=0, concat_axis=0, tiled=True)
+        ids, rows_grad, outputs, pick, slope, activated, down_mats, hop_of(0)
+    )
+    d_copies = run_d_copy(d_pre_gate, d_pre_up, gate_mats, up_mats, chips, hop_of(1))
+
+    returned = lax.all_to_all(per_token, "ep", split_axis=0, concat_axis=0, tiled=True)
+    behind = {(step, 0): (mixed_hops[step][-1],) for step in (1, -1)}
+    d_tokens, _ = ring_reduce(scatter_rows(d_copies), chips, -1, behind)
     chip_ids = jnp.arange(chips, dtype=jnp.int32)
     served = jnp.stack([core * chips + chip_ids, (1 - core) * chips + chip_ids], axis=1)
     chosen = routes.T[None, None] == served[:, :, None, None]

time: 216 us -> 225 us (1.042)
  matrix products: 19.9 us -> 33.1 us
  waiting for transfers between devices: 92.9 us -> 97.4 us
  starting transfers between devices: 44 us -> 40.4 us
  other arithmetic: 4.61 us -> 2.13 us
    dot_general x16, matrix products: 12.5 us -> 19.9 us  [share_of(): lax.dot_general(spread[s], blocks[s], (((0,), (0,)), ((), ())), preferred...]
    dot_general x16, matrix products: 7.26 us -> 13.2 us  [gather_rows(): jnp.dot(pick[s], shards[s], preferred_element_type=f32).astype(bf16)]
    ppermute x28, starting transfers between devices: 33.8 us -> 30.6 us  [ring_shift(): return lax.ppermute(array, 'ep', pairs)]
    all_to_all x1, waiting for transfers between devices: 3.75 us -> 6.61 us  [body_ring(): lax.all_to_all(copies, 'ep', split_axis=0, concat_axis=0, tiled=True)]
    pallas_call x4 -> x7, Pallas kernels: 39.7 us -> 38.5 us  [the longest x5 38.5 us: call_kernel(): pl.pallas_call(body, out_shape=outs, in_specs=[pl.BlockSpec(memory_space=...]
  transfers between devices with their start and end apart: 33 -> 33, of which waited for: 16 -> 13; matrix products, arithmetic and copies ran while one was open for 13% -> 16% of each run, Pallas kernels for 18% -> 17%
where the time goes in v3:
time: 225 us; the launch traced here: 224 us
  waiting for transfers between devices  97.4 us (43%)
  starting transfers between devices  40.4 us (18%)
  Pallas kernels  38.5 us (17%)
  matrix products  33.1 us (15%)
  local copies, waits for them, and re-layouts  7.53 us (3%)
  between operations  5.06 us (2%)
    ppermute x28, waiting for transfers between devices, ring_shift(): return lax.ppermute(array, 'ep', pairs)  84.4 us
    pallas_call x5, Pallas kernels, call_kernel(): pl.pallas_call(body, out_shape=outs, in_specs=[pl.BlockSpec(memory_space=...  38.5 us
    ppermute x28, starting transfers between devices, ring_shift(): return lax.ppermute(array, 'ep', pairs)  30.6 us
    dot_general x16, matrix products, share_of(): lax.dot_general(spread[s], blocks[s], (((0,), (0,)), ((), ())), preferred...  19.9 us
    dot_general x16, matrix products, gather_rows(): jnp.dot(pick[s], shards[s], preferred_element_type=f32).astype(bf16)  13.2 us
    all_to_all x1, waiting for transfers between devices, body_ring(): lax.all_to_all(copies, 'ep', split_axis=0, concat_axis=0, tiled=True)  6.61 us
    all_to_all x1, waiting for transfers between devices, body_ring(): lax.all_to_all(per_token, 'ep', split_axis=0, concat_axis=0, tiled=True)  6.44 us
    all_to_all x1, starting transfers between devices, body_ring(): lax.all_to_all(copies, 'ep', split_axis=0, concat_axis=0, tiled=True)  6.06 us
  transfers between devices with their start and end apart: 33, of which 13 were waited for; matrix products, arithmetic and copies ran while one was open for 16% of the time, Pallas kernels for 17%

profile of v3, /device:TPU:0, one launch (start us, length us, event | category | flops | bytes accessed | tf_op | source)
XLA Modules:
  0.0 224.2 jit_solution(2457636604757956973)
XLA Ops:
  1.7 3.0 %collective-permute-start.1 = (bf16[128,2048]{1,0:T(8,128)(2,1)}, bf16[128,2048]{1,0:T(8,128)(2,1)S(1)}, u32[]{:S(2)}, u32[]{:S(2)}) collective-permute-start(bf16[128,2048]{1,0:T(8,128)(2,1)} %param.7), channel_id=1, source_target_pairs={{0,2},{2,4},{4,6},{6,7},{7,5},{5,3},{3,1},{1,0},{8,10},{10,12},{12... | collective-permute-start | bytes 1572872 | tf_op jit(solution)/shard_map/ppermute | solution.py:95
  4.7 12.0 %collective-permute-done.1 = bf16[128,2048]{1,0:T(8,128)(2,1)S(1)} collective-permute-done((bf16[128,2048]{1,0:T(8,128)(2,1)}, bf16[128,2048]{1,0:T(8,128)(2,1)S(1)}, u32[]{:S(2)}, u32[]{:S(2)}) %collective-permute-start.1) | collective-permute-done | bytes 524320 | tf_op jit(solution)/shard_map/ppermute | solution.py:95
  16.7 1.8 collective-permute-start.4
  24.5 6.1 %all-to-all-start = ((f32[8,8,128]{2,1,0:T(8,128)}), f32[8,8,128]{2,1,0:T(8,128)S(1)}, u32[]{:S(2)}, u32[]{:S(2)}) async-start(f32[8,8,128]{2,1,0:T(8,128)} %broadcast_in_dim.10), calls=%async_computation | async-start | bytes 65536 | tf_op jit(solution)/shard_map/all_to_all | solution.py:440
  30.7 6.6 %all-to-all-done.refs_1_ = f32[8,8,128]{2,1,0:T(8,128)S(1)} async-done(((f32[8,8,128]{2,1,0:T(8,128)}), f32[8,8,128]{2,1,0:T(8,128)S(1)}, u32[]{:S(2)}, u32[]{:S(2)}) %all-to-all-start) | async-done | bytes 32800 | tf_op jit(solution)/shard_map/all_to_all | solution.py:440
  38.5 1.7 collective-permute-start.3
  40.2 1.3 convolution_convert_fusion.19.refs_0_
  42.6 1.3 convolution_convert_fusion.12.refs_7_
  43.9 7.4 %collective-permute-done.3.refs_1_ = bf16[128,2048]{1,0:T(8,128)(2,1)S(1)} collective-permute-done((bf16[128,2048]{1,0:T(8,128)(2,1)S(1)}, bf16[128,2048]{1,0:T(8,128)(2,1)S(1)}, u32[]{:S(2)}, u32[]{:S(2)}) %collective-permute-start.3) | collective-permute-done | bytes 524320 | tf_op jit(solution)/shard_map/ppermute | solution.py:95
  52.0 1.6 collective-permute-start.17
  54.1 1.3 convolution_convert_fusion.18.refs_1_
  55.4 1.3 convolution_convert_fusion.13.refs_6_
  56.7 1.3 convolution_convert_fusion.17.refs_2_
  58.0 7.4 %collective-permute-done.6.refs_1_ = bf16[128,2048]{1,0:T(8,128)(2,1)S(1)} collective-permute-done((bf16[128,2048]{1,0:T(8,128)(2,1)}, bf16[128,2048]{1,0:T(8,128)(2,1)S(1)}, u32[]{:S(2)}, u32[]{:S(2)}) %collective-permute-start.6) | collective-permute-done | bytes 524320 | tf_op jit(solution)/shard_map/ppermute | solution.py:95
  66.6 1.6 collective-permute-start.18
  68.2 1.3 convolution_convert_fusion.14.refs_5_
  69.8 1.3 convolution_convert_fusion.15.refs_4_
  71.1 7.4 %collective-permute-done.10 = bf16[128,2048]{1,0:T(8,128)(2,1)S(1)} collective-permute-done((bf16[128,2048]{1,0:T(8,128)(2,1)}, bf16[128,2048]{1,0:T(8,128)(2,1)S(1)}, u32[]{:S(2)}, u32[]{:S(2)}) %collective-permute-start.10) | collective-permute-done | bytes 524320 | tf_op jit(solution)/shard_map/ppermute | solution.py:95
  78.9 1.6 collective-permute-start.19
  80.5 1.3 convolution_convert_fusion.10.refs_2_
  82.4 8.2 %collective-permute-done.11 = bf16[128,2048]{1,0:T(8,128)(2,1)S(1)} collective-permute-done((bf16[128,2048]{1,0:T(8,128)(2,1)S(1)}, bf16[128,2048]{1,0:T(8,128)(2,1)S(1)}, u32[]{:S(2)}, u32[]{:S(2)}) %collective-permute-start.11) | collective-permute-done | bytes 524320 | tf_op jit(solution)/shard_map/ppermute | solution.py:95
  91.0 1.6 collective-permute-start.20
  92.6 10.5 %shard_map.95 = (bf16[2,384,768]{2,1,0:T(8,128)(2,1)S(1)}, f32[2,384,768]{2,1,0:T(8,128)}, f32[2,384,768]{2,1,0:T(8,128)}) custom-call(bf16[96,2048]{1,0:T(8,128)(2,1)S(1)} %convolution_convert_fusion.19.refs_0_, bf16[96,2048]{1,0:T(8,128)(2,1)S(1)} %convolution_convert_fusion.18.refs_1_, bf16[96,2048]{1,0:T(8,128)(2,1)S(1)} %convolution_convert_fusion.17.refs_2_, ...), custom_call_target="tpu_custom_call" | custom-call | flops 4831838208 | bytes 1048576 | tf_op jit(solution)/shard_map/pallas_call | solution.py:163
  103.1 4.7 %shard_map.96.refs_9_ = bf16[8,96,2048]{2,1,0:T(8,128)(2,1)S(1)} custom-call(bf16[2,384,768]{2,1,0:T(8,128)(2,1)S(1)} %get-tuple-element.13.refs_0_, bf16[768,2048]{1,0:T(8,128)(2,1)} %bitcast.168, bf16[768,2048]{1,0:T(8,128)(2,1)} %collective-permute-done.9.refs_2_.refs_14_), custom_call_target="tpu_custom_call" | custom-call | flops 2415919104 | bytes 1048576 | tf_op jit(solution)/shard_map/pallas_call | solution.py:163
  112.2 1.5 collective-permute-start.13
  114.2 11.4 %collective-permute-done.21.refs_16_ = bf16[128,2048]{1,0:T(8,128)(2,1)S(1)} collective-permute-done((bf16[128,2048]{1,0:T(8,128)(2,1)S(1)}, bf16[128,2048]{1,0:T(8,128)(2,1)S(1)}, u32[]{:S(2)}, u32[]{:S(2)}) %collective-permute-start.21) | collective-permute-done | bytes 524320 | tf_op jit(solution)/shard_map/ppermute | solution.py:95
  128.7 12.3 %shard_map.99 = (bf16[2,384,768]{2,1,0:T(8,128)(2,1)S(1)}, bf16[2,384,768]{2,1,0:T(8,128)(2,1)}, f32[8,2,128]{2,1,0:T(2,128)}) custom-call(s32[2]{0:T(128)S(1)} %pad_add_fusion.1.refs_0_, bf16[96,2048]{1,0:T(8,128)(2,1)S(1)} %copy-done.2, bf16[96,2048]{1,0:T(8,128)(2,1)S(1)} %convolution_convert_fusion.10.refs_2_, ...), custom_call_target="tpu_custom_call" | custom-call | flops 2415919104 | bytes 1048576 | tf_op jit(solution)/shard_map/pallas_call | solution.py:163
  142.8 1.1 collective-permute-start.15
  143.9 10.3 %shard_map.100 = bf16[8,96,2048]{2,1,0:T(8,128)(2,1)} custom-call(bf16[2,384,768]{2,1,0:T(8,128)(2,1)S(1)} %get-tuple-element.16.refs_0_, bf16[2,384,768]{2,1,0:T(8,128)(2,1)S(1)} %copy-done.3, bf16[2048,768]{1,0:T(8,128)(2,1)} %bitcast.172, bf16[2048,768]{1,0:T(8,128)(2,1)} %collective-permute-done.7.refs_9_.refs_3_, bf16[2048,768]{1,0:T(8,128)(2,1)} %bitcast.175, ...), custom_call_target="tpu_custom_call" | custom-call | flops 4831838208 | bytes 1048576 | tf_op jit(solution)/shard_map/pallas_call | solution.py:163
  154.2 1.3 collective-permute-done.23
  156.6 1.3 fusion.14
  159.2 1.2 collective-permute-start.16
  160.4 11.2 %collective-permute-done.24 = bf16[128,2048]{1,0:T(8,128)(2,1)S(1)} collective-permute-done((bf16[128,2048]{1,0:T(8,128)(2,1)S(1)}, bf16[128,2048]{1,0:T(8,128)(2,1)S(1)}, u32[]{:S(2)}, u32[]{:S(2)}) %collective-permute-start.24) | collective-permute-done | bytes 524320 | tf_op jit(solution)/shard_map/ppermute | solution.py:95
  171.6 1.3 fusion.11
  175.1 1.3 fusion.15
  176.5 1.1 collective-permute-start.28
  177.6 9.0 %collective-permute-done.25 = bf16[128,2048]{1,0:T(8,128)(2,1)S(1)} collective-permute-done((bf16[128,2048]{1,0:T(8,128)(2,1)S(1)}, bf16[128,2048]{1,0:T(8,128)(2,1)S(1)}, u32[]{:S(2)}, u32[]{:S(2)}) %collective-permute-start.25) | collective-permute-done | bytes 524320 | tf_op jit(solution)/shard_map/ppermute | solution.py:95
  186.6 2.1 fusion.10
  190.1 2.1 fusion.13
  192.2 1.1 collective-permute-start.29
  193.3 8.8 %collective-permute-done.26 = bf16[128,2048]{1,0:T(8,128)(2,1)} collective-permute-done((bf16[128,2048]{1,0:T(8,128)(2,1)}, bf16[128,2048]{1,0:T(8,128)(2,1)}, u32[]{:S(2)}, u32[]{:S(2)}) %collective-permute-start.26) | collective-permute-done | bytes 524320 | tf_op jit(solution)/shard_map/ppermute | solution.py:95
  202.1 2.3 %fusion.9 = bf16[128,2048]{1,0:T(8,128)(2,1)} fusion(bf16[128,2048]{1,0:T(8,128)(2,1)} %collective-permute-done.26, bf16[8,96,2048]{2,1,0:T(8,128)(2,1)} %shard_map.100, bf16[8,96,128]{2,1,0:T(8,128)(2,1)S(1)} %get-tuple-element.11), kind=kOutput, calls=%fused_computation.21 | convolution fusion | flops 51118080 | bytes 1466368 | tf_op jit(solution)/shard_map/dot_general | solution.py:451
  204.4 1.2 collective-permute-start.27
  205.6 2.3 %fusion.12 = bf16[128,2048]{1,0:T(8,128)(2,1)} fusion(bf16[128,2048]{1,0:T(8,128)(2,1)} %collective-permute-done.29, bf16[8,96,2048]{2,1,0:T(8,128)(2,1)} %shard_map.100, bf16[8,96,128]{2,1,0:T(8,128)(2,1)S(1)} %get-tuple-element.11), kind=kOutput, calls=%fused_computation.24 | convolution fusion | flops 51118080 | bytes 1466368 | tf_op jit(solution)/shard_map/dot_general | solution.py:451
  208.9 3.3 %all-to-all-start.1 = ((f32[8,2,128]{2,1,0:T(2,128)}), f32[8,2,128]{2,1,0:T(2,128)S(1)}, u32[]{:S(2)}, u32[]{:S(2)}) async-start(f32[8,2,128]{2,1,0:T(2,128)} %get-tuple-element.18), calls=%async_computation.1 | async-start | bytes 16384 | tf_op jit(solution)/shard_map/all_to_all | solution.py:475
  212.3 6.4 %all-to-all-done.1 = f32[8,2,128]{2,1,0:T(2,128)S(1)} async-done(((f32[8,2,128]{2,1,0:T(2,128)}), f32[8,2,128]{2,1,0:T(2,128)S(1)}, u32[]{:S(2)}, u32[]{:S(2)}) %all-to-all-start.1) | async-done | bytes 8224 | tf_op jit(solution)/shard_map/all_to_all | solution.py:475
  219.4 2.3 %fusion.2 = bf16[128,2048]{1,0:T(8,128)(2,1)} fusion(bf16[128,2048]{1,0:T(8,128)(2,1)} %copy-done.12, bf16[128,2048]{1,0:T(8,128)(2,1)} %copy-done.13, bf16[8,96,2048]{2,1,0:T(8,128)(2,1)S(1)} %copy-done.1, bf16[8,96,128]{2,1,0:T(8,128)(2,1)S(1)} %get-tuple-element.11), kind=kOutput, calls=%fused_computation.14 | convolution fusion | flops 51642368 | bytes 1990656 | tf_op jit(solution)/shard_map/dot_general | solution.py:451
  221.7 2.5 %fusion.8 = bf16[128,2048]{1,0:T(8,128)(2,1)} fusion(bf16[128,2048]{1,0:T(8,128)(2,1)} %collective-permute-done.30, bf16[128,2048]{1,0:T(8,128)(2,1)} %collective-permute-done.27, bf16[8,96,2048]{2,1,0:T(8,128)(2,1)} %shard_map.100, bf16[8,96,128]{2,1,0:T(8,128)(2,1)S(1)} %get-tuple-element.11), kind=kOutput, calls=%fused_computation.20 | convolution fusion | flops 51642368 | bytes 1990656 | tf_op jit(solution)/shard_map/dot_general | solution.py:451
  (104 shorter events, 26.6 us)
Async XLA Ops:
  1.7 49.6 %copy-start.4 = (bf16[128,2048]{1,0:T(8,128)(2,1)}, bf16[128,2048]{1,0:T(8,128)(2,1)S(1)}, u32[]{:S(2)}) copy-start(bf16[128,2048]{1,0:T(8,128)(2,1)S(1)} %copy.17.refs_0_) | copy-start | bytes 1572868
  1.7 15.1 %collective-permute-start.1 = (bf16[128,2048]{1,0:T(8,128)(2,1)}, bf16[128,2048]{1,0:T(8,128)(2,1)S(1)}, u32[]{:S(2)}, u32[]{:S(2)}) collective-permute-start(bf16[128,2048]{1,0:T(8,128)(2,1)} %param.7), channel_id=1, source_target_pairs={{0,2},{2,4},{4,6},{6,7},{7,5},{5,3},{3,1},{1,0},{8,10},{10,12},{12... | collective-permute-start | bytes 1572872 | tf_op jit(solution)/shard_map/ppermute | solution.py:95
  4.7 13.9 %collective-permute-start = (bf16[128,2048]{1,0:T(8,128)(2,1)}, bf16[128,2048]{1,0:T(8,128)(2,1)S(1)}, u32[]{:S(2)}, u32[]{:S(2)}) collective-permute-start(bf16[128,2048]{1,0:T(8,128)(2,1)} %param.7), channel_id=1, source_target_pairs={{0,1},{2,0},{4,2},{6,4},{7,6},{5,7},{3,5},{1,3},{8,9},{10,8},{12,1... | collective-permute-start | bytes 1572872 | tf_op jit(solution)/shard_map/ppermute | solution.py:95
  16.7 21.8 %copy-start.11 = (bf16[128,2048]{1,0:T(8,128)(2,1)}, bf16[128,2048]{1,0:T(8,128)(2,1)S(1)}, u32[]{:S(2)}) copy-start(bf16[128,2048]{1,0:T(8,128)(2,1)S(1)} %collective-permute-done.1) | copy-start | bytes 1572868
  16.7 21.3 %collective-permute-start.4 = (bf16[128,2048]{1,0:T(8,128)(2,1)S(1)}, bf16[128,2048]{1,0:T(8,128)(2,1)S(1)}, u32[]{:S(2)}, u32[]{:S(2)}) collective-permute-start(bf16[128,2048]{1,0:T(8,128)(2,1)S(1)} %collective-permute-done.1), channel_id=1, source_target_pairs={{0,2},{2,4},{4,6},{6,7},{7,5},{5,3},{3,1},{1,0},{8,10},{10,12},{12... | collective-permute-start | bytes 1572872 | tf_op jit(solution)/shard_map/ppermute | solution.py:95
  18.6 21.6 %copy-start.8 = (bf16[128,2048]{1,0:T(8,128)(2,1)}, bf16[128,2048]{1,0:T(8,128)(2,1)S(1)}, u32[]{:S(2)}) copy-start(bf16[128,2048]{1,0:T(8,128)(2,1)S(1)} %collective-permute-done) | copy-start | bytes 1572868
  18.6 20.0 %collective-permute-start.2 = (bf16[128,2048]{1,0:T(8,128)(2,1)S(1)}, bf16[128,2048]{1,0:T(8,128)(2,1)S(1)}, u32[]{:S(2)}, u32[]{:S(2)}) collective-permute-start(bf16[128,2048]{1,0:T(8,128)(2,1)S(1)} %collective-permute-done), channel_id=1, source_target_pairs={{0,1},{2,0},{4,2},{6,4},{7,6},{5,7},{3,5},{1,3},{8,9},{10,8},{12,1... | collective-permute-start | bytes 1572872 | tf_op jit(solution)/shard_map/ppermute | solution.py:95
  18.8 73.9 %collective-permute-start.7 = (bf16[2048,768]{1,0:T(8,128)(2,1)}, bf16[2048,768]{1,0:T(8,128)(2,1)}, u32[]{:S(2)}, u32[]{:S(2)}) collective-permute-start(bf16[2048,768]{1,0:T(8,128)(2,1)} %bitcast.170), channel_id=1, source_target_pairs={{0,8},{8,0},{1,9},{9,1},{2,10},{10,2},{3,11},{11,3},{4,12},{12,4},... | collective-permute-start | bytes 9437192 | tf_op jit(solution)/shard_map/ppermute | solution.py:416
  18.8 73.9 %collective-permute-start.8 = (bf16[2048,768]{1,0:T(8,128)(2,1)}, bf16[2048,768]{1,0:T(8,128)(2,1)}, u32[]{:S(2)}, u32[]{:S(2)}) collective-permute-start(bf16[2048,768]{1,0:T(8,128)(2,1)} %bitcast.173), channel_id=1, source_target_pairs={{0,8},{8,0},{1,9},{9,1},{2,10},{10,2},{3,11},{11,3},{4,12},{12,4},... | collective-permute-start | bytes 9437192 | tf_op jit(solution)/shard_map/ppermute | solution.py:416
  19.3 83.8 %collective-permute-start.9 = (bf16[768,2048]{1,0:T(8,128)(2,1)}, bf16[768,2048]{1,0:T(8,128)(2,1)}, u32[]{:S(2)}, u32[]{:S(2)}) collective-permute-start(bf16[768,2048]{1,0:T(8,128)(2,1)} %bitcast.167), channel_id=1, source_target_pairs={{0,8},{8,0},{1,9},{9,1},{2,10},{10,2},{3,11},{11,3},{4,12},{12,4},... | collective-permute-start | bytes 9437192 | tf_op jit(solution)/shard_map/ppermute | solution.py:416
  24.5 12.7 %all-to-all-start = ((f32[8,8,128]{2,1,0:T(8,128)}), f32[8,8,128]{2,1,0:T(8,128)S(1)}, u32[]{:S(2)}, u32[]{:S(2)}) async-start(f32[8,8,128]{2,1,0:T(8,128)} %broadcast_in_dim.10), calls=%async_computation | async-start | bytes 65536 | tf_op jit(solution)/shard_map/all_to_all | solution.py:440
  38.1 15.6 %copy-start.9 = (bf16[128,2048]{1,0:T(8,128)(2,1)}, bf16[128,2048]{1,0:T(8,128)(2,1)S(1)}, u32[]{:S(2)}) copy-start(bf16[128,2048]{1,0:T(8,128)(2,1)S(1)} %collective-permute-done.4) | copy-start | bytes 1572868
  38.1 15.6 %collective-permute-start.5 = (bf16[128,2048]{1,0:T(8,128)(2,1)S(1)}, bf16[128,2048]{1,0:T(8,128)(2,1)}, u32[]{:S(2)}, u32[]{:S(2)}) collective-permute-start(bf16[128,2048]{1,0:T(8,128)(2,1)S(1)} %collective-permute-done.4), channel_id=1, source_target_pairs={{0,2},{2,4},{4,6},{6,7},{7,5},{5,3},{3,1},{1,0},{8,10},{10,12},{12... | collective-permute-start | bytes 1572872 | tf_op jit(solution)/shard_map/ppermute | solution.py:95
  38.5 12.7 %copy-start.10 = (bf16[128,2048]{1,0:T(8,128)(2,1)}, bf16[128,2048]{1,0:T(8,128)(2,1)S(1)}, u32[]{:S(2)}) copy-start(bf16[128,2048]{1,0:T(8,128)(2,1)S(1)} %collective-permute-done.2) | copy-start | bytes 1572868
  38.5 12.7 %collective-permute-start.3 = (bf16[128,2048]{1,0:T(8,128)(2,1)S(1)}, bf16[128,2048]{1,0:T(8,128)(2,1)S(1)}, u32[]{:S(2)}, u32[]{:S(2)}) collective-permute-start(bf16[128,2048]{1,0:T(8,128)(2,1)S(1)} %collective-permute-done.2), channel_id=1, source_target_pairs={{0,1},{2,0},{4,2},{6,4},{7,6},{5,7},{3,5},{1,3},{8,9},{10,8},{12,1... | collective-permute-start | bytes 1572872 | tf_op jit(solution)/shard_map/ppermute | solution.py:95
  51.2 0.8 copy-start.5
  52.0 17.5 %copy-start.6 = (bf16[128,2048]{1,0:T(8,128)(2,1)S(1)}, bf16[128,2048]{1,0:T(8,128)(2,1)}, u32[]{:S(2)}) copy-start(bf16[128,2048]{1,0:T(8,128)(2,1)} %copy-done.5) | copy-start | bytes 1572868
  52.0 14.6 %collective-permute-start.17 = (bf16[128,2048]{1,0:T(8,128)(2,1)}, bf16[128,2048]{1,0:T(8,128)(2,1)}, u32[]{:S(2)}, u32[]{:S(2)}) collective-permute-start(bf16[128,2048]{1,0:T(8,128)(2,1)} %shard_map.98), channel_id=1, source_target_pairs={{0,1},{2,0},{4,2},{6,4},{7,6},{5,7},{3,5},{1,3},{8,9},{10,8},{12,1... | collective-permute-start | bytes 1572872 | tf_op jit(solution)/shard_map/ppermute | solution.py:95
  53.7 11.7 %collective-permute-start.6 = (bf16[128,2048]{1,0:T(8,128)(2,1)}, bf16[128,2048]{1,0:T(8,128)(2,1)S(1)}, u32[]{:S(2)}, u32[]{:S(2)}) collective-permute-start(bf16[128,2048]{1,0:T(8,128)(2,1)} %collective-permute-done.5), channel_id=1, source_target_pairs={{0,2},{2,4},{4,6},{6,7},{7,5},{5,3},{3,1},{1,0},{8,10},{10,12},{12... | collective-permute-start | bytes 1572872 | tf_op jit(solution)/shard_map/ppermute | solution.py:95
  65.4 0.8 copy-start.7
  66.2 12.3 %collective-permute-start.10 = (bf16[128,2048]{1,0:T(8,128)(2,1)}, bf16[128,2048]{1,0:T(8,128)(2,1)S(1)}, u32[]{:S(2)}, u32[]{:S(2)}) collective-permute-start(bf16[128,2048]{1,0:T(8,128)(2,1)} %shard_map.97), channel_id=1, source_target_pairs={{0,2},{2,4},{4,6},{6,7},{7,5},{5,3},{3,1},{1,0},{8,10},{10,12},{12... | collective-permute-start | bytes 1572872 | tf_op jit(solution)/shard_map/ppermute | solution.py:95
  66.6 12.3 %collective-permute-start.18 = (bf16[128,2048]{1,0:T(8,128)(2,1)}, bf16[128,2048]{1,0:T(8,128)(2,1)S(1)}, u32[]{:S(2)}, u32[]{:S(2)}) collective-permute-start(bf16[128,2048]{1,0:T(8,128)(2,1)} %collective-permute-done.17), channel_id=1, source_target_pairs={{0,1},{2,0},{4,2},{6,4},{7,6},{5,7},{3,5},{1,3},{8,9},{10,8},{12,1... | collective-permute-start | bytes 1572872 | tf_op jit(solution)/shard_map/ppermute | solution.py:95
  78.5 12.1 %collective-permute-start.11 = (bf16[128,2048]{1,0:T(8,128)(2,1)S(1)}, bf16[128,2048]{1,0:T(8,128)(2,1)S(1)}, u32[]{:S(2)}, u32[]{:S(2)}) collective-permute-start(bf16[128,2048]{1,0:T(8,128)(2,1)S(1)} %collective-permute-done.10), channel_id=1, source_target_pairs={{0,2},{2,4},{4,6},{6,7},{7,5},{5,3},{3,1},{1,0},{8,10},{10,12},{12... | collective-permute-start | bytes 1572872 | tf_op jit(solution)/shard_map/ppermute | solution.py:95
  78.9 12.1 %collective-permute-start.19 = (bf16[128,2048]{1,0:T(8,128)(2,1)S(1)}, bf16[128,2048]{1,0:T(8,128)(2,1)S(1)}, u32[]{:S(2)}, u32[]{:S(2)}) collective-permute-start(bf16[128,2048]{1,0:T(8,128)(2,1)S(1)} %collective-permute-done.18), channel_id=1, source_target_pairs={{0,1},{2,0},{4,2},{6,4},{7,6},{5,7},{3,5},{1,3},{8,9},{10,8},{12,1... | collective-permute-start | bytes 1572872 | tf_op jit(solution)/shard_map/ppermute | solution.py:95
  90.6 17.5 %collective-permute-start.12 = (bf16[128,2048]{1,0:T(8,128)(2,1)S(1)}, bf16[128,2048]{1,0:T(8,128)(2,1)S(1)}, u32[]{:S(2)}, u32[]{:S(2)}) collective-permute-start(bf16[128,2048]{1,0:T(8,128)(2,1)S(1)} %collective-permute-done.11), channel_id=1, source_target_pairs={{0,2},{2,4},{4,6},{6,7},{7,5},{5,3},{3,1},{1,0},{8,10},{10,12},{12... | collective-permute-start | bytes 1572872 | tf_op jit(solution)/shard_map/ppermute | solution.py:95
  91.0 18.5 %collective-permute-start.20 = (bf16[128,2048]{1,0:T(8,128)(2,1)S(1)}, bf16[128,2048]{1,0:T(8,128)(2,1)S(1)}, u32[]{:S(2)}, u32[]{:S(2)}) collective-permute-start(bf16[128,2048]{1,0:T(8,128)(2,1)S(1)} %collective-permute-done.19), channel_id=1, source_target_pairs={{0,1},{2,0},{4,2},{6,4},{7,6},{5,7},{3,5},{1,3},{8,9},{10,8},{12,1... | collective-permute-start | bytes 1572872 | tf_op jit(solution)/shard_map/ppermute | solution.py:95
  107.8 19.5 %copy-start = (bf16[8,96,2048]{2,1,0:T(8,128)(2,1)}, bf16[8,96,2048]{2,1,0:T(8,128)(2,1)S(1)}, u32[]{:S(2)}) copy-start(bf16[8,96,2048]{2,1,0:T(8,128)(2,1)S(1)} %shard_map.96.refs_9_) | copy-start | bytes 9437188
  111.0 14.6 %collective-permute-start.21 = (bf16[128,2048]{1,0:T(8,128)(2,1)S(1)}, bf16[128,2048]{1,0:T(8,128)(2,1)S(1)}, u32[]{:S(2)}, u32[]{:S(2)}) collective-permute-start(bf16[128,2048]{1,0:T(8,128)(2,1)S(1)} %broadcast_add_fusion), channel_id=1, source_target_pairs={{0,1},{2,0},{4,2},{6,4},{7,6},{5,7},{3,5},{1,3},{8,9},{10,8},{12,1... | collective-permute-start | bytes 1572872 | tf_op jit(solution)/shard_map/ppermute | solution.py:95
  111.8 16.9 %copy-start.2 = (bf16[96,2048]{1,0:T(8,128)(2,1)S(1)}, bf16[96,2048]{1,0:T(8,128)(2,1)}, u32[]{:S(2)}) copy-start(bf16[96,2048]{1,0:T(8,128)(2,1)} %convolution_convert_fusion.11.refs_1_) | copy-start | bytes 1179652
  112.2 14.8 %collective-permute-start.13 = (bf16[128,2048]{1,0:T(8,128)(2,1)S(1)}, bf16[128,2048]{1,0:T(8,128)(2,1)S(1)}, u32[]{:S(2)}, u32[]{:S(2)}) collective-permute-start(bf16[128,2048]{1,0:T(8,128)(2,1)S(1)} %broadcast_add_fusion.1), channel_id=1, source_target_pairs={{0,2},{2,4},{4,6},{6,7},{7,5},{5,3},{3,1},{1,0},{8,10},{10,12},{12... | collective-permute-start | bytes 1572872 | tf_op jit(solution)/shard_map/ppermute | solution.py:95
  126.0 15.1 %collective-permute-start.22 = (bf16[128,2048]{1,0:T(8,128)(2,1)S(1)}, bf16[128,2048]{1,0:T(8,128)(2,1)S(1)}, u32[]{:S(2)}, u32[]{:S(2)}) collective-permute-start(bf16[128,2048]{1,0:T(8,128)(2,1)S(1)} %fusion.7), channel_id=1, source_target_pairs={{0,1},{2,0},{4,2},{6,4},{7,6},{5,7},{3,5},{1,3},{8,9},{10,8},{12,1... | collective-permute-start | bytes 1572872 | tf_op jit(solution)/shard_map/ppermute | solution.py:95
  127.3 15.1 %collective-permute-start.14 = (bf16[128,2048]{1,0:T(8,128)(2,1)S(1)}, bf16[128,2048]{1,0:T(8,128)(2,1)S(1)}, u32[]{:S(2)}, u32[]{:S(2)}) collective-permute-start(bf16[128,2048]{1,0:T(8,128)(2,1)S(1)} %fusion.5), channel_id=1, source_target_pairs={{0,2},{2,4},{4,6},{6,7},{7,5},{5,3},{3,1},{1,0},{8,10},{10,12},{12... | collective-permute-start | bytes 1572872 | tf_op jit(solution)/shard_map/ppermute | solution.py:95
  128.7 12.4 %copy-start.1 = (bf16[8,96,2048]{2,1,0:T(8,128)(2,1)S(1)}, bf16[8,96,2048]{2,1,0:T(8,128)(2,1)}, u32[]{:S(2)}) copy-start(bf16[8,96,2048]{2,1,0:T(8,128)(2,1)} %copy-done) | copy-start | bytes 9437188
  141.1 2.8 %copy-start.3 = (bf16[2,384,768]{2,1,0:T(8,128)(2,1)S(1)}, bf16[2,384,768]{2,1,0:T(8,128)(2,1)}, u32[]{:S(2)}) copy-start(bf16[2,384,768]{2,1,0:T(8,128)(2,1)} %get-tuple-element.17.refs_1_) | copy-start | bytes 3538948
  141.4 14.0 %collective-permute-start.23 = (bf16[128,2048]{1,0:T(8,128)(2,1)S(1)}, bf16[128,2048]{1,0:T(8,128)(2,1)S(1)}, u32[]{:S(2)}, u32[]{:S(2)}) collective-permute-start(bf16[128,2048]{1,0:T(8,128)(2,1)S(1)} %fusion.6), channel_id=1, source_target_pairs={{0,1},{2,0},{4,2},{6,4},{7,6},{5,7},{3,5},{1,3},{8,9},{10,8},{12,1... | collective-permute-start | bytes 1572872 | tf_op jit(solution)/shard_map/ppermute | solution.py:95
  142.8 16.1 %collective-permute-start.15 = (bf16[128,2048]{1,0:T(8,128)(2,1)S(1)}, bf16[128,2048]{1,0:T(8,128)(2,1)S(1)}, u32[]{:S(2)}, u32[]{:S(2)}) collective-permute-start(bf16[128,2048]{1,0:T(8,128)(2,1)S(1)} %fusion.4), channel_id=1, source_target_pairs={{0,2},{2,4},{4,6},{6,7},{7,5},{5,3},{3,1},{1,0},{8,10},{10,12},{12... | collective-permute-start | bytes 1572872 | tf_op jit(solution)/shard_map/ppermute | solution.py:95
  155.4 33.3 %copy-start.12 = (bf16[128,2048]{1,0:T(8,128)(2,1)}, bf16[128,2048]{1,0:T(8,128)(2,1)S(1)}, u32[]{:S(2)}) copy-start(bf16[128,2048]{1,0:T(8,128)(2,1)S(1)} %collective-permute-done.23) | copy-start | bytes 1572868
  158.0 13.6 %collective-permute-start.24 = (bf16[128,2048]{1,0:T(8,128)(2,1)S(1)}, bf16[128,2048]{1,0:T(8,128)(2,1)S(1)}, u32[]{:S(2)}, u32[]{:S(2)}) collective-permute-start(bf16[128,2048]{1,0:T(8,128)(2,1)S(1)} %fusion.14), channel_id=1, source_target_pairs={{0,1},{2,0},{4,2},{6,4},{7,6},{5,7},{3,5},{1,3},{8,9},{10,8},{12,1... | collective-permute-start | bytes 1572872 | tf_op jit(solution)/shard_map/ppermute | solution.py:95
  159.2 14.7 %collective-permute-start.16 = (bf16[128,2048]{1,0:T(8,128)(2,1)S(1)}, bf16[128,2048]{1,0:T(8,128)(2,1)S(1)}, u32[]{:S(2)}, u32[]{:S(2)}) collective-permute-start(bf16[128,2048]{1,0:T(8,128)(2,1)S(1)} %fusion.3), channel_id=1, source_target_pairs={{0,2},{2,4},{4,6},{6,7},{7,5},{5,3},{3,1},{1,0},{8,10},{10,12},{12... | collective-permute-start | bytes 1572872 | tf_op jit(solution)/shard_map/ppermute | solution.py:95
  172.9 13.7 %collective-permute-start.25 = (bf16[128,2048]{1,0:T(8,128)(2,1)S(1)}, bf16[128,2048]{1,0:T(8,128)(2,1)S(1)}, u32[]{:S(2)}, u32[]{:S(2)}) collective-permute-start(bf16[128,2048]{1,0:T(8,128)(2,1)S(1)} %fusion.11), channel_id=1, source_target_pairs={{0,1},{2,0},{4,2},{6,4},{7,6},{5,7},{3,5},{1,3},{8,9},{10,8},{12,1... | collective-permute-start | bytes 1572872 | tf_op jit(solution)/shard_map/ppermute | solution.py:95
  173.9 16.1 %copy-start.13 = (bf16[128,2048]{1,0:T(8,128)(2,1)}, bf16[128,2048]{1,0:T(8,128)(2,1)S(1)}, u32[]{:S(2)}) copy-start(bf16[128,2048]{1,0:T(8,128)(2,1)S(1)} %collective-permute-done.16) | copy-start | bytes 1572868
  176.5 42.2 %copy-start.14 = (s32[128,4]{0,1:T(4,128)S(1)}, s32[128,4]{0,1:T(4,128)}, u32[]{:S(2)}) copy-start(s32[128,4]{0,1:T(4,128)} %param.9) | copy-start | bytes 6148
  176.5 13.6 %collective-permute-start.28 = (bf16[128,2048]{1,0:T(8,128)(2,1)S(1)}, bf16[128,2048]{1,0:T(8,128)(2,1)S(1)}, u32[]{:S(2)}, u32[]{:S(2)}) collective-permute-start(bf16[128,2048]{1,0:T(8,128)(2,1)S(1)} %fusion.15), channel_id=1, source_target_pairs={{0,2},{2,4},{4,6},{6,7},{7,5},{5,3},{3,1},{1,0},{8,10},{10,12},{12... | collective-permute-start | bytes 1572872 | tf_op jit(solution)/shard_map/ppermute | solution.py:95
  188.8 13.3 %collective-permute-start.26 = (bf16[128,2048]{1,0:T(8,128)(2,1)}, bf16[128,2048]{1,0:T(8,128)(2,1)}, u32[]{:S(2)}, u32[]{:S(2)}) collective-permute-start(bf16[128,2048]{1,0:T(8,128)(2,1)} %fusion.10), channel_id=1, source_target_pairs={{0,1},{2,0},{4,2},{6,4},{7,6},{5,7},{3,5},{1,3},{8,9},{10,8},{12,1... | collective-permute-start | bytes 1572872 | tf_op jit(solution)/shard_map/ppermute | solution.py:95
  192.2 13.4 %collective-permute-start.29 = (bf16[128,2048]{1,0:T(8,128)(2,1)}, bf16[128,2048]{1,0:T(8,128)(2,1)}, u32[]{:S(2)}, u32[]{:S(2)}) collective-permute-start(bf16[128,2048]{1,0:T(8,128)(2,1)} %fusion.13), channel_id=1, source_target_pairs={{0,2},{2,4},{4,6},{6,7},{7,5},{5,3},{3,1},{1,0},{8,10},{10,12},{12... | collective-permute-start | bytes 1572872 | tf_op jit(solution)/shard_map/ppermute | solution.py:95
  204.4 17.3 %collective-permute-start.27 = (bf16[128,2048]{1,0:T(8,128)(2,1)}, bf16[128,2048]{1,0:T(8,128)(2,1)}, u32[]{:S(2)}, u32[]{:S(2)}) collective-permute-start(bf16[128,2048]{1,0:T(8,128)(2,1)} %fusion.9), channel_id=1, source_target_pairs={{0,1},{2,0},{4,2},{6,4},{7,6},{5,7},{3,5},{1,3},{8,9},{10,8},{12,1... | collective-permute-start | bytes 1572872 | tf_op jit(solution)/shard_map/ppermute | solution.py:95
  207.9 13.8 %collective-permute-start.30 = (bf16[128,2048]{1,0:T(8,128)(2,1)}, bf16[128,2048]{1,0:T(8,128)(2,1)}, u32[]{:S(2)}, u32[]{:S(2)}) collective-permute-start(bf16[128,2048]{1,0:T(8,128)(2,1)} %fusion.12), channel_id=1, source_target_pairs={{0,2},{2,4},{4,6},{6,7},{7,5},{5,3},{3,1},{1,0},{8,10},{10,12},{12... | collective-permute-start | bytes 1572872 | tf_op jit(solution)/shard_map/ppermute | solution.py:95
  208.9 9.8 %all-to-all-start.1 = ((f32[8,2,128]{2,1,0:T(2,128)}), f32[8,2,128]{2,1,0:T(2,128)S(1)}, u32[]{:S(2)}, u32[]{:S(2)}) async-start(f32[8,2,128]{2,1,0:T(2,128)} %get-tuple-element.18), calls=%async_computation.1 | async-start | bytes 16384 | tf_op jit(solution)/shard_map/all_to_all | solution.py:475

commit v4 on v3

--- a/solution.py
+++ b/solution.py
@@ -97,15 +97,20 @@
 
 def ring_gather(shard, count, far_step, behind={}):
     held = {0: shard}
-    latest = {}
+    arrivals = {}
     for step in (far_step, -far_step):
         hops = count // 2 if step == far_step else (count - 1) // 2
-        moving = held_back(shard, behind[step]) if step in behind else shard
+        moving = shard
+        arrivals[step] = []
         for hop in range(1, hops + 1):
+            if (step, hop) in behind:
+                moving = held_back(moving, behind[step, hop])
+                if hop > 1:
+                    held[(-step * (hop - 1)) % count] = moving
             moving = ring_shift(moving, count, step)
             held[(-step * hop) % count] = moving
-        latest[step] = (moving,)
-    return [held[place] for place in range(count)], latest
+            arrivals[step].append(moving)
+    return [held[place] for place in range(count)], arrivals
 
 
 def after(array, *others):
@@ -425,20 +430,21 @@
     capacity = max(2, 3 * token_count * top_count // (2 * expert_count))
     f32, bf16 = jnp.float32, jnp.bfloat16
 
-    in_shards, in_latest = ring_gather(tokens, chips, 1)
-    grad_shards, grad_latest = ring_gather(cotangent, chips, -1, in_latest)
-    gate_mats = (w_gate[0], swap_cores(w_gate[0]))
-    up_mats = (w_up[0], swap_cores(w_up[0]))
-    down_mats = (w_down[0], swap_cores(w_down[0]))
-
     core = lax.axis_index("grp")
     chip = lax.axis_index("ep")
     ids = jnp.stack([core, chip]).astype(jnp.int32)
     table = jnp.concatenate([routes.astype(f32), gates.astype(f32)], axis=1).T
-    table = after(table, in_shards[1], in_shards[-1])
     copies = jnp.broadcast_to(table[None], (chips,) + table.shape)
     tables = lax.all_to_all(copies, "ep", split_axis=0, concat_axis=0, tiled=True)
     pick, spread = run_routing(ids, tables, top_count, capacity)
+
+    behind = {(step, 2): (tables,) for step in (1, -1)}
+    in_shards, in_hops = ring_gather(tokens, chips, 1, behind)
+    behind = {(step, 1): (in_hops[step][0],) for step in (1, -1)}
+    grad_shards, _ = ring_gather(cotangent, chips, -1, behind)
+    gate_mats = (w_gate[0], swap_cores(w_gate[0]))
+    up_mats = (w_up[0], swap_cores(w_up[0]))
+    down_mats = (w_down[0], swap_cores(w_down[0]))
 
     def gather_rows(shards):
         return [
@@ -462,18 +468,22 @@
     rows_in = gather_rows(in_shards)
     hidden, slope, activated = run_hidden(rows_in, gate_mats, up_mats)
     outputs = run_down(hidden, down_mats, chips)
-    behind = {(step, 0): grad_latest[step] for step in (1, -1)}
+    rows_grad = gather_rows(grad_shards)
+    d_pre_gate, d_pre_up, per_token = run_d_hidden(
+        ids, rows_grad, outputs, pick, slope, activated, down_mats, ()
+    )
+    behind = {(step, 1): (per_token,) for step in (1, -1)}
     mixed, mixed_hops = ring_reduce(scatter_rows(outputs), chips, 1, behind)
-
-    rows_grad = gather_rows(grad_shards)
-    hop_of = lambda hop: [mixed_hops[step][min(hop, len(mixed_hops[step]) - 1)] for step in (1, -1)]
-    d_pre_gate, d_pre_up, per_token = run_d_hidden(
-        ids, rows_grad, outputs, pick, slope, activated, down_mats, hop_of(0)
-    )
-    d_copies = run_d_copy(d_pre_gate, d_pre_up, gate_mats, up_mats, chips, hop_of(1))
+    d_copies = run_d_copy(
+        d_pre_gate, d_pre_up, gate_mats, up_mats, chips, [mixed_hops[step][0] for step in (1, -1)]
+    )
 
     returned = lax.all_to_all(per_token, "ep", split_axis=0, concat_axis=0, tiled=True)
-    behind = {(step, 0): (mixed_hops[step][-1],) for step in (1, -1)}
+    behind = {
+        (step, hop): (mixed_hops[step][hop + 1],)
+        for step in (1, -1)
+        for hop in range(len(mixed_hops[step]) - 1)
+    }
     d_tokens, _ = ring_reduce(scatter_rows(d_copies), chips, -1, behind)
     chip_ids = jnp.arange(chips, dtype=jnp.int32)
     served = jnp.stack([core * chips + chip_ids, (1 - core) * chips + chip_ids], axis=1)

time: 225 us -> 221 us (0.982)
  matrix products: 33.1 us -> 27.6 us
  local copies, waits for them, and re-layouts: 7.53 us -> 11 us
    dot_general x16, matrix products: 13.2 us -> 9.04 us  [gather_rows(): jnp.dot(pick[s], shards[s], preferred_element_type=f32).astype(bf16)]
    unnamed x32 -> x26, local copies, waits for them, and re-layouts: 3.49 us -> 6.01 us
    ppermute x28, waiting for transfers between devices: 84.4 us -> 82 us  [ring_shift(): return lax.ppermute(array, 'ep', pairs)]
  transfers between devices with their start and end apart: 33 -> 33, of which waited for: 13 -> 18; matrix products, arithmetic and copies ran while one was open for 16% -> 15% of each run, Pallas kernels for 17% -> 17%
where the time goes in v4:
time: 221 us; the launch traced here: 220 us
  waiting for transfers between devices  95.4 us (43%)
  starting transfers between devices  40.9 us (19%)
  Pallas kernels  38.1 us (17%)
  matrix products  27.6 us (12%)
  local copies, waits for them, and re-layouts  11 us (5%)
  between operations  4.98 us (2%)
    ppermute x28, waiting for transfers between devices, ring_shift(): return lax.ppermute(array, 'ep', pairs)  82 us
    pallas_call x5, Pallas kernels, call_kernel(): pl.pallas_call(body, out_shape=outs, in_specs=[pl.BlockSpec(memory_space=...  38.1 us
    ppermute x28, starting transfers between devices, ring_shift(): return lax.ppermute(array, 'ep', pairs)  31.3 us
    dot_general x16, matrix products, share_of(): lax.dot_general(spread[s], blocks[s], (((0,), (0,)), ((), ())), preferred...  18.6 us
    dot_general x16, matrix products, gather_rows(): jnp.dot(pick[s], shards[s], preferred_element_type=f32).astype(bf16)  9.04 us
    all_to_all x1, waiting for transfers between devices, body_ring(): lax.all_to_all(copies, 'ep', split_axis=0, concat_axis=0, tiled=True)  6.91 us
    all_to_all x1, waiting for transfers between devices, body_ring(): lax.all_to_all(per_token, 'ep', split_axis=0, concat_axis=0, tiled=True)  6.44 us
    all_to_all x1, starting transfers between devices, body_ring(): lax.all_to_all(copies, 'ep', split_axis=0, concat_axis=0, tiled=True)  6.25 us
  transfers between devices with their start and end apart: 33, of which 18 were waited for; matrix products, arithmetic and copies ran while one was open for 15% of the time, Pallas kernels for 17%

profile of v4, /device:TPU:0, one launch (start us, length us, event | category | flops | bytes accessed | tf_op | source)
XLA Modules:
  0.0 220.1 jit_solution(15325776691097989046)
XLA Ops:
  1.7 3.0 %collective-permute-start.3 = (bf16[128,2048]{1,0:T(8,128)(2,1)}, bf16[128,2048]{1,0:T(8,128)(2,1)S(1)}, u32[]{:S(2)}, u32[]{:S(2)}) collective-permute-start(bf16[128,2048]{1,0:T(8,128)(2,1)} %param.7), channel_id=1, source_target_pairs={{0,2},{2,4},{4,6},{6,7},{7,5},{5,3},{3,1},{1,0},{8,10},{10,12},{12... | collective-permute-start | bytes 1572872 | tf_op jit(solution)/shard_map/ppermute | solution.py:95
  6.7 6.3 %all-to-all-start = ((f32[8,8,128]{2,1,0:T(8,128)}), f32[8,8,128]{2,1,0:T(8,128)S(1)}, u32[]{:S(2)}, u32[]{:S(2)}) async-start(f32[8,8,128]{2,1,0:T(8,128)} %broadcast_in_dim.10), calls=%async_computation | async-start | bytes 65536 | tf_op jit(solution)/shard_map/all_to_all | solution.py:438
  13.9 6.9 %all-to-all-done.refs_1_ = f32[8,8,128]{2,1,0:T(8,128)S(1)} async-done(((f32[8,8,128]{2,1,0:T(8,128)}), f32[8,8,128]{2,1,0:T(8,128)S(1)}, u32[]{:S(2)}, u32[]{:S(2)}) %all-to-all-start) | async-done | bytes 32800 | tf_op jit(solution)/shard_map/all_to_all | solution.py:438
  24.1 1.4 collective-permute-start.1
  25.5 1.4 collective-permute-start.11
  27.5 1.3 convolution_convert_fusion.19.refs_0_
  28.8 9.8 %collective-permute-done.4 = bf16[128,2048]{1,0:T(8,128)(2,1)} collective-permute-done((bf16[128,2048]{1,0:T(8,128)(2,1)}, bf16[128,2048]{1,0:T(8,128)(2,1)}, u32[]{:S(2)}, u32[]{:S(2)}) %collective-permute-start.4) | collective-permute-done | bytes 524320 | tf_op jit(solution)/shard_map/ppermute | solution.py:95
  41.0 1.3 convolution_convert_fusion.18.refs_1_
  42.3 5.2 %collective-permute-done.11 = bf16[128,2048]{1,0:T(8,128)(2,1)S(1)} collective-permute-done((bf16[128,2048]{1,0:T(8,128)(2,1)}, bf16[128,2048]{1,0:T(8,128)(2,1)S(1)}, u32[]{:S(2)}, u32[]{:S(2)}) %collective-permute-start.11) | collective-permute-done | bytes 524320 | tf_op jit(solution)/shard_map/ppermute | solution.py:95
  47.4 2.3 %collective-permute-done.15 = bf16[128,2048]{1,0:T(8,128)(2,1)S(1)} collective-permute-done((bf16[128,2048]{1,0:T(8,128)(2,1)}, bf16[128,2048]{1,0:T(8,128)(2,1)S(1)}, u32[]{:S(2)}, u32[]{:S(2)}) %collective-permute-start.15) | collective-permute-done | bytes 524320 | tf_op jit(solution)/shard_map/ppermute | solution.py:95
  49.7 1.4 collective-permute-start.2
  51.1 1.3 convolution_convert_fusion.13.refs_6_
  52.4 5.8 %collective-permute-done.5 = bf16[128,2048]{1,0:T(8,128)(2,1)S(1)} collective-permute-done((bf16[128,2048]{1,0:T(8,128)(2,1)}, bf16[128,2048]{1,0:T(8,128)(2,1)S(1)}, u32[]{:S(2)}, u32[]{:S(2)}) %collective-permute-start.5) | collective-permute-done | bytes 524320 | tf_op jit(solution)/shard_map/ppermute | solution.py:95
  60.0 4.6 %collective-permute-done.2 = bf16[128,2048]{1,0:T(8,128)(2,1)S(1)} collective-permute-done((bf16[128,2048]{1,0:T(8,128)(2,1)S(1)}, bf16[128,2048]{1,0:T(8,128)(2,1)S(1)}, u32[]{:S(2)}, u32[]{:S(2)}) %collective-permute-start.2) | collective-permute-done | bytes 524320 | tf_op jit(solution)/shard_map/ppermute | solution.py:95
  65.5 7.5 %collective-permute-done.12 = bf16[128,2048]{1,0:T(8,128)(2,1)S(1)} collective-permute-done((bf16[128,2048]{1,0:T(8,128)(2,1)S(1)}, bf16[128,2048]{1,0:T(8,128)(2,1)S(1)}, u32[]{:S(2)}, u32[]{:S(2)}) %collective-permute-start.12) | collective-permute-done | bytes 524320 | tf_op jit(solution)/shard_map/ppermute | solution.py:95
  73.1 1.4 collective-permute-start.13
  76.0 8.3 %collective-permute-done.13 = bf16[128,2048]{1,0:T(8,128)(2,1)S(1)} collective-permute-done((bf16[128,2048]{1,0:T(8,128)(2,1)S(1)}, bf16[128,2048]{1,0:T(8,128)(2,1)S(1)}, u32[]{:S(2)}, u32[]{:S(2)}) %collective-permute-start.13) | collective-permute-done | bytes 524320 | tf_op jit(solution)/shard_map/ppermute | solution.py:95
  86.1 2.2 collective-permute-done.6
  88.2 1.8 collective-permute-start.14
  90.3 6.7 %collective-permute-done.17 = bf16[128,2048]{1,0:T(8,128)(2,1)S(1)} collective-permute-done((bf16[128,2048]{1,0:T(8,128)(2,1)S(1)}, bf16[128,2048]{1,0:T(8,128)(2,1)S(1)}, u32[]{:S(2)}, u32[]{:S(2)}) %collective-permute-start.17) | collective-permute-done | bytes 524320 | tf_op jit(solution)/shard_map/ppermute | solution.py:95
  97.3 1.7 copy-done.9
  99.0 10.5 %shard_map.97 = (bf16[2,384,768]{2,1,0:T(8,128)(2,1)S(1)}, f32[2,384,768]{2,1,0:T(8,128)}, f32[2,384,768]{2,1,0:T(8,128)}) custom-call(bf16[96,2048]{1,0:T(8,128)(2,1)S(1)} %convolution_convert_fusion.19.refs_0_, bf16[96,2048]{1,0:T(8,128)(2,1)S(1)} %convolution_convert_fusion.18.refs_1_, bf16[96,2048]{1,0:T(8,128)(2,1)S(1)} %convolution_convert_fusion.17.refs_2_, ...), custom_call_target="tpu_custom_call" | custom-call | flops 4831838208 | bytes 1048576 | tf_op jit(solution)/shard_map/pallas_call | solution.py:168
  109.5 1.6 copy-done.6
  111.2 4.7 %shard_map.98.refs_9_ = bf16[8,96,2048]{2,1,0:T(8,128)(2,1)S(1)} custom-call(bf16[2,384,768]{2,1,0:T(8,128)(2,1)S(1)} %get-tuple-element.13.refs_0_, bf16[768,2048]{1,0:T(8,128)(2,1)} %bitcast.159, bf16[768,2048]{1,0:T(8,128)(2,1)} %copy-done.6), custom_call_target="tpu_custom_call" | custom-call | flops 2415919104 | bytes 1048576 | tf_op jit(solution)/shard_map/pallas_call | solution.py:168
  116.2 1.8 collective-permute-start.21
  119.1 11.8 %shard_map.101 = (bf16[2,384,768]{2,1,0:T(8,128)(2,1)S(1)}, bf16[2,384,768]{2,1,0:T(8,128)(2,1)S(1)}, f32[8,2,128]{2,1,0:T(2,128)}) custom-call(s32[2]{0:T(128)S(1)} %pad_add_fusion.1.refs_0_, bf16[96,2048]{1,0:T(8,128)(2,1)S(1)} %copy-done.2, bf16[96,2048]{1,0:T(8,128)(2,1)S(1)} %convolution_convert_fusion.10.refs_2_, ...), custom_call_target="tpu_custom_call" | custom-call | flops 2415919104 | bytes 1048576 | tf_op jit(solution)/shard_map/pallas_call | solution.py:168
  132.8 1.3 fusion.19
  134.1 1.8 collective-permute-start.22
  135.9 1.3 fusion.20
  137.6 10.3 %shard_map.102 = bf16[8,96,2048]{2,1,0:T(8,128)(2,1)} custom-call(bf16[2,384,768]{2,1,0:T(8,128)(2,1)S(1)} %get-tuple-element.17.refs_0_, bf16[2,384,768]{2,1,0:T(8,128)(2,1)S(1)} %get-tuple-element.18.refs_1_, bf16[2048,768]{1,0:T(8,128)(2,1)} %bitcast.164, bf16[2048,768]{1,0:T(8,128)(2,1)} %copy-done.9, bf16[2048,768]{1,0:T(8,128)(2,1)} %bitcast.167, ...), custom_call_target="tpu_custom_call" | custom-call | flops 4831838208 | bytes 1048576 | tf_op jit(solution)/shard_map/pallas_call | solution.py:168
  148.3 1.8 collective-permute-start.23
  151.2 1.3 fusion.14
  152.5 1.3 collective-permute-start.24
  156.8 6.3 %collective-permute-done.23 = bf16[128,2048]{1,0:T(8,128)(2,1)S(1)} collective-permute-done((bf16[128,2048]{1,0:T(8,128)(2,1)S(1)}, bf16[128,2048]{1,0:T(8,128)(2,1)S(1)}, u32[]{:S(2)}, u32[]{:S(2)}) %collective-permute-start.23) | collective-permute-done | bytes 524320 | tf_op jit(solution)/shard_map/ppermute | solution.py:95
  164.4 6.9 %collective-permute-done.24 = bf16[128,2048]{1,0:T(8,128)(2,1)S(1)} collective-permute-done((bf16[128,2048]{1,0:T(8,128)(2,1)S(1)}, bf16[128,2048]{1,0:T(8,128)(2,1)S(1)}, u32[]{:S(2)}, u32[]{:S(2)}) %collective-permute-start.24) | collective-permute-done | bytes 524320 | tf_op jit(solution)/shard_map/ppermute | solution.py:95
  171.6 1.8 collective-permute-start.25
  175.9 2.6 %collective-permute-done.28 = bf16[128,2048]{1,0:T(8,128)(2,1)S(1)} collective-permute-done((bf16[128,2048]{1,0:T(8,128)(2,1)S(1)}, bf16[128,2048]{1,0:T(8,128)(2,1)S(1)}, u32[]{:S(2)}, u32[]{:S(2)}) %collective-permute-start.28) | collective-permute-done | bytes 524320 | tf_op jit(solution)/shard_map/ppermute | solution.py:95
  180.3 2.1 collective-permute-done.25
  183.5 1.7 collective-permute-start.26
  185.2 5.6 %collective-permute-done.20 = bf16[128,2048]{1,0:T(8,128)(2,1)} collective-permute-done((bf16[128,2048]{1,0:T(8,128)(2,1)}, bf16[128,2048]{1,0:T(8,128)(2,1)}, u32[]{:S(2)}, u32[]{:S(2)}) %collective-permute-start.20) | collective-permute-done | bytes 524320 | tf_op jit(solution)/shard_map/ppermute | solution.py:95
  192.6 5.6 %collective-permute-done.29 = bf16[128,2048]{1,0:T(8,128)(2,1)} collective-permute-done((bf16[128,2048]{1,0:T(8,128)(2,1)}, bf16[128,2048]{1,0:T(8,128)(2,1)}, u32[]{:S(2)}, u32[]{:S(2)}) %collective-permute-start.29) | collective-permute-done | bytes 524320 | tf_op jit(solution)/shard_map/ppermute | solution.py:95
  198.3 2.3 %fusion.17 = bf16[128,2048]{1,0:T(8,128)(2,1)} fusion(bf16[128,2048]{1,0:T(8,128)(2,1)} %collective-permute-done.29, bf16[8,96,2048]{2,1,0:T(8,128)(2,1)} %shard_map.102, bf16[]{:T(256)} %bitcast.43, bf16[8,96,128]{2,1,0:T(8,128)(2,1)S(1)} %get-tuple-element.11), kind=kOutput, calls=%fused_computation.49 | convolution fusion | flops 51380224 | bytes 1466880 | tf_op jit(solution)/shard_map/dot_general | solution.py:457
  200.9 2.3 %fusion.9 = bf16[128,2048]{1,0:T(8,128)(2,1)} fusion(bf16[128,2048]{1,0:T(8,128)(2,1)} %collective-permute-done.26, bf16[8,96,2048]{2,1,0:T(8,128)(2,1)} %shard_map.102, bf16[8,96,128]{2,1,0:T(8,128)(2,1)S(1)} %get-tuple-element.11), kind=kOutput, calls=%fused_computation.21 | convolution fusion | flops 51118080 | bytes 1466368 | tf_op jit(solution)/shard_map/dot_general | solution.py:457
  203.2 1.7 collective-permute-start.27
  204.9 3.3 %all-to-all-start.1 = ((f32[8,2,128]{2,1,0:T(2,128)}), f32[8,2,128]{2,1,0:T(2,128)S(1)}, u32[]{:S(2)}, u32[]{:S(2)}) async-start(f32[8,2,128]{2,1,0:T(2,128)} %get-tuple-element.16), calls=%async_computation.1 | async-start | bytes 16384 | tf_op jit(solution)/shard_map/all_to_all | solution.py:481
  208.2 6.4 %all-to-all-done.1 = f32[8,2,128]{2,1,0:T(2,128)S(1)} async-done(((f32[8,2,128]{2,1,0:T(2,128)}), f32[8,2,128]{2,1,0:T(2,128)S(1)}, u32[]{:S(2)}, u32[]{:S(2)}) %all-to-all-start.1) | async-done | bytes 8224 | tf_op jit(solution)/shard_map/all_to_all | solution.py:481
  215.3 2.3 %fusion.2 = bf16[128,2048]{1,0:T(8,128)(2,1)} fusion(bf16[128,2048]{1,0:T(8,128)(2,1)} %copy-done.10, bf16[128,2048]{1,0:T(8,128)(2,1)} %collective-permute-done.20, bf16[8,96,2048]{2,1,0:T(8,128)(2,1)S(1)} %copy-done.1, bf16[8,96,128]{2,1,0:T(8,128)(2,1)S(1)} %get-tuple-element.11), kind=kOutput, calls=%fused_computation.14 | convolution fusion | flops 51642368 | bytes 1990656 | tf_op jit(solution)/shard_map/dot_general | solution.py:457
  217.7 2.5 %fusion.8 = bf16[128,2048]{1,0:T(8,128)(2,1)} fusion(bf16[128,2048]{1,0:T(8,128)(2,1)} %collective-permute-done.30, bf16[128,2048]{1,0:T(8,128)(2,1)} %collective-permute-done.27, bf16[8,96,2048]{2,1,0:T(8,128)(2,1)} %shard_map.102, bf16[8,96,128]{2,1,0:T(8,128)(2,1)S(1)} %get-tuple-element.11), kind=kOutput, calls=%fused_computation.20 | convolution fusion | flops 51642368 | bytes 1990656 | tf_op jit(solution)/shard_map/dot_general | solution.py:457
  (100 shorter events, 30.7 us)
Async XLA Ops:
  1.7 21.7 %copy-start.7 = (bf16[128,2048]{1,0:T(8,128)(2,1)}, bf16[128,2048]{1,0:T(8,128)(2,1)S(1)}, u32[]{:S(2)}) copy-start(bf16[128,2048]{1,0:T(8,128)(2,1)S(1)} %copy.21.refs_0_) | copy-start | bytes 1572868
  1.7 20.9 %collective-permute-start.3 = (bf16[128,2048]{1,0:T(8,128)(2,1)}, bf16[128,2048]{1,0:T(8,128)(2,1)S(1)}, u32[]{:S(2)}, u32[]{:S(2)}) collective-permute-start(bf16[128,2048]{1,0:T(8,128)(2,1)} %param.7), channel_id=1, source_target_pairs={{0,2},{2,4},{4,6},{6,7},{7,5},{5,3},{3,1},{1,0},{8,10},{10,12},{12... | collective-permute-start | bytes 1572872 | tf_op jit(solution)/shard_map/ppermute | solution.py:95
  4.7 19.4 %collective-permute-start = (bf16[128,2048]{1,0:T(8,128)(2,1)}, bf16[128,2048]{1,0:T(8,128)(2,1)}, u32[]{:S(2)}, u32[]{:S(2)}) collective-permute-start(bf16[128,2048]{1,0:T(8,128)(2,1)} %param.7), channel_id=1, source_target_pairs={{0,1},{2,0},{4,2},{6,4},{7,6},{5,7},{3,5},{1,3},{8,9},{10,8},{12,1... | collective-permute-start | bytes 1572872 | tf_op jit(solution)/shard_map/ppermute | solution.py:95
  6.7 14.1 %all-to-all-start = ((f32[8,8,128]{2,1,0:T(8,128)}), f32[8,8,128]{2,1,0:T(8,128)S(1)}, u32[]{:S(2)}, u32[]{:S(2)}) async-start(f32[8,8,128]{2,1,0:T(8,128)} %broadcast_in_dim.10), calls=%async_computation | async-start | bytes 65536 | tf_op jit(solution)/shard_map/all_to_all | solution.py:438
  20.8 2.6 %copy-start.3 = (f32[8,8,128]{2,1,0:T(8,128)}, f32[8,8,128]{2,1,0:T(8,128)S(1)}, u32[]{:S(2)}) copy-start(f32[8,8,128]{2,1,0:T(8,128)S(1)} %all-to-all-done.refs_1_) | copy-start | bytes 98308
  22.6 0.8 copy-start.8
  23.4 24.1 %copy-start.5 = (bf16[1,768,2048]{2,1,0:T(8,128)(2,1)S(1)}, bf16[1,768,2048]{2,1,0:T(8,128)(2,1)}, u32[]{:S(2)}) copy-start(bf16[1,768,2048]{2,1,0:T(8,128)(2,1)} %param.13) | copy-start | bytes 9437188
  23.4 15.2 %collective-permute-start.4 = (bf16[128,2048]{1,0:T(8,128)(2,1)}, bf16[128,2048]{1,0:T(8,128)(2,1)}, u32[]{:S(2)}, u32[]{:S(2)}) collective-permute-start(bf16[128,2048]{1,0:T(8,128)(2,1)} %shard_map.96), channel_id=1, source_target_pairs={{0,2},{2,4},{4,6},{6,7},{7,5},{5,3},{3,1},{1,0},{8,10},{10,12},{12... | collective-permute-start | bytes 1572872 | tf_op jit(solution)/shard_map/ppermute | solution.py:95
  24.1 15.1 %collective-permute-start.1 = (bf16[128,2048]{1,0:T(8,128)(2,1)}, bf16[128,2048]{1,0:T(8,128)(2,1)S(1)}, u32[]{:S(2)}, u32[]{:S(2)}) collective-permute-start(bf16[128,2048]{1,0:T(8,128)(2,1)} %shard_map.95), channel_id=1, source_target_pairs={{0,1},{2,0},{4,2},{6,4},{7,6},{5,7},{3,5},{1,3},{8,9},{10,8},{12,1... | collective-permute-start | bytes 1572872 | tf_op jit(solution)/shard_map/ppermute | solution.py:95
  25.5 71.8 %collective-permute-start.7 = (bf16[2048,768]{1,0:T(8,128)(2,1)}, bf16[2048,768]{1,0:T(8,128)(2,1)S(1)}, u32[]{:S(2)}, u32[]{:S(2)}) collective-permute-start(bf16[2048,768]{1,0:T(8,128)(2,1)} %bitcast.162), channel_id=1, source_target_pairs={{0,8},{8,0},{1,9},{9,1},{2,10},{10,2},{3,11},{11,3},{4,12},{12,4},... | collective-permute-start | bytes 9437192 | tf_op jit(solution)/shard_map/ppermute | solution.py:421
  25.5 22.0 %collective-permute-start.11 = (bf16[128,2048]{1,0:T(8,128)(2,1)}, bf16[128,2048]{1,0:T(8,128)(2,1)S(1)}, u32[]{:S(2)}, u32[]{:S(2)}) collective-permute-start(bf16[128,2048]{1,0:T(8,128)(2,1)} %shard_map.99), channel_id=1, source_target_pairs={{0,1},{2,0},{4,2},{6,4},{7,6},{5,7},{3,5},{1,3},{8,9},{10,8},{12,1... | collective-permute-start | bytes 1572872 | tf_op jit(solution)/shard_map/ppermute | solution.py:95
  26.8 22.9 %collective-permute-start.15 = (bf16[128,2048]{1,0:T(8,128)(2,1)}, bf16[128,2048]{1,0:T(8,128)(2,1)S(1)}, u32[]{:S(2)}, u32[]{:S(2)}) collective-permute-start(bf16[128,2048]{1,0:T(8,128)(2,1)} %shard_map.100), channel_id=1, source_target_pairs={{0,2},{2,4},{4,6},{6,7},{7,5},{5,3},{3,1},{1,0},{8,10},{10,12},{12... | collective-permute-start | bytes 1572872 | tf_op jit(solution)/shard_map/ppermute | solution.py:95
  38.6 60.4 %collective-permute-start.8 = (bf16[2048,768]{1,0:T(8,128)(2,1)}, bf16[2048,768]{1,0:T(8,128)(2,1)}, u32[]{:S(2)}, u32[]{:S(2)}) collective-permute-start(bf16[2048,768]{1,0:T(8,128)(2,1)} %bitcast.165), channel_id=1, source_target_pairs={{0,8},{8,0},{1,9},{9,1},{2,10},{10,2},{3,11},{11,3},{4,12},{12,4},... | collective-permute-start | bytes 9437192 | tf_op jit(solution)/shard_map/ppermute | solution.py:421
  39.2 19.1 %collective-permute-start.5 = (bf16[128,2048]{1,0:T(8,128)(2,1)}, bf16[128,2048]{1,0:T(8,128)(2,1)S(1)}, u32[]{:S(2)}, u32[]{:S(2)}) collective-permute-start(bf16[128,2048]{1,0:T(8,128)(2,1)} %collective-permute-done.4), channel_id=1, source_target_pairs={{0,2},{2,4},{4,6},{6,7},{7,5},{5,3},{3,1},{1,0},{8,10},{10,12},{12... | collective-permute-start | bytes 1572872 | tf_op jit(solution)/shard_map/ppermute | solution.py:95
  47.4 62.1 %collective-permute-start.9 = (bf16[768,2048]{1,0:T(8,128)(2,1)S(1)}, bf16[768,2048]{1,0:T(8,128)(2,1)S(1)}, u32[]{:S(2)}, u32[]{:S(2)}) collective-permute-start(bf16[768,2048]{1,0:T(8,128)(2,1)S(1)} %bitcast.161), channel_id=1, source_target_pairs={{0,8},{8,0},{1,9},{9,1},{2,10},{10,2},{3,11},{11,3},{4,12},{12,4},... | collective-permute-start | bytes 9437192 | tf_op jit(solution)/shard_map/ppermute | solution.py:421
  49.7 14.9 %collective-permute-start.2 = (bf16[128,2048]{1,0:T(8,128)(2,1)S(1)}, bf16[128,2048]{1,0:T(8,128)(2,1)S(1)}, u32[]{:S(2)}, u32[]{:S(2)}) collective-permute-start(bf16[128,2048]{1,0:T(8,128)(2,1)S(1)} %collective-permute-done.1), channel_id=1, source_target_pairs={{0,1},{2,0},{4,2},{6,4},{7,6},{5,7},{3,5},{1,3},{8,9},{10,8},{12,1... | collective-permute-start | bytes 1572872 | tf_op jit(solution)/shard_map/ppermute | solution.py:95
  58.2 14.8 %collective-permute-start.12 = (bf16[128,2048]{1,0:T(8,128)(2,1)S(1)}, bf16[128,2048]{1,0:T(8,128)(2,1)S(1)}, u32[]{:S(2)}, u32[]{:S(2)}) collective-permute-start(bf16[128,2048]{1,0:T(8,128)(2,1)S(1)} %collective-permute-done.11), channel_id=1, source_target_pairs={{0,1},{2,0},{4,2},{6,4},{7,6},{5,7},{3,5},{1,3},{8,9},{10,8},{12,1... | collective-permute-start | bytes 1572872 | tf_op jit(solution)/shard_map/ppermute | solution.py:95
  64.6 10.4 %collective-permute-start.16 = (bf16[128,2048]{1,0:T(8,128)(2,1)S(1)}, bf16[128,2048]{1,0:T(8,128)(2,1)S(1)}, u32[]{:S(2)}, u32[]{:S(2)}) collective-permute-start(bf16[128,2048]{1,0:T(8,128)(2,1)S(1)} %collective-permute-done.15), channel_id=1, source_target_pairs={{0,2},{2,4},{4,6},{6,7},{7,5},{5,3},{3,1},{1,0},{8,10},{10,12},{12... | collective-permute-start | bytes 1572872 | tf_op jit(solution)/shard_map/ppermute | solution.py:95
  73.1 11.2 %collective-permute-start.13 = (bf16[128,2048]{1,0:T(8,128)(2,1)S(1)}, bf16[128,2048]{1,0:T(8,128)(2,1)S(1)}, u32[]{:S(2)}, u32[]{:S(2)}) collective-permute-start(bf16[128,2048]{1,0:T(8,128)(2,1)S(1)} %collective-permute-done.12), channel_id=1, source_target_pairs={{0,1},{2,0},{4,2},{6,4},{7,6},{5,7},{3,5},{1,3},{8,9},{10,8},{12,1... | collective-permute-start | bytes 1572872 | tf_op jit(solution)/shard_map/ppermute | solution.py:95
  75.0 13.2 %collective-permute-start.6 = (bf16[128,2048]{1,0:T(8,128)(2,1)S(1)}, bf16[128,2048]{1,0:T(8,128)(2,1)S(1)}, u32[]{:S(2)}, u32[]{:S(2)}) collective-permute-start(bf16[128,2048]{1,0:T(8,128)(2,1)S(1)} %collective-permute-done.5), channel_id=1, source_target_pairs={{0,2},{2,4},{4,6},{6,7},{7,5},{5,3},{3,1},{1,0},{8,10},{10,12},{12... | collective-permute-start | bytes 1572872 | tf_op jit(solution)/shard_map/ppermute | solution.py:95
  84.3 12.8 %collective-permute-start.17 = (bf16[128,2048]{1,0:T(8,128)(2,1)S(1)}, bf16[128,2048]{1,0:T(8,128)(2,1)S(1)}, u32[]{:S(2)}, u32[]{:S(2)}) collective-permute-start(bf16[128,2048]{1,0:T(8,128)(2,1)S(1)} %collective-permute-done.16), channel_id=1, source_target_pairs={{0,2},{2,4},{4,6},{6,7},{7,5},{5,3},{3,1},{1,0},{8,10},{10,12},{12... | collective-permute-start | bytes 1572872 | tf_op jit(solution)/shard_map/ppermute | solution.py:95
  88.2 30.6 %collective-permute-start.14 = (bf16[128,2048]{1,0:T(8,128)(2,1)S(1)}, bf16[128,2048]{1,0:T(8,128)(2,1)S(1)}, u32[]{:S(2)}, u32[]{:S(2)}) collective-permute-start(bf16[128,2048]{1,0:T(8,128)(2,1)S(1)} %collective-permute-done.13), channel_id=1, source_target_pairs={{0,1},{2,0},{4,2},{6,4},{7,6},{5,7},{3,5},{1,3},{8,9},{10,8},{12,1... | collective-permute-start | bytes 1572872 | tf_op jit(solution)/shard_map/ppermute | solution.py:95
  97.3 1.7 copy-start.9
  109.5 1.6 copy-start.6
  111.1 8.0 %copy-start.2 = (bf16[96,2048]{1,0:T(8,128)(2,1)S(1)}, bf16[96,2048]{1,0:T(8,128)(2,1)}, u32[]{:S(2)}) copy-start(bf16[96,2048]{1,0:T(8,128)(2,1)} %convolution_convert_fusion.11.refs_1_) | copy-start | bytes 1179652
  115.9 3.2 %copy-start = (bf16[8,96,2048]{2,1,0:T(8,128)(2,1)}, bf16[8,96,2048]{2,1,0:T(8,128)(2,1)S(1)}, u32[]{:S(2)}) copy-start(bf16[8,96,2048]{2,1,0:T(8,128)(2,1)S(1)} %shard_map.98.refs_9_) | copy-start | bytes 9437188
  116.2 16.5 %collective-permute-start.21 = (bf16[128,2048]{1,0:T(8,128)(2,1)S(1)}, bf16[128,2048]{1,0:T(8,128)(2,1)S(1)}, u32[]{:S(2)}, u32[]{:S(2)}) collective-permute-start(bf16[128,2048]{1,0:T(8,128)(2,1)S(1)} %convolution_convert_fusion.2), channel_id=1, source_target_pairs={{0,1},{2,0},{4,2},{6,4},{7,6},{5,7},{3,5},{1,3},{8,9},{10,8},{12,1... | collective-permute-start | bytes 1572872 | tf_op jit(solution)/shard_map/ppermute | solution.py:95
  118.3 17.5 %collective-permute-start.10 = (bf16[128,2048]{1,0:T(8,128)(2,1)S(1)}, bf16[128,2048]{1,0:T(8,128)(2,1)S(1)}, u32[]{:S(2)}, u32[]{:S(2)}) collective-permute-start(bf16[128,2048]{1,0:T(8,128)(2,1)S(1)} %convolution_convert_fusion.3), channel_id=1, source_target_pairs={{0,2},{2,4},{4,6},{6,7},{7,5},{5,3},{3,1},{1,0},{8,10},{10,12},{12... | collective-permute-start | bytes 1572872 | tf_op jit(solution)/shard_map/ppermute | solution.py:95
  134.1 13.8 %collective-permute-start.22 = (bf16[128,2048]{1,0:T(8,128)(2,1)S(1)}, bf16[128,2048]{1,0:T(8,128)(2,1)S(1)}, u32[]{:S(2)}, u32[]{:S(2)}) collective-permute-start(bf16[128,2048]{1,0:T(8,128)(2,1)S(1)} %fusion.19), channel_id=1, source_target_pairs={{0,1},{2,0},{4,2},{6,4},{7,6},{5,7},{3,5},{1,3},{8,9},{10,8},{12,1... | collective-permute-start | bytes 1572872 | tf_op jit(solution)/shard_map/ppermute | solution.py:95
  137.2 16.7 %collective-permute-start.18 = (bf16[128,2048]{1,0:T(8,128)(2,1)S(1)}, bf16[128,2048]{1,0:T(8,128)(2,1)S(1)}, u32[]{:S(2)}, u32[]{:S(2)}) collective-permute-start(bf16[128,2048]{1,0:T(8,128)(2,1)S(1)} %fusion.20), channel_id=1, source_target_pairs={{0,2},{2,4},{4,6},{6,7},{7,5},{5,3},{3,1},{1,0},{8,10},{10,12},{12... | collective-permute-start | bytes 1572872 | tf_op jit(solution)/shard_map/ppermute | solution.py:95
  137.6 10.4 %copy-start.1 = (bf16[8,96,2048]{2,1,0:T(8,128)(2,1)S(1)}, bf16[8,96,2048]{2,1,0:T(8,128)(2,1)}, u32[]{:S(2)}) copy-start(bf16[8,96,2048]{2,1,0:T(8,128)(2,1)} %copy-done) | copy-start | bytes 9437188
  147.9 8.3 %copy-start.4 = (bf16[8,96,2048]{2,1,0:T(8,128)(2,1)S(1)}, bf16[8,96,2048]{2,1,0:T(8,128)(2,1)}, u32[]{:S(2)}) copy-start(bf16[8,96,2048]{2,1,0:T(8,128)(2,1)} %shard_map.102) | copy-start | bytes 9437188
  148.3 14.9 %collective-permute-start.23 = (bf16[128,2048]{1,0:T(8,128)(2,1)S(1)}, bf16[128,2048]{1,0:T(8,128)(2,1)S(1)}, u32[]{:S(2)}, u32[]{:S(2)}) collective-permute-start(bf16[128,2048]{1,0:T(8,128)(2,1)S(1)} %fusion.6), channel_id=1, source_target_pairs={{0,1},{2,0},{4,2},{6,4},{7,6},{5,7},{3,5},{1,3},{8,9},{10,8},{12,1... | collective-permute-start | bytes 1572872 | tf_op jit(solution)/shard_map/ppermute | solution.py:95
  152.5 18.7 %collective-permute-start.24 = (bf16[128,2048]{1,0:T(8,128)(2,1)S(1)}, bf16[128,2048]{1,0:T(8,128)(2,1)S(1)}, u32[]{:S(2)}, u32[]{:S(2)}) collective-permute-start(bf16[128,2048]{1,0:T(8,128)(2,1)S(1)} %fusion.14), channel_id=1, source_target_pairs={{0,1},{2,0},{4,2},{6,4},{7,6},{5,7},{3,5},{1,3},{8,9},{10,8},{12,1... | collective-permute-start | bytes 1572872 | tf_op jit(solution)/shard_map/ppermute | solution.py:95
  154.2 19.2 %collective-permute-start.19 = (bf16[128,2048]{1,0:T(8,128)(2,1)S(1)}, bf16[128,2048]{1,0:T(8,128)(2,1)S(1)}, u32[]{:S(2)}, u32[]{:S(2)}) collective-permute-start(bf16[128,2048]{1,0:T(8,128)(2,1)S(1)} %fusion.4), channel_id=1, source_target_pairs={{0,2},{2,4},{4,6},{6,7},{7,5},{5,3},{3,1},{1,0},{8,10},{10,12},{12... | collective-permute-start | bytes 1572872 | tf_op jit(solution)/shard_map/ppermute | solution.py:95
  156.5 22.0 %collective-permute-start.28 = (bf16[128,2048]{1,0:T(8,128)(2,1)S(1)}, bf16[128,2048]{1,0:T(8,128)(2,1)S(1)}, u32[]{:S(2)}, u32[]{:S(2)}) collective-permute-start(bf16[128,2048]{1,0:T(8,128)(2,1)S(1)} %fusion.15), channel_id=1, source_target_pairs={{0,2},{2,4},{4,6},{6,7},{7,5},{5,3},{3,1},{1,0},{8,10},{10,12},{12... | collective-permute-start | bytes 1572872 | tf_op jit(solution)/shard_map/ppermute | solution.py:95
  163.2 8.1 %copy-start.10 = (bf16[128,2048]{1,0:T(8,128)(2,1)}, bf16[128,2048]{1,0:T(8,128)(2,1)S(1)}, u32[]{:S(2)}) copy-start(bf16[128,2048]{1,0:T(8,128)(2,1)S(1)} %collective-permute-done.23) | copy-start | bytes 1572868
  171.6 10.8 %collective-permute-start.25 = (bf16[128,2048]{1,0:T(8,128)(2,1)S(1)}, bf16[128,2048]{1,0:T(8,128)(2,1)S(1)}, u32[]{:S(2)}, u32[]{:S(2)}) collective-permute-start(bf16[128,2048]{1,0:T(8,128)(2,1)S(1)} %fusion.18), channel_id=1, source_target_pairs={{0,1},{2,0},{4,2},{6,4},{7,6},{5,7},{3,5},{1,3},{8,9},{10,8},{12,1... | collective-permute-start | bytes 1572872 | tf_op jit(solution)/shard_map/ppermute | solution.py:95
  175.7 39.0 %copy-start.11 = (s32[128,4]{0,1:T(4,128)S(1)}, s32[128,4]{0,1:T(4,128)}, u32[]{:S(2)}) copy-start(s32[128,4]{0,1:T(4,128)} %param.9) | copy-start | bytes 6148
  175.7 15.2 %collective-permute-start.20 = (bf16[128,2048]{1,0:T(8,128)(2,1)}, bf16[128,2048]{1,0:T(8,128)(2,1)}, u32[]{:S(2)}, u32[]{:S(2)}) collective-permute-start(bf16[128,2048]{1,0:T(8,128)(2,1)} %fusion.3), channel_id=1, source_target_pairs={{0,2},{2,4},{4,6},{6,7},{7,5},{5,3},{3,1},{1,0},{8,10},{10,12},{12... | collective-permute-start | bytes 1572872 | tf_op jit(solution)/shard_map/ppermute | solution.py:95
  179.6 18.6 %collective-permute-start.29 = (bf16[128,2048]{1,0:T(8,128)(2,1)}, bf16[128,2048]{1,0:T(8,128)(2,1)}, u32[]{:S(2)}, u32[]{:S(2)}) collective-permute-start(bf16[128,2048]{1,0:T(8,128)(2,1)} %fusion.16), channel_id=1, source_target_pairs={{0,2},{2,4},{4,6},{6,7},{7,5},{5,3},{3,1},{1,0},{8,10},{10,12},{12... | collective-permute-start | bytes 1572872 | tf_op jit(solution)/shard_map/ppermute | solution.py:95
  183.5 17.4 %collective-permute-start.26 = (bf16[128,2048]{1,0:T(8,128)(2,1)}, bf16[128,2048]{1,0:T(8,128)(2,1)}, u32[]{:S(2)}, u32[]{:S(2)}) collective-permute-start(bf16[128,2048]{1,0:T(8,128)(2,1)} %fusion.10), channel_id=1, source_target_pairs={{0,1},{2,0},{4,2},{6,4},{7,6},{5,7},{3,5},{1,3},{8,9},{10,8},{12,1... | collective-permute-start | bytes 1572872 | tf_op jit(solution)/shard_map/ppermute | solution.py:95
  200.6 17.1 %collective-permute-start.30 = (bf16[128,2048]{1,0:T(8,128)(2,1)}, bf16[128,2048]{1,0:T(8,128)(2,1)}, u32[]{:S(2)}, u32[]{:S(2)}) collective-permute-start(bf16[128,2048]{1,0:T(8,128)(2,1)} %fusion.17), channel_id=1, source_target_pairs={{0,2},{2,4},{4,6},{6,7},{7,5},{5,3},{3,1},{1,0},{8,10},{10,12},{12... | collective-permute-start | bytes 1572872 | tf_op jit(solution)/shard_map/ppermute | solution.py:95
  203.2 14.5 %collective-permute-start.27 = (bf16[128,2048]{1,0:T(8,128)(2,1)}, bf16[128,2048]{1,0:T(8,128)(2,1)}, u32[]{:S(2)}, u32[]{:S(2)}) collective-permute-start(bf16[128,2048]{1,0:T(8,128)(2,1)} %fusion.9), channel_id=1, source_target_pairs={{0,1},{2,0},{4,2},{6,4},{7,6},{5,7},{3,5},{1,3},{8,9},{10,8},{12,1... | collective-permute-start | bytes 1572872 | tf_op jit(solution)/shard_map/ppermute | solution.py:95
  204.9 9.8 %all-to-all-start.1 = ((f32[8,2,128]{2,1,0:T(2,128)}), f32[8,2,128]{2,1,0:T(2,128)S(1)}, u32[]{:S(2)}, u32[]{:S(2)}) async-start(f32[8,2,128]{2,1,0:T(2,128)} %get-tuple-element.16), calls=%async_computation.1 | async-start | bytes 16384 | tf_op jit(solution)/shard_map/all_to_all | solution.py:481

commit v5 on v4

--- a/solution.py
+++ b/solution.py
@@ -113,12 +113,6 @@
     return [held[place] for place in range(count)], arrivals
 
 
-def after(array, *others):
-    for other in others:
-        array = array + other[(slice(0, 1),) * other.ndim].reshape((1,) * array.ndim).astype(array.dtype) * 0
-    return array
-
-
 def held_back(array, others):
     def kernel(*refs):
         pass
@@ -129,6 +123,21 @@
         in_specs=[pl.BlockSpec(memory_space=pl.ANY) for _ in range(1 + len(others))],
         out_specs=pl.BlockSpec(memory_space=pl.ANY),
         input_output_aliases={0: 0},
+    )(array, *others)
+
+
+def copied(array, others):
+    def kernel(*refs):
+        copy = pltpu.make_async_copy(refs[0], refs[-2], refs[-1])
+        copy.start()
+        copy.wait()
+
+    return pl.pallas_call(
+        kernel,
+        out_shape=jax.ShapeDtypeStruct(array.shape, array.dtype),
+        in_specs=[pl.BlockSpec(memory_space=pl.ANY) for _ in range(1 + len(others))],
+        out_specs=pl.BlockSpec(memory_space=pl.ANY),
+        scratch_shapes=[pltpu.SemaphoreType.DMA],
     )(array, *others)
 
 
@@ -438,13 +447,21 @@
     tables = lax.all_to_all(copies, "ep", split_axis=0, concat_axis=0, tiled=True)
     pick, spread = run_routing(ids, tables, top_count, capacity)
 
-    behind = {(step, 2): (tables,) for step in (1, -1)}
-    in_shards, in_hops = ring_gather(tokens, chips, 1, behind)
-    behind = {(step, 1): (in_hops[step][0],) for step in (1, -1)}
-    grad_shards, _ = ring_gather(cotangent, chips, -1, behind)
     gate_mats = (w_gate[0], swap_cores(w_gate[0]))
     up_mats = (w_up[0], swap_cores(w_up[0]))
     down_mats = (w_down[0], swap_cores(w_down[0]))
+    behind = {(step, 2): (tables, gate_mats[1], up_mats[1]) for step in (1, -1)}
+    behind.update({(step, 3): (down_mats[1],) for step in (1, -1)})
+    in_shards, in_hops = ring_gather(tokens, chips, 1, behind)
+    grad_later = copied(
+        cotangent, [in_hops[1][0], in_hops[-1][0], tables, gate_mats[1], up_mats[1]]
+    )
+    behind = {
+        (step, hop): (in_hops[step][hop - 1],)
+        for step in (1, -1)
+        for hop in range(2, len(in_hops[step]) + 1)
+    }
+    grad_shards, _ = ring_gather(grad_later, chips, -1, behind)
 
     def gather_rows(shards):
         return [
@@ -461,7 +478,8 @@
                 total = total + partial.astype(f32)
             if add_waits:
                 return (total + waits[0].astype(f32)).astype(bf16)
-            return after(total.astype(bf16), *waits)
+            total = total.astype(bf16)
+            return held_back(total, waits) if waits else total
 
         return share_of
 

time: 221 us -> 255 us (1.15)
  matrix products: 27.6 us -> 49.9 us
  Pallas kernels: 38.1 us -> 55.1 us
  between operations: 4.98 us -> 1.06 us
    pallas_call x0 -> x1, Pallas kernels: none -> 17 us  [copied(): pl.pallas_call(kernel, out_shape=jax.ShapeDtypeStruct(array.shape, array....]
    dot_general x16, matrix products: 18.6 us -> 32.2 us  [share_of(): lax.dot_general(spread[s], blocks[s], (((0,), (0,)), ((), ())), preferred...]
    dot_general x16, matrix products: 9.04 us -> 17.7 us  [gather_rows(): jnp.dot(pick[s], shards[s], preferred_element_type=f32).astype(bf16)]
    slice x6 -> x0, local copies, waits for them, and re-layouts: 4.39 us -> none  [after(): other[(slice(0, 1),) * other.ndim].reshape((1,) * array.ndim)]
    ppermute x28, starting transfers between devices: 31.3 us -> 27.2 us  [ring_shift(): return lax.ppermute(array, 'ep', pairs)]
    unnamed x26 -> x42, local copies, waits for them, and re-layouts: 6.01 us -> 8.72 us
  transfers between devices with their start and end apart: 33 -> 33, of which waited for: 18 -> 14; matrix products, arithmetic and copies ran while one was open for 15% -> 20% of each run, Pallas kernels for 17% -> 22%
where the time goes in v5:
time: 255 us; the launch traced here: 254 us
  waiting for transfers between devices  96.1 us (38%)
  Pallas kernels  55.1 us (22%)
  matrix products  49.9 us (20%)
  starting transfers between devices  40.3 us (16%)
  local copies, waits for them, and re-layouts  9.34 us (4%)
    ppermute x28, waiting for transfers between devices, ring_shift(): return lax.ppermute(array, 'ep', pairs)  80.3 us
    pallas_call x5, Pallas kernels, call_kernel(): pl.pallas_call(body, out_shape=outs, in_specs=[pl.BlockSpec(memory_space=...  38.1 us
    dot_general x16, matrix products, share_of(): lax.dot_general(spread[s], blocks[s], (((0,), (0,)), ((), ())), preferred...  32.2 us
    ppermute x28, starting transfers between devices, ring_shift(): return lax.ppermute(array, 'ep', pairs)  27.2 us
    dot_general x16, matrix products, gather_rows(): jnp.dot(pick[s], shards[s], preferred_element_type=f32).astype(bf16)  17.7 us
    pallas_call x1, Pallas kernels, copied(): pl.pallas_call(kernel, out_shape=jax.ShapeDtypeStruct(array.shape, array....  17 us
    all_to_all x1, waiting for transfers between devices, body_ring(): lax.all_to_all(copies, 'ep', split_axis=0, concat_axis=0, tiled=True)  9.31 us
    unnamed x42, local copies, waits for them, and re-layouts  8.72 us
  transfers between devices with their start and end apart: 33, of which 14 were waited for; matrix products, arithmetic and copies ran while one was open for 20% of the time, Pallas kernels for 22%

profile of v5, /device:TPU:0, one launch (start us, length us, event | category | flops | bytes accessed | tf_op | source)
XLA Modules:
  0.0 253.9 jit_solution(2328444156965814712)
XLA Ops:
  1.7 2.6 %collective-permute-start = (bf16[128,2048]{1,0:T(8,128)(2,1)}, bf16[128,2048]{1,0:T(8,128)(2,1)S(1)}, u32[]{:S(2)}, u32[]{:S(2)}) collective-permute-start(bf16[128,2048]{1,0:T(8,128)(2,1)} %param.7), channel_id=1, source_target_pairs={{0,1},{2,0},{4,2},{6,4},{7,6},{5,7},{3,5},{1,3},{8,9},{10,8},{12,1... | collective-permute-start | bytes 1572872 | tf_op jit(solution)/shard_map/ppermute | solution.py:95
  6.3 6.3 %all-to-all-start = ((f32[8,8,128]{2,1,0:T(8,128)}), f32[8,8,128]{2,1,0:T(8,128)S(1)}, u32[]{:S(2)}, u32[]{:S(2)}) async-start(f32[8,8,128]{2,1,0:T(8,128)} %broadcast_in_dim.10), calls=%async_computation | async-start | bytes 65536 | tf_op jit(solution)/shard_map/all_to_all | solution.py:447
  12.6 9.3 %all-to-all-done.refs_1_.refs_3_ = f32[8,8,128]{2,1,0:T(8,128)S(1)} async-done(((f32[8,8,128]{2,1,0:T(8,128)}), f32[8,8,128]{2,1,0:T(8,128)S(1)}, u32[]{:S(2)}, u32[]{:S(2)}) %all-to-all-start) | async-done | bytes 32800 | tf_op jit(solution)/shard_map/all_to_all | solution.py:447
  25.0 17.0 %shard_map.101 = bf16[128,2048]{1,0:T(8,128)(2,1)} custom-call(bf16[128,2048]{1,0:T(8,128)(2,1)} %refs_0_.1, bf16[128,2048]{1,0:T(8,128)(2,1)} %copy-done.14, bf16[128,2048]{1,0:T(8,128)(2,1)} %copy-done.13, f32[8,8,128]{2,1,0:T(8,128)} %copy-done.12, bf16[2048,768]{1,0:T(8,128)(2,1)} %collective-permute-done.1.refs_2_.refs_9_.refs_4_.refs_3_, ...), custom_call_target="tpu_custom_call" | custom-call | tf_op jit(solution)/shard_map/pallas_call | solution.py:135
  42.5 1.6 collective-permute-start.11
  44.5 1.3 convolution_convert_fusion.12.refs_7_
  45.8 1.7 collective-permute-start.3
  47.5 1.3 convolution_convert_fusion.18.refs_1_
  49.9 7.3 %collective-permute-done.15.refs_0_ = bf16[128,2048]{1,0:T(8,128)(2,1)} collective-permute-done((bf16[128,2048]{1,0:T(8,128)(2,1)}, bf16[128,2048]{1,0:T(8,128)(2,1)}, u32[]{:S(2)}, u32[]{:S(2)}) %collective-permute-start.15) | collective-permute-done | bytes 524320 | tf_op jit(solution)/shard_map/ppermute | solution.py:95
  57.2 9.1 %collective-permute-done.7.refs_0_.refs_1_ = bf16[128,2048]{1,0:T(8,128)(2,1)S(1)} collective-permute-done((bf16[128,2048]{1,0:T(8,128)(2,1)}, bf16[128,2048]{1,0:T(8,128)(2,1)S(1)}, u32[]{:S(2)}, u32[]{:S(2)}) %collective-permute-start.7) | collective-permute-done | bytes 524320 | tf_op jit(solution)/shard_map/ppermute | solution.py:95
  73.0 1.8 collective-permute-start.12
  74.7 2.0 convolution_convert_fusion.4.refs_8_
  76.8 2.1 convolution_convert_fusion.10.refs_2_
  78.8 11.6 %collective-permute-done.8.refs_1_ = bf16[128,2048]{1,0:T(8,128)(2,1)S(1)} collective-permute-done((bf16[128,2048]{1,0:T(8,128)(2,1)}, bf16[128,2048]{1,0:T(8,128)(2,1)S(1)}, u32[]{:S(2)}, u32[]{:S(2)}) %collective-permute-start.8) | collective-permute-done | bytes 524320 | tf_op jit(solution)/shard_map/ppermute | solution.py:95
  91.6 2.1 convolution_convert_fusion.5.refs_7_
  93.6 1.8 collective-permute-start.13
  98.6 15.2 %collective-permute-done.9 = bf16[128,2048]{1,0:T(8,128)(2,1)S(1)} collective-permute-done((bf16[128,2048]{1,0:T(8,128)(2,1)}, bf16[128,2048]{1,0:T(8,128)(2,1)S(1)}, u32[]{:S(2)}, u32[]{:S(2)}) %collective-permute-start.9) | collective-permute-done | bytes 524320 | tf_op jit(solution)/shard_map/ppermute | solution.py:95
  114.1 10.4 %shard_map.99 = (bf16[2,384,768]{2,1,0:T(8,128)(2,1)S(1)}, f32[2,384,768]{2,1,0:T(8,128)}, f32[2,384,768]{2,1,0:T(8,128)}) custom-call(bf16[96,2048]{1,0:T(8,128)(2,1)S(1)} %convolution_convert_fusion.19.refs_0_, bf16[96,2048]{1,0:T(8,128)(2,1)S(1)} %convolution_convert_fusion.18.refs_1_, bf16[96,2048]{1,0:T(8,128)(2,1)S(1)} %convolution_convert_fusion.17.refs_2_, ...), custom_call_target="tpu_custom_call" | custom-call | flops 4831838208 | bytes 1048576 | tf_op jit(solution)/shard_map/pallas_call | solution.py:177
  124.5 4.7 %shard_map.100.refs_9_ = bf16[8,96,2048]{2,1,0:T(8,128)(2,1)S(1)} custom-call(bf16[2,384,768]{2,1,0:T(8,128)(2,1)S(1)} %get-tuple-element.13.refs_0_, bf16[768,2048]{1,0:T(8,128)(2,1)} %bitcast.154, bf16[768,2048]{1,0:T(8,128)(2,1)} %collective-permute-done.4.refs_1_.refs_2_.refs_14_), custom_call_target="tpu_custom_call" | custom-call | flops 2415919104 | bytes 1048576 | tf_op jit(solution)/shard_map/pallas_call | solution.py:177
  130.2 1.9 collective-permute-start.10
  132.8 11.7 %collective-permute-done.14 = bf16[128,2048]{1,0:T(8,128)(2,1)S(1)} collective-permute-done((bf16[128,2048]{1,0:T(8,128)(2,1)S(1)}, bf16[128,2048]{1,0:T(8,128)(2,1)S(1)}, u32[]{:S(2)}, u32[]{:S(2)}) %collective-permute-start.14) | collective-permute-done | bytes 524320 | tf_op jit(solution)/shard_map/ppermute | solution.py:95
  144.8 11.8 %shard_map.106 = (bf16[2,384,768]{2,1,0:T(8,128)(2,1)S(1)}, bf16[2,384,768]{2,1,0:T(8,128)(2,1)S(1)}, f32[8,2,128]{2,1,0:T(2,128)}) custom-call(s32[2]{0:T(128)S(1)} %pad_add_fusion.1.refs_0_, bf16[96,2048]{1,0:T(8,128)(2,1)S(1)} %copy-done.4, bf16[96,2048]{1,0:T(8,128)(2,1)S(1)} %copy-done.6, bf16[96,2048]{1,0:T(8,128)(2,1)S(1)} %convolution_convert_fusion.9.refs_3_, ...), custom_call_target="tpu_custom_call" | custom-call | flops 2415919104 | bytes 1048576 | tf_op jit(solution)/shard_map/pallas_call | solution.py:177
  157.6 2.4 fusion.7.refs_0_
  161.0 2.3 fusion.5.refs_0_
  163.3 1.8 collective-permute-start.18
  168.7 10.4 %shard_map.109 = bf16[8,96,2048]{2,1,0:T(8,128)(2,1)} custom-call(bf16[2,384,768]{2,1,0:T(8,128)(2,1)S(1)} %copy-done.9, bf16[2,384,768]{2,1,0:T(8,128)(2,1)S(1)} %copy-done.11, bf16[2048,768]{1,0:T(8,128)(2,1)} %bitcast.158, bf16[2048,768]{1,0:T(8,128)(2,1)} %collective-permute-done.1.refs_2_.refs_9_.refs_4_.refs_3_, bf16[2048,768]{1,0:T(8,128)(2,1)} %bitcast.161, ...), custom_call_target="tpu_custom_call" | custom-call | flops 4831838208 | bytes 1048576 | tf_op jit(solution)/shard_map/pallas_call | solution.py:177
  179.1 2.1 convolution_convert_fusion.1.refs_0_
  181.4 2.2 fusion.6
  184.7 2.1 convolution_convert_fusion.refs_0_
  187.7 2.2 fusion.4
  189.9 1.8 collective-permute-start.19
  191.7 1.6 collective-permute-done.24
  193.3 2.3 fusion.11.refs_0_
  195.6 6.9 %collective-permute-done.23.refs_1_ = bf16[128,2048]{1,0:T(8,128)(2,1)} collective-permute-done((bf16[128,2048]{1,0:T(8,128)(2,1)}, bf16[128,2048]{1,0:T(8,128)(2,1)}, u32[]{:S(2)}, u32[]{:S(2)}) %collective-permute-start.23) | collective-permute-done | bytes 524320 | tf_op jit(solution)/shard_map/ppermute | solution.py:95
  202.9 2.3 fusion.13.refs_0_
  205.2 4.9 %collective-permute-done.19.refs_1_ = bf16[128,2048]{1,0:T(8,128)(2,1)} collective-permute-done((bf16[128,2048]{1,0:T(8,128)(2,1)}, bf16[128,2048]{1,0:T(8,128)(2,1)}, u32[]{:S(2)}, u32[]{:S(2)}) %collective-permute-start.19) | collective-permute-done | bytes 524320 | tf_op jit(solution)/shard_map/ppermute | solution.py:95
  211.0 2.2 fusion.3
  213.2 1.8 collective-permute-start.20
  215.0 2.0 collective-permute-done.25
  217.0 2.3 fusion.10
  219.9 3.0 %collective-permute-done.29 = bf16[128,2048]{1,0:T(8,128)(2,1)} collective-permute-done((bf16[128,2048]{1,0:T(8,128)(2,1)}, bf16[128,2048]{1,0:T(8,128)(2,1)}, u32[]{:S(2)}, u32[]{:S(2)}) %collective-permute-start.29) | collective-permute-done | bytes 524320 | tf_op jit(solution)/shard_map/ppermute | solution.py:95
  222.9 2.3 fusion.12.refs_0_
  225.2 5.7 %collective-permute-done.20.refs_1_ = bf16[128,2048]{1,0:T(8,128)(2,1)} collective-permute-done((bf16[128,2048]{1,0:T(8,128)(2,1)}, bf16[128,2048]{1,0:T(8,128)(2,1)}, u32[]{:S(2)}, u32[]{:S(2)}) %collective-permute-start.20) | collective-permute-done | bytes 524320 | tf_op jit(solution)/shard_map/ppermute | solution.py:95
  232.9 2.3 fusion.9
  236.1 5.8 %all-to-all-start.1 = ((f32[8,2,128]{2,1,0:T(2,128)}), f32[8,2,128]{2,1,0:T(2,128)S(1)}, u32[]{:S(2)}, u32[]{:S(2)}) async-start(f32[8,2,128]{2,1,0:T(2,128)} %get-tuple-element.16.refs_1_), calls=%async_computation.1 | async-start | bytes 16384 | tf_op jit(solution)/shard_map/all_to_all | solution.py:499
  241.9 6.5 %all-to-all-done.1 = f32[8,2,128]{2,1,0:T(2,128)S(1)} async-done(((f32[8,2,128]{2,1,0:T(2,128)}), f32[8,2,128]{2,1,0:T(2,128)S(1)}, u32[]{:S(2)}, u32[]{:S(2)}) %all-to-all-start.1) | async-done | bytes 8224 | tf_op jit(solution)/shard_map/all_to_all | solution.py:499
  249.1 2.3 fusion.2
  251.4 2.5 fusion.8
  (122 shorter events, 34.3 us)
Async XLA Ops:
  0.6 23.5 %collective-permute-start.1 = (bf16[2048,768]{1,0:T(8,128)(2,1)}, bf16[2048,768]{1,0:T(8,128)(2,1)}, u32[]{:S(2)}, u32[]{:S(2)}) collective-permute-start(bf16[2048,768]{1,0:T(8,128)(2,1)} %bitcast.156), channel_id=1, source_target_pairs={{0,8},{8,0},{1,9},{9,1},{2,10},{10,2},{3,11},{11,3},{4,12},{12,4},... | collective-permute-start | bytes 9437192 | tf_op jit(solution)/shard_map/ppermute | solution.py:430
  1.1 22.9 %collective-permute-start.2 = (bf16[2048,768]{1,0:T(8,128)(2,1)}, bf16[2048,768]{1,0:T(8,128)(2,1)}, u32[]{:S(2)}, u32[]{:S(2)}) collective-permute-start(bf16[2048,768]{1,0:T(8,128)(2,1)} %bitcast.159), channel_id=1, source_target_pairs={{0,8},{8,0},{1,9},{9,1},{2,10},{10,2},{3,11},{11,3},{4,12},{12,4},... | collective-permute-start | bytes 9437192 | tf_op jit(solution)/shard_map/ppermute | solution.py:430
  1.2 66.2 %collective-permute-start.4 = (bf16[768,2048]{1,0:T(8,128)(2,1)}, bf16[768,2048]{1,0:T(8,128)(2,1)}, u32[]{:S(2)}, u32[]{:S(2)}) collective-permute-start(bf16[768,2048]{1,0:T(8,128)(2,1)} %bitcast.153), channel_id=1, source_target_pairs={{0,8},{8,0},{1,9},{9,1},{2,10},{10,2},{3,11},{11,3},{4,12},{12,4},... | collective-permute-start | bytes 9437192 | tf_op jit(solution)/shard_map/ppermute | solution.py:430
  1.7 22.4 %collective-permute-start = (bf16[128,2048]{1,0:T(8,128)(2,1)}, bf16[128,2048]{1,0:T(8,128)(2,1)S(1)}, u32[]{:S(2)}, u32[]{:S(2)}) collective-permute-start(bf16[128,2048]{1,0:T(8,128)(2,1)} %param.7), channel_id=1, source_target_pairs={{0,1},{2,0},{4,2},{6,4},{7,6},{5,7},{3,5},{1,3},{8,9},{10,8},{12,1... | collective-permute-start | bytes 1572872 | tf_op jit(solution)/shard_map/ppermute | solution.py:95
  4.2 19.8 %collective-permute-start.6 = (bf16[128,2048]{1,0:T(8,128)(2,1)}, bf16[128,2048]{1,0:T(8,128)(2,1)S(1)}, u32[]{:S(2)}, u32[]{:S(2)}) collective-permute-start(bf16[128,2048]{1,0:T(8,128)(2,1)} %param.7), channel_id=1, source_target_pairs={{0,2},{2,4},{4,6},{6,7},{7,5},{5,3},{3,1},{1,0},{8,10},{10,12},{12... | collective-permute-start | bytes 1572872 | tf_op jit(solution)/shard_map/ppermute | solution.py:95
  6.3 15.6 %all-to-all-start = ((f32[8,8,128]{2,1,0:T(8,128)}), f32[8,8,128]{2,1,0:T(8,128)S(1)}, u32[]{:S(2)}, u32[]{:S(2)}) async-start(f32[8,8,128]{2,1,0:T(8,128)} %broadcast_in_dim.10), calls=%async_computation | async-start | bytes 65536 | tf_op jit(solution)/shard_map/all_to_all | solution.py:447
  21.9 2.2 copy-start.12
  42.0 15.2 %collective-permute-start.15 = (bf16[128,2048]{1,0:T(8,128)(2,1)}, bf16[128,2048]{1,0:T(8,128)(2,1)}, u32[]{:S(2)}, u32[]{:S(2)}) collective-permute-start(bf16[128,2048]{1,0:T(8,128)(2,1)} %shard_map.101), channel_id=1, source_target_pairs={{0,2},{2,4},{4,6},{6,7},{7,5},{5,3},{3,1},{1,0},{8,10},{10,12},{12... | collective-permute-start | bytes 1572872 | tf_op jit(solution)/shard_map/ppermute | solution.py:95
  42.5 27.1 %collective-permute-start.11 = (bf16[128,2048]{1,0:T(8,128)(2,1)}, bf16[128,2048]{1,0:T(8,128)(2,1)}, u32[]{:S(2)}, u32[]{:S(2)}) collective-permute-start(bf16[128,2048]{1,0:T(8,128)(2,1)} %shard_map.101), channel_id=1, source_target_pairs={{0,1},{2,0},{4,2},{6,4},{7,6},{5,7},{3,5},{1,3},{8,9},{10,8},{12,1... | collective-permute-start | bytes 1572872 | tf_op jit(solution)/shard_map/ppermute | solution.py:95
  44.1 22.2 %collective-permute-start.7 = (bf16[128,2048]{1,0:T(8,128)(2,1)}, bf16[128,2048]{1,0:T(8,128)(2,1)S(1)}, u32[]{:S(2)}, u32[]{:S(2)}) collective-permute-start(bf16[128,2048]{1,0:T(8,128)(2,1)} %shard_map.97), channel_id=1, source_target_pairs={{0,2},{2,4},{4,6},{6,7},{7,5},{5,3},{3,1},{1,0},{8,10},{10,12},{12... | collective-permute-start | bytes 1572872 | tf_op jit(solution)/shard_map/ppermute | solution.py:95
  45.8 3.0 %copy-start.19 = (bf16[128,2048]{1,0:T(8,128)(2,1)S(1)}, bf16[128,2048]{1,0:T(8,128)(2,1)}, u32[]{:S(2)}) copy-start(bf16[128,2048]{1,0:T(8,128)(2,1)} %shard_map.101) | copy-start | bytes 1572868
  45.8 23.8 %collective-permute-start.3 = (bf16[128,2048]{1,0:T(8,128)(2,1)}, bf16[128,2048]{1,0:T(8,128)(2,1)S(1)}, u32[]{:S(2)}, u32[]{:S(2)}) collective-permute-start(bf16[128,2048]{1,0:T(8,128)(2,1)} %shard_map.95), channel_id=1, source_target_pairs={{0,1},{2,0},{4,2},{6,4},{7,6},{5,7},{3,5},{1,3},{8,9},{10,8},{12,1... | collective-permute-start | bytes 1572872 | tf_op jit(solution)/shard_map/ppermute | solution.py:95
  67.1 23.3 %collective-permute-start.16 = (bf16[128,2048]{1,0:T(8,128)(2,1)}, bf16[128,2048]{1,0:T(8,128)(2,1)}, u32[]{:S(2)}, u32[]{:S(2)}) collective-permute-start(bf16[128,2048]{1,0:T(8,128)(2,1)} %shard_map.104), channel_id=1, source_target_pairs={{0,2},{2,4},{4,6},{6,7},{7,5},{5,3},{3,1},{1,0},{8,10},{10,12},{12... | collective-permute-start | bytes 1572872 | tf_op jit(solution)/shard_map/ppermute | solution.py:95
  67.4 23.1 %collective-permute-start.8 = (bf16[128,2048]{1,0:T(8,128)(2,1)}, bf16[128,2048]{1,0:T(8,128)(2,1)S(1)}, u32[]{:S(2)}, u32[]{:S(2)}) collective-permute-start(bf16[128,2048]{1,0:T(8,128)(2,1)} %shard_map.98), channel_id=1, source_target_pairs={{0,2},{2,4},{4,6},{6,7},{7,5},{5,3},{3,1},{1,0},{8,10},{10,12},{12... | collective-permute-start | bytes 1572872 | tf_op jit(solution)/shard_map/ppermute | solution.py:95
  70.4 23.2 %collective-permute-start.5 = (bf16[128,2048]{1,0:T(8,128)(2,1)}, bf16[128,2048]{1,0:T(8,128)(2,1)}, u32[]{:S(2)}, u32[]{:S(2)}) collective-permute-start(bf16[128,2048]{1,0:T(8,128)(2,1)} %shard_map.96), channel_id=1, source_target_pairs={{0,1},{2,0},{4,2},{6,4},{7,6},{5,7},{3,5},{1,3},{8,9},{10,8},{12,1... | collective-permute-start | bytes 1572872 | tf_op jit(solution)/shard_map/ppermute | solution.py:95
  73.0 20.7 %collective-permute-start.12 = (bf16[128,2048]{1,0:T(8,128)(2,1)}, bf16[128,2048]{1,0:T(8,128)(2,1)}, u32[]{:S(2)}, u32[]{:S(2)}) collective-permute-start(bf16[128,2048]{1,0:T(8,128)(2,1)} %shard_map.102), channel_id=1, source_target_pairs={{0,1},{2,0},{4,2},{6,4},{7,6},{5,7},{3,5},{1,3},{8,9},{10,8},{12,1... | collective-permute-start | bytes 1572872 | tf_op jit(solution)/shard_map/ppermute | solution.py:95
  91.3 5.7 %copy-start.18 = (bf16[128,2048]{1,0:T(8,128)(2,1)S(1)}, bf16[128,2048]{1,0:T(8,128)(2,1)}, u32[]{:S(2)}) copy-start(bf16[128,2048]{1,0:T(8,128)(2,1)} %copy-done.17) | copy-start | bytes 1572868
  91.3 41.2 %collective-permute-start.17 = (bf16[128,2048]{1,0:T(8,128)(2,1)}, bf16[128,2048]{1,0:T(8,128)(2,1)S(1)}, u32[]{:S(2)}, u32[]{:S(2)}) collective-permute-start(bf16[128,2048]{1,0:T(8,128)(2,1)} %shard_map.105), channel_id=1, source_target_pairs={{0,2},{2,4},{4,6},{6,7},{7,5},{5,3},{3,1},{1,0},{8,10},{10,12},{12... | collective-permute-start | bytes 1572872 | tf_op jit(solution)/shard_map/ppermute | solution.py:95
  93.6 35.9 %collective-permute-start.13 = (bf16[128,2048]{1,0:T(8,128)(2,1)}, bf16[128,2048]{1,0:T(8,128)(2,1)S(1)}, u32[]{:S(2)}, u32[]{:S(2)}) collective-permute-start(bf16[128,2048]{1,0:T(8,128)(2,1)} %shard_map.103), channel_id=1, source_target_pairs={{0,1},{2,0},{4,2},{6,4},{7,6},{5,7},{3,5},{1,3},{8,9},{10,8},{12,1... | collective-permute-start | bytes 1572872 | tf_op jit(solution)/shard_map/ppermute | solution.py:95
  95.4 18.4 %collective-permute-start.9 = (bf16[128,2048]{1,0:T(8,128)(2,1)}, bf16[128,2048]{1,0:T(8,128)(2,1)S(1)}, u32[]{:S(2)}, u32[]{:S(2)}) collective-permute-start(bf16[128,2048]{1,0:T(8,128)(2,1)} %copy-done.17), channel_id=1, source_target_pairs={{0,2},{2,4},{4,6},{6,7},{7,5},{5,3},{3,1},{1,0},{8,10},{10,12},{12... | collective-permute-start | bytes 1572872 | tf_op jit(solution)/shard_map/ppermute | solution.py:95
  129.2 15.6 %copy-start = (bf16[8,96,2048]{2,1,0:T(8,128)(2,1)}, bf16[8,96,2048]{2,1,0:T(8,128)(2,1)S(1)}, u32[]{:S(2)}) copy-start(bf16[8,96,2048]{2,1,0:T(8,128)(2,1)S(1)} %shard_map.100.refs_9_) | copy-start | bytes 9437188
  129.2 15.6 %copy-start.4 = (bf16[96,2048]{1,0:T(8,128)(2,1)S(1)}, bf16[96,2048]{1,0:T(8,128)(2,1)}, u32[]{:S(2)}) copy-start(bf16[96,2048]{1,0:T(8,128)(2,1)} %convolution_convert_fusion.11.refs_1_) | copy-start | bytes 1179652
  129.2 15.6 %copy-start.5 = (bf16[96,2048]{1,0:T(8,128)(2,1)S(1)}, bf16[96,2048]{1,0:T(8,128)(2,1)}, u32[]{:S(2)}) copy-start(bf16[96,2048]{1,0:T(8,128)(2,1)} %convolution_convert_fusion.4.refs_8_) | copy-start | bytes 1179652
  129.2 15.6 %copy-start.6 = (bf16[96,2048]{1,0:T(8,128)(2,1)S(1)}, bf16[96,2048]{1,0:T(8,128)(2,1)}, u32[]{:S(2)}) copy-start(bf16[96,2048]{1,0:T(8,128)(2,1)} %convolution_convert_fusion.10.refs_2_) | copy-start | bytes 1179652
  129.2 15.6 %copy-start.7 = (bf16[96,2048]{1,0:T(8,128)(2,1)S(1)}, bf16[96,2048]{1,0:T(8,128)(2,1)}, u32[]{:S(2)}) copy-start(bf16[96,2048]{1,0:T(8,128)(2,1)} %convolution_convert_fusion.5.refs_7_) | copy-start | bytes 1179652
  129.6 14.9 %collective-permute-start.14 = (bf16[128,2048]{1,0:T(8,128)(2,1)S(1)}, bf16[128,2048]{1,0:T(8,128)(2,1)S(1)}, u32[]{:S(2)}, u32[]{:S(2)}) collective-permute-start(bf16[128,2048]{1,0:T(8,128)(2,1)S(1)} %collective-permute-done.13), channel_id=1, source_target_pairs={{0,1},{2,0},{4,2},{6,4},{7,6},{5,7},{3,5},{1,3},{8,9},{10,8},{12,1... | collective-permute-start | bytes 1572872 | tf_op jit(solution)/shard_map/ppermute | solution.py:95
  130.2 30.8 %collective-permute-start.10 = (bf16[128,2048]{1,0:T(8,128)(2,1)S(1)}, bf16[128,2048]{1,0:T(8,128)(2,1)}, u32[]{:S(2)}, u32[]{:S(2)}) collective-permute-start(bf16[128,2048]{1,0:T(8,128)(2,1)S(1)} %convolution_convert_fusion.3), channel_id=1, source_target_pairs={{0,2},{2,4},{4,6},{6,7},{7,5},{5,3},{3,1},{1,0},{8,10},{10,12},{12... | collective-permute-start | bytes 1572872 | tf_op jit(solution)/shard_map/ppermute | solution.py:95
  132.0 25.6 %collective-permute-start.21 = (bf16[128,2048]{1,0:T(8,128)(2,1)S(1)}, bf16[128,2048]{1,0:T(8,128)(2,1)S(1)}, u32[]{:S(2)}, u32[]{:S(2)}) collective-permute-start(bf16[128,2048]{1,0:T(8,128)(2,1)S(1)} %convolution_convert_fusion.2), channel_id=1, source_target_pairs={{0,1},{2,0},{4,2},{6,4},{7,6},{5,7},{3,5},{1,3},{8,9},{10,8},{12,1... | collective-permute-start | bytes 1572872 | tf_op jit(solution)/shard_map/ppermute | solution.py:95
  156.6 1.0 copy-start.10
  157.6 2.4 copy-start.8
  160.8 20.4 %collective-permute-start.22 = (bf16[128,2048]{1,0:T(8,128)(2,1)}, bf16[128,2048]{1,0:T(8,128)(2,1)}, u32[]{:S(2)}, u32[]{:S(2)}) collective-permute-start(bf16[128,2048]{1,0:T(8,128)(2,1)} %shard_map.108), channel_id=1, source_target_pairs={{0,1},{2,0},{4,2},{6,4},{7,6},{5,7},{3,5},{1,3},{8,9},{10,8},{12,1... | collective-permute-start | bytes 1572872 | tf_op jit(solution)/shard_map/ppermute | solution.py:95
  163.3 23.5 %collective-permute-start.18 = (bf16[128,2048]{1,0:T(8,128)(2,1)}, bf16[128,2048]{1,0:T(8,128)(2,1)}, u32[]{:S(2)}, u32[]{:S(2)}) collective-permute-start(bf16[128,2048]{1,0:T(8,128)(2,1)} %shard_map.107), channel_id=1, source_target_pairs={{0,2},{2,4},{4,6},{6,7},{7,5},{5,3},{3,1},{1,0},{8,10},{10,12},{12... | collective-permute-start | bytes 1572872 | tf_op jit(solution)/shard_map/ppermute | solution.py:95
  165.1 1.0 copy-start.3
  166.1 1.3 copy-start.9
  167.4 1.3 copy-start.11
  168.7 12.7 %copy-start.1 = (bf16[8,96,2048]{2,1,0:T(8,128)(2,1)S(1)}, bf16[8,96,2048]{2,1,0:T(8,128)(2,1)}, u32[]{:S(2)}) copy-start(bf16[8,96,2048]{2,1,0:T(8,128)(2,1)} %copy-done) | copy-start | bytes 9437188
  181.2 12.1 %collective-permute-start.24 = (bf16[128,2048]{1,0:T(8,128)(2,1)}, bf16[128,2048]{1,0:T(8,128)(2,1)}, u32[]{:S(2)}, u32[]{:S(2)}) collective-permute-start(bf16[128,2048]{1,0:T(8,128)(2,1)} %shard_map.110), channel_id=1, source_target_pairs={{0,1},{2,0},{4,2},{6,4},{7,6},{5,7},{3,5},{1,3},{8,9},{10,8},{12,1... | collective-permute-start | bytes 1572872 | tf_op jit(solution)/shard_map/ppermute | solution.py:95
  183.6 18.9 %collective-permute-start.23 = (bf16[128,2048]{1,0:T(8,128)(2,1)}, bf16[128,2048]{1,0:T(8,128)(2,1)}, u32[]{:S(2)}, u32[]{:S(2)}) collective-permute-start(bf16[128,2048]{1,0:T(8,128)(2,1)} %fusion.6), channel_id=1, source_target_pairs={{0,1},{2,0},{4,2},{6,4},{7,6},{5,7},{3,5},{1,3},{8,9},{10,8},{12,1... | collective-permute-start | bytes 1572872 | tf_op jit(solution)/shard_map/ppermute | solution.py:95
  186.8 16.1 %collective-permute-start.28 = (bf16[128,2048]{1,0:T(8,128)(2,1)}, bf16[128,2048]{1,0:T(8,128)(2,1)}, u32[]{:S(2)}, u32[]{:S(2)}) collective-permute-start(bf16[128,2048]{1,0:T(8,128)(2,1)} %shard_map.112), channel_id=1, source_target_pairs={{0,2},{2,4},{4,6},{6,7},{7,5},{5,3},{3,1},{1,0},{8,10},{10,12},{12... | collective-permute-start | bytes 1572872 | tf_op jit(solution)/shard_map/ppermute | solution.py:95
  189.9 20.2 %collective-permute-start.19 = (bf16[128,2048]{1,0:T(8,128)(2,1)}, bf16[128,2048]{1,0:T(8,128)(2,1)}, u32[]{:S(2)}, u32[]{:S(2)}) collective-permute-start(bf16[128,2048]{1,0:T(8,128)(2,1)} %fusion.4), channel_id=1, source_target_pairs={{0,2},{2,4},{4,6},{6,7},{7,5},{5,3},{3,1},{1,0},{8,10},{10,12},{12... | collective-permute-start | bytes 1572872 | tf_op jit(solution)/shard_map/ppermute | solution.py:95
  202.5 14.5 %collective-permute-start.25 = (bf16[128,2048]{1,0:T(8,128)(2,1)}, bf16[128,2048]{1,0:T(8,128)(2,1)}, u32[]{:S(2)}, u32[]{:S(2)}) collective-permute-start(bf16[128,2048]{1,0:T(8,128)(2,1)} %shard_map.111), channel_id=1, source_target_pairs={{0,1},{2,0},{4,2},{6,4},{7,6},{5,7},{3,5},{1,3},{8,9},{10,8},{12,1... | collective-permute-start | bytes 1572872 | tf_op jit(solution)/shard_map/ppermute | solution.py:95
  210.1 12.8 %collective-permute-start.29 = (bf16[128,2048]{1,0:T(8,128)(2,1)}, bf16[128,2048]{1,0:T(8,128)(2,1)}, u32[]{:S(2)}, u32[]{:S(2)}) collective-permute-start(bf16[128,2048]{1,0:T(8,128)(2,1)} %shard_map.113), channel_id=1, source_target_pairs={{0,2},{2,4},{4,6},{6,7},{7,5},{5,3},{3,1},{1,0},{8,10},{10,12},{12... | collective-permute-start | bytes 1572872 | tf_op jit(solution)/shard_map/ppermute | solution.py:95
  213.2 35.2 %copy-start.20 = (s32[128,4]{0,1:T(4,128)S(1)}, s32[128,4]{0,1:T(4,128)}, u32[]{:S(2)}) copy-start(s32[128,4]{0,1:T(4,128)} %param.9) | copy-start | bytes 6148
  213.2 17.7 %collective-permute-start.20 = (bf16[128,2048]{1,0:T(8,128)(2,1)}, bf16[128,2048]{1,0:T(8,128)(2,1)}, u32[]{:S(2)}, u32[]{:S(2)}) collective-permute-start(bf16[128,2048]{1,0:T(8,128)(2,1)} %fusion.3), channel_id=1, source_target_pairs={{0,2},{2,4},{4,6},{6,7},{7,5},{5,3},{3,1},{1,0},{8,10},{10,12},{12... | collective-permute-start | bytes 1572872 | tf_op jit(solution)/shard_map/ppermute | solution.py:95
  219.2 13.7 %collective-permute-start.26 = (bf16[128,2048]{1,0:T(8,128)(2,1)}, bf16[128,2048]{1,0:T(8,128)(2,1)}, u32[]{:S(2)}, u32[]{:S(2)}) collective-permute-start(bf16[128,2048]{1,0:T(8,128)(2,1)} %fusion.10), channel_id=1, source_target_pairs={{0,1},{2,0},{4,2},{6,4},{7,6},{5,7},{3,5},{1,3},{8,9},{10,8},{12,1... | collective-permute-start | bytes 1572872 | tf_op jit(solution)/shard_map/ppermute | solution.py:95
  230.9 20.5 %collective-permute-start.30 = (bf16[128,2048]{1,0:T(8,128)(2,1)}, bf16[128,2048]{1,0:T(8,128)(2,1)}, u32[]{:S(2)}, u32[]{:S(2)}) collective-permute-start(bf16[128,2048]{1,0:T(8,128)(2,1)} %shard_map.114), channel_id=1, source_target_pairs={{0,2},{2,4},{4,6},{6,7},{7,5},{5,3},{3,1},{1,0},{8,10},{10,12},{12... | collective-permute-start | bytes 1572872 | tf_op jit(solution)/shard_map/ppermute | solution.py:95
  235.2 16.2 %collective-permute-start.27 = (bf16[128,2048]{1,0:T(8,128)(2,1)}, bf16[128,2048]{1,0:T(8,128)(2,1)}, u32[]{:S(2)}, u32[]{:S(2)}) collective-permute-start(bf16[128,2048]{1,0:T(8,128)(2,1)} %fusion.9), channel_id=1, source_target_pairs={{0,1},{2,0},{4,2},{6,4},{7,6},{5,7},{3,5},{1,3},{8,9},{10,8},{12,1... | collective-permute-start | bytes 1572872 | tf_op jit(solution)/shard_map/ppermute | solution.py:95
  236.1 12.3 %all-to-all-start.1 = ((f32[8,2,128]{2,1,0:T(2,128)}), f32[8,2,128]{2,1,0:T(2,128)S(1)}, u32[]{:S(2)}, u32[]{:S(2)}) async-start(f32[8,2,128]{2,1,0:T(2,128)} %get-tuple-element.16.refs_1_), calls=%async_computation.1 | async-start | bytes 16384 | tf_op jit(solution)/shard_map/all_to_all | solution.py:499
  (6 other events, 4.9 us)

commit v6 on v4

--- a/solution.py
+++ b/solution.py
@@ -95,57 +95,40 @@
     return lax.ppermute(array, "ep", pairs)
 
 
-def ring_gather(shard, count, far_step, behind={}):
-    held = {0: shard}
-    arrivals = {}
-    for step in (far_step, -far_step):
-        hops = count // 2 if step == far_step else (count - 1) // 2
-        moving = shard
-        arrivals[step] = []
-        for hop in range(1, hops + 1):
-            if (step, hop) in behind:
-                moving = held_back(moving, behind[step, hop])
-                if hop > 1:
-                    held[(-step * (hop - 1)) % count] = moving
-            moving = ring_shift(moving, count, step)
-            held[(-step * hop) % count] = moving
-            arrivals[step].append(moving)
-    return [held[place] for place in range(count)], arrivals
-
-
-def after(array, *others):
-    for other in others:
-        array = array + other[(slice(0, 1),) * other.ndim].reshape((1,) * array.ndim).astype(array.dtype) * 0
-    return array
-
-
-def held_back(array, others):
-    def kernel(*refs):
-        pass
-
-    return pl.pallas_call(
-        kernel,
-        out_shape=jax.ShapeDtypeStruct(array.shape, array.dtype),
-        in_specs=[pl.BlockSpec(memory_space=pl.ANY) for _ in range(1 + len(others))],
-        out_specs=pl.BlockSpec(memory_space=pl.ANY),
-        input_output_aliases={0: 0},
-    )(array, *others)
-
-
-def ring_reduce(share_of, count, far_step, behind={}):
-    arrived = {}
-    for step in (far_step, -far_step):
-        hops = count // 2 if step == far_step else (count - 1) // 2
-        moving = None
-        steps = []
-        for hop in range(hops, 0, -1):
-            waits = behind.get((step, hops - hop), ())
-            share = share_of((step * hop) % count, moving, waits)
-            moving = ring_shift(share, count, step)
-            steps.append(moving)
-        arrived[step] = steps
-    total = share_of(0, arrived[far_step][-1], (arrived[-far_step][-1],), True)
-    return total, arrived
+def hops_of(count, step, far_step):
+    return count // 2 if step == far_step else (count - 1) // 2
+
+
+def ring_gather(first, second, count, behind):
+    rows = first.shape[0]
+    held = [{0: (first, 0)}, {0: (second, 0)}]
+    for step in (1, -1):
+        hops = hops_of(count, step, 1), hops_of(count, step, -1)
+        low, high = (first, 0), None
+        for stage in range(1, max(hops[0], hops[1] + 1) + 1):
+            if stage == 2:
+                high = (second, 0)
+            one = low if stage <= hops[0] else None
+            two = high if 1 < stage <= hops[1] + 1 else None
+            last = stage >= hops[0]
+            if one and two and not last:
+                if one[0] is two[0]:
+                    both = one[0]
+                else:
+                    both = run_join(one[0], two[0], behind)
+                both = ring_shift(both, count, step)
+                low, high = (both, 0), (both, rows)
+            else:
+                cuts = [None if v is None else v[0][v[1] : v[1] + rows] for v in (one, two)]
+                if one:
+                    low = (ring_shift(cuts[0], count, step), 0)
+                if two:
+                    high = (ring_shift(cuts[1], count, step), 0)
+            if one:
+                held[0][(-step * stage) % count] = low
+            if two:
+                held[1][(-step * (stage - 1)) % count] = high
+    return [[h[place] for place in range(count)] for h in held]
 
 
 VMEM_LIMIT = 48 * 1024 * 1024
@@ -157,7 +140,7 @@
 
 
 def call_kernel(kernel, operands, kinds, outs, scratch, flops, behind=()):
-    spaces = {"any": pl.ANY, "vmem": pltpu.VMEM, "smem": pltpu.SMEM}
+    spaces = {"any": pltpu.HBM, "vmem": pltpu.VMEM, "smem": pltpu.SMEM}
     count = len(operands)
     operands = [*operands, *behind]
     kinds = [*kinds, *["any" for _ in behind]]
@@ -222,6 +205,87 @@
 
     shape = jax.ShapeDtypeStruct((count, 2 * capacity, tokens), bf16)
     return call_kernel(kernel, [ids, tables], ["smem", "vmem"], [shape, shape], [], 1 << 20)
+
+
+def run_join(upper, lower, behind):
+    rows, width = upper.shape
+    tile = cut(width, 512)
+
+    def kernel(*refs):
+        refs[-1][:rows, :] = refs[0][...]
+        refs[-1][rows:, :] = refs[1][...]
+
+    return pl.pallas_call(
+        kernel,
+        grid=(width // tile,),
+        out_shape=jax.ShapeDtypeStruct((2 * rows, width), upper.dtype),
+        in_specs=[pl.BlockSpec((rows, tile), lambda i: (0, i)) for _ in range(2)]
+        + [pl.BlockSpec(memory_space=pltpu.HBM) for _ in behind],
+        out_specs=pl.BlockSpec((2 * rows, tile), lambda i: (0, i)),
+    )(upper, lower, *behind)
+
+
+def run_pick(pick, wanted):
+    _, slots, tokens = pick.shape
+    width = wanted[0][0].shape[1]
+    tile = cut(width, 512)
+    count = len(wanted)
+
+    def kernel(*refs):
+        for i in range(count):
+            refs[2 * count + i][...] = jnp.dot(
+                refs[i][0], refs[count + i][...], preferred_element_type=jnp.float32
+            ).astype(jnp.bfloat16)
+
+    return pl.pallas_call(
+        kernel,
+        grid=(width // tile,),
+        out_shape=[jax.ShapeDtypeStruct((slots, width), jnp.bfloat16) for _ in wanted],
+        in_specs=[
+            pl.BlockSpec((1, slots, tokens), lambda i, s=s: (s, 0, 0)) for _, _, s in wanted
+        ]
+        + [pl.BlockSpec((tokens, tile), lambda i, r=r: (r // tokens, i)) for _, r, _ in wanted],
+        out_specs=[pl.BlockSpec((slots, tile), lambda i: (0, i)) for _ in wanted],
+    )(*[pick for _ in wanted], *[buffer for buffer, _, _ in wanted])
+
+
+def run_shares(spread, wanted, behind=()):
+    _, slots, tokens = spread.shape
+    width = wanted[0][0].shape[2]
+    tile = cut(width, 512)
+    count = len(wanted)
+    extra = [partial for _, _, partials in wanted for partial in partials]
+
+    def kernel(*refs):
+        rest = list(refs[2 * count : 2 * count + len(extra)])
+        for i, (_, _, partials) in enumerate(wanted):
+            total = lax.dot_general(
+                refs[i][0],
+                refs[count + i][0],
+                (((0,), (0,)), ((), ())),
+                preferred_element_type=jnp.float32,
+            )
+            for _ in partials:
+                total = total + rest.pop(0)[...].astype(jnp.float32)
+            refs[-1][i * tokens : (i + 1) * tokens, :] = total.astype(jnp.bfloat16)
+
+    return pl.pallas_call(
+        kernel,
+        grid=(width // tile,),
+        out_shape=jax.ShapeDtypeStruct((count * tokens, width), jnp.bfloat16),
+        in_specs=[
+            pl.BlockSpec((1, slots, tokens), lambda i, s=s: (s, 0, 0)) for _, s, _ in wanted
+        ]
+        + [pl.BlockSpec((1, slots, tile), lambda i, s=s: (s, 0, i)) for _, s, _ in wanted]
+        + [pl.BlockSpec((tokens, tile), lambda i, r=r: (r // tokens, i)) for _, r in extra]
+        + [pl.BlockSpec(memory_space=pltpu.HBM) for _ in behind],
+        out_specs=pl.BlockSpec((count * tokens, tile), lambda i: (0, i)),
+    )(
+        *[spread for _ in wanted],
+        *[outputs for outputs, _, _ in wanted],
+        *[buffer for buffer, _ in extra],
+        *behind,
+    )
 
 
 def run_hidden(parts, gate_mats, up_mats):
@@ -438,53 +502,60 @@
     tables = lax.all_to_all(copies, "ep", split_axis=0, concat_axis=0, tiled=True)
     pick, spread = run_routing(ids, tables, top_count, capacity)
 
-    behind = {(step, 2): (tables,) for step in (1, -1)}
-    in_shards, in_hops = ring_gather(tokens, chips, 1, behind)
-    behind = {(step, 1): (in_hops[step][0],) for step in (1, -1)}
-    grad_shards, _ = ring_gather(cotangent, chips, -1, behind)
     gate_mats = (w_gate[0], swap_cores(w_gate[0]))
     up_mats = (w_up[0], swap_cores(w_up[0]))
     down_mats = (w_down[0], swap_cores(w_down[0]))
 
-    def gather_rows(shards):
-        return [
-            jnp.dot(pick[s], shards[s], preferred_element_type=f32).astype(bf16)
-            for s in range(chips)
-        ]
-
-    def scatter_rows(blocks):
-        def share_of(s, partial, waits=(), add_waits=False):
-            total = lax.dot_general(
-                spread[s], blocks[s], (((0,), (0,)), ((), ())), preferred_element_type=f32
-            )
-            if partial is not None:
-                total = total + partial.astype(f32)
-            if add_waits:
-                return (total + waits[0].astype(f32)).astype(bf16)
-            return after(total.astype(bf16), *waits)
-
-        return share_of
-
-    rows_in = gather_rows(in_shards)
+    in_held, grad_held = ring_gather(
+        tokens, cotangent, chips, (tables, gate_mats[1], up_mats[1])
+    )
+    rows_in, rows_grad = [None] * chips, [None] * chips
+    grouped = {}
+    for rows, held in ((rows_in, in_held), (rows_grad, grad_held)):
+        for s, (buffer, offset) in enumerate(held):
+            grouped.setdefault(id(buffer), []).append((rows, (buffer, offset, s)))
+    for group in grouped.values():
+        for (rows, (_, _, s)), picked in zip(group, run_pick(pick, [w for _, w in group])):
+            rows[s] = picked
+
     hidden, slope, activated = run_hidden(rows_in, gate_mats, up_mats)
     outputs = run_down(hidden, down_mats, chips)
-    rows_grad = gather_rows(grad_shards)
     d_pre_gate, d_pre_up, per_token = run_d_hidden(
         ids, rows_grad, outputs, pick, slope, activated, down_mats, ()
     )
-    behind = {(step, 1): (per_token,) for step in (1, -1)}
-    mixed, mixed_hops = ring_reduce(scatter_rows(outputs), chips, 1, behind)
+
+    lag = 2
+    arrived = {}
+    for step in (1, -1):
+        now = ring_shift(
+            run_shares(spread, [(outputs, (step * hops_of(chips, step, 1)) % chips, [])]), chips, step
+        )
+        arrived[step] = [(now, 0)]
     d_copies = run_d_copy(
-        d_pre_gate, d_pre_up, gate_mats, up_mats, chips, [mixed_hops[step][0] for step in (1, -1)]
-    )
+        d_pre_gate, d_pre_up, gate_mats, up_mats, chips, [arrived[step][0][0] for step in (1, -1)]
+    )
+    mixed_last, grad_last = {}, {}
+    for step in (1, -1):
+        ahead, later = hops_of(chips, step, 1), hops_of(chips, step, -1)
+        partial, grad_partial = arrived[step][0], None
+        for stage in range(2, max(ahead, later + lag) + 1):
+            wanted = []
+            if stage <= ahead:
+                wanted.append((outputs, (step * (ahead - stage + 1)) % chips, [partial]))
+            if stage > lag:
+                place = (step * (later - stage + lag + 1)) % chips
+                wanted.append((d_copies, place, [grad_partial] if grad_partial else []))
+            behind = (per_token,) if stage == 2 else ()
+            now = ring_shift(run_shares(spread, wanted, behind), chips, step)
+            if stage <= ahead:
+                partial = (now, 0)
+            if stage > lag:
+                grad_partial = (now, (len(wanted) - 1) * token_count)
+        mixed_last[step], grad_last[step] = partial, grad_partial
+    mixed = run_shares(spread, [(outputs, 0, [mixed_last[1], mixed_last[-1]])])
+    d_tokens = run_shares(spread, [(d_copies, 0, [grad_last[1], grad_last[-1]])])
 
     returned = lax.all_to_all(per_token, "ep", split_axis=0, concat_axis=0, tiled=True)
-    behind = {
-        (step, hop): (mixed_hops[step][hop + 1],)
-        for step in (1, -1)
-        for hop in range(len(mixed_hops[step]) - 1)
-    }
-    d_tokens, _ = ring_reduce(scatter_rows(d_copies), chips, -1, behind)
     chip_ids = jnp.arange(chips, dtype=jnp.int32)
     served = jnp.stack([core * chips + chip_ids, (1 - core) * chips + chip_ids], axis=1)
     chosen = routes.T[None, None] == served[:, :, None, None]
@@ -493,7 +564,7 @@
 
 
 def solution(mesh):
-    plan = body_ring if mesh.shape["ep"] <= 8 and mesh.shape["grp"] == 2 else body_exchange
+    plan = body_ring if 4 <= mesh.shape["ep"] <= 8 and mesh.shape["grp"] == 2 else body_exchange
     return jax.shard_map(
         plan,
         mesh=mesh,

time: 221 us -> 285 us (1.29)
  Pallas kernels: 38.1 us -> 140 us
  waiting for transfers between devices: 95.4 us -> 66.8 us
  matrix products: 27.6 us -> 0 us
  local copies, waits for them, and re-layouts: 11 us -> 29.3 us
  blocking collectives: 0 us -> 15 us
  starting transfers between devices: 40.9 us -> 28.4 us
  between operations: 4.98 us -> 0.9 us
    pallas_call x4 -> x28, Pallas kernels: 0.01 us -> 102 us  [the longest x13 48.9 us: run_shares(): pl.pallas_call(kernel, grid=(width // tile,), out_shape=jax.ShapeDtypeStr...]
    dot_general x32 -> x0, matrix products: 27.6 us -> none  [the longest x16 18.6 us: share_of(): lax.dot_general(spread[s], blocks[s], (((0,), (0,)), ((), ())), preferred...]
    ppermute x28 -> x22, waiting for transfers between devices: 82 us -> 60.4 us  [ring_shift(): return lax.ppermute(array, 'ep', pairs)]
    unnamed x26 -> x86, local copies, waits for them, and re-layouts: 6.01 us -> 27.3 us
    all_to_all x0 -> x1, blocking collectives: none -> 15 us  [body_ring(): lax.all_to_all(copies, 'ep', split_axis=0, concat_axis=0, tiled=True)]
    all_to_all x1 -> x0, waiting for transfers between devices: 6.91 us -> none  [body_ring(): lax.all_to_all(copies, 'ep', split_axis=0, concat_axis=0, tiled=True)]
    ppermute x28 -> x22, starting transfers between devices: 31.3 us -> 24.5 us  [ring_shift(): return lax.ppermute(array, 'ep', pairs)]
    all_to_all x1 -> x0, starting transfers between devices: 6.25 us -> none  [body_ring(): lax.all_to_all(copies, 'ep', split_axis=0, concat_axis=0, tiled=True)]
  transfers between devices with their start and end apart: 33 -> 26, of which waited for: 18 -> 8; matrix products, arithmetic and copies ran while one was open for 15% -> 1% of each run, Pallas kernels for 17% -> 48%
where the time goes in v6:
time: 285 us; the launch traced here: 283 us
  Pallas kernels  140 us (49%)
  waiting for transfers between devices  66.8 us (23%)
  local copies, waits for them, and re-layouts  29.3 us (10%)
  starting transfers between devices  28.4 us (10%)
  blocking collectives  15 us (5%)
    ppermute x22, waiting for transfers between devices, ring_shift(): return lax.ppermute(array, 'ep', pairs)  60.4 us
    pallas_call x13, Pallas kernels, run_shares(): pl.pallas_call(kernel, grid=(width // tile,), out_shape=jax.ShapeDtypeStr...  48.9 us
    pallas_call x13, Pallas kernels, run_pick(): pl.pallas_call(kernel, grid=(width // tile,), out_shape=[jax.ShapeDtypeSt...  46 us
    pallas_call x5, Pallas kernels, call_kernel(): pl.pallas_call(body, out_shape=outs, in_specs=[pl.BlockSpec(memory_space=...  38.1 us
    unnamed x86, local copies, waits for them, and re-layouts  27.3 us
    ppermute x22, starting transfers between devices, ring_shift(): return lax.ppermute(array, 'ep', pairs)  24.5 us
    all_to_all x1, blocking collectives, body_ring(): lax.all_to_all(copies, 'ep', split_axis=0, concat_axis=0, tiled=True)  15 us
    pallas_call x2, Pallas kernels, run_join(): pl.pallas_call(kernel, grid=(width // tile,), out_shape=jax.ShapeDtypeStr...  6.95 us
  transfers between devices with their start and end apart: 26, of which 8 were waited for; matrix products, arithmetic and copies ran while one was open for 1% of the time, Pallas kernels for 48%

profile of v6, /device:TPU:0, one launch (start us, length us, event | category | flops | bytes accessed | tf_op | source)
XLA Modules:
  0.0 282.5 jit_solution(8058279412683049269)
XLA Ops:
  1.2 3.0 %collective-permute-start.5 = (bf16[128,2048]{1,0:T(8,128)(2,1)}, bf16[128,2048]{1,0:T(8,128)(2,1)S(1)}, u32[]{:S(2)}, u32[]{:S(2)}) collective-permute-start(bf16[128,2048]{1,0:T(8,128)(2,1)} %refs_1_.4), channel_id=1, source_target_pairs={{0,2},{2,4},{4,6},{6,7},{7,5},{5,3},{3,1},{1,0},{8,10},{10,12},{12... | collective-permute-start | bytes 1572872 | tf_op jit(solution)/shard_map/ppermute | solution.py:95
  5.6 15.0 %all_to_all.10.refs_1_.refs_2_ = f32[8,8,128]{2,1,0:T(8,128)} all-to-all(f32[8,8,128]{2,1,0:T(8,128)S(1)} %broadcast_in_dim.10), channel_id=1, replica_groups=mesh['rep'=2,'grp'=2,'ep'=8] {'ep'}, dimensions={0} | all-to-all | bytes 65536 | tf_op jit(solution)/shard_map/all_to_all | solution.py:502
  23.1 3.5 %shard_map.100 = bf16[256,2048]{1,0:T(8,128)(2,1)} custom-call(bf16[128,2048]{1,0:T(8,128)(2,1)} %copy-done.34, bf16[128,2048]{1,0:T(8,128)(2,1)} %refs_1_.7, f32[8,8,128]{2,1,0:T(8,128)} %all_to_all.10.refs_1_.refs_2_, bf16[2048,768]{1,0:T(8,128)(2,1)} %copy-done.27, bf16[2048,768]{1,0:T(8,128)(2,1)} %collective-permute-done.2.refs_4_.refs_11_.refs_5_), custom_call_target="tpu_custom_call" | custom-call | tf_op jit(solution)/shard_map/pallas_call | solution.py:218
  27.2 3.5 %shard_map.97 = bf16[256,2048]{1,0:T(8,128)(2,1)} custom-call(bf16[128,2048]{1,0:T(8,128)(2,1)} %collective-permute-done.refs_1_.refs_0_, bf16[128,2048]{1,0:T(8,128)(2,1)} %refs_1_.7, f32[8,8,128]{2,1,0:T(8,128)} %all_to_all.10.refs_1_.refs_2_, bf16[2048,768]{1,0:T(8,128)(2,1)} %copy-done.27, bf16[2048,768]{1,0:T(8,128)(2,1)} %collective-permute-done.2.refs_4_.refs_11_.refs_5_), custom_call_target="tpu_custom_call" | custom-call | tf_op jit(solution)/shard_map/pallas_call | solution.py:218
  32.1 18.3 %collective-permute-done.6.refs_2_.refs_3_ = bf16[256,2048]{1,0:T(8,128)(2,1)S(1)} collective-permute-done((bf16[256,2048]{1,0:T(8,128)(2,1)}, bf16[256,2048]{1,0:T(8,128)(2,1)S(1)}, u32[]{:S(2)}, u32[]{:S(2)}) %collective-permute-start.6) | collective-permute-done | bytes 1048608 | tf_op jit(solution)/shard_map/ppermute | solution.py:95
  51.4 3.2 %collective-permute-done.3.refs_2_.refs_3_ = bf16[256,2048]{1,0:T(8,128)(2,1)S(1)} collective-permute-done((bf16[256,2048]{1,0:T(8,128)(2,1)}, bf16[256,2048]{1,0:T(8,128)(2,1)S(1)}, u32[]{:S(2)}, u32[]{:S(2)}) %collective-permute-start.3) | collective-permute-done | bytes 1048608 | tf_op jit(solution)/shard_map/ppermute | solution.py:95
  57.9 12.5 %collective-permute-done.10.refs_1_ = bf16[128,2048]{1,0:T(8,128)(2,1)S(1)} collective-permute-done((bf16[128,2048]{1,0:T(8,128)(2,1)S(1)}, bf16[128,2048]{1,0:T(8,128)(2,1)S(1)}, u32[]{:S(2)}, u32[]{:S(2)}) %collective-permute-start.10) | collective-permute-done | bytes 524320 | tf_op jit(solution)/shard_map/ppermute | solution.py:95
  78.6 3.5 %shard_map.95.refs_0_ = bf16[96,2048]{1,0:T(8,128)(2,1)} custom-call(bf16[8,96,128]{2,1,0:T(8,128)(2,1)} %copy-done.1, bf16[128,2048]{1,0:T(8,128)(2,1)} %refs_1_.4), custom_call_target="tpu_custom_call" | custom-call | tf_op jit(solution)/shard_map/pallas_call | solution.py:240
  82.1 3.4 %shard_map.96.refs_1_ = bf16[96,2048]{1,0:T(8,128)(2,1)} custom-call(bf16[8,96,128]{2,1,0:T(8,128)(2,1)} %copy-done.1, bf16[128,2048]{1,0:T(8,128)(2,1)} %collective-permute-done.refs_1_.refs_0_), custom_call_target="tpu_custom_call" | custom-call | tf_op jit(solution)/shard_map/pallas_call | solution.py:240
  85.6 3.5 %shard_map.104.refs_7_ = bf16[96,2048]{1,0:T(8,128)(2,1)} custom-call(bf16[8,96,128]{2,1,0:T(8,128)(2,1)} %copy-done.1, bf16[128,2048]{1,0:T(8,128)(2,1)} %copy-done.34), custom_call_target="tpu_custom_call" | custom-call | tf_op jit(solution)/shard_map/pallas_call | solution.py:240
  89.0 3.7 %shard_map.98 = (bf16[96,2048]{1,0:T(8,128)(2,1)}, bf16[96,2048]{1,0:T(8,128)(2,1)}) custom-call(bf16[8,96,128]{2,1,0:T(8,128)(2,1)} %copy-done.1, bf16[8,96,128]{2,1,0:T(8,128)(2,1)} %copy-done.1, bf16[256,2048]{1,0:T(8,128)(2,1)} %copy-done.29, bf16[256,2048]{1,0:T(8,128)(2,1)} %copy-done.29), custom_call_target="tpu_custom_call" | custom-call | tf_op jit(solution)/shard_map/pallas_call | solution.py:240
  92.8 3.8 %shard_map.103 = (bf16[96,2048]{1,0:T(8,128)(2,1)}, bf16[96,2048]{1,0:T(8,128)(2,1)}) custom-call(bf16[8,96,128]{2,1,0:T(8,128)(2,1)} %copy-done.1, bf16[8,96,128]{2,1,0:T(8,128)(2,1)} %copy-done.1, bf16[256,2048]{1,0:T(8,128)(2,1)} %copy-done.31, bf16[256,2048]{1,0:T(8,128)(2,1)} %copy-done.31), custom_call_target="tpu_custom_call" | custom-call | tf_op jit(solution)/shard_map/pallas_call | solution.py:240
  96.6 3.5 %shard_map.99.refs_3_ = bf16[96,2048]{1,0:T(8,128)(2,1)} custom-call(bf16[8,96,128]{2,1,0:T(8,128)(2,1)} %copy-done.1, bf16[128,2048]{1,0:T(8,128)(2,1)} %collective-permute-done.4.refs_1_), custom_call_target="tpu_custom_call" | custom-call | tf_op jit(solution)/shard_map/pallas_call | solution.py:240
  102.1 3.7 %shard_map.102 = (bf16[96,2048]{1,0:T(8,128)(2,1)}, bf16[96,2048]{1,0:T(8,128)(2,1)}) custom-call(bf16[8,96,128]{2,1,0:T(8,128)(2,1)} %copy-done.1, bf16[8,96,128]{2,1,0:T(8,128)(2,1)} %copy-done.1, bf16[256,2048]{1,0:T(8,128)(2,1)} %copy-done.28, bf16[256,2048]{1,0:T(8,128)(2,1)} %copy-done.28), custom_call_target="tpu_custom_call" | custom-call | tf_op jit(solution)/shard_map/pallas_call | solution.py:240
  106.6 3.5 %shard_map.101.refs_4_ = bf16[96,2048]{1,0:T(8,128)(2,1)} custom-call(bf16[8,96,128]{2,1,0:T(8,128)(2,1)} %copy-done.1, bf16[128,2048]{1,0:T(8,128)(2,1)} %copy-done.41), custom_call_target="tpu_custom_call" | custom-call | tf_op jit(solution)/shard_map/pallas_call | solution.py:240
  112.1 10.5 %shard_map.105 = (bf16[2,384,768]{2,1,0:T(8,128)(2,1)S(1)}, f32[2,384,768]{2,1,0:T(8,128)}, f32[2,384,768]{2,1,0:T(8,128)}) custom-call(bf16[96,2048]{1,0:T(8,128)(2,1)S(1)} %copy-done.16, bf16[96,2048]{1,0:T(8,128)(2,1)S(1)} %copy-done.17, bf16[96,2048]{1,0:T(8,128)(2,1)S(1)} %copy-done.24, bf16[96,2048]{1,0:T(8,128)(2,1)S(1)} %copy-done.19, ...), custom_call_target="tpu_custom_call" | custom-call | flops 4831838208 | bytes 1048576 | tf_op jit(solution)/shard_map/pallas_call | solution.py:151
  122.6 4.7 %shard_map.106.refs_9_.refs_1_.refs_2_ = bf16[8,96,2048]{2,1,0:T(8,128)(2,1)S(1)} custom-call(bf16[2,384,768]{2,1,0:T(8,128)(2,1)S(1)} %get-tuple-element.22.refs_0_, bf16[768,2048]{1,0:T(8,128)(2,1)} %bitcast.5.refs_1_.refs_13_, bf16[768,2048]{1,0:T(8,128)(2,1)} %collective-permute-done.9.refs_2_.refs_14_), custom_call_target="tpu_custom_call" | custom-call | flops 2415919104 | bytes 1048576 | tf_op jit(solution)/shard_map/pallas_call | solution.py:151
  127.4 1.8 copy-done
  129.1 3.5 %shard_map.113 = bf16[128,2048]{1,0:T(8,128)(2,1)} custom-call(bf16[8,96,128]{2,1,0:T(8,128)(2,1)} %copy-done.3, bf16[8,96,2048]{2,1,0:T(8,128)(2,1)} %copy-done), custom_call_target="tpu_custom_call" | custom-call | tf_op jit(solution)/shard_map/pallas_call | solution.py:272
  132.9 3.5 %shard_map.114 = bf16[128,2048]{1,0:T(8,128)(2,1)} custom-call(bf16[8,96,128]{2,1,0:T(8,128)(2,1)} %copy-done.3, bf16[8,96,2048]{2,1,0:T(8,128)(2,1)} %copy-done), custom_call_target="tpu_custom_call" | custom-call | tf_op jit(solution)/shard_map/pallas_call | solution.py:272
  136.5 1.7 collective-permute-start.15
  138.2 3.5 %shard_map.107.refs_1_ = bf16[96,2048]{1,0:T(8,128)(2,1)} custom-call(bf16[8,96,128]{2,1,0:T(8,128)(2,1)} %copy-done.1, bf16[128,2048]{1,0:T(8,128)(2,1)} %refs_1_.7), custom_call_target="tpu_custom_call" | custom-call | tf_op jit(solution)/shard_map/pallas_call | solution.py:240
  141.7 3.5 %shard_map.108.refs_3_ = bf16[96,2048]{1,0:T(8,128)(2,1)} custom-call(bf16[8,96,128]{2,1,0:T(8,128)(2,1)} %copy-done.1, bf16[128,2048]{1,0:T(8,128)(2,1)} %copy-done.40), custom_call_target="tpu_custom_call" | custom-call | tf_op jit(solution)/shard_map/pallas_call | solution.py:240
  145.2 3.5 %shard_map.109.refs_4_ = bf16[96,2048]{1,0:T(8,128)(2,1)} custom-call(bf16[8,96,128]{2,1,0:T(8,128)(2,1)} %copy-done.1, bf16[128,2048]{1,0:T(8,128)(2,1)} %collective-permute-done.11.refs_1_), custom_call_target="tpu_custom_call" | custom-call | tf_op jit(solution)/shard_map/pallas_call | solution.py:240
  148.7 3.4 %shard_map.110.refs_5_ = bf16[96,2048]{1,0:T(8,128)(2,1)} custom-call(bf16[8,96,128]{2,1,0:T(8,128)(2,1)} %copy-done.1, bf16[128,2048]{1,0:T(8,128)(2,1)} %collective-permute-done.12.refs_1_), custom_call_target="tpu_custom_call" | custom-call | tf_op jit(solution)/shard_map/pallas_call | solution.py:240
  152.1 3.5 %shard_map.111.refs_6_ = bf16[96,2048]{1,0:T(8,128)(2,1)} custom-call(bf16[8,96,128]{2,1,0:T(8,128)(2,1)} %copy-done.1, bf16[128,2048]{1,0:T(8,128)(2,1)} %collective-permute-done.13.refs_1_), custom_call_target="tpu_custom_call" | custom-call | tf_op jit(solution)/shard_map/pallas_call | solution.py:240
  161.6 11.8 %shard_map.112 = (bf16[2,384,768]{2,1,0:T(8,128)(2,1)S(1)}, bf16[2,384,768]{2,1,0:T(8,128)(2,1)S(1)}, f32[8,2,128]{2,1,0:T(2,128)}) custom-call(s32[2]{0:T(128)S(1)} %pad_add_fusion.1.refs_0_, bf16[96,2048]{1,0:T(8,128)(2,1)S(1)} %copy-done.8, bf16[96,2048]{1,0:T(8,128)(2,1)S(1)} %copy-done.21, bf16[96,2048]{1,0:T(8,128)(2,1)S(1)} %copy-done.9, ...), custom_call_target="tpu_custom_call" | custom-call | flops 2415919104 | bytes 1048576 | tf_op jit(solution)/shard_map/pallas_call | solution.py:151
  175.3 3.7 %shard_map.116 = bf16[128,2048]{1,0:T(8,128)(2,1)} custom-call(bf16[8,96,128]{2,1,0:T(8,128)(2,1)} %copy-done.3, bf16[8,96,2048]{2,1,0:T(8,128)(2,1)} %copy-done, bf16[128,2048]{1,0:T(8,128)(2,1)} %copy-done.4, f32[8,2,128]{2,1,0:T(2,128)} %get-tuple-element.30.refs_3_), custom_call_target="tpu_custom_call" | custom-call | tf_op jit(solution)/shard_map/pallas_call | solution.py:272
  180.1 3.7 %shard_map.119 = bf16[128,2048]{1,0:T(8,128)(2,1)} custom-call(bf16[8,96,128]{2,1,0:T(8,128)(2,1)} %copy-done.3, bf16[8,96,2048]{2,1,0:T(8,128)(2,1)} %copy-done, bf16[128,2048]{1,0:T(8,128)(2,1)} %copy-done.6, f32[8,2,128]{2,1,0:T(2,128)} %get-tuple-element.30.refs_3_), custom_call_target="tpu_custom_call" | custom-call | tf_op jit(solution)/shard_map/pallas_call | solution.py:272
  183.8 1.7 collective-permute-start.19
  187.8 10.3 %shard_map.115.refs_3_.refs_1_ = bf16[8,96,2048]{2,1,0:T(8,128)(2,1)} custom-call(bf16[2,384,768]{2,1,0:T(8,128)(2,1)S(1)} %get-tuple-element.28.refs_0_, bf16[2,384,768]{2,1,0:T(8,128)(2,1)S(1)} %copy-done.14, bf16[2048,768]{1,0:T(8,128)(2,1)} %bitcast.11, bf16[2048,768]{1,0:T(8,128)(2,1)} %copy-done.27, bf16[2048,768]{1,0:T(8,128)(2,1)} %bitcast.14, ...), custom_call_target="tpu_custom_call" | custom-call | flops 4831838208 | bytes 1048576 | tf_op jit(solution)/shard_map/pallas_call | solution.py:151
  198.1 4.0 %shard_map.117 = bf16[256,2048]{1,0:T(8,128)(2,1)} custom-call(bf16[8,96,128]{2,1,0:T(8,128)(2,1)} %copy-done.3, bf16[8,96,128]{2,1,0:T(8,128)(2,1)} %copy-done.3, bf16[8,96,2048]{2,1,0:T(8,128)(2,1)} %copy-done, bf16[8,96,2048]{2,1,0:T(8,128)(2,1)} %shard_map.115.refs_3_.refs_1_, bf16[128,2048]{1,0:T(8,128)(2,1)} %collective-permute-done.16.refs_4_), custom_call_target="tpu_custom_call" | custom-call | tf_op jit(solution)/shard_map/pallas_call | solution.py:272
  203.2 4.0 %shard_map.120 = bf16[256,2048]{1,0:T(8,128)(2,1)} custom-call(bf16[8,96,128]{2,1,0:T(8,128)(2,1)} %copy-done.3, bf16[8,96,128]{2,1,0:T(8,128)(2,1)} %copy-done.3, bf16[8,96,2048]{2,1,0:T(8,128)(2,1)} %copy-done, bf16[8,96,2048]{2,1,0:T(8,128)(2,1)} %shard_map.115.refs_3_.refs_1_, bf16[128,2048]{1,0:T(8,128)(2,1)} %copy-done.37), custom_call_target="tpu_custom_call" | custom-call | tf_op jit(solution)/shard_map/pallas_call | solution.py:272
  209.0 13.6 %collective-permute-done.17.refs_4_.refs_5_ = bf16[256,2048]{1,0:T(8,128)(2,1)S(1)} collective-permute-done((bf16[256,2048]{1,0:T(8,128)(2,1)}, bf16[256,2048]{1,0:T(8,128)(2,1)S(1)}, u32[]{:S(2)}, u32[]{:S(2)}) %collective-permute-start.17) | collective-permute-done | bytes 1048608 | tf_op jit(solution)/shard_map/ppermute | solution.py:95
  223.6 4.1 %shard_map.118 = bf16[256,2048]{1,0:T(8,128)(2,1)} custom-call(bf16[8,96,128]{2,1,0:T(8,128)(2,1)} %copy-done.3, bf16[8,96,128]{2,1,0:T(8,128)(2,1)} %copy-done.3, bf16[8,96,2048]{2,1,0:T(8,128)(2,1)} %copy-done, bf16[8,96,2048]{2,1,0:T(8,128)(2,1)} %shard_map.115.refs_3_.refs_1_, bf16[256,2048]{1,0:T(8,128)(2,1)} %copy-done.30, bf16[256,2048]{1,0:T(8,128)(2,1)} %copy-done.30), custom_call_target="tpu_custom_call" | custom-call | tf_op jit(solution)/shard_map/pallas_call | solution.py:272
  229.0 3.7 %shard_map.123 = bf16[128,2048]{1,0:T(8,128)(2,1)} custom-call(bf16[8,96,128]{2,1,0:T(8,128)(2,1)} %copy-done.3, bf16[8,96,2048]{2,1,0:T(8,128)(2,1)} %shard_map.115.refs_3_.refs_1_, bf16[256,2048]{1,0:T(8,128)(2,1)} %copy-done.32), custom_call_target="tpu_custom_call" | custom-call | tf_op jit(solution)/shard_map/pallas_call | solution.py:272
  232.7 1.7 collective-permute-start.22
  234.4 7.7 %collective-permute-done.22.refs_2_ = bf16[128,2048]{1,0:T(8,128)(2,1)S(1)} collective-permute-done((bf16[128,2048]{1,0:T(8,128)(2,1)}, bf16[128,2048]{1,0:T(8,128)(2,1)S(1)}, u32[]{:S(2)}, u32[]{:S(2)}) %collective-permute-start.22) | collective-permute-done | bytes 524320 | tf_op jit(solution)/shard_map/ppermute | solution.py:95
  242.9 3.7 %shard_map.124 = bf16[128,2048]{1,0:T(8,128)(2,1)} custom-call(bf16[8,96,128]{2,1,0:T(8,128)(2,1)} %copy-done.3, bf16[8,96,2048]{2,1,0:T(8,128)(2,1)} %shard_map.115.refs_3_.refs_1_, bf16[128,2048]{1,0:T(8,128)(2,1)} %copy-done.39), custom_call_target="tpu_custom_call" | custom-call | tf_op jit(solution)/shard_map/pallas_call | solution.py:272
  246.5 1.7 collective-permute-start.23
  249.2 3.7 %shard_map.122 = bf16[128,2048]{1,0:T(8,128)(2,1)} custom-call(bf16[8,96,128]{2,1,0:T(8,128)(2,1)} %copy-done.3, bf16[8,96,2048]{2,1,0:T(8,128)(2,1)} %shard_map.115.refs_3_.refs_1_, bf16[256,2048]{1,0:T(8,128)(2,1)} %copy-done.33), custom_call_target="tpu_custom_call" | custom-call | tf_op jit(solution)/shard_map/pallas_call | solution.py:272
  253.2 3.4 %collective-permute-done.23.refs_2_ = bf16[128,2048]{1,0:T(8,128)(2,1)S(1)} collective-permute-done((bf16[128,2048]{1,0:T(8,128)(2,1)}, bf16[128,2048]{1,0:T(8,128)(2,1)S(1)}, u32[]{:S(2)}, u32[]{:S(2)}) %collective-permute-start.23) | collective-permute-done | bytes 524320 | tf_op jit(solution)/shard_map/ppermute | solution.py:95
  257.4 3.7 %shard_map.125 = bf16[128,2048]{1,0:T(8,128)(2,1)} custom-call(bf16[8,96,128]{2,1,0:T(8,128)(2,1)} %copy-done.3, bf16[8,96,2048]{2,1,0:T(8,128)(2,1)} %shard_map.115.refs_3_.refs_1_, bf16[128,2048]{1,0:T(8,128)(2,1)} %copy-done.38), custom_call_target="tpu_custom_call" | custom-call | tf_op jit(solution)/shard_map/pallas_call | solution.py:272
  261.1 1.7 collective-permute-start.24
  262.8 3.3 %all-to-all-start.1 = ((f32[8,2,128]{2,1,0:T(2,128)}), f32[8,2,128]{2,1,0:T(2,128)S(1)}, u32[]{:S(2)}, u32[]{:S(2)}) async-start(f32[8,2,128]{2,1,0:T(2,128)} %get-tuple-element.30.refs_3_), calls=%async_computation.1 | async-start | bytes 16384 | tf_op jit(solution)/shard_map/all_to_all | solution.py:558
  266.2 6.4 %all-to-all-done.1 = f32[8,2,128]{2,1,0:T(2,128)S(1)} async-done(((f32[8,2,128]{2,1,0:T(2,128)}), f32[8,2,128]{2,1,0:T(2,128)S(1)}, u32[]{:S(2)}, u32[]{:S(2)}) %all-to-all-start.1) | async-done | bytes 8224 | tf_op jit(solution)/shard_map/all_to_all | solution.py:558
  273.3 3.8 %shard_map.121 = bf16[128,2048]{1,0:T(8,128)(2,1)} custom-call(bf16[8,96,128]{2,1,0:T(8,128)(2,1)} %copy-done.3, bf16[8,96,2048]{2,1,0:T(8,128)(2,1)} %copy-done, bf16[256,2048]{1,0:T(8,128)(2,1)} %copy-done.33, bf16[256,2048]{1,0:T(8,128)(2,1)} %copy-done.32), custom_call_target="tpu_custom_call" | custom-call | tf_op jit(solution)/shard_map/pallas_call | solution.py:272
  278.7 3.8 %shard_map.126 = bf16[128,2048]{1,0:T(8,128)(2,1)} custom-call(bf16[8,96,128]{2,1,0:T(8,128)(2,1)} %copy-done.3, bf16[8,96,2048]{2,1,0:T(8,128)(2,1)} %shard_map.115.refs_3_.refs_1_, bf16[128,2048]{1,0:T(8,128)(2,1)} %copy-done.35, bf16[128,2048]{1,0:T(8,128)(2,1)} %copy-done.36), custom_call_target="tpu_custom_call" | custom-call | tf_op jit(solution)/shard_map/pallas_call | solution.py:272
  (135 shorter events, 45.6 us)
Async XLA Ops:
  0.6 20.0 %collective-permute-start.1 = (bf16[2048,768]{1,0:T(8,128)(2,1)}, bf16[2048,768]{1,0:T(8,128)(2,1)S(1)}, u32[]{:S(2)}, u32[]{:S(2)}) collective-permute-start(bf16[2048,768]{1,0:T(8,128)(2,1)} %bitcast.9), channel_id=1, source_target_pairs={{0,8},{8,0},{1,9},{9,1},{2,10},{10,2},{3,11},{11,3},{4,12},{12,4},... | collective-permute-start | bytes 9437192 | tf_op jit(solution)/shard_map/ppermute | solution.py:485
  1.1 20.3 %collective-permute-start.2 = (bf16[2048,768]{1,0:T(8,128)(2,1)}, bf16[2048,768]{1,0:T(8,128)(2,1)}, u32[]{:S(2)}, u32[]{:S(2)}) collective-permute-start(bf16[2048,768]{1,0:T(8,128)(2,1)} %bitcast.12), channel_id=1, source_target_pairs={{0,8},{8,0},{1,9},{9,1},{2,10},{10,2},{3,11},{11,3},{4,12},{12,4},... | collective-permute-start | bytes 9437192 | tf_op jit(solution)/shard_map/ppermute | solution.py:485
  1.2 19.4 %collective-permute-start.5 = (bf16[128,2048]{1,0:T(8,128)(2,1)}, bf16[128,2048]{1,0:T(8,128)(2,1)S(1)}, u32[]{:S(2)}, u32[]{:S(2)}) collective-permute-start(bf16[128,2048]{1,0:T(8,128)(2,1)} %refs_1_.4), channel_id=1, source_target_pairs={{0,2},{2,4},{4,6},{6,7},{7,5},{5,3},{3,1},{1,0},{8,10},{10,12},{12... | collective-permute-start | bytes 1572872 | tf_op jit(solution)/shard_map/ppermute | solution.py:95
  4.2 23.0 %collective-permute-start = (bf16[128,2048]{1,0:T(8,128)(2,1)}, bf16[128,2048]{1,0:T(8,128)(2,1)}, u32[]{:S(2)}, u32[]{:S(2)}) collective-permute-start(bf16[128,2048]{1,0:T(8,128)(2,1)} %refs_1_.4), channel_id=1, source_target_pairs={{0,1},{2,0},{4,2},{6,4},{7,6},{5,7},{3,5},{1,3},{8,9},{10,8},{12,1... | collective-permute-start | bytes 1572872 | tf_op jit(solution)/shard_map/ppermute | solution.py:95
  21.4 1.7 copy-start.27
  26.6 23.8 %collective-permute-start.6 = (bf16[256,2048]{1,0:T(8,128)(2,1)}, bf16[256,2048]{1,0:T(8,128)(2,1)S(1)}, u32[]{:S(2)}, u32[]{:S(2)}) collective-permute-start(bf16[256,2048]{1,0:T(8,128)(2,1)} %shard_map.100), channel_id=1, source_target_pairs={{0,2},{2,4},{4,6},{6,7},{7,5},{5,3},{3,1},{1,0},{8,10},{10,12},{12... | collective-permute-start | bytes 3145736 | tf_op jit(solution)/shard_map/ppermute | solution.py:95
  30.7 45.8 %copy-start.15 = (f32[8,8,128]{2,1,0:T(8,128)S(1)}, f32[8,8,128]{2,1,0:T(8,128)}, u32[]{:S(2)}) copy-start(f32[8,8,128]{2,1,0:T(8,128)} %all_to_all.10.refs_1_.refs_2_) | copy-start | bytes 98308
  30.7 23.9 %collective-permute-start.3 = (bf16[256,2048]{1,0:T(8,128)(2,1)}, bf16[256,2048]{1,0:T(8,128)(2,1)S(1)}, u32[]{:S(2)}, u32[]{:S(2)}) collective-permute-start(bf16[256,2048]{1,0:T(8,128)(2,1)} %shard_map.97), channel_id=1, source_target_pairs={{0,1},{2,0},{4,2},{6,4},{7,6},{5,7},{3,5},{1,3},{8,9},{10,8},{12,1... | collective-permute-start | bytes 3145736 | tf_op jit(solution)/shard_map/ppermute | solution.py:95
  32.1 90.5 %collective-permute-start.9 = (bf16[768,2048]{1,0:T(8,128)(2,1)}, bf16[768,2048]{1,0:T(8,128)(2,1)}, u32[]{:S(2)}, u32[]{:S(2)}) collective-permute-start(bf16[768,2048]{1,0:T(8,128)(2,1)} %bitcast.5.refs_1_.refs_13_), channel_id=1, source_target_pairs={{0,8},{8,0},{1,9},{9,1},{2,10},{10,2},{3,11},{11,3},{4,12},{12,4},... | collective-permute-start | bytes 9437192 | tf_op jit(solution)/shard_map/ppermute | solution.py:485
  50.4 35.1 %copy-start.31 = (bf16[256,2048]{1,0:T(8,128)(2,1)}, bf16[256,2048]{1,0:T(8,128)(2,1)S(1)}, u32[]{:S(2)}) copy-start(bf16[256,2048]{1,0:T(8,128)(2,1)S(1)} %collective-permute-done.6.refs_2_.refs_3_) | copy-start | bytes 3145732
  50.4 22.7 %collective-permute-start.7 = (bf16[256,2048]{1,0:T(8,128)(2,1)S(1)}, bf16[256,2048]{1,0:T(8,128)(2,1)S(1)}, u32[]{:S(2)}, u32[]{:S(2)}) collective-permute-start(bf16[256,2048]{1,0:T(8,128)(2,1)S(1)} %collective-permute-done.6.refs_2_.refs_3_), channel_id=1, source_target_pairs={{0,2},{2,4},{4,6},{6,7},{7,5},{5,3},{3,1},{1,0},{8,10},{10,12},{12... | collective-permute-start | bytes 3145736 | tf_op jit(solution)/shard_map/ppermute | solution.py:95
  54.6 31.0 %copy-start.29 = (bf16[256,2048]{1,0:T(8,128)(2,1)}, bf16[256,2048]{1,0:T(8,128)(2,1)S(1)}, u32[]{:S(2)}) copy-start(bf16[256,2048]{1,0:T(8,128)(2,1)S(1)} %collective-permute-done.3.refs_2_.refs_3_) | copy-start | bytes 3145732
  55.6 14.9 %collective-permute-start.10 = (bf16[128,2048]{1,0:T(8,128)(2,1)S(1)}, bf16[128,2048]{1,0:T(8,128)(2,1)S(1)}, u32[]{:S(2)}, u32[]{:S(2)}) collective-permute-start(bf16[128,2048]{1,0:T(8,128)(2,1)S(1)} %get-tuple-element.33), channel_id=1, source_target_pairs={{0,1},{2,0},{4,2},{6,4},{7,6},{5,7},{3,5},{1,3},{8,9},{10,8},{12,1... | collective-permute-start | bytes 1572872 | tf_op jit(solution)/shard_map/ppermute | solution.py:95
  56.7 39.9 %collective-permute-start.4 = (bf16[128,2048]{1,0:T(8,128)(2,1)}, bf16[128,2048]{1,0:T(8,128)(2,1)}, u32[]{:S(2)}, u32[]{:S(2)}) collective-permute-start(bf16[128,2048]{1,0:T(8,128)(2,1)} %get-tuple-element.34), channel_id=1, source_target_pairs={{0,1},{2,0},{4,2},{6,4},{7,6},{5,7},{3,5},{1,3},{8,9},{10,8},{12,1... | collective-permute-start | bytes 1572872 | tf_op jit(solution)/shard_map/ppermute | solution.py:95
  70.4 52.2 %copy-start.40 = (bf16[128,2048]{1,0:T(8,128)(2,1)}, bf16[128,2048]{1,0:T(8,128)(2,1)S(1)}, u32[]{:S(2)}) copy-start(bf16[128,2048]{1,0:T(8,128)(2,1)S(1)} %collective-permute-done.10.refs_1_) | copy-start | bytes 1572868
  70.4 29.7 %collective-permute-start.11 = (bf16[128,2048]{1,0:T(8,128)(2,1)S(1)}, bf16[128,2048]{1,0:T(8,128)(2,1)}, u32[]{:S(2)}, u32[]{:S(2)}) collective-permute-start(bf16[128,2048]{1,0:T(8,128)(2,1)S(1)} %collective-permute-done.10.refs_1_), channel_id=1, source_target_pairs={{0,1},{2,0},{4,2},{6,4},{7,6},{5,7},{3,5},{1,3},{8,9},{10,8},{12,1... | collective-permute-start | bytes 1572872 | tf_op jit(solution)/shard_map/ppermute | solution.py:95
  75.2 30.6 %collective-permute-start.8 = (bf16[128,2048]{1,0:T(8,128)(2,1)}, bf16[128,2048]{1,0:T(8,128)(2,1)S(1)}, u32[]{:S(2)}, u32[]{:S(2)}) collective-permute-start(bf16[128,2048]{1,0:T(8,128)(2,1)} %get-tuple-element.32), channel_id=1, source_target_pairs={{0,2},{2,4},{4,6},{6,7},{7,5},{5,3},{3,1},{1,0},{8,10},{10,12},{12... | collective-permute-start | bytes 1572872 | tf_op jit(solution)/shard_map/ppermute | solution.py:95
  92.7 17.3 %copy-start.16 = (bf16[96,2048]{1,0:T(8,128)(2,1)S(1)}, bf16[96,2048]{1,0:T(8,128)(2,1)}, u32[]{:S(2)}) copy-start(bf16[96,2048]{1,0:T(8,128)(2,1)} %shard_map.95.refs_0_) | copy-start | bytes 1179652
  92.7 17.3 %copy-start.17 = (bf16[96,2048]{1,0:T(8,128)(2,1)S(1)}, bf16[96,2048]{1,0:T(8,128)(2,1)}, u32[]{:S(2)}) copy-start(bf16[96,2048]{1,0:T(8,128)(2,1)} %shard_map.96.refs_1_) | copy-start | bytes 1179652
  92.7 17.3 %copy-start.18 = (bf16[96,2048]{1,0:T(8,128)(2,1)S(1)}, bf16[96,2048]{1,0:T(8,128)(2,1)}, u32[]{:S(2)}) copy-start(bf16[96,2048]{1,0:T(8,128)(2,1)} %shard_map.104.refs_7_) | copy-start | bytes 1179652
  92.7 17.3 %copy-start.24 = (bf16[96,2048]{1,0:T(8,128)(2,1)S(1)}, bf16[96,2048]{1,0:T(8,128)(2,1)}, u32[]{:S(2)}) copy-start(bf16[96,2048]{1,0:T(8,128)(2,1)} %get-tuple-element.19.refs_2_) | copy-start | bytes 1179652
  96.6 13.5 %copy-start.25 = (bf16[96,2048]{1,0:T(8,128)(2,1)S(1)}, bf16[96,2048]{1,0:T(8,128)(2,1)}, u32[]{:S(2)}) copy-start(bf16[96,2048]{1,0:T(8,128)(2,1)} %get-tuple-element.21.refs_6_) | copy-start | bytes 1179652
  100.1 10.0 %copy-start.19 = (bf16[96,2048]{1,0:T(8,128)(2,1)S(1)}, bf16[96,2048]{1,0:T(8,128)(2,1)}, u32[]{:S(2)}) copy-start(bf16[96,2048]{1,0:T(8,128)(2,1)} %shard_map.99.refs_3_) | copy-start | bytes 1179652
  100.1 48.6 %collective-permute-start.12 = (bf16[128,2048]{1,0:T(8,128)(2,1)}, bf16[128,2048]{1,0:T(8,128)(2,1)}, u32[]{:S(2)}, u32[]{:S(2)}) collective-permute-start(bf16[128,2048]{1,0:T(8,128)(2,1)} %collective-permute-done.11.refs_1_), channel_id=1, source_target_pairs={{0,1},{2,0},{4,2},{6,4},{7,6},{5,7},{3,5},{1,3},{8,9},{10,8},{12,1... | collective-permute-start | bytes 1572872 | tf_op jit(solution)/shard_map/ppermute | solution.py:95
  100.9 51.2 %collective-permute-start.13 = (bf16[128,2048]{1,0:T(8,128)(2,1)}, bf16[128,2048]{1,0:T(8,128)(2,1)}, u32[]{:S(2)}, u32[]{:S(2)}) collective-permute-start(bf16[128,2048]{1,0:T(8,128)(2,1)} %get-tuple-element.31), channel_id=1, source_target_pairs={{0,2},{2,4},{4,6},{6,7},{7,5},{5,3},{3,1},{1,0},{8,10},{10,12},{12... | collective-permute-start | bytes 1572872 | tf_op jit(solution)/shard_map/ppermute | solution.py:95
  127.3 1.8 copy-start
  132.6 41.9 %collective-permute-start.14 = (bf16[128,2048]{1,0:T(8,128)(2,1)}, bf16[128,2048]{1,0:T(8,128)(2,1)S(1)}, u32[]{:S(2)}, u32[]{:S(2)}) collective-permute-start(bf16[128,2048]{1,0:T(8,128)(2,1)} %shard_map.113), channel_id=1, source_target_pairs={{0,2},{2,4},{4,6},{6,7},{7,5},{5,3},{3,1},{1,0},{8,10},{10,12},{12... | collective-permute-start | bytes 1572872 | tf_op jit(solution)/shard_map/ppermute | solution.py:95
  136.5 19.1 %copy-start.2 = (bf16[8,96,128]{2,1,0:T(8,128)(2,1)S(1)}, bf16[8,96,128]{2,1,0:T(8,128)(2,1)}, u32[]{:S(2)}) copy-start(bf16[8,96,128]{2,1,0:T(8,128)(2,1)} %copy-done.1) | copy-start | bytes 589828
  136.5 42.8 %collective-permute-start.15 = (bf16[128,2048]{1,0:T(8,128)(2,1)}, bf16[128,2048]{1,0:T(8,128)(2,1)S(1)}, u32[]{:S(2)}, u32[]{:S(2)}) collective-permute-start(bf16[128,2048]{1,0:T(8,128)(2,1)} %shard_map.114), channel_id=1, source_target_pairs={{0,1},{2,0},{4,2},{6,4},{7,6},{5,7},{3,5},{1,3},{8,9},{10,8},{12,1... | collective-permute-start | bytes 1572872 | tf_op jit(solution)/shard_map/ppermute | solution.py:95
  141.7 13.9 %copy-start.8 = (bf16[96,2048]{1,0:T(8,128)(2,1)S(1)}, bf16[96,2048]{1,0:T(8,128)(2,1)}, u32[]{:S(2)}) copy-start(bf16[96,2048]{1,0:T(8,128)(2,1)} %shard_map.107.refs_1_) | copy-start | bytes 1179652
  145.2 10.4 %copy-start.9 = (bf16[96,2048]{1,0:T(8,128)(2,1)S(1)}, bf16[96,2048]{1,0:T(8,128)(2,1)}, u32[]{:S(2)}) copy-start(bf16[96,2048]{1,0:T(8,128)(2,1)} %shard_map.108.refs_3_) | copy-start | bytes 1179652
  173.5 1.1 copy-start.13
  179.0 6.5 %copy-start.5 = (bf16[128,2048]{1,0:T(8,128)(2,1)S(1)}, bf16[128,2048]{1,0:T(8,128)(2,1)}, u32[]{:S(2)}) copy-start(bf16[128,2048]{1,0:T(8,128)(2,1)} %copy-done.4) | copy-start | bytes 1572868
  179.0 19.1 %collective-permute-start.16 = (bf16[128,2048]{1,0:T(8,128)(2,1)}, bf16[128,2048]{1,0:T(8,128)(2,1)}, u32[]{:S(2)}, u32[]{:S(2)}) collective-permute-start(bf16[128,2048]{1,0:T(8,128)(2,1)} %shard_map.116), channel_id=1, source_target_pairs={{0,2},{2,4},{4,6},{6,7},{7,5},{5,3},{3,1},{1,0},{8,10},{10,12},{12... | collective-permute-start | bytes 1572872 | tf_op jit(solution)/shard_map/ppermute | solution.py:95
  183.8 18.7 %collective-permute-start.19 = (bf16[128,2048]{1,0:T(8,128)(2,1)}, bf16[128,2048]{1,0:T(8,128)(2,1)S(1)}, u32[]{:S(2)}, u32[]{:S(2)}) collective-permute-start(bf16[128,2048]{1,0:T(8,128)(2,1)} %shard_map.119), channel_id=1, source_target_pairs={{0,1},{2,0},{4,2},{6,4},{7,6},{5,7},{3,5},{1,3},{8,9},{10,8},{12,1... | collective-permute-start | bytes 1572872 | tf_op jit(solution)/shard_map/ppermute | solution.py:95
  185.5 1.0 copy-start.7
  186.5 1.3 copy-start.14
  202.1 20.4 %collective-permute-start.17 = (bf16[256,2048]{1,0:T(8,128)(2,1)}, bf16[256,2048]{1,0:T(8,128)(2,1)S(1)}, u32[]{:S(2)}, u32[]{:S(2)}) collective-permute-start(bf16[256,2048]{1,0:T(8,128)(2,1)} %shard_map.117), channel_id=1, source_target_pairs={{0,2},{2,4},{4,6},{6,7},{7,5},{5,3},{3,1},{1,0},{8,10},{10,12},{12... | collective-permute-start | bytes 3145736 | tf_op jit(solution)/shard_map/ppermute | solution.py:95
  207.2 20.8 %collective-permute-start.20 = (bf16[256,2048]{1,0:T(8,128)(2,1)}, bf16[256,2048]{1,0:T(8,128)(2,1)S(1)}, u32[]{:S(2)}, u32[]{:S(2)}) collective-permute-start(bf16[256,2048]{1,0:T(8,128)(2,1)} %shard_map.120), channel_id=1, source_target_pairs={{0,1},{2,0},{4,2},{6,4},{7,6},{5,7},{3,5},{1,3},{8,9},{10,8},{12,1... | collective-permute-start | bytes 3145736 | tf_op jit(solution)/shard_map/ppermute | solution.py:95
  222.6 1.0 copy-start.30
  227.7 20.6 %collective-permute-start.18 = (bf16[256,2048]{1,0:T(8,128)(2,1)}, bf16[256,2048]{1,0:T(8,128)(2,1)S(1)}, u32[]{:S(2)}, u32[]{:S(2)}) collective-permute-start(bf16[256,2048]{1,0:T(8,128)(2,1)} %shard_map.118), channel_id=1, source_target_pairs={{0,2},{2,4},{4,6},{6,7},{7,5},{5,3},{3,1},{1,0},{8,10},{10,12},{12... | collective-permute-start | bytes 3145736 | tf_op jit(solution)/shard_map/ppermute | solution.py:95
  228.0 1.0 copy-start.32
  232.7 9.4 %collective-permute-start.22 = (bf16[128,2048]{1,0:T(8,128)(2,1)}, bf16[128,2048]{1,0:T(8,128)(2,1)S(1)}, u32[]{:S(2)}, u32[]{:S(2)}) collective-permute-start(bf16[128,2048]{1,0:T(8,128)(2,1)} %shard_map.123), channel_id=1, source_target_pairs={{0,1},{2,0},{4,2},{6,4},{7,6},{5,7},{3,5},{1,3},{8,9},{10,8},{12,1... | collective-permute-start | bytes 1572872 | tf_op jit(solution)/shard_map/ppermute | solution.py:95
  246.5 10.0 %collective-permute-start.23 = (bf16[128,2048]{1,0:T(8,128)(2,1)}, bf16[128,2048]{1,0:T(8,128)(2,1)S(1)}, u32[]{:S(2)}, u32[]{:S(2)}) collective-permute-start(bf16[128,2048]{1,0:T(8,128)(2,1)} %shard_map.124), channel_id=1, source_target_pairs={{0,1},{2,0},{4,2},{6,4},{7,6},{5,7},{3,5},{1,3},{8,9},{10,8},{12,1... | collective-permute-start | bytes 1572872 | tf_op jit(solution)/shard_map/ppermute | solution.py:95
  252.9 19.7 %copy-start.42 = (s32[128,4]{0,1:T(4,128)S(1)}, s32[128,4]{0,1:T(4,128)}, u32[]{:S(2)}) copy-start(s32[128,4]{0,1:T(4,128)} %param.9) | copy-start | bytes 6148
  252.9 24.2 %collective-permute-start.21 = (bf16[128,2048]{1,0:T(8,128)(2,1)}, bf16[128,2048]{1,0:T(8,128)(2,1)S(1)}, u32[]{:S(2)}, u32[]{:S(2)}) collective-permute-start(bf16[128,2048]{1,0:T(8,128)(2,1)} %shard_map.122), channel_id=1, source_target_pairs={{0,2},{2,4},{4,6},{6,7},{7,5},{5,3},{3,1},{1,0},{8,10},{10,12},{12... | collective-permute-start | bytes 1572872 | tf_op jit(solution)/shard_map/ppermute | solution.py:95
  261.1 16.0 %collective-permute-start.24 = (bf16[128,2048]{1,0:T(8,128)(2,1)}, bf16[128,2048]{1,0:T(8,128)(2,1)S(1)}, u32[]{:S(2)}, u32[]{:S(2)}) collective-permute-start(bf16[128,2048]{1,0:T(8,128)(2,1)} %shard_map.125), channel_id=1, source_target_pairs={{0,1},{2,0},{4,2},{6,4},{7,6},{5,7},{3,5},{1,3},{8,9},{10,8},{12,1... | collective-permute-start | bytes 1572872 | tf_op jit(solution)/shard_map/ppermute | solution.py:95
  262.8 9.8 %all-to-all-start.1 = ((f32[8,2,128]{2,1,0:T(2,128)}), f32[8,2,128]{2,1,0:T(2,128)S(1)}, u32[]{:S(2)}, u32[]{:S(2)}) async-start(f32[8,2,128]{2,1,0:T(2,128)} %get-tuple-element.30.refs_3_), calls=%async_computation.1 | async-start | bytes 16384 | tf_op jit(solution)/shard_map/all_to_all | solution.py:558
  (21 other events, 18.5 us)

commit v7 on v4

--- a/solution.py
+++ b/solution.py
@@ -95,41 +95,47 @@
     return lax.ppermute(array, "ep", pairs)
 
 
-def ring_gather(shard, count, far_step, behind={}):
-    held = {0: shard}
-    arrivals = {}
-    for step in (far_step, -far_step):
-        hops = count // 2 if step == far_step else (count - 1) // 2
-        moving = shard
-        arrivals[step] = []
-        for hop in range(1, hops + 1):
-            if (step, hop) in behind:
-                moving = held_back(moving, behind[step, hop])
-                if hop > 1:
-                    held[(-step * (hop - 1)) % count] = moving
-            moving = ring_shift(moving, count, step)
-            held[(-step * hop) % count] = moving
-            arrivals[step].append(moving)
-    return [held[place] for place in range(count)], arrivals
+def hops_of(count, step, far_step):
+    return count // 2 if step == far_step else (count - 1) // 2
+
+
+def ring_gather(first, second, count, behind, rows_of):
+    rows = first.shape[0]
+    held = [{0: (first, 0)}, {0: (second, 0)}]
+    opening = {step: ring_shift(first, count, step) for step in (1, -1)}
+    joined = dict(zip((1, -1), run_join([opening[1], opening[-1]], second, behind)))
+    for step in (1, -1):
+        hops = hops_of(count, step, 1), hops_of(count, step, -1)
+        low, high = (first, 0), None
+        for stage in range(1, max(hops[0], hops[1] + 1) + 1):
+            if stage == 2:
+                high = (second, 0)
+            one = low if stage <= hops[0] else None
+            two = high if 1 < stage <= hops[1] + 1 else None
+            last = stage >= hops[0]
+            if one and two and not last:
+                both = ring_shift(joined[step] if stage == 2 else one[0], count, step)
+                low, high = (both, 0), (both, rows)
+            else:
+                cuts = [None if v is None else v[0][v[1] : v[1] + rows] for v in (one, two)]
+                if one and two:
+                    cuts[1] = after(cuts[1], rows_of((-step * (stage - 1)) % count, low))
+                if one:
+                    sent = opening[step] if stage == 1 else ring_shift(cuts[0], count, step)
+                    low = (sent, 0)
+                if two:
+                    high = (ring_shift(cuts[1], count, step), 0)
+            if one:
+                held[0][(-step * stage) % count] = low
+            if two:
+                held[1][(-step * (stage - 1)) % count] = high
+    return [[h[place] for place in range(count)] for h in held]
 
 
 def after(array, *others):
     for other in others:
         array = array + other[(slice(0, 1),) * other.ndim].reshape((1,) * array.ndim).astype(array.dtype) * 0
     return array
-
-
-def held_back(array, others):
-    def kernel(*refs):
-        pass
-
-    return pl.pallas_call(
-        kernel,
-        out_shape=jax.ShapeDtypeStruct(array.shape, array.dtype),
-        in_specs=[pl.BlockSpec(memory_space=pl.ANY) for _ in range(1 + len(others))],
-        out_specs=pl.BlockSpec(memory_space=pl.ANY),
-        input_output_aliases={0: 0},
-    )(array, *others)
 
 
 def ring_reduce(share_of, count, far_step, behind={}):
@@ -157,7 +163,7 @@
 
 
 def call_kernel(kernel, operands, kinds, outs, scratch, flops, behind=()):
-    spaces = {"any": pl.ANY, "vmem": pltpu.VMEM, "smem": pltpu.SMEM}
+    spaces = {"any": pltpu.HBM, "vmem": pltpu.VMEM, "smem": pltpu.SMEM}
     count = len(operands)
     operands = [*operands, *behind]
     kinds = [*kinds, *["any" for _ in behind]]
@@ -222,6 +228,21 @@
 
     shape = jax.ShapeDtypeStruct((count, 2 * capacity, tokens), bf16)
     return call_kernel(kernel, [ids, tables], ["smem", "vmem"], [shape, shape], [], 1 << 20)
+
+
+def run_join(uppers, lower, behind):
+    rows, width = lower.shape
+    count = len(uppers)
+
+    def kernel(*refs):
+        for upper_ref, out_ref in zip(refs[:count], refs[count + 1 :]):
+            out_ref[:rows, :] = upper_ref[...]
+            out_ref[rows:, :] = refs[count][...]
+
+    shape = jax.ShapeDtypeStruct((2 * rows, width), lower.dtype)
+    return call_kernel(
+        kernel, [*uppers, lower], ["vmem"] * (count + 1), [shape] * count, [], 1, behind
+    )
 
 
 def run_hidden(parts, gate_mats, up_mats):
@@ -438,19 +459,22 @@
     tables = lax.all_to_all(copies, "ep", split_axis=0, concat_axis=0, tiled=True)
     pick, spread = run_routing(ids, tables, top_count, capacity)
 
-    behind = {(step, 2): (tables,) for step in (1, -1)}
-    in_shards, in_hops = ring_gather(tokens, chips, 1, behind)
-    behind = {(step, 1): (in_hops[step][0],) for step in (1, -1)}
-    grad_shards, _ = ring_gather(cotangent, chips, -1, behind)
     gate_mats = (w_gate[0], swap_cores(w_gate[0]))
     up_mats = (w_up[0], swap_cores(w_up[0]))
     down_mats = (w_down[0], swap_cores(w_down[0]))
 
-    def gather_rows(shards):
-        return [
-            jnp.dot(pick[s], shards[s], preferred_element_type=f32).astype(bf16)
-            for s in range(chips)
-        ]
+    def rows_of(s, held):
+        buffer, row = held
+        return jnp.dot(
+            pick[s], buffer[row : row + token_count], preferred_element_type=f32
+        ).astype(bf16)
+
+    def gather_rows(held):
+        return [rows_of(s, at) for s, at in enumerate(held)]
+
+    in_held, grad_held = ring_gather(
+        tokens, cotangent, chips, (tables, gate_mats[1], up_mats[1]), rows_of
+    )
 
     def scatter_rows(blocks):
         def share_of(s, partial, waits=(), add_waits=False):
@@ -465,10 +489,10 @@
 
         return share_of
 
-    rows_in = gather_rows(in_shards)
+    rows_in = gather_rows(in_held)
     hidden, slope, activated = run_hidden(rows_in, gate_mats, up_mats)
     outputs = run_down(hidden, down_mats, chips)
-    rows_grad = gather_rows(grad_shards)
+    rows_grad = gather_rows(grad_held)
     d_pre_gate, d_pre_up, per_token = run_d_hidden(
         ids, rows_grad, outputs, pick, slope, activated, down_mats, ()
     )
@@ -493,7 +517,7 @@
 
 
 def solution(mesh):
-    plan = body_ring if mesh.shape["ep"] <= 8 and mesh.shape["grp"] == 2 else body_exchange
+    plan = body_ring if 4 <= mesh.shape["ep"] <= 8 and mesh.shape["grp"] == 2 else body_exchange
     return jax.shard_map(
         plan,
         mesh=mesh,

time: 221 us -> 227 us (1.027)
  blocking collectives: 0 us -> 15.9 us
  starting transfers between devices: 40.9 us -> 30.1 us
  matrix products: 27.6 us -> 24.8 us
    all_to_all x0 -> x1, blocking collectives: none -> 15.9 us  [body_ring(): lax.all_to_all(copies, 'ep', split_axis=0, concat_axis=0, tiled=True)]
    ppermute x28 -> x25, waiting for transfers between devices: 82 us -> 89.3 us  [ring_shift(): return lax.ppermute(array, 'ep', pairs)]
    all_to_all x1 -> x0, waiting for transfers between devices: 6.91 us -> none  [body_ring(): lax.all_to_all(copies, 'ep', split_axis=0, concat_axis=0, tiled=True)]
    all_to_all x1 -> x0, starting transfers between devices: 6.25 us -> none  [body_ring(): lax.all_to_all(copies, 'ep', split_axis=0, concat_axis=0, tiled=True)]
    ppermute x28 -> x25, starting transfers between devices: 31.3 us -> 25.7 us  [ring_shift(): return lax.ppermute(array, 'ep', pairs)]
    dot_general x16, matrix products: 9.04 us -> 6.19 us  [rows_of(): jnp.dot(pick[s], buffer[row:row + token_count], preferred_element_type=f32)]
    unnamed x26 -> x20, local copies, waits for them, and re-layouts: 6.01 us -> 4.42 us
    pallas_call x5 -> x6, Pallas kernels: 38.1 us -> 39.3 us  [call_kernel(): pl.pallas_call(body, out_shape=outs, in_specs=[pl.BlockSpec(memory_space=...]
  transfers between devices with their start and end apart: 33 -> 29, of which waited for: 18 -> 12; matrix products, arithmetic and copies ran while one was open for 15% -> 14% of each run, Pallas kernels for 17% -> 17%
where the time goes in v7:
time: 227 us; the launch traced here: 226 us
  waiting for transfers between devices  95.8 us (42%)
  Pallas kernels  39.3 us (17%)
  starting transfers between devices  30.1 us (13%)
  matrix products  24.8 us (11%)
  blocking collectives  15.9 us (7%)
  local copies, waits for them, and re-layouts  9.91 us (4%)
  between operations  6.55 us (3%)
  other arithmetic  3.47 us (2%)
    ppermute x25, waiting for transfers between devices, ring_shift(): return lax.ppermute(array, 'ep', pairs)  89.3 us
    pallas_call x6, Pallas kernels, call_kernel(): pl.pallas_call(body, out_shape=outs, in_specs=[pl.BlockSpec(memory_space=...  39.3 us
    ppermute x25, starting transfers between devices, ring_shift(): return lax.ppermute(array, 'ep', pairs)  25.7 us
    dot_general x16, matrix products, share_of(): lax.dot_general(spread[s], blocks[s], (((0,), (0,)), ((), ())), preferred...  18.6 us
    all_to_all x1, blocking collectives, body_ring(): lax.all_to_all(copies, 'ep', split_axis=0, concat_axis=0, tiled=True)  15.9 us
    all_to_all x1, waiting for transfers between devices, body_ring(): lax.all_to_all(per_token, 'ep', split_axis=0, concat_axis=0, tiled=True)  6.51 us
    dot_general x16, matrix products, rows_of(): jnp.dot(pick[s], buffer[row:row + token_count], preferred_element_type=f32)  6.19 us
    slice x8, local copies, waits for them, and re-layouts, after(): other[(slice(0, 1),) * other.ndim].reshape((1,) * array.ndim)  5.47 us
  transfers between devices with their start and end apart: 29, of which 12 were waited for; matrix products, arithmetic and copies ran while one was open for 14% of the time, Pallas kernels for 17%

profile of v7, /device:TPU:0, one launch (start us, length us, event | category | flops | bytes accessed | tf_op | source)
XLA Modules:
  0.0 225.8 jit_solution(8233336624011918306)
XLA Ops:
  1.2 2.9 %collective-permute-start = (bf16[128,2048]{1,0:T(8,128)(2,1)}, bf16[128,2048]{1,0:T(8,128)(2,1)S(1)}, u32[]{:S(2)}, u32[]{:S(2)}) collective-permute-start(bf16[128,2048]{1,0:T(8,128)(2,1)} %param.7), channel_id=1, source_target_pairs={{0,1},{2,0},{4,2},{6,4},{7,6},{5,7},{3,5},{1,3},{8,9},{10,8},{12,1... | collective-permute-start | bytes 1572872 | tf_op jit(solution)/shard_map/ppermute | solution.py:95
  5.6 15.9 %all_to_all.10.refs_1_.refs_3_ = f32[8,8,128]{2,1,0:T(8,128)S(1)} all-to-all(f32[8,8,128]{2,1,0:T(8,128)S(1)} %broadcast_in_dim.10), channel_id=1, replica_groups=mesh['rep'=2,'grp'=2,'ep'=8] {'ep'}, dimensions={0} | all-to-all | bytes 65536 | tf_op jit(solution)/shard_map/all_to_all | solution.py:459
  21.5 1.7 copy-done.5
  23.2 1.7 copy-done.6
  24.9 1.0 copy-done.2
  25.9 1.1 shard_map.95
  28.9 1.6 collective-permute-start.6
  30.8 20.2 %collective-permute-done.4 = bf16[256,2048]{1,0:T(8,128)(2,1)} collective-permute-done((bf16[256,2048]{1,0:T(8,128)(2,1)}, bf16[256,2048]{1,0:T(8,128)(2,1)}, u32[]{:S(2)}, u32[]{:S(2)}) %collective-permute-start.4) | collective-permute-done | bytes 1048608 | tf_op jit(solution)/shard_map/ppermute | solution.py:95
  51.0 1.3 convolution_convert_fusion.17.refs_2_
  53.5 1.3 slice_add_fusion.1
  56.5 1.3 collective-permute-start.7
  58.1 1.3 convolution_convert_fusion.10.refs_2_
  59.4 10.3 %collective-permute-done.11 = bf16[128,2048]{1,0:T(8,128)(2,1)S(1)} collective-permute-done((bf16[128,2048]{1,0:T(8,128)(2,1)S(1)}, bf16[128,2048]{1,0:T(8,128)(2,1)S(1)}, u32[]{:S(2)}, u32[]{:S(2)}) %collective-permute-start.11) | collective-permute-done | bytes 524320 | tf_op jit(solution)/shard_map/ppermute | solution.py:95
  70.9 10.1 %collective-permute-done.5 = bf16[128,2048]{1,0:T(8,128)(2,1)S(1)} collective-permute-done((bf16[128,2048]{1,0:T(8,128)(2,1)S(1)}, bf16[128,2048]{1,0:T(8,128)(2,1)S(1)}, u32[]{:S(2)}, u32[]{:S(2)}) %collective-permute-start.5) | collective-permute-done | bytes 524320 | tf_op jit(solution)/shard_map/ppermute | solution.py:95
  81.2 8.2 %collective-permute-done.12 = bf16[128,2048]{1,0:T(8,128)(2,1)S(1)} collective-permute-done((bf16[128,2048]{1,0:T(8,128)(2,1)S(1)}, bf16[128,2048]{1,0:T(8,128)(2,1)S(1)}, u32[]{:S(2)}, u32[]{:S(2)}) %collective-permute-start.12) | collective-permute-done | bytes 524320 | tf_op jit(solution)/shard_map/ppermute | solution.py:95
  91.5 1.4 collective-permute-start.8
  93.8 6.2 %collective-permute-done.13 = bf16[128,2048]{1,0:T(8,128)(2,1)S(1)} collective-permute-done((bf16[128,2048]{1,0:T(8,128)(2,1)S(1)}, bf16[128,2048]{1,0:T(8,128)(2,1)S(1)}, u32[]{:S(2)}, u32[]{:S(2)}) %collective-permute-start.13) | collective-permute-done | bytes 524320 | tf_op jit(solution)/shard_map/ppermute | solution.py:95
  100.3 6.2 %collective-permute-done.8 = bf16[128,2048]{1,0:T(8,128)(2,1)S(1)} collective-permute-done((bf16[128,2048]{1,0:T(8,128)(2,1)S(1)}, bf16[128,2048]{1,0:T(8,128)(2,1)S(1)}, u32[]{:S(2)}, u32[]{:S(2)}) %collective-permute-start.8) | collective-permute-done | bytes 524320 | tf_op jit(solution)/shard_map/ppermute | solution.py:95
  106.7 10.5 %shard_map.96 = (bf16[2,384,768]{2,1,0:T(8,128)(2,1)S(1)}, f32[2,384,768]{2,1,0:T(8,128)}, f32[2,384,768]{2,1,0:T(8,128)}) custom-call(bf16[96,2048]{1,0:T(8,128)(2,1)S(1)} %convolution_convert_fusion.19.refs_0_, bf16[96,2048]{1,0:T(8,128)(2,1)S(1)} %convolution_convert_fusion.18.refs_1_, bf16[96,2048]{1,0:T(8,128)(2,1)S(1)} %convolution_convert_fusion.17.refs_2_, ...), custom_call_target="tpu_custom_call" | custom-call | flops 4831838208 | bytes 1048576 | tf_op jit(solution)/shard_map/pallas_call | solution.py:174
  117.2 4.7 %shard_map.97.refs_9_ = bf16[8,96,2048]{2,1,0:T(8,128)(2,1)S(1)} custom-call(bf16[2,384,768]{2,1,0:T(8,128)(2,1)S(1)} %get-tuple-element.17.refs_0_, bf16[768,2048]{1,0:T(8,128)(2,1)} %bitcast.14.refs_1_.refs_13_, bf16[768,2048]{1,0:T(8,128)(2,1)} %collective-permute-done.9.refs_2_.refs_14_), custom_call_target="tpu_custom_call" | custom-call | flops 2415919104 | bytes 1048576 | tf_op jit(solution)/shard_map/pallas_call | solution.py:174
  123.4 1.6 collective-permute-start.10
  125.2 11.9 %shard_map.98 = (bf16[2,384,768]{2,1,0:T(8,128)(2,1)S(1)}, bf16[2,384,768]{2,1,0:T(8,128)(2,1)S(1)}, f32[8,2,128]{2,1,0:T(2,128)}) custom-call(s32[2]{0:T(128)S(1)} %pad_add_fusion.1.refs_0_, bf16[96,2048]{1,0:T(8,128)(2,1)S(1)} %convolution_convert_fusion.11.refs_1_, bf16[96,2048]{1,0:T(8,128)(2,1)S(1)} %convolution_convert_fusion.10.refs_2_, ...), custom_call_target="tpu_custom_call" | custom-call | flops 2415919104 | bytes 1048576 | tf_op jit(solution)/shard_map/pallas_call | solution.py:174
  137.1 1.2 slice.223
  139.0 1.3 fusion.19
  141.0 1.3 fusion.20
  142.4 1.4 collective-permute-start.15
  143.7 10.4 %shard_map.99 = bf16[8,96,2048]{2,1,0:T(8,128)(2,1)} custom-call(bf16[2,384,768]{2,1,0:T(8,128)(2,1)S(1)} %get-tuple-element.21.refs_0_, bf16[2,384,768]{2,1,0:T(8,128)(2,1)S(1)} %get-tuple-element.22.refs_1_, bf16[2048,768]{1,0:T(8,128)(2,1)} %bitcast.157, bf16[2048,768]{1,0:T(8,128)(2,1)} %copy-done.5, bf16[2048,768]{1,0:T(8,128)(2,1)} %bitcast.160, ...), custom_call_target="tpu_custom_call" | custom-call | flops 4831838208 | bytes 1048576 | tf_op jit(solution)/shard_map/pallas_call | solution.py:174
  156.6 1.3 fusion.14
  158.7 1.7 collective-permute-start.16
  161.9 1.4 collective-permute-start.25
  163.3 4.3 %collective-permute-done.20 = bf16[128,2048]{1,0:T(8,128)(2,1)S(1)} collective-permute-done((bf16[128,2048]{1,0:T(8,128)(2,1)S(1)}, bf16[128,2048]{1,0:T(8,128)(2,1)S(1)}, u32[]{:S(2)}, u32[]{:S(2)}) %collective-permute-start.20) | collective-permute-done | bytes 524320 | tf_op jit(solution)/shard_map/ppermute | solution.py:95
  168.9 8.7 %collective-permute-done.21 = bf16[128,2048]{1,0:T(8,128)(2,1)S(1)} collective-permute-done((bf16[128,2048]{1,0:T(8,128)(2,1)S(1)}, bf16[128,2048]{1,0:T(8,128)(2,1)S(1)}, u32[]{:S(2)}, u32[]{:S(2)}) %collective-permute-start.21) | collective-permute-done | bytes 524320 | tf_op jit(solution)/shard_map/ppermute | solution.py:95
  179.9 1.1 fusion.3
  181.0 1.3 collective-permute-start.17
  182.3 1.1 fusion.16
  183.4 1.4 collective-permute-start.26
  184.8 6.8 %collective-permute-done.22 = bf16[128,2048]{1,0:T(8,128)(2,1)S(1)} collective-permute-done((bf16[128,2048]{1,0:T(8,128)(2,1)S(1)}, bf16[128,2048]{1,0:T(8,128)(2,1)S(1)}, u32[]{:S(2)}, u32[]{:S(2)}) %collective-permute-start.22) | collective-permute-done | bytes 524320 | tf_op jit(solution)/shard_map/ppermute | solution.py:95
  191.6 1.1 fusion.10
  193.4 1.2 slice.239
  195.2 6.8 %collective-permute-done.26 = bf16[128,2048]{1,0:T(8,128)(2,1)} collective-permute-done((bf16[128,2048]{1,0:T(8,128)(2,1)}, bf16[128,2048]{1,0:T(8,128)(2,1)}, u32[]{:S(2)}, u32[]{:S(2)}) %collective-permute-start.26) | collective-permute-done | bytes 524320 | tf_op jit(solution)/shard_map/ppermute | solution.py:95
  202.0 2.3 %fusion.17 = bf16[128,2048]{1,0:T(8,128)(2,1)} fusion(bf16[128,2048]{1,0:T(8,128)(2,1)} %collective-permute-done.26, bf16[8,96,2048]{2,1,0:T(8,128)(2,1)} %shard_map.99, bf16[]{:T(256)} %bitcast.45, bf16[8,96,128]{2,1,0:T(8,128)(2,1)S(1)} %get-tuple-element.13), kind=kOutput, calls=%fused_computation.49 | convolution fusion | flops 51380224 | bytes 1466880 | tf_op jit(solution)/shard_map/dot_general | solution.py:481
  204.3 1.3 collective-permute-start.27
  205.6 1.4 collective-permute-done.23
  207.0 2.3 %fusion.9 = bf16[128,2048]{1,0:T(8,128)(2,1)} fusion(bf16[128,2048]{1,0:T(8,128)(2,1)} %collective-permute-done.23, bf16[8,96,2048]{2,1,0:T(8,128)(2,1)} %shard_map.99, bf16[8,96,128]{2,1,0:T(8,128)(2,1)S(1)} %get-tuple-element.13), kind=kOutput, calls=%fused_computation.21 | convolution fusion | flops 51118080 | bytes 1466368 | tf_op jit(solution)/shard_map/dot_general | solution.py:481
  210.0 3.8 %all-to-all-start.1 = ((f32[8,2,128]{2,1,0:T(2,128)}), f32[8,2,128]{2,1,0:T(2,128)S(1)}, u32[]{:S(2)}, u32[]{:S(2)}) async-start(f32[8,2,128]{2,1,0:T(2,128)} %get-tuple-element.20), calls=%async_computation.1 | async-start | bytes 16384 | tf_op jit(solution)/shard_map/all_to_all | solution.py:505
  213.8 6.5 %all-to-all-done.1 = f32[8,2,128]{2,1,0:T(2,128)S(1)} async-done(((f32[8,2,128]{2,1,0:T(2,128)}), f32[8,2,128]{2,1,0:T(2,128)S(1)}, u32[]{:S(2)}, u32[]{:S(2)}) %all-to-all-start.1) | async-done | bytes 8224 | tf_op jit(solution)/shard_map/all_to_all | solution.py:505
  221.0 2.3 %fusion.2 = bf16[128,2048]{1,0:T(8,128)(2,1)} fusion(bf16[128,2048]{1,0:T(8,128)(2,1)} %copy-done.8, bf16[128,2048]{1,0:T(8,128)(2,1)} %collective-permute-done.17, bf16[8,96,2048]{2,1,0:T(8,128)(2,1)S(1)} %copy-done.1, bf16[8,96,128]{2,1,0:T(8,128)(2,1)S(1)} %get-tuple-element.13), kind=kOutput, calls=%fused_computation.14 | convolution fusion | flops 51642368 | bytes 1990656 | tf_op jit(solution)/shard_map/dot_general | solution.py:481
  223.3 2.5 %fusion.8 = bf16[128,2048]{1,0:T(8,128)(2,1)} fusion(bf16[128,2048]{1,0:T(8,128)(2,1)} %collective-permute-done.27, bf16[128,2048]{1,0:T(8,128)(2,1)} %collective-permute-done.24, bf16[8,96,2048]{2,1,0:T(8,128)(2,1)} %shard_map.99, bf16[8,96,128]{2,1,0:T(8,128)(2,1)S(1)} %get-tuple-element.13), kind=kOutput, calls=%fused_computation.20 | convolution fusion | flops 51642368 | bytes 1990656 | tf_op jit(solution)/shard_map/dot_general | solution.py:481
  (88 shorter events, 20.6 us)
Async XLA Ops:
  0.6 20.9 %collective-permute-start.2 = (bf16[2048,768]{1,0:T(8,128)(2,1)}, bf16[2048,768]{1,0:T(8,128)(2,1)S(1)}, u32[]{:S(2)}, u32[]{:S(2)}) collective-permute-start(bf16[2048,768]{1,0:T(8,128)(2,1)} %bitcast.155), channel_id=1, source_target_pairs={{0,8},{8,0},{1,9},{9,1},{2,10},{10,2},{3,11},{11,3},{4,12},{12,4},... | collective-permute-start | bytes 9437192 | tf_op jit(solution)/shard_map/ppermute | solution.py:442
  1.1 20.4 %collective-permute-start.3 = (bf16[2048,768]{1,0:T(8,128)(2,1)}, bf16[2048,768]{1,0:T(8,128)(2,1)S(1)}, u32[]{:S(2)}, u32[]{:S(2)}) collective-permute-start(bf16[2048,768]{1,0:T(8,128)(2,1)} %bitcast.158), channel_id=1, source_target_pairs={{0,8},{8,0},{1,9},{9,1},{2,10},{10,2},{3,11},{11,3},{4,12},{12,4},... | collective-permute-start | bytes 9437192 | tf_op jit(solution)/shard_map/ppermute | solution.py:442
  1.2 20.3 %collective-permute-start = (bf16[128,2048]{1,0:T(8,128)(2,1)}, bf16[128,2048]{1,0:T(8,128)(2,1)S(1)}, u32[]{:S(2)}, u32[]{:S(2)}) collective-permute-start(bf16[128,2048]{1,0:T(8,128)(2,1)} %param.7), channel_id=1, source_target_pairs={{0,1},{2,0},{4,2},{6,4},{7,6},{5,7},{3,5},{1,3},{8,9},{10,8},{12,1... | collective-permute-start | bytes 1572872 | tf_op jit(solution)/shard_map/ppermute | solution.py:95
  4.1 17.4 %collective-permute-start.1 = (bf16[128,2048]{1,0:T(8,128)(2,1)}, bf16[128,2048]{1,0:T(8,128)(2,1)S(1)}, u32[]{:S(2)}, u32[]{:S(2)}) collective-permute-start(bf16[128,2048]{1,0:T(8,128)(2,1)} %param.7), channel_id=1, source_target_pairs={{0,2},{2,4},{4,6},{6,7},{7,5},{5,3},{3,1},{1,0},{8,10},{10,12},{12... | collective-permute-start | bytes 1572872 | tf_op jit(solution)/shard_map/ppermute | solution.py:95
  21.5 1.7 copy-start.5
  23.2 1.7 copy-start.6
  24.9 1.0 copy-start.2
  25.9 2.5 %copy-start.7 = (bf16[128,2048]{1,0:T(8,128)(2,1)S(1)}, bf16[128,2048]{1,0:T(8,128)(2,1)}, u32[]{:S(2)}) copy-start(bf16[128,2048]{1,0:T(8,128)(2,1)} %param.7) | copy-start | bytes 1572868
  25.9 2.7 %copy-start.3 = (bf16[128,2048]{1,0:T(8,128)(2,1)S(1)}, bf16[128,2048]{1,0:T(8,128)(2,1)}, u32[]{:S(2)}) copy-start(bf16[128,2048]{1,0:T(8,128)(2,1)} %refs_2_.1) | copy-start | bytes 1572868
  27.1 24.0 %collective-permute-start.4 = (bf16[256,2048]{1,0:T(8,128)(2,1)}, bf16[256,2048]{1,0:T(8,128)(2,1)}, u32[]{:S(2)}, u32[]{:S(2)}) collective-permute-start(bf16[256,2048]{1,0:T(8,128)(2,1)} %get-tuple-element.15), channel_id=1, source_target_pairs={{0,1},{2,0},{4,2},{6,4},{7,6},{5,7},{3,5},{1,3},{8,9},{10,8},{12,1... | collective-permute-start | bytes 3145736 | tf_op jit(solution)/shard_map/ppermute | solution.py:95
  27.5 89.7 %collective-permute-start.9 = (bf16[768,2048]{1,0:T(8,128)(2,1)}, bf16[768,2048]{1,0:T(8,128)(2,1)}, u32[]{:S(2)}, u32[]{:S(2)}) collective-permute-start(bf16[768,2048]{1,0:T(8,128)(2,1)} %bitcast.14.refs_1_.refs_13_), channel_id=1, source_target_pairs={{0,8},{8,0},{1,9},{9,1},{2,10},{10,2},{3,11},{11,3},{4,12},{12,4},... | collective-permute-start | bytes 9437192 | tf_op jit(solution)/shard_map/ppermute | solution.py:442
  28.9 27.5 %collective-permute-start.6 = (bf16[256,2048]{1,0:T(8,128)(2,1)S(1)}, bf16[256,2048]{1,0:T(8,128)(2,1)S(1)}, u32[]{:S(2)}, u32[]{:S(2)}) collective-permute-start(bf16[256,2048]{1,0:T(8,128)(2,1)S(1)} %get-tuple-element.16), channel_id=1, source_target_pairs={{0,2},{2,4},{4,6},{6,7},{7,5},{5,3},{3,1},{1,0},{8,10},{10,12},{12... | collective-permute-start | bytes 3145736 | tf_op jit(solution)/shard_map/ppermute | solution.py:95
  54.8 14.9 %collective-permute-start.11 = (bf16[128,2048]{1,0:T(8,128)(2,1)S(1)}, bf16[128,2048]{1,0:T(8,128)(2,1)S(1)}, u32[]{:S(2)}, u32[]{:S(2)}) collective-permute-start(bf16[128,2048]{1,0:T(8,128)(2,1)S(1)} %get-tuple-element.25), channel_id=1, source_target_pairs={{0,1},{2,0},{4,2},{6,4},{7,6},{5,7},{3,5},{1,3},{8,9},{10,8},{12,1... | collective-permute-start | bytes 1572872 | tf_op jit(solution)/shard_map/ppermute | solution.py:95
  55.7 25.2 %collective-permute-start.5 = (bf16[128,2048]{1,0:T(8,128)(2,1)S(1)}, bf16[128,2048]{1,0:T(8,128)(2,1)S(1)}, u32[]{:S(2)}, u32[]{:S(2)}) collective-permute-start(bf16[128,2048]{1,0:T(8,128)(2,1)S(1)} %get-tuple-element.26), channel_id=1, source_target_pairs={{0,1},{2,0},{4,2},{6,4},{7,6},{5,7},{3,5},{1,3},{8,9},{10,8},{12,1... | collective-permute-start | bytes 1572872 | tf_op jit(solution)/shard_map/ppermute | solution.py:95
  56.5 33.6 %collective-permute-start.7 = (bf16[256,2048]{1,0:T(8,128)(2,1)S(1)}, bf16[256,2048]{1,0:T(8,128)(2,1)S(1)}, u32[]{:S(2)}, u32[]{:S(2)}) collective-permute-start(bf16[256,2048]{1,0:T(8,128)(2,1)S(1)} %collective-permute-done.6), channel_id=1, source_target_pairs={{0,2},{2,4},{4,6},{6,7},{7,5},{5,3},{3,1},{1,0},{8,10},{10,12},{12... | collective-permute-start | bytes 3145736 | tf_op jit(solution)/shard_map/ppermute | solution.py:95
  69.7 19.7 %collective-permute-start.12 = (bf16[128,2048]{1,0:T(8,128)(2,1)S(1)}, bf16[128,2048]{1,0:T(8,128)(2,1)S(1)}, u32[]{:S(2)}, u32[]{:S(2)}) collective-permute-start(bf16[128,2048]{1,0:T(8,128)(2,1)S(1)} %collective-permute-done.11), channel_id=1, source_target_pairs={{0,1},{2,0},{4,2},{6,4},{7,6},{5,7},{3,5},{1,3},{8,9},{10,8},{12,1... | collective-permute-start | bytes 1572872 | tf_op jit(solution)/shard_map/ppermute | solution.py:95
  89.4 10.6 %collective-permute-start.13 = (bf16[128,2048]{1,0:T(8,128)(2,1)S(1)}, bf16[128,2048]{1,0:T(8,128)(2,1)S(1)}, u32[]{:S(2)}, u32[]{:S(2)}) collective-permute-start(bf16[128,2048]{1,0:T(8,128)(2,1)S(1)} %collective-permute-done.12), channel_id=1, source_target_pairs={{0,1},{2,0},{4,2},{6,4},{7,6},{5,7},{3,5},{1,3},{8,9},{10,8},{12,1... | collective-permute-start | bytes 1572872 | tf_op jit(solution)/shard_map/ppermute | solution.py:95
  91.5 14.9 %collective-permute-start.8 = (bf16[128,2048]{1,0:T(8,128)(2,1)S(1)}, bf16[128,2048]{1,0:T(8,128)(2,1)S(1)}, u32[]{:S(2)}, u32[]{:S(2)}) collective-permute-start(bf16[128,2048]{1,0:T(8,128)(2,1)S(1)} %get-tuple-element.24), channel_id=1, source_target_pairs={{0,2},{2,4},{4,6},{6,7},{7,5},{5,3},{3,1},{1,0},{8,10},{10,12},{12... | collective-permute-start | bytes 1572872 | tf_op jit(solution)/shard_map/ppermute | solution.py:95
  93.2 31.7 %collective-permute-start.14 = (bf16[128,2048]{1,0:T(8,128)(2,1)S(1)}, bf16[128,2048]{1,0:T(8,128)(2,1)S(1)}, u32[]{:S(2)}, u32[]{:S(2)}) collective-permute-start(bf16[128,2048]{1,0:T(8,128)(2,1)S(1)} %get-tuple-element.23), channel_id=1, source_target_pairs={{0,2},{2,4},{4,6},{6,7},{7,5},{5,3},{3,1},{1,0},{8,10},{10,12},{12... | collective-permute-start | bytes 1572872 | tf_op jit(solution)/shard_map/ppermute | solution.py:95
  122.0 3.2 %copy-start = (bf16[8,96,2048]{2,1,0:T(8,128)(2,1)}, bf16[8,96,2048]{2,1,0:T(8,128)(2,1)S(1)}, u32[]{:S(2)}) copy-start(bf16[8,96,2048]{2,1,0:T(8,128)(2,1)S(1)} %shard_map.97.refs_9_) | copy-start | bytes 9437188
  122.3 16.6 %collective-permute-start.18 = (bf16[128,2048]{1,0:T(8,128)(2,1)S(1)}, bf16[128,2048]{1,0:T(8,128)(2,1)S(1)}, u32[]{:S(2)}, u32[]{:S(2)}) collective-permute-start(bf16[128,2048]{1,0:T(8,128)(2,1)S(1)} %convolution_convert_fusion.2), channel_id=1, source_target_pairs={{0,1},{2,0},{4,2},{6,4},{7,6},{5,7},{3,5},{1,3},{8,9},{10,8},{12,1... | collective-permute-start | bytes 1572872 | tf_op jit(solution)/shard_map/ppermute | solution.py:95
  123.4 17.7 %collective-permute-start.10 = (bf16[128,2048]{1,0:T(8,128)(2,1)S(1)}, bf16[128,2048]{1,0:T(8,128)(2,1)S(1)}, u32[]{:S(2)}, u32[]{:S(2)}) collective-permute-start(bf16[128,2048]{1,0:T(8,128)(2,1)S(1)} %convolution_convert_fusion.3), channel_id=1, source_target_pairs={{0,2},{2,4},{4,6},{6,7},{7,5},{5,3},{3,1},{1,0},{8,10},{10,12},{12... | collective-permute-start | bytes 1572872 | tf_op jit(solution)/shard_map/ppermute | solution.py:95
  140.3 13.8 %collective-permute-start.19 = (bf16[128,2048]{1,0:T(8,128)(2,1)S(1)}, bf16[128,2048]{1,0:T(8,128)(2,1)S(1)}, u32[]{:S(2)}, u32[]{:S(2)}) collective-permute-start(bf16[128,2048]{1,0:T(8,128)(2,1)S(1)} %fusion.19), channel_id=1, source_target_pairs={{0,1},{2,0},{4,2},{6,4},{7,6},{5,7},{3,5},{1,3},{8,9},{10,8},{12,1... | collective-permute-start | bytes 1572872 | tf_op jit(solution)/shard_map/ppermute | solution.py:95
  142.4 16.1 %collective-permute-start.15 = (bf16[128,2048]{1,0:T(8,128)(2,1)S(1)}, bf16[128,2048]{1,0:T(8,128)(2,1)S(1)}, u32[]{:S(2)}, u32[]{:S(2)}) collective-permute-start(bf16[128,2048]{1,0:T(8,128)(2,1)S(1)} %fusion.20), channel_id=1, source_target_pairs={{0,2},{2,4},{4,6},{6,7},{7,5},{5,3},{3,1},{1,0},{8,10},{10,12},{12... | collective-permute-start | bytes 1572872 | tf_op jit(solution)/shard_map/ppermute | solution.py:95
  143.7 11.8 %copy-start.1 = (bf16[8,96,2048]{2,1,0:T(8,128)(2,1)S(1)}, bf16[8,96,2048]{2,1,0:T(8,128)(2,1)}, u32[]{:S(2)}) copy-start(bf16[8,96,2048]{2,1,0:T(8,128)(2,1)} %copy-done) | copy-start | bytes 9437188
  154.1 7.5 %copy-start.4 = (bf16[8,96,2048]{2,1,0:T(8,128)(2,1)S(1)}, bf16[8,96,2048]{2,1,0:T(8,128)(2,1)}, u32[]{:S(2)}) copy-start(bf16[8,96,2048]{2,1,0:T(8,128)(2,1)} %shard_map.99) | copy-start | bytes 9437188
  155.9 11.8 %collective-permute-start.20 = (bf16[128,2048]{1,0:T(8,128)(2,1)S(1)}, bf16[128,2048]{1,0:T(8,128)(2,1)S(1)}, u32[]{:S(2)}, u32[]{:S(2)}) collective-permute-start(bf16[128,2048]{1,0:T(8,128)(2,1)S(1)} %fusion.6), channel_id=1, source_target_pairs={{0,1},{2,0},{4,2},{6,4},{7,6},{5,7},{3,5},{1,3},{8,9},{10,8},{12,1... | collective-permute-start | bytes 1572872 | tf_op jit(solution)/shard_map/ppermute | solution.py:95
  158.0 19.6 %collective-permute-start.21 = (bf16[128,2048]{1,0:T(8,128)(2,1)S(1)}, bf16[128,2048]{1,0:T(8,128)(2,1)S(1)}, u32[]{:S(2)}, u32[]{:S(2)}) collective-permute-start(bf16[128,2048]{1,0:T(8,128)(2,1)S(1)} %fusion.14), channel_id=1, source_target_pairs={{0,1},{2,0},{4,2},{6,4},{7,6},{5,7},{3,5},{1,3},{8,9},{10,8},{12,1... | collective-permute-start | bytes 1572872 | tf_op jit(solution)/shard_map/ppermute | solution.py:95
  158.7 19.9 %collective-permute-start.16 = (bf16[128,2048]{1,0:T(8,128)(2,1)S(1)}, bf16[128,2048]{1,0:T(8,128)(2,1)S(1)}, u32[]{:S(2)}, u32[]{:S(2)}) collective-permute-start(bf16[128,2048]{1,0:T(8,128)(2,1)S(1)} %fusion.4), channel_id=1, source_target_pairs={{0,2},{2,4},{4,6},{6,7},{7,5},{5,3},{3,1},{1,0},{8,10},{10,12},{12... | collective-permute-start | bytes 1572872 | tf_op jit(solution)/shard_map/ppermute | solution.py:95
  161.9 20.4 %collective-permute-start.25 = (bf16[128,2048]{1,0:T(8,128)(2,1)S(1)}, bf16[128,2048]{1,0:T(8,128)(2,1)S(1)}, u32[]{:S(2)}, u32[]{:S(2)}) collective-permute-start(bf16[128,2048]{1,0:T(8,128)(2,1)S(1)} %fusion.15), channel_id=1, source_target_pairs={{0,2},{2,4},{4,6},{6,7},{7,5},{5,3},{3,1},{1,0},{8,10},{10,12},{12... | collective-permute-start | bytes 1572872 | tf_op jit(solution)/shard_map/ppermute | solution.py:95
  167.7 25.0 %copy-start.8 = (bf16[128,2048]{1,0:T(8,128)(2,1)}, bf16[128,2048]{1,0:T(8,128)(2,1)S(1)}, u32[]{:S(2)}) copy-start(bf16[128,2048]{1,0:T(8,128)(2,1)S(1)} %collective-permute-done.20) | copy-start | bytes 1572868
  177.9 13.7 %collective-permute-start.22 = (bf16[128,2048]{1,0:T(8,128)(2,1)S(1)}, bf16[128,2048]{1,0:T(8,128)(2,1)S(1)}, u32[]{:S(2)}, u32[]{:S(2)}) collective-permute-start(bf16[128,2048]{1,0:T(8,128)(2,1)S(1)} %fusion.18), channel_id=1, source_target_pairs={{0,1},{2,0},{4,2},{6,4},{7,6},{5,7},{3,5},{1,3},{8,9},{10,8},{12,1... | collective-permute-start | bytes 1572872 | tf_op jit(solution)/shard_map/ppermute | solution.py:95
  181.0 39.3 %copy-start.9 = (s32[128,4]{0,1:T(4,128)S(1)}, s32[128,4]{0,1:T(4,128)}, u32[]{:S(2)}) copy-start(s32[128,4]{0,1:T(4,128)} %param.9) | copy-start | bytes 6148
  181.0 12.4 %collective-permute-start.17 = (bf16[128,2048]{1,0:T(8,128)(2,1)}, bf16[128,2048]{1,0:T(8,128)(2,1)}, u32[]{:S(2)}, u32[]{:S(2)}) collective-permute-start(bf16[128,2048]{1,0:T(8,128)(2,1)} %fusion.3), channel_id=1, source_target_pairs={{0,2},{2,4},{4,6},{6,7},{7,5},{5,3},{3,1},{1,0},{8,10},{10,12},{12... | collective-permute-start | bytes 1572872 | tf_op jit(solution)/shard_map/ppermute | solution.py:95
  183.4 18.6 %collective-permute-start.26 = (bf16[128,2048]{1,0:T(8,128)(2,1)}, bf16[128,2048]{1,0:T(8,128)(2,1)}, u32[]{:S(2)}, u32[]{:S(2)}) collective-permute-start(bf16[128,2048]{1,0:T(8,128)(2,1)} %fusion.16), channel_id=1, source_target_pairs={{0,2},{2,4},{4,6},{6,7},{7,5},{5,3},{3,1},{1,0},{8,10},{10,12},{12... | collective-permute-start | bytes 1572872 | tf_op jit(solution)/shard_map/ppermute | solution.py:95
  192.7 14.3 %collective-permute-start.23 = (bf16[128,2048]{1,0:T(8,128)(2,1)}, bf16[128,2048]{1,0:T(8,128)(2,1)}, u32[]{:S(2)}, u32[]{:S(2)}) collective-permute-start(bf16[128,2048]{1,0:T(8,128)(2,1)} %fusion.10), channel_id=1, source_target_pairs={{0,1},{2,0},{4,2},{6,4},{7,6},{5,7},{3,5},{1,3},{8,9},{10,8},{12,1... | collective-permute-start | bytes 1572872 | tf_op jit(solution)/shard_map/ppermute | solution.py:95
  204.3 19.0 %collective-permute-start.27 = (bf16[128,2048]{1,0:T(8,128)(2,1)}, bf16[128,2048]{1,0:T(8,128)(2,1)}, u32[]{:S(2)}, u32[]{:S(2)}) collective-permute-start(bf16[128,2048]{1,0:T(8,128)(2,1)} %fusion.17), channel_id=1, source_target_pairs={{0,2},{2,4},{4,6},{6,7},{7,5},{5,3},{3,1},{1,0},{8,10},{10,12},{12... | collective-permute-start | bytes 1572872 | tf_op jit(solution)/shard_map/ppermute | solution.py:95
  209.3 14.0 %collective-permute-start.24 = (bf16[128,2048]{1,0:T(8,128)(2,1)}, bf16[128,2048]{1,0:T(8,128)(2,1)}, u32[]{:S(2)}, u32[]{:S(2)}) collective-permute-start(bf16[128,2048]{1,0:T(8,128)(2,1)} %fusion.9), channel_id=1, source_target_pairs={{0,1},{2,0},{4,2},{6,4},{7,6},{5,7},{3,5},{1,3},{8,9},{10,8},{12,1... | collective-permute-start | bytes 1572872 | tf_op jit(solution)/shard_map/ppermute | solution.py:95
  210.0 10.3 %all-to-all-start.1 = ((f32[8,2,128]{2,1,0:T(2,128)}), f32[8,2,128]{2,1,0:T(2,128)S(1)}, u32[]{:S(2)}, u32[]{:S(2)}) async-start(f32[8,2,128]{2,1,0:T(2,128)} %get-tuple-element.20), calls=%async_computation.1 | async-start | bytes 16384 | tf_op jit(solution)/shard_map/all_to_all | solution.py:505

commit v8 on v4

--- a/solution.py
+++ b/solution.py
@@ -126,8 +126,8 @@
     return pl.pallas_call(
         kernel,
         out_shape=jax.ShapeDtypeStruct(array.shape, array.dtype),
-        in_specs=[pl.BlockSpec(memory_space=pl.ANY) for _ in range(1 + len(others))],
-        out_specs=pl.BlockSpec(memory_space=pl.ANY),
+        in_specs=[pl.BlockSpec(memory_space=pltpu.HBM) for _ in range(1 + len(others))],
+        out_specs=pl.BlockSpec(memory_space=pltpu.HBM),
         input_output_aliases={0: 0},
     )(array, *others)
 
@@ -157,7 +157,7 @@
 
 
 def call_kernel(kernel, operands, kinds, outs, scratch, flops, behind=()):
-    spaces = {"any": pl.ANY, "vmem": pltpu.VMEM, "smem": pltpu.SMEM}
+    spaces = {"any": pltpu.HBM, "vmem": pltpu.VMEM, "smem": pltpu.SMEM}
     count = len(operands)
     operands = [*operands, *behind]
     kinds = [*kinds, *["any" for _ in behind]]
@@ -187,6 +187,14 @@
     place = jnp.where(chip % 2 == 0, chip // 2, count - (chip + 1) // 2)
     place = (place + distance) % count
     return jnp.where(place < count // 2, 2 * place, 2 * (count - place) - 1)
+
+
+def run_hold(array, behind):
+    def kernel(in_ref, out_ref):
+        out_ref[...] = in_ref[...]
+
+    shape = jax.ShapeDtypeStruct(array.shape, array.dtype)
+    return call_kernel(kernel, [array], ["vmem"], [shape], [], 1, behind)[0]
 
 
 def run_routing(ids, tables, top_count, capacity):
@@ -438,13 +446,16 @@
     tables = lax.all_to_all(copies, "ep", split_axis=0, concat_axis=0, tiled=True)
     pick, spread = run_routing(ids, tables, top_count, capacity)
 
-    behind = {(step, 2): (tables,) for step in (1, -1)}
-    in_shards, in_hops = ring_gather(tokens, chips, 1, behind)
-    behind = {(step, 1): (in_hops[step][0],) for step in (1, -1)}
-    grad_shards, _ = ring_gather(cotangent, chips, -1, behind)
     gate_mats = (w_gate[0], swap_cores(w_gate[0]))
     up_mats = (w_up[0], swap_cores(w_up[0]))
     down_mats = (w_down[0], swap_cores(w_down[0]))
+    swapped = (gate_mats[1], up_mats[1], down_mats[1])
+
+    behind = {(step, 2): (tables,) for step in (1, -1)}
+    behind.update({(step, 3): swapped for step in (1, -1)})
+    in_shards, in_hops = ring_gather(tokens, chips, 1, behind)
+    grad_later = run_hold(cotangent, (in_hops[1][1], in_hops[-1][1], *swapped))
+    grad_shards, _ = ring_gather(grad_later, chips, -1)
 
     def gather_rows(shards):
         return [
@@ -472,10 +483,9 @@
     d_pre_gate, d_pre_up, per_token = run_d_hidden(
         ids, rows_grad, outputs, pick, slope, activated, down_mats, ()
     )
-    behind = {(step, 1): (per_token,) for step in (1, -1)}
-    mixed, mixed_hops = ring_reduce(scatter_rows(outputs), chips, 1, behind)
+    mixed, mixed_hops = ring_reduce(scatter_rows(outputs), chips, 1)
     d_copies = run_d_copy(
-        d_pre_gate, d_pre_up, gate_mats, up_mats, chips, [mixed_hops[step][0] for step in (1, -1)]
+        d_pre_gate, d_pre_up, gate_mats, up_mats, chips, [mixed_hops[step][1] for step in (1, -1)]
     )
 
     returned = lax.all_to_all(per_token, "ep", split_axis=0, concat_axis=0, tiled=True)

time: 221 us -> 232 us (1.050)
  waiting for transfers between devices: 95.4 us -> 104 us
  matrix products: 27.6 us -> 32 us
  local copies, waits for them, and re-layouts: 11 us -> 8.54 us
    ppermute x28, waiting for transfers between devices: 82 us -> 88.1 us  [ring_shift(): return lax.ppermute(array, 'ep', pairs)]
    dot_general x16, matrix products: 9.04 us -> 12.4 us  [gather_rows(): jnp.dot(pick[s], shards[s], preferred_element_type=f32).astype(bf16)]
    all_to_all x1, waiting for transfers between devices: 6.91 us -> 9.31 us  [body_ring(): lax.all_to_all(copies, 'ep', split_axis=0, concat_axis=0, tiled=True)]
    unnamed x26 -> x30, local copies, waits for them, and re-layouts: 6.01 us -> 4.66 us
    pallas_call x5 -> x6, Pallas kernels: 38.1 us -> 38 us  [call_kernel(): pl.pallas_call(body, out_shape=outs, in_specs=[pl.BlockSpec(memory_space=...]
  transfers between devices with their start and end apart: 33 -> 33, of which waited for: 18 -> 17; matrix products, arithmetic and copies ran while one was open for 15% -> 15% of each run, Pallas kernels for 17% -> 16%
where the time goes in v8:
time: 232 us; the launch traced here: 231 us
  waiting for transfers between devices  104 us (45%)
  starting transfers between devices  42.1 us (18%)
  Pallas kernels  38 us (16%)
  matrix products  32 us (14%)
  local copies, waits for them, and re-layouts  8.54 us (4%)
  between operations  4.3 us (2%)
    ppermute x28, waiting for transfers between devices, ring_shift(): return lax.ppermute(array, 'ep', pairs)  88.1 us
    pallas_call x6, Pallas kernels, call_kernel(): pl.pallas_call(body, out_shape=outs, in_specs=[pl.BlockSpec(memory_space=...  38 us
    ppermute x28, starting transfers between devices, ring_shift(): return lax.ppermute(array, 'ep', pairs)  30.1 us
    dot_general x16, matrix products, share_of(): lax.dot_general(spread[s], blocks[s], (((0,), (0,)), ((), ())), preferred...  19.5 us
    dot_general x16, matrix products, gather_rows(): jnp.dot(pick[s], shards[s], preferred_element_type=f32).astype(bf16)  12.4 us
    all_to_all x1, waiting for transfers between devices, body_ring(): lax.all_to_all(copies, 'ep', split_axis=0, concat_axis=0, tiled=True)  9.31 us
    all_to_all x1, waiting for transfers between devices, body_ring(): lax.all_to_all(per_token, 'ep', split_axis=0, concat_axis=0, tiled=True)  6.51 us
    all_to_all x1, starting transfers between devices, body_ring(): lax.all_to_all(copies, 'ep', split_axis=0, concat_axis=0, tiled=True)  6.25 us
  transfers between devices with their start and end apart: 33, of which 17 were waited for; matrix products, arithmetic and copies ran while one was open for 15% of the time, Pallas kernels for 16%

profile of v8, /device:TPU:0, one launch (start us, length us, event | category | flops | bytes accessed | tf_op | source)
XLA Modules:
  0.0 230.9 jit_solution(15510332395352406350)
XLA Ops:
  1.7 2.6 %collective-permute-start = (bf16[128,2048]{1,0:T(8,128)(2,1)}, bf16[128,2048]{1,0:T(8,128)(2,1)}, u32[]{:S(2)}, u32[]{:S(2)}) collective-permute-start(bf16[128,2048]{1,0:T(8,128)(2,1)} %param.7), channel_id=1, source_target_pairs={{0,1},{2,0},{4,2},{6,4},{7,6},{5,7},{3,5},{1,3},{8,9},{10,8},{12,1... | collective-permute-start | bytes 1572872 | tf_op jit(solution)/shard_map/ppermute | solution.py:95
  6.3 6.3 %all-to-all-start = ((f32[8,8,128]{2,1,0:T(8,128)}), f32[8,8,128]{2,1,0:T(8,128)S(1)}, u32[]{:S(2)}, u32[]{:S(2)}) async-start(f32[8,8,128]{2,1,0:T(8,128)} %broadcast_in_dim.10), calls=%async_computation | async-start | bytes 65536 | tf_op jit(solution)/shard_map/all_to_all | solution.py:446
  12.6 9.3 %all-to-all-done.refs_1_ = f32[8,8,128]{2,1,0:T(8,128)S(1)} async-done(((f32[8,8,128]{2,1,0:T(8,128)}), f32[8,8,128]{2,1,0:T(8,128)S(1)}, u32[]{:S(2)}, u32[]{:S(2)}) %all-to-all-start) | async-done | bytes 32800 | tf_op jit(solution)/shard_map/all_to_all | solution.py:446
  24.7 1.6 collective-permute-start.7
  26.2 2.1 convolution_convert_fusion.19.refs_0_
  28.3 2.0 convolution_convert_fusion.12.refs_7_
  30.3 2.1 convolution_convert_fusion.18.refs_1_
  32.4 4.9 %collective-permute-done.1.refs_0_.refs_2_ = bf16[128,2048]{1,0:T(8,128)(2,1)} collective-permute-done((bf16[128,2048]{1,0:T(8,128)(2,1)}, bf16[128,2048]{1,0:T(8,128)(2,1)}, u32[]{:S(2)}, u32[]{:S(2)}) %collective-permute-start.1) | collective-permute-done | bytes 524320 | tf_op jit(solution)/shard_map/ppermute | solution.py:95
  37.4 1.7 copy-done
  40.7 1.6 collective-permute-start.8
  42.3 2.1 convolution_convert_fusion.13.refs_6_
  45.7 1.3 convolution_convert_fusion.17.refs_2_
  48.5 7.2 %collective-permute-done.8 = bf16[128,2048]{1,0:T(8,128)(2,1)S(1)} collective-permute-done((bf16[128,2048]{1,0:T(8,128)(2,1)}, bf16[128,2048]{1,0:T(8,128)(2,1)S(1)}, u32[]{:S(2)}, u32[]{:S(2)}) %collective-permute-start.8) | collective-permute-done | bytes 524320 | tf_op jit(solution)/shard_map/ppermute | solution.py:95
  55.7 1.6 collective-permute-start.9
  57.6 1.8 collective-permute-done.17
  60.1 6.8 %collective-permute-done.21 = bf16[128,2048]{1,0:T(8,128)(2,1)S(1)} collective-permute-done((bf16[128,2048]{1,0:T(8,128)(2,1)S(1)}, bf16[128,2048]{1,0:T(8,128)(2,1)S(1)}, u32[]{:S(2)}, u32[]{:S(2)}) %collective-permute-start.21) | collective-permute-done | bytes 524320 | tf_op jit(solution)/shard_map/ppermute | solution.py:95
  67.0 1.6 collective-permute-start.22
  68.9 1.8 collective-permute-done.5
  71.0 7.2 %collective-permute-done.9 = bf16[128,2048]{1,0:T(8,128)(2,1)S(1)} collective-permute-done((bf16[128,2048]{1,0:T(8,128)(2,1)S(1)}, bf16[128,2048]{1,0:T(8,128)(2,1)S(1)}, u32[]{:S(2)}, u32[]{:S(2)}) %collective-permute-start.9) | collective-permute-done | bytes 524320 | tf_op jit(solution)/shard_map/ppermute | solution.py:95
  78.5 10.5 %shard_map.99 = (bf16[2,384,768]{2,1,0:T(8,128)(2,1)S(1)}, f32[2,384,768]{2,1,0:T(8,128)}, f32[2,384,768]{2,1,0:T(8,128)}) custom-call(bf16[96,2048]{1,0:T(8,128)(2,1)S(1)} %copy-done.8, bf16[96,2048]{1,0:T(8,128)(2,1)S(1)} %copy-done.10, bf16[96,2048]{1,0:T(8,128)(2,1)S(1)} %convolution_convert_fusion.17.refs_2_, ...), custom_call_target="tpu_custom_call" | custom-call | flops 4831838208 | bytes 1048576 | tf_op jit(solution)/shard_map/pallas_call | solution.py:168
  89.0 4.7 %shard_map.100.refs_9_ = bf16[8,96,2048]{2,1,0:T(8,128)(2,1)S(1)} custom-call(bf16[2,384,768]{2,1,0:T(8,128)(2,1)S(1)} %get-tuple-element.13.refs_0_, bf16[768,2048]{1,0:T(8,128)(2,1)} %bitcast.159, bf16[768,2048]{1,0:T(8,128)(2,1)} %collective-permute-done.4.refs_3_.refs_2_.refs_5_.refs_14_), custom_call_target="tpu_custom_call" | custom-call | flops 2415919104 | bytes 1048576 | tf_op jit(solution)/shard_map/pallas_call | solution.py:168
  96.5 1.6 collective-permute-start.23
  99.1 9.8 %collective-permute-done.14 = bf16[128,2048]{1,0:T(8,128)(2,1)S(1)} collective-permute-done((bf16[128,2048]{1,0:T(8,128)(2,1)S(1)}, bf16[128,2048]{1,0:T(8,128)(2,1)S(1)}, u32[]{:S(2)}, u32[]{:S(2)}) %collective-permute-start.14) | collective-permute-done | bytes 524320 | tf_op jit(solution)/shard_map/ppermute | solution.py:95
  111.9 8.3 %collective-permute-done.19 = bf16[128,2048]{1,0:T(8,128)(2,1)S(1)} collective-permute-done((bf16[128,2048]{1,0:T(8,128)(2,1)S(1)}, bf16[128,2048]{1,0:T(8,128)(2,1)S(1)}, u32[]{:S(2)}, u32[]{:S(2)}) %collective-permute-start.19) | collective-permute-done | bytes 524320 | tf_op jit(solution)/shard_map/ppermute | solution.py:95
  121.5 9.9 %collective-permute-done.15.refs_7_ = bf16[128,2048]{1,0:T(8,128)(2,1)S(1)} collective-permute-done((bf16[128,2048]{1,0:T(8,128)(2,1)S(1)}, bf16[128,2048]{1,0:T(8,128)(2,1)S(1)}, u32[]{:S(2)}, u32[]{:S(2)}) %collective-permute-start.15) | collective-permute-done | bytes 524320 | tf_op jit(solution)/shard_map/ppermute | solution.py:95
  133.8 7.6 %collective-permute-done.20 = bf16[128,2048]{1,0:T(8,128)(2,1)S(1)} collective-permute-done((bf16[128,2048]{1,0:T(8,128)(2,1)S(1)}, bf16[128,2048]{1,0:T(8,128)(2,1)S(1)}, u32[]{:S(2)}, u32[]{:S(2)}) %collective-permute-start.20) | collective-permute-done | bytes 524320 | tf_op jit(solution)/shard_map/ppermute | solution.py:95
  141.7 11.8 %shard_map.102 = (bf16[2,384,768]{2,1,0:T(8,128)(2,1)S(1)}, bf16[2,384,768]{2,1,0:T(8,128)(2,1)S(1)}, f32[8,2,128]{2,1,0:T(2,128)}) custom-call(s32[2]{0:T(128)S(1)} %pad_add_fusion.1.refs_0_, bf16[96,2048]{1,0:T(8,128)(2,1)S(1)} %convolution_convert_fusion.11.refs_1_, bf16[96,2048]{1,0:T(8,128)(2,1)S(1)} %convolution_convert_fusion.10.refs_2_, ...), custom_call_target="tpu_custom_call" | custom-call | flops 2415919104 | bytes 1048576 | tf_op jit(solution)/shard_map/pallas_call | solution.py:168
  153.5 10.2 %shard_map.103 = bf16[8,96,2048]{2,1,0:T(8,128)(2,1)} custom-call(bf16[2,384,768]{2,1,0:T(8,128)(2,1)S(1)} %get-tuple-element.16.refs_0_, bf16[2,384,768]{2,1,0:T(8,128)(2,1)S(1)} %get-tuple-element.17.refs_1_, bf16[2048,768]{1,0:T(8,128)(2,1)} %bitcast.163, bf16[2048,768]{1,0:T(8,128)(2,1)} %copy-done, bf16[2048,768]{1,0:T(8,128)(2,1)} %bitcast.166, ...), custom_call_target="tpu_custom_call" | custom-call | flops 4831838208 | bytes 1048576 | tf_op jit(solution)/shard_map/pallas_call | solution.py:168
  163.7 1.5 fusion.14
  165.8 1.3 fusion.4
  167.1 1.5 collective-permute-start.12
  169.8 1.3 fusion.15
  171.1 1.4 collective-permute-start.28
  173.7 2.0 collective-permute-done.24
  176.4 5.6 %collective-permute-done.12 = bf16[128,2048]{1,0:T(8,128)(2,1)S(1)} collective-permute-done((bf16[128,2048]{1,0:T(8,128)(2,1)S(1)}, bf16[128,2048]{1,0:T(8,128)(2,1)S(1)}, u32[]{:S(2)}, u32[]{:S(2)}) %collective-permute-start.12) | collective-permute-done | bytes 524320 | tf_op jit(solution)/shard_map/ppermute | solution.py:95
  183.2 2.1 fusion.3
  185.4 1.4 collective-permute-start.13
  186.8 4.1 %collective-permute-done.28 = bf16[128,2048]{1,0:T(8,128)(2,1)S(1)} collective-permute-done((bf16[128,2048]{1,0:T(8,128)(2,1)S(1)}, bf16[128,2048]{1,0:T(8,128)(2,1)S(1)}, u32[]{:S(2)}, u32[]{:S(2)}) %collective-permute-start.28) | collective-permute-done | bytes 524320 | tf_op jit(solution)/shard_map/ppermute | solution.py:95
  192.0 1.7 collective-permute-start.29
  195.2 4.1 %collective-permute-done.13 = bf16[128,2048]{1,0:T(8,128)(2,1)} collective-permute-done((bf16[128,2048]{1,0:T(8,128)(2,1)}, bf16[128,2048]{1,0:T(8,128)(2,1)}, u32[]{:S(2)}, u32[]{:S(2)}) %collective-permute-start.13) | collective-permute-done | bytes 524320 | tf_op jit(solution)/shard_map/ppermute | solution.py:95
  201.2 6.7 %collective-permute-done.29 = bf16[128,2048]{1,0:T(8,128)(2,1)} collective-permute-done((bf16[128,2048]{1,0:T(8,128)(2,1)}, bf16[128,2048]{1,0:T(8,128)(2,1)}, u32[]{:S(2)}, u32[]{:S(2)}) %collective-permute-start.29) | collective-permute-done | bytes 524320 | tf_op jit(solution)/shard_map/ppermute | solution.py:95
  207.9 2.2 fusion.17
  210.1 1.7 collective-permute-start.30
  211.8 2.2 fusion.9
  214.3 4.7 %all-to-all-start.1 = ((f32[8,2,128]{2,1,0:T(2,128)}), f32[8,2,128]{2,1,0:T(2,128)S(1)}, u32[]{:S(2)}, u32[]{:S(2)}) async-start(f32[8,2,128]{2,1,0:T(2,128)} %get-tuple-element.18), calls=%async_computation.1 | async-start | bytes 16384 | tf_op jit(solution)/shard_map/all_to_all | solution.py:491
  219.0 6.5 %all-to-all-done.1 = f32[8,2,128]{2,1,0:T(2,128)S(1)} async-done(((f32[8,2,128]{2,1,0:T(2,128)}), f32[8,2,128]{2,1,0:T(2,128)S(1)}, u32[]{:S(2)}, u32[]{:S(2)}) %all-to-all-start.1) | async-done | bytes 8224 | tf_op jit(solution)/shard_map/all_to_all | solution.py:491
  226.1 2.5 %fusion.2 = bf16[128,2048]{1,0:T(8,128)(2,1)} fusion(bf16[128,2048]{1,0:T(8,128)(2,1)} %copy-done.13, bf16[128,2048]{1,0:T(8,128)(2,1)} %collective-permute-done.13, bf16[8,96,2048]{2,1,0:T(8,128)(2,1)} %copy-done.1, bf16[8,96,128]{2,1,0:T(8,128)(2,1)S(1)} %get-tuple-element.11), kind=kOutput, calls=%fused_computation.14 | convolution fusion | flops 51642368 | bytes 1990656 | tf_op jit(solution)/shard_map/dot_general | solution.py:468
  228.6 2.3 %fusion.8 = bf16[128,2048]{1,0:T(8,128)(2,1)} fusion(bf16[128,2048]{1,0:T(8,128)(2,1)} %collective-permute-done.30, bf16[128,2048]{1,0:T(8,128)(2,1)} %collective-permute-done.27, bf16[8,96,2048]{2,1,0:T(8,128)(2,1)S(1)} %copy-done.12, bf16[8,96,128]{2,1,0:T(8,128)(2,1)S(1)} %get-tuple-element.11), kind=kOutput, calls=%fused_computation.20 | convolution fusion | flops 51642368 | bytes 1990656 | tf_op jit(solution)/shard_map/dot_general | solution.py:468
  (104 shorter events, 29.6 us)
Async XLA Ops:
  0.6 36.7 %collective-permute-start.2 = (bf16[2048,768]{1,0:T(8,128)(2,1)}, bf16[2048,768]{1,0:T(8,128)(2,1)S(1)}, u32[]{:S(2)}, u32[]{:S(2)}) collective-permute-start(bf16[2048,768]{1,0:T(8,128)(2,1)} %bitcast.161), channel_id=1, source_target_pairs={{0,8},{8,0},{1,9},{9,1},{2,10},{10,2},{3,11},{11,3},{4,12},{12,4},... | collective-permute-start | bytes 9437192 | tf_op jit(solution)/shard_map/ppermute | solution.py:429
  1.1 36.2 %collective-permute-start.3 = (bf16[2048,768]{1,0:T(8,128)(2,1)}, bf16[2048,768]{1,0:T(8,128)(2,1)}, u32[]{:S(2)}, u32[]{:S(2)}) collective-permute-start(bf16[2048,768]{1,0:T(8,128)(2,1)} %bitcast.164), channel_id=1, source_target_pairs={{0,8},{8,0},{1,9},{9,1},{2,10},{10,2},{3,11},{11,3},{4,12},{12,4},... | collective-permute-start | bytes 9437192 | tf_op jit(solution)/shard_map/ppermute | solution.py:429
  1.2 36.1 %collective-permute-start.4 = (bf16[768,2048]{1,0:T(8,128)(2,1)}, bf16[768,2048]{1,0:T(8,128)(2,1)}, u32[]{:S(2)}, u32[]{:S(2)}) collective-permute-start(bf16[768,2048]{1,0:T(8,128)(2,1)} %bitcast.158), channel_id=1, source_target_pairs={{0,8},{8,0},{1,9},{9,1},{2,10},{10,2},{3,11},{11,3},{4,12},{12,4},... | collective-permute-start | bytes 9437192 | tf_op jit(solution)/shard_map/ppermute | solution.py:429
  1.7 22.4 %collective-permute-start = (bf16[128,2048]{1,0:T(8,128)(2,1)}, bf16[128,2048]{1,0:T(8,128)(2,1)}, u32[]{:S(2)}, u32[]{:S(2)}) collective-permute-start(bf16[128,2048]{1,0:T(8,128)(2,1)} %param.7), channel_id=1, source_target_pairs={{0,1},{2,0},{4,2},{6,4},{7,6},{5,7},{3,5},{1,3},{8,9},{10,8},{12,1... | collective-permute-start | bytes 1572872 | tf_op jit(solution)/shard_map/ppermute | solution.py:95
  4.2 20.4 %collective-permute-start.6 = (bf16[128,2048]{1,0:T(8,128)(2,1)}, bf16[128,2048]{1,0:T(8,128)(2,1)}, u32[]{:S(2)}, u32[]{:S(2)}) collective-permute-start(bf16[128,2048]{1,0:T(8,128)(2,1)} %param.7), channel_id=1, source_target_pairs={{0,2},{2,4},{4,6},{6,7},{7,5},{5,3},{3,1},{1,0},{8,10},{10,12},{12... | collective-permute-start | bytes 1572872 | tf_op jit(solution)/shard_map/ppermute | solution.py:95
  6.3 15.6 %all-to-all-start = ((f32[8,8,128]{2,1,0:T(8,128)}), f32[8,8,128]{2,1,0:T(8,128)S(1)}, u32[]{:S(2)}, u32[]{:S(2)}) async-start(f32[8,8,128]{2,1,0:T(8,128)} %broadcast_in_dim.10), calls=%async_computation | async-start | bytes 65536 | tf_op jit(solution)/shard_map/all_to_all | solution.py:446
  21.9 0.6 copy-start.6
  22.6 0.8 copy-start.7
  24.1 13.2 %collective-permute-start.1 = (bf16[128,2048]{1,0:T(8,128)(2,1)}, bf16[128,2048]{1,0:T(8,128)(2,1)}, u32[]{:S(2)}, u32[]{:S(2)}) collective-permute-start(bf16[128,2048]{1,0:T(8,128)(2,1)} %shard_map.95), channel_id=1, source_target_pairs={{0,1},{2,0},{4,2},{6,4},{7,6},{5,7},{3,5},{1,3},{8,9},{10,8},{12,1... | collective-permute-start | bytes 1572872 | tf_op jit(solution)/shard_map/ppermute | solution.py:95
  24.7 12.7 %copy-start.5 = (bf16[128,2048]{1,0:T(8,128)(2,1)S(1)}, bf16[128,2048]{1,0:T(8,128)(2,1)}, u32[]{:S(2)}) copy-start(bf16[128,2048]{1,0:T(8,128)(2,1)} %refs_0_.1) | copy-start | bytes 1572868
  24.7 12.7 %collective-permute-start.7 = (bf16[128,2048]{1,0:T(8,128)(2,1)}, bf16[128,2048]{1,0:T(8,128)(2,1)S(1)}, u32[]{:S(2)}, u32[]{:S(2)}) collective-permute-start(bf16[128,2048]{1,0:T(8,128)(2,1)} %shard_map.97), channel_id=1, source_target_pairs={{0,2},{2,4},{4,6},{6,7},{7,5},{5,3},{3,1},{1,0},{8,10},{10,12},{12... | collective-permute-start | bytes 1572872 | tf_op jit(solution)/shard_map/ppermute | solution.py:95
  37.3 1.7 copy-start
  39.1 0.8 copy-start.2
  39.9 0.8 copy-start.3
  40.7 15.1 %collective-permute-start.8 = (bf16[128,2048]{1,0:T(8,128)(2,1)}, bf16[128,2048]{1,0:T(8,128)(2,1)S(1)}, u32[]{:S(2)}, u32[]{:S(2)}) collective-permute-start(bf16[128,2048]{1,0:T(8,128)(2,1)} %shard_map.98), channel_id=1, source_target_pairs={{0,2},{2,4},{4,6},{6,7},{7,5},{5,3},{3,1},{1,0},{8,10},{10,12},{12... | collective-permute-start | bytes 1572872 | tf_op jit(solution)/shard_map/ppermute | solution.py:95
  44.4 2.6 %copy-start.4 = (bf16[128,2048]{1,0:T(8,128)(2,1)S(1)}, bf16[128,2048]{1,0:T(8,128)(2,1)}, u32[]{:S(2)}) copy-start(bf16[128,2048]{1,0:T(8,128)(2,1)} %copy-done.3) | copy-start | bytes 1572868
  44.4 15.1 %collective-permute-start.17 = (bf16[128,2048]{1,0:T(8,128)(2,1)}, bf16[128,2048]{1,0:T(8,128)(2,1)S(1)}, u32[]{:S(2)}, u32[]{:S(2)}) collective-permute-start(bf16[128,2048]{1,0:T(8,128)(2,1)} %copy-done.3), channel_id=1, source_target_pairs={{0,1},{2,0},{4,2},{6,4},{7,6},{5,7},{3,5},{1,3},{8,9},{10,8},{12,1... | collective-permute-start | bytes 1572872 | tf_op jit(solution)/shard_map/ppermute | solution.py:95
  44.8 33.7 %copy-start.8 = (bf16[96,2048]{1,0:T(8,128)(2,1)S(1)}, bf16[96,2048]{1,0:T(8,128)(2,1)}, u32[]{:S(2)}) copy-start(bf16[96,2048]{1,0:T(8,128)(2,1)} %convolution_convert_fusion.19.refs_0_) | copy-start | bytes 1179652
  44.8 33.7 %copy-start.9 = (bf16[96,2048]{1,0:T(8,128)(2,1)S(1)}, bf16[96,2048]{1,0:T(8,128)(2,1)}, u32[]{:S(2)}) copy-start(bf16[96,2048]{1,0:T(8,128)(2,1)} %convolution_convert_fusion.12.refs_7_) | copy-start | bytes 1179652
  44.8 33.7 %copy-start.10 = (bf16[96,2048]{1,0:T(8,128)(2,1)S(1)}, bf16[96,2048]{1,0:T(8,128)(2,1)}, u32[]{:S(2)}) copy-start(bf16[96,2048]{1,0:T(8,128)(2,1)} %convolution_convert_fusion.18.refs_1_) | copy-start | bytes 1179652
  44.8 33.7 %copy-start.11 = (bf16[96,2048]{1,0:T(8,128)(2,1)S(1)}, bf16[96,2048]{1,0:T(8,128)(2,1)}, u32[]{:S(2)}) copy-start(bf16[96,2048]{1,0:T(8,128)(2,1)} %convolution_convert_fusion.13.refs_6_) | copy-start | bytes 1179652
  44.8 25.9 %collective-permute-start.5 = (bf16[128,2048]{1,0:T(8,128)(2,1)}, bf16[128,2048]{1,0:T(8,128)(2,1)S(1)}, u32[]{:S(2)}, u32[]{:S(2)}) collective-permute-start(bf16[128,2048]{1,0:T(8,128)(2,1)} %shard_map.96), channel_id=1, source_target_pairs={{0,1},{2,0},{4,2},{6,4},{7,6},{5,7},{3,5},{1,3},{8,9},{10,8},{12,1... | collective-permute-start | bytes 1572872 | tf_op jit(solution)/shard_map/ppermute | solution.py:95
  47.0 19.9 %collective-permute-start.21 = (bf16[128,2048]{1,0:T(8,128)(2,1)S(1)}, bf16[128,2048]{1,0:T(8,128)(2,1)S(1)}, u32[]{:S(2)}, u32[]{:S(2)}) collective-permute-start(bf16[128,2048]{1,0:T(8,128)(2,1)S(1)} %copy-done.4), channel_id=1, source_target_pairs={{0,2},{2,4},{4,6},{6,7},{7,5},{5,3},{3,1},{1,0},{8,10},{10,12},{12... | collective-permute-start | bytes 1572872 | tf_op jit(solution)/shard_map/ppermute | solution.py:95
  55.7 22.5 %collective-permute-start.9 = (bf16[128,2048]{1,0:T(8,128)(2,1)S(1)}, bf16[128,2048]{1,0:T(8,128)(2,1)S(1)}, u32[]{:S(2)}, u32[]{:S(2)}) collective-permute-start(bf16[128,2048]{1,0:T(8,128)(2,1)S(1)} %collective-permute-done.8), channel_id=1, source_target_pairs={{0,2},{2,4},{4,6},{6,7},{7,5},{5,3},{3,1},{1,0},{8,10},{10,12},{12... | collective-permute-start | bytes 1572872 | tf_op jit(solution)/shard_map/ppermute | solution.py:95
  59.5 38.9 %collective-permute-start.18 = (bf16[128,2048]{1,0:T(8,128)(2,1)S(1)}, bf16[128,2048]{1,0:T(8,128)(2,1)S(1)}, u32[]{:S(2)}, u32[]{:S(2)}) collective-permute-start(bf16[128,2048]{1,0:T(8,128)(2,1)S(1)} %collective-permute-done.17), channel_id=1, source_target_pairs={{0,1},{2,0},{4,2},{6,4},{7,6},{5,7},{3,5},{1,3},{8,9},{10,8},{12,1... | collective-permute-start | bytes 1572872 | tf_op jit(solution)/shard_map/ppermute | solution.py:95
  67.0 29.5 %collective-permute-start.22 = (bf16[128,2048]{1,0:T(8,128)(2,1)S(1)}, bf16[128,2048]{1,0:T(8,128)(2,1)S(1)}, u32[]{:S(2)}, u32[]{:S(2)}) collective-permute-start(bf16[128,2048]{1,0:T(8,128)(2,1)S(1)} %collective-permute-done.21), channel_id=1, source_target_pairs={{0,2},{2,4},{4,6},{6,7},{7,5},{5,3},{3,1},{1,0},{8,10},{10,12},{12... | collective-permute-start | bytes 1572872 | tf_op jit(solution)/shard_map/ppermute | solution.py:95
  93.7 37.7 %copy-start.1 = (bf16[8,96,2048]{2,1,0:T(8,128)(2,1)}, bf16[8,96,2048]{2,1,0:T(8,128)(2,1)S(1)}, u32[]{:S(2)}) copy-start(bf16[8,96,2048]{2,1,0:T(8,128)(2,1)S(1)} %shard_map.100.refs_9_) | copy-start | bytes 9437188
  94.0 14.9 %collective-permute-start.14 = (bf16[128,2048]{1,0:T(8,128)(2,1)S(1)}, bf16[128,2048]{1,0:T(8,128)(2,1)S(1)}, u32[]{:S(2)}, u32[]{:S(2)}) collective-permute-start(bf16[128,2048]{1,0:T(8,128)(2,1)S(1)} %convolution_convert_fusion.2), channel_id=1, source_target_pairs={{0,1},{2,0},{4,2},{6,4},{7,6},{5,7},{3,5},{1,3},{8,9},{10,8},{12,1... | collective-permute-start | bytes 1572872 | tf_op jit(solution)/shard_map/ppermute | solution.py:95
  95.2 15.1 %collective-permute-start.10 = (bf16[128,2048]{1,0:T(8,128)(2,1)S(1)}, bf16[128,2048]{1,0:T(8,128)(2,1)S(1)}, u32[]{:S(2)}, u32[]{:S(2)}) collective-permute-start(bf16[128,2048]{1,0:T(8,128)(2,1)S(1)} %convolution_convert_fusion.3), channel_id=1, source_target_pairs={{0,2},{2,4},{4,6},{6,7},{7,5},{5,3},{3,1},{1,0},{8,10},{10,12},{12... | collective-permute-start | bytes 1572872 | tf_op jit(solution)/shard_map/ppermute | solution.py:95
  96.5 24.8 %collective-permute-start.23 = (bf16[128,2048]{1,0:T(8,128)(2,1)S(1)}, bf16[128,2048]{1,0:T(8,128)(2,1)S(1)}, u32[]{:S(2)}, u32[]{:S(2)}) collective-permute-start(bf16[128,2048]{1,0:T(8,128)(2,1)S(1)} %collective-permute-done.22), channel_id=1, source_target_pairs={{0,2},{2,4},{4,6},{6,7},{7,5},{5,3},{3,1},{1,0},{8,10},{10,12},{12... | collective-permute-start | bytes 1572872 | tf_op jit(solution)/shard_map/ppermute | solution.py:95
  98.4 21.8 %collective-permute-start.19 = (bf16[128,2048]{1,0:T(8,128)(2,1)S(1)}, bf16[128,2048]{1,0:T(8,128)(2,1)S(1)}, u32[]{:S(2)}, u32[]{:S(2)}) collective-permute-start(bf16[128,2048]{1,0:T(8,128)(2,1)S(1)} %collective-permute-done.18), channel_id=1, source_target_pairs={{0,1},{2,0},{4,2},{6,4},{7,6},{5,7},{3,5},{1,3},{8,9},{10,8},{12,1... | collective-permute-start | bytes 1572872 | tf_op jit(solution)/shard_map/ppermute | solution.py:95
  109.3 22.1 %collective-permute-start.15 = (bf16[128,2048]{1,0:T(8,128)(2,1)S(1)}, bf16[128,2048]{1,0:T(8,128)(2,1)S(1)}, u32[]{:S(2)}, u32[]{:S(2)}) collective-permute-start(bf16[128,2048]{1,0:T(8,128)(2,1)S(1)} %fusion.7), channel_id=1, source_target_pairs={{0,1},{2,0},{4,2},{6,4},{7,6},{5,7},{3,5},{1,3},{8,9},{10,8},{12,1... | collective-permute-start | bytes 1572872 | tf_op jit(solution)/shard_map/ppermute | solution.py:95
  110.7 42.8 %collective-permute-start.11 = (bf16[128,2048]{1,0:T(8,128)(2,1)S(1)}, bf16[128,2048]{1,0:T(8,128)(2,1)S(1)}, u32[]{:S(2)}, u32[]{:S(2)}) collective-permute-start(bf16[128,2048]{1,0:T(8,128)(2,1)S(1)} %fusion.5), channel_id=1, source_target_pairs={{0,2},{2,4},{4,6},{6,7},{7,5},{5,3},{3,1},{1,0},{8,10},{10,12},{12... | collective-permute-start | bytes 1572872 | tf_op jit(solution)/shard_map/ppermute | solution.py:95
  120.2 21.2 %collective-permute-start.20 = (bf16[128,2048]{1,0:T(8,128)(2,1)S(1)}, bf16[128,2048]{1,0:T(8,128)(2,1)S(1)}, u32[]{:S(2)}, u32[]{:S(2)}) collective-permute-start(bf16[128,2048]{1,0:T(8,128)(2,1)S(1)} %collective-permute-done.19), channel_id=1, source_target_pairs={{0,1},{2,0},{4,2},{6,4},{7,6},{5,7},{3,5},{1,3},{8,9},{10,8},{12,1... | collective-permute-start | bytes 1572872 | tf_op jit(solution)/shard_map/ppermute | solution.py:95
  131.7 40.8 %collective-permute-start.16 = (bf16[128,2048]{1,0:T(8,128)(2,1)S(1)}, bf16[128,2048]{1,0:T(8,128)(2,1)S(1)}, u32[]{:S(2)}, u32[]{:S(2)}) collective-permute-start(bf16[128,2048]{1,0:T(8,128)(2,1)S(1)} %fusion.6), channel_id=1, source_target_pairs={{0,1},{2,0},{4,2},{6,4},{7,6},{5,7},{3,5},{1,3},{8,9},{10,8},{12,1... | collective-permute-start | bytes 1572872 | tf_op jit(solution)/shard_map/ppermute | solution.py:95
  163.7 12.0 %copy-start.12 = (bf16[8,96,2048]{2,1,0:T(8,128)(2,1)S(1)}, bf16[8,96,2048]{2,1,0:T(8,128)(2,1)}, u32[]{:S(2)}) copy-start(bf16[8,96,2048]{2,1,0:T(8,128)(2,1)} %shard_map.103) | copy-start | bytes 9437188
  165.2 10.5 %collective-permute-start.24 = (bf16[128,2048]{1,0:T(8,128)(2,1)S(1)}, bf16[128,2048]{1,0:T(8,128)(2,1)S(1)}, u32[]{:S(2)}, u32[]{:S(2)}) collective-permute-start(bf16[128,2048]{1,0:T(8,128)(2,1)S(1)} %fusion.14), channel_id=1, source_target_pairs={{0,1},{2,0},{4,2},{6,4},{7,6},{5,7},{3,5},{1,3},{8,9},{10,8},{12,1... | collective-permute-start | bytes 1572872 | tf_op jit(solution)/shard_map/ppermute | solution.py:95
  167.1 14.9 %collective-permute-start.12 = (bf16[128,2048]{1,0:T(8,128)(2,1)S(1)}, bf16[128,2048]{1,0:T(8,128)(2,1)S(1)}, u32[]{:S(2)}, u32[]{:S(2)}) collective-permute-start(bf16[128,2048]{1,0:T(8,128)(2,1)S(1)} %fusion.4), channel_id=1, source_target_pairs={{0,2},{2,4},{4,6},{6,7},{7,5},{5,3},{3,1},{1,0},{8,10},{10,12},{12... | collective-permute-start | bytes 1572872 | tf_op jit(solution)/shard_map/ppermute | solution.py:95
  171.1 19.8 %collective-permute-start.28 = (bf16[128,2048]{1,0:T(8,128)(2,1)S(1)}, bf16[128,2048]{1,0:T(8,128)(2,1)S(1)}, u32[]{:S(2)}, u32[]{:S(2)}) collective-permute-start(bf16[128,2048]{1,0:T(8,128)(2,1)S(1)} %fusion.15), channel_id=1, source_target_pairs={{0,2},{2,4},{4,6},{6,7},{7,5},{5,3},{3,1},{1,0},{8,10},{10,12},{12... | collective-permute-start | bytes 1572872 | tf_op jit(solution)/shard_map/ppermute | solution.py:95
  172.5 21.3 %copy-start.13 = (bf16[128,2048]{1,0:T(8,128)(2,1)}, bf16[128,2048]{1,0:T(8,128)(2,1)S(1)}, u32[]{:S(2)}) copy-start(bf16[128,2048]{1,0:T(8,128)(2,1)S(1)} %collective-permute-done.16) | copy-start | bytes 1572868
  176.1 17.7 %collective-permute-start.25 = (bf16[128,2048]{1,0:T(8,128)(2,1)S(1)}, bf16[128,2048]{1,0:T(8,128)(2,1)S(1)}, u32[]{:S(2)}, u32[]{:S(2)}) collective-permute-start(bf16[128,2048]{1,0:T(8,128)(2,1)S(1)} %fusion.18), channel_id=1, source_target_pairs={{0,1},{2,0},{4,2},{6,4},{7,6},{5,7},{3,5},{1,3},{8,9},{10,8},{12,1... | collective-permute-start | bytes 1572872 | tf_op jit(solution)/shard_map/ppermute | solution.py:95
  185.3 40.1 %copy-start.14 = (s32[128,4]{0,1:T(4,128)S(1)}, s32[128,4]{0,1:T(4,128)}, u32[]{:S(2)}) copy-start(s32[128,4]{0,1:T(4,128)} %param.9) | copy-start | bytes 6148
  185.4 14.0 %collective-permute-start.13 = (bf16[128,2048]{1,0:T(8,128)(2,1)}, bf16[128,2048]{1,0:T(8,128)(2,1)}, u32[]{:S(2)}, u32[]{:S(2)}) collective-permute-start(bf16[128,2048]{1,0:T(8,128)(2,1)} %fusion.3), channel_id=1, source_target_pairs={{0,2},{2,4},{4,6},{6,7},{7,5},{5,3},{3,1},{1,0},{8,10},{10,12},{12... | collective-permute-start | bytes 1572872 | tf_op jit(solution)/shard_map/ppermute | solution.py:95
  192.0 15.8 %collective-permute-start.29 = (bf16[128,2048]{1,0:T(8,128)(2,1)}, bf16[128,2048]{1,0:T(8,128)(2,1)}, u32[]{:S(2)}, u32[]{:S(2)}) collective-permute-start(bf16[128,2048]{1,0:T(8,128)(2,1)} %fusion.16), channel_id=1, source_target_pairs={{0,2},{2,4},{4,6},{6,7},{7,5},{5,3},{3,1},{1,0},{8,10},{10,12},{12... | collective-permute-start | bytes 1572872 | tf_op jit(solution)/shard_map/ppermute | solution.py:95
  194.9 16.9 %collective-permute-start.26 = (bf16[128,2048]{1,0:T(8,128)(2,1)}, bf16[128,2048]{1,0:T(8,128)(2,1)}, u32[]{:S(2)}, u32[]{:S(2)}) collective-permute-start(bf16[128,2048]{1,0:T(8,128)(2,1)} %fusion.10), channel_id=1, source_target_pairs={{0,1},{2,0},{4,2},{6,4},{7,6},{5,7},{3,5},{1,3},{8,9},{10,8},{12,1... | collective-permute-start | bytes 1572872 | tf_op jit(solution)/shard_map/ppermute | solution.py:95
  210.1 18.5 %collective-permute-start.30 = (bf16[128,2048]{1,0:T(8,128)(2,1)}, bf16[128,2048]{1,0:T(8,128)(2,1)}, u32[]{:S(2)}, u32[]{:S(2)}) collective-permute-start(bf16[128,2048]{1,0:T(8,128)(2,1)} %fusion.17), channel_id=1, source_target_pairs={{0,2},{2,4},{4,6},{6,7},{7,5},{5,3},{3,1},{1,0},{8,10},{10,12},{12... | collective-permute-start | bytes 1572872 | tf_op jit(solution)/shard_map/ppermute | solution.py:95
  214.0 14.6 %collective-permute-start.27 = (bf16[128,2048]{1,0:T(8,128)(2,1)}, bf16[128,2048]{1,0:T(8,128)(2,1)}, u32[]{:S(2)}, u32[]{:S(2)}) collective-permute-start(bf16[128,2048]{1,0:T(8,128)(2,1)} %fusion.9), channel_id=1, source_target_pairs={{0,1},{2,0},{4,2},{6,4},{7,6},{5,7},{3,5},{1,3},{8,9},{10,8},{12,1... | collective-permute-start | bytes 1572872 | tf_op jit(solution)/shard_map/ppermute | solution.py:95
  214.3 11.2 %all-to-all-start.1 = ((f32[8,2,128]{2,1,0:T(2,128)}), f32[8,2,128]{2,1,0:T(2,128)S(1)}, u32[]{:S(2)}, u32[]{:S(2)}) async-start(f32[8,2,128]{2,1,0:T(2,128)} %get-tuple-element.18), calls=%async_computation.1 | async-start | bytes 16384 | tf_op jit(solution)/shard_map/all_to_all | solution.py:491

commit v9 on v8

--- a/solution.py
+++ b/solution.py
@@ -126,8 +126,8 @@
     return pl.pallas_call(
         kernel,
         out_shape=jax.ShapeDtypeStruct(array.shape, array.dtype),
-        in_specs=[pl.BlockSpec(memory_space=pltpu.HBM) for _ in range(1 + len(others))],
-        out_specs=pl.BlockSpec(memory_space=pltpu.HBM),
+        in_specs=[pl.BlockSpec(memory_space=pl.ANY) for _ in range(1 + len(others))],
+        out_specs=pl.BlockSpec(memory_space=pl.ANY),
         input_output_aliases={0: 0},
     )(array, *others)
 
@@ -232,7 +232,7 @@
     return call_kernel(kernel, [ids, tables], ["smem", "vmem"], [shape, shape], [], 1 << 20)
 
 
-def run_hidden(parts, gate_mats, up_mats):
+def run_hidden(parts, gate_mats, up_mats, behind):
     count, rows, width = len(parts), parts[0].shape[0], parts[0].shape[1]
     units = gate_mats[0].shape[1]
     total = count * rows // 2
@@ -278,10 +278,11 @@
             pltpu.SemaphoreType.DMA((2, 2)),
         ],
         8 * total * width * units,
-    )
-
-
-def run_down(hidden, down_mats, count):
+        behind,
+    )
+
+
+def run_down(hidden, down_mats, count, behind):
     _, total, units = hidden.shape
     width = down_mats[0].shape[1]
     half = total // count
@@ -312,22 +313,20 @@
             pltpu.SemaphoreType.DMA((2,)),
         ],
         4 * total * width * units,
+        behind,
     )[0]
 
 
-def run_d_hidden(ids, parts, outputs, pick, slope, activated, down_mats, behind):
+def run_d_hidden(parts, slope, activated, down_mats):
     count, rows, width = len(parts), parts[0].shape[0], parts[0].shape[1]
-    half = rows // 2
     _, total, units = slope.shape
     tile = cut(units, 256)
     tiles = units // tile
-    tokens = pick.shape[2]
 
     def kernel(*refs):
-        ids_ref, refs = refs[0], refs[1:]
         part_refs = refs[:count]
-        out_ref, pick_ref, slope_ref, act_ref, own_ref, other_ref = refs[count : count + 6]
-        d_gate_ref, d_up_ref, token_ref, packed, held, sems = refs[count + 6 :]
+        slope_ref, act_ref, own_ref, other_ref = refs[count : count + 4]
+        d_gate_ref, d_up_ref, packed, held, sems = refs[count + 4 :]
         copies = {}
         for e, mat in enumerate((own_ref, other_ref)):
             for n in range(tiles):
@@ -345,6 +344,29 @@
                 )
                 d_gate_ref[e, :, span] = (d_hidden * slope_ref[e, :, span]).astype(jnp.bfloat16)
                 d_up_ref[e, :, span] = (d_hidden * act_ref[e, :, span]).astype(jnp.bfloat16)
+
+    return call_kernel(
+        kernel,
+        [*parts, slope, activated, *down_mats],
+        ["vmem"] * (count + 2) + ["any"] * 2,
+        [jax.ShapeDtypeStruct((2, total, units), jnp.bfloat16)] * 2,
+        [
+            pltpu.VMEM((2, total, width), jnp.bfloat16),
+            pltpu.VMEM((2, tiles, tile, width), jnp.bfloat16),
+            pltpu.SemaphoreType.DMA((2, tiles)),
+        ],
+        4 * total * width * units,
+    )
+
+
+def run_d_gates(ids, parts, outputs, pick, behind):
+    count, rows = len(parts), parts[0].shape[0]
+    half = rows // 2
+    tokens = pick.shape[2]
+
+    def kernel(*refs):
+        ids_ref, part_refs = refs[0], refs[1 : 1 + count]
+        out_ref, pick_ref, token_ref = refs[1 + count :]
         for s in range(count):
             inner = jnp.sum(
                 part_refs[s][...].astype(jnp.float32) * out_ref[s].astype(jnp.float32),
@@ -360,21 +382,13 @@
 
     return call_kernel(
         kernel,
-        [ids, *parts, outputs, pick, slope, activated, *down_mats],
-        ["smem"] + ["vmem"] * (count + 4) + ["any"] * 2,
-        [
-            jax.ShapeDtypeStruct((2, total, units), jnp.bfloat16),
-            jax.ShapeDtypeStruct((2, total, units), jnp.bfloat16),
-            jax.ShapeDtypeStruct((count, 2, tokens), jnp.float32),
-        ],
-        [
-            pltpu.VMEM((2, total, width), jnp.bfloat16),
-            pltpu.VMEM((2, tiles, tile, width), jnp.bfloat16),
-            pltpu.SemaphoreType.DMA((2, tiles)),
-        ],
-        4 * total * width * units,
+        [ids, *parts, outputs, pick],
+        ["smem"] + ["vmem"] * (count + 2),
+        [jax.ShapeDtypeStruct((count, 2, tokens), jnp.float32)],
+        [],
+        1 << 20,
         behind,
-    )
+    )[0]
 
 
 def run_d_copy(d_pre_gate, d_pre_up, gate_mats, up_mats, count, behind):
@@ -455,7 +469,7 @@
     behind.update({(step, 3): swapped for step in (1, -1)})
     in_shards, in_hops = ring_gather(tokens, chips, 1, behind)
     grad_later = run_hold(cotangent, (in_hops[1][1], in_hops[-1][1], *swapped))
-    grad_shards, _ = ring_gather(grad_later, chips, -1)
+    grad_shards, grad_hops = ring_gather(grad_later, chips, -1)
 
     def gather_rows(shards):
         return [
@@ -477,23 +491,26 @@
         return share_of
 
     rows_in = gather_rows(in_shards)
-    hidden, slope, activated = run_hidden(rows_in, gate_mats, up_mats)
-    outputs = run_down(hidden, down_mats, chips)
+    hidden, slope, activated = run_hidden(
+        rows_in, gate_mats, up_mats, [grad_hops[step][1] for step in (1, -1)]
+    )
+    outputs = run_down(hidden, down_mats, chips, [grad_hops[step][2] for step in (1, -1)])
     rows_grad = gather_rows(grad_shards)
-    d_pre_gate, d_pre_up, per_token = run_d_hidden(
-        ids, rows_grad, outputs, pick, slope, activated, down_mats, ()
-    )
-    mixed, mixed_hops = ring_reduce(scatter_rows(outputs), chips, 1)
+    d_pre_gate, d_pre_up = run_d_hidden(rows_grad, slope, activated, down_mats)
+    behind = {(step, 1): (d_pre_gate,) for step in (1, -1)}
+    mixed, mixed_hops = ring_reduce(scatter_rows(outputs), chips, 1, behind)
     d_copies = run_d_copy(
-        d_pre_gate, d_pre_up, gate_mats, up_mats, chips, [mixed_hops[step][1] for step in (1, -1)]
-    )
-
+        d_pre_gate, d_pre_up, gate_mats, up_mats, chips, [mixed_hops[step][0] for step in (1, -1)]
+    )
+
+    per_token = run_d_gates(ids, rows_grad, outputs, pick, (d_pre_gate,))
     returned = lax.all_to_all(per_token, "ep", split_axis=0, concat_axis=0, tiled=True)
     behind = {
         (step, hop): (mixed_hops[step][hop + 1],)
         for step in (1, -1)
         for hop in range(len(mixed_hops[step]) - 1)
     }
+    behind[-1, 1] += (per_token,)
     d_tokens, _ = ring_reduce(scatter_rows(d_copies), chips, -1, behind)
     chip_ids = jnp.arange(chips, dtype=jnp.int32)
     served = jnp.stack([core * chips + chip_ids, (1 - core) * chips + chip_ids], axis=1)

time: 232 us -> 215 us (0.927)
  waiting for transfers between devices: 104 us -> 88.2 us
  matrix products: 32 us -> 29.1 us
  starting transfers between devices: 42.1 us -> 39.3 us
    ppermute x28, waiting for transfers between devices: 88.1 us -> 72.4 us  [ring_shift(): return lax.ppermute(array, 'ep', pairs)]
    slice x5 -> x7, local copies, waits for them, and re-layouts: 3.25 us -> 4.95 us  [after(): other[(slice(0, 1),) * other.ndim].reshape((1,) * array.ndim)]
    pallas_call x6 -> x7, Pallas kernels: 38 us -> 39.2 us  [call_kernel(): pl.pallas_call(body, out_shape=outs, in_specs=[pl.BlockSpec(memory_space=...]
    unnamed x30 -> x28, local copies, waits for them, and re-layouts: 4.66 us -> 4.67 us
  transfers between devices with their start and end apart: 33 -> 33, of which waited for: 17 -> 12; matrix products, arithmetic and copies ran while one was open for 15% -> 16% of each run, Pallas kernels for 16% -> 16%
where the time goes in v9:
time: 215 us; the launch traced here: 214 us
  waiting for transfers between devices  88.2 us (41%)
  starting transfers between devices  39.3 us (18%)
  Pallas kernels  39.2 us (18%)
  matrix products  29.1 us (14%)
  local copies, waits for them, and re-layouts  10.2 us (5%)
  between operations  5.69 us (3%)
    ppermute x28, waiting for transfers between devices, ring_shift(): return lax.ppermute(array, 'ep', pairs)  72.4 us
    pallas_call x7, Pallas kernels, call_kernel(): pl.pallas_call(body, out_shape=outs, in_specs=[pl.BlockSpec(memory_space=...  39.2 us
    ppermute x28, starting transfers between devices, ring_shift(): return lax.ppermute(array, 'ep', pairs)  28.7 us
    dot_general x16, matrix products, share_of(): lax.dot_general(spread[s], blocks[s], (((0,), (0,)), ((), ())), preferred...  17.4 us
    dot_general x16, matrix products, gather_rows(): jnp.dot(pick[s], shards[s], preferred_element_type=f32).astype(bf16)  11.7 us
    all_to_all x1, waiting for transfers between devices, body_ring(): lax.all_to_all(copies, 'ep', split_axis=0, concat_axis=0, tiled=True)  9.31 us
    all_to_all x1, waiting for transfers between devices, body_ring(): lax.all_to_all(per_token, 'ep', split_axis=0, concat_axis=0, tiled=True)  6.44 us
    all_to_all x1, starting transfers between devices, body_ring(): lax.all_to_all(copies, 'ep', split_axis=0, concat_axis=0, tiled=True)  6.25 us
  transfers between devices with their start and end apart: 33, of which 12 were waited for; matrix products, arithmetic and copies ran while one was open for 16% of the time, Pallas kernels for 16%

profile of v9, /device:TPU:0, one launch (start us, length us, event | category | flops | bytes accessed | tf_op | source)
XLA Modules:
  0.0 213.9 jit_solution(8181599583634035517)
XLA Ops:
  1.7 2.6 %collective-permute-start = (bf16[128,2048]{1,0:T(8,128)(2,1)}, bf16[128,2048]{1,0:T(8,128)(2,1)}, u32[]{:S(2)}, u32[]{:S(2)}) collective-permute-start(bf16[128,2048]{1,0:T(8,128)(2,1)} %param.7), channel_id=1, source_target_pairs={{0,1},{2,0},{4,2},{6,4},{7,6},{5,7},{3,5},{1,3},{8,9},{10,8},{12,1... | collective-permute-start | bytes 1572872 | tf_op jit(solution)/shard_map/ppermute | solution.py:95
  6.3 6.3 %all-to-all-start = ((f32[8,8,128]{2,1,0:T(8,128)}), f32[8,8,128]{2,1,0:T(8,128)S(1)}, u32[]{:S(2)}, u32[]{:S(2)}) async-start(f32[8,8,128]{2,1,0:T(8,128)} %broadcast_in_dim.10), calls=%async_computation | async-start | bytes 65536 | tf_op jit(solution)/shard_map/all_to_all | solution.py:460
  12.6 9.3 %all-to-all-done.refs_1_ = f32[8,8,128]{2,1,0:T(8,128)S(1)} async-done(((f32[8,8,128]{2,1,0:T(8,128)}), f32[8,8,128]{2,1,0:T(8,128)S(1)}, u32[]{:S(2)}, u32[]{:S(2)}) %all-to-all-start) | async-done | bytes 32800 | tf_op jit(solution)/shard_map/all_to_all | solution.py:460
  24.7 1.6 collective-permute-start.7
  26.2 2.1 convolution_convert_fusion.19.refs_0_
  28.3 2.0 convolution_convert_fusion.12.refs_7_
  30.3 2.1 convolution_convert_fusion.18.refs_1_
  32.4 4.9 %collective-permute-done.1.refs_0_.refs_2_ = bf16[128,2048]{1,0:T(8,128)(2,1)} collective-permute-done((bf16[128,2048]{1,0:T(8,128)(2,1)}, bf16[128,2048]{1,0:T(8,128)(2,1)}, u32[]{:S(2)}, u32[]{:S(2)}) %collective-permute-start.1) | collective-permute-done | bytes 524320 | tf_op jit(solution)/shard_map/ppermute | solution.py:95
  37.4 1.7 copy-done
  40.7 1.6 collective-permute-start.8
  42.3 1.3 convolution_convert_fusion.13.refs_6_
  44.0 1.7 collective-permute-start.12
  46.1 1.3 convolution_convert_fusion.17.refs_2_
  47.8 8.0 %collective-permute-done.8 = bf16[128,2048]{1,0:T(8,128)(2,1)S(1)} collective-permute-done((bf16[128,2048]{1,0:T(8,128)(2,1)}, bf16[128,2048]{1,0:T(8,128)(2,1)S(1)}, u32[]{:S(2)}, u32[]{:S(2)}) %collective-permute-start.8) | collective-permute-done | bytes 524320 | tf_op jit(solution)/shard_map/ppermute | solution.py:95
  55.7 1.6 collective-permute-start.9
  57.6 9.3 %collective-permute-done.10 = bf16[128,2048]{1,0:T(8,128)(2,1)S(1)} collective-permute-done((bf16[128,2048]{1,0:T(8,128)(2,1)}, bf16[128,2048]{1,0:T(8,128)(2,1)S(1)}, u32[]{:S(2)}, u32[]{:S(2)}) %collective-permute-start.10) | collective-permute-done | bytes 524320 | tf_op jit(solution)/shard_map/ppermute | solution.py:95
  67.0 1.6 collective-permute-start.11
  69.8 10.4 %collective-permute-done.13.refs_13_ = bf16[128,2048]{1,0:T(8,128)(2,1)S(1)} collective-permute-done((bf16[128,2048]{1,0:T(8,128)(2,1)S(1)}, bf16[128,2048]{1,0:T(8,128)(2,1)S(1)}, u32[]{:S(2)}, u32[]{:S(2)}) %collective-permute-start.13) | collective-permute-done | bytes 524320 | tf_op jit(solution)/shard_map/ppermute | solution.py:95
  81.1 5.6 %collective-permute-done.11.refs_12_ = bf16[128,2048]{1,0:T(8,128)(2,1)S(1)} collective-permute-done((bf16[128,2048]{1,0:T(8,128)(2,1)S(1)}, bf16[128,2048]{1,0:T(8,128)(2,1)S(1)}, u32[]{:S(2)}, u32[]{:S(2)}) %collective-permute-start.11) | collective-permute-done | bytes 524320 | tf_op jit(solution)/shard_map/ppermute | solution.py:95
  86.7 1.6 collective-permute-start.14
  89.2 10.5 %shard_map.100 = (bf16[2,384,768]{2,1,0:T(8,128)(2,1)S(1)}, f32[2,384,768]{2,1,0:T(8,128)}, f32[2,384,768]{2,1,0:T(8,128)}) custom-call(bf16[96,2048]{1,0:T(8,128)(2,1)S(1)} %copy-done.8, bf16[96,2048]{1,0:T(8,128)(2,1)S(1)} %copy-done.10, bf16[96,2048]{1,0:T(8,128)(2,1)S(1)} %convolution_convert_fusion.17.refs_2_, ...), custom_call_target="tpu_custom_call" | custom-call | flops 4831838208 | bytes 1048576 | tf_op jit(solution)/shard_map/pallas_call | solution.py:168
  99.7 4.7 %shard_map.101.refs_9_ = bf16[8,96,2048]{2,1,0:T(8,128)(2,1)S(1)} custom-call(bf16[2,384,768]{2,1,0:T(8,128)(2,1)S(1)} %get-tuple-element.12.refs_0_, bf16[768,2048]{1,0:T(8,128)(2,1)} %bitcast.161, bf16[768,2048]{1,0:T(8,128)(2,1)} %collective-permute-done.4.refs_3_.refs_5_.refs_2_.refs_11_, bf16[128,2048]{1,0:T(8,128)(2,1)S(1)} %collective-permute-done.14.refs_3_, ...), custom_call_target="tpu_custom_call" | custom-call | flops 2415919104 | bytes 1048576 | tf_op jit(solution)/shard_map/pallas_call | solution.py:168
  105.5 1.7 collective-permute-start.16
  108.1 11.5 %collective-permute-done.17 = bf16[128,2048]{1,0:T(8,128)(2,1)S(1)} collective-permute-done((bf16[128,2048]{1,0:T(8,128)(2,1)S(1)}, bf16[128,2048]{1,0:T(8,128)(2,1)S(1)}, u32[]{:S(2)}, u32[]{:S(2)}) %collective-permute-start.17) | collective-permute-done | bytes 524320 | tf_op jit(solution)/shard_map/ppermute | solution.py:95
  119.9 9.6 %shard_map.102 = (bf16[2,384,768]{2,1,0:T(8,128)(2,1)S(1)}, bf16[2,384,768]{2,1,0:T(8,128)(2,1)S(1)}) custom-call(bf16[96,2048]{1,0:T(8,128)(2,1)S(1)} %convolution_convert_fusion.11.refs_0_.refs_1_, bf16[96,2048]{1,0:T(8,128)(2,1)S(1)} %convolution_convert_fusion.10.refs_1_.refs_2_, bf16[96,2048]{1,0:T(8,128)(2,1)S(1)} %convolution_convert_fusion.9.refs_2_.refs_3_, ...), custom_call_target="tpu_custom_call" | custom-call | flops 2415919104 | bytes 1048576 | tf_op jit(solution)/shard_map/pallas_call | solution.py:168
  131.8 1.7 collective-permute-start.18
  133.5 10.2 %shard_map.103 = bf16[8,96,2048]{2,1,0:T(8,128)(2,1)} custom-call(bf16[2,384,768]{2,1,0:T(8,128)(2,1)S(1)} %get-tuple-element.15.refs_0_.refs_11_, bf16[2,384,768]{2,1,0:T(8,128)(2,1)S(1)} %get-tuple-element.16.refs_1_, bf16[2048,768]{1,0:T(8,128)(2,1)} %bitcast.165, bf16[2048,768]{1,0:T(8,128)(2,1)} %copy-done, bf16[2048,768]{1,0:T(8,128)(2,1)} %bitcast.168, ...), custom_call_target="tpu_custom_call" | custom-call | flops 4831838208 | bytes 1048576 | tf_op jit(solution)/shard_map/pallas_call | solution.py:168
  145.7 1.3 fusion.14
  147.0 0.9 collective-permute-start.24
  148.2 1.2 collective-permute-start.19
  149.5 3.4 %shard_map.104 = f32[8,2,128]{2,1,0:T(2,128)} custom-call(s32[2]{0:T(128)S(1)} %pad_add_fusion.1.refs_0_, bf16[96,2048]{1,0:T(8,128)(2,1)S(1)} %convolution_convert_fusion.11.refs_0_.refs_1_, bf16[96,2048]{1,0:T(8,128)(2,1)S(1)} %convolution_convert_fusion.10.refs_1_.refs_2_, bf16[96,2048]{1,0:T(8,128)(2,1)S(1)} %convolution_convert_fusion.9.refs_2_.refs_3_, ...), custom_call_target="tpu_custom_call" | custom-call | flops 1048576 | bytes 1048576 | tf_op jit(solution)/shard_map/pallas_call | solution.py:168
  152.9 1.2 slice.189
  156.2 1.7 collective-permute-start.28
  159.1 7.9 %collective-permute-done.24 = bf16[128,2048]{1,0:T(8,128)(2,1)S(1)} collective-permute-done((bf16[128,2048]{1,0:T(8,128)(2,1)S(1)}, bf16[128,2048]{1,0:T(8,128)(2,1)S(1)}, u32[]{:S(2)}, u32[]{:S(2)}) %collective-permute-start.24) | collective-permute-done | bytes 524320 | tf_op jit(solution)/shard_map/ppermute | solution.py:95
  169.0 2.1 fusion.3
  171.1 1.6 collective-permute-start.20
  172.8 1.1 fusion.16
  174.2 6.6 %collective-permute-done.25 = bf16[128,2048]{1,0:T(8,128)(2,1)S(1)} collective-permute-done((bf16[128,2048]{1,0:T(8,128)(2,1)S(1)}, bf16[128,2048]{1,0:T(8,128)(2,1)S(1)}, u32[]{:S(2)}, u32[]{:S(2)}) %collective-permute-start.25) | collective-permute-done | bytes 524320 | tf_op jit(solution)/shard_map/ppermute | solution.py:95
  180.8 1.1 fusion.10
  182.8 1.2 slice.195
  184.6 7.6 %collective-permute-done.29 = bf16[128,2048]{1,0:T(8,128)(2,1)} collective-permute-done((bf16[128,2048]{1,0:T(8,128)(2,1)}, bf16[128,2048]{1,0:T(8,128)(2,1)}, u32[]{:S(2)}, u32[]{:S(2)}) %collective-permute-start.29) | collective-permute-done | bytes 524320 | tf_op jit(solution)/shard_map/ppermute | solution.py:95
  192.3 2.2 %fusion.17 = bf16[128,2048]{1,0:T(8,128)(2,1)} fusion(bf16[128,2048]{1,0:T(8,128)(2,1)} %collective-permute-done.29, bf16[8,96,2048]{2,1,0:T(8,128)(2,1)S(1)} %copy-done.11, bf16[]{:T(256)} %bitcast.44, bf16[8,96,128]{2,1,0:T(8,128)(2,1)S(1)} %get-tuple-element.10), kind=kOutput, calls=%fused_computation.49 | convolution fusion | flops 51380224 | bytes 1466370 | tf_op jit(solution)/shard_map/dot_general | solution.py:482
  194.4 1.6 collective-permute-start.30
  196.1 2.2 %fusion.9 = bf16[128,2048]{1,0:T(8,128)(2,1)} fusion(bf16[128,2048]{1,0:T(8,128)(2,1)} %collective-permute-done.26, bf16[8,96,2048]{2,1,0:T(8,128)(2,1)S(1)} %copy-done.11, bf16[8,96,128]{2,1,0:T(8,128)(2,1)S(1)} %get-tuple-element.10), kind=kOutput, calls=%fused_computation.21 | convolution fusion | flops 51118080 | bytes 1466368 | tf_op jit(solution)/shard_map/dot_general | solution.py:482
  198.6 3.3 %all-to-all-start.1 = ((f32[8,2,128]{2,1,0:T(2,128)}), f32[8,2,128]{2,1,0:T(2,128)S(1)}, u32[]{:S(2)}, u32[]{:S(2)}) async-start(f32[8,2,128]{2,1,0:T(2,128)} %shard_map.104), calls=%async_computation.1 | async-start | bytes 16384 | tf_op jit(solution)/shard_map/all_to_all | solution.py:507
  202.0 6.4 %all-to-all-done.1 = f32[8,2,128]{2,1,0:T(2,128)S(1)} async-done(((f32[8,2,128]{2,1,0:T(2,128)}), f32[8,2,128]{2,1,0:T(2,128)S(1)}, u32[]{:S(2)}, u32[]{:S(2)}) %all-to-all-start.1) | async-done | bytes 8224 | tf_op jit(solution)/shard_map/all_to_all | solution.py:507
  209.1 2.5 %fusion.2 = bf16[128,2048]{1,0:T(8,128)(2,1)} fusion(bf16[128,2048]{1,0:T(8,128)(2,1)} %copy-done.12, bf16[128,2048]{1,0:T(8,128)(2,1)} %collective-permute-done.20, bf16[8,96,2048]{2,1,0:T(8,128)(2,1)} %copy-done.1, bf16[8,96,128]{2,1,0:T(8,128)(2,1)S(1)} %get-tuple-element.10), kind=kOutput, calls=%fused_computation.14 | convolution fusion | flops 51642368 | bytes 1990656 | tf_op jit(solution)/shard_map/dot_general | solution.py:482
  211.6 2.3 %fusion.8 = bf16[128,2048]{1,0:T(8,128)(2,1)} fusion(bf16[128,2048]{1,0:T(8,128)(2,1)} %collective-permute-done.30, bf16[128,2048]{1,0:T(8,128)(2,1)} %collective-permute-done.27, bf16[8,96,2048]{2,1,0:T(8,128)(2,1)S(1)} %copy-done.11, bf16[8,96,128]{2,1,0:T(8,128)(2,1)S(1)} %get-tuple-element.10), kind=kOutput, calls=%fused_computation.20 | convolution fusion | flops 51642368 | bytes 1990656 | tf_op jit(solution)/shard_map/dot_general | solution.py:482
  (105 shorter events, 21.9 us)
Async XLA Ops:
  0.6 36.7 %collective-permute-start.2 = (bf16[2048,768]{1,0:T(8,128)(2,1)}, bf16[2048,768]{1,0:T(8,128)(2,1)S(1)}, u32[]{:S(2)}, u32[]{:S(2)}) collective-permute-start(bf16[2048,768]{1,0:T(8,128)(2,1)} %bitcast.163), channel_id=1, source_target_pairs={{0,8},{8,0},{1,9},{9,1},{2,10},{10,2},{3,11},{11,3},{4,12},{12,4},... | collective-permute-start | bytes 9437192 | tf_op jit(solution)/shard_map/ppermute | solution.py:443
  1.1 36.2 %collective-permute-start.3 = (bf16[2048,768]{1,0:T(8,128)(2,1)}, bf16[2048,768]{1,0:T(8,128)(2,1)}, u32[]{:S(2)}, u32[]{:S(2)}) collective-permute-start(bf16[2048,768]{1,0:T(8,128)(2,1)} %bitcast.166), channel_id=1, source_target_pairs={{0,8},{8,0},{1,9},{9,1},{2,10},{10,2},{3,11},{11,3},{4,12},{12,4},... | collective-permute-start | bytes 9437192 | tf_op jit(solution)/shard_map/ppermute | solution.py:443
  1.2 36.1 %collective-permute-start.4 = (bf16[768,2048]{1,0:T(8,128)(2,1)}, bf16[768,2048]{1,0:T(8,128)(2,1)}, u32[]{:S(2)}, u32[]{:S(2)}) collective-permute-start(bf16[768,2048]{1,0:T(8,128)(2,1)} %bitcast.160), channel_id=1, source_target_pairs={{0,8},{8,0},{1,9},{9,1},{2,10},{10,2},{3,11},{11,3},{4,12},{12,4},... | collective-permute-start | bytes 9437192 | tf_op jit(solution)/shard_map/ppermute | solution.py:443
  1.7 22.4 %collective-permute-start = (bf16[128,2048]{1,0:T(8,128)(2,1)}, bf16[128,2048]{1,0:T(8,128)(2,1)}, u32[]{:S(2)}, u32[]{:S(2)}) collective-permute-start(bf16[128,2048]{1,0:T(8,128)(2,1)} %param.7), channel_id=1, source_target_pairs={{0,1},{2,0},{4,2},{6,4},{7,6},{5,7},{3,5},{1,3},{8,9},{10,8},{12,1... | collective-permute-start | bytes 1572872 | tf_op jit(solution)/shard_map/ppermute | solution.py:95
  4.2 20.4 %collective-permute-start.6 = (bf16[128,2048]{1,0:T(8,128)(2,1)}, bf16[128,2048]{1,0:T(8,128)(2,1)}, u32[]{:S(2)}, u32[]{:S(2)}) collective-permute-start(bf16[128,2048]{1,0:T(8,128)(2,1)} %param.7), channel_id=1, source_target_pairs={{0,2},{2,4},{4,6},{6,7},{7,5},{5,3},{3,1},{1,0},{8,10},{10,12},{12... | collective-permute-start | bytes 1572872 | tf_op jit(solution)/shard_map/ppermute | solution.py:95
  6.3 15.6 %all-to-all-start = ((f32[8,8,128]{2,1,0:T(8,128)}), f32[8,8,128]{2,1,0:T(8,128)S(1)}, u32[]{:S(2)}, u32[]{:S(2)}) async-start(f32[8,8,128]{2,1,0:T(8,128)} %broadcast_in_dim.10), calls=%async_computation | async-start | bytes 65536 | tf_op jit(solution)/shard_map/all_to_all | solution.py:460
  21.9 0.6 copy-start.6
  22.6 0.8 copy-start.7
  24.1 13.2 %collective-permute-start.1 = (bf16[128,2048]{1,0:T(8,128)(2,1)}, bf16[128,2048]{1,0:T(8,128)(2,1)}, u32[]{:S(2)}, u32[]{:S(2)}) collective-permute-start(bf16[128,2048]{1,0:T(8,128)(2,1)} %shard_map.95), channel_id=1, source_target_pairs={{0,1},{2,0},{4,2},{6,4},{7,6},{5,7},{3,5},{1,3},{8,9},{10,8},{12,1... | collective-permute-start | bytes 1572872 | tf_op jit(solution)/shard_map/ppermute | solution.py:95
  24.7 12.7 %copy-start.5 = (bf16[128,2048]{1,0:T(8,128)(2,1)S(1)}, bf16[128,2048]{1,0:T(8,128)(2,1)}, u32[]{:S(2)}) copy-start(bf16[128,2048]{1,0:T(8,128)(2,1)} %refs_0_.1) | copy-start | bytes 1572868
  24.7 12.7 %collective-permute-start.7 = (bf16[128,2048]{1,0:T(8,128)(2,1)}, bf16[128,2048]{1,0:T(8,128)(2,1)S(1)}, u32[]{:S(2)}, u32[]{:S(2)}) collective-permute-start(bf16[128,2048]{1,0:T(8,128)(2,1)} %shard_map.97), channel_id=1, source_target_pairs={{0,2},{2,4},{4,6},{6,7},{7,5},{5,3},{3,1},{1,0},{8,10},{10,12},{12... | collective-permute-start | bytes 1572872 | tf_op jit(solution)/shard_map/ppermute | solution.py:95
  37.3 1.7 copy-start
  39.1 0.8 copy-start.2
  39.9 0.8 copy-start.3
  40.7 15.1 %collective-permute-start.8 = (bf16[128,2048]{1,0:T(8,128)(2,1)}, bf16[128,2048]{1,0:T(8,128)(2,1)S(1)}, u32[]{:S(2)}, u32[]{:S(2)}) collective-permute-start(bf16[128,2048]{1,0:T(8,128)(2,1)} %shard_map.98), channel_id=1, source_target_pairs={{0,2},{2,4},{4,6},{6,7},{7,5},{5,3},{3,1},{1,0},{8,10},{10,12},{12... | collective-permute-start | bytes 1572872 | tf_op jit(solution)/shard_map/ppermute | solution.py:95
  43.6 3.8 %copy-start.4 = (bf16[128,2048]{1,0:T(8,128)(2,1)S(1)}, bf16[128,2048]{1,0:T(8,128)(2,1)}, u32[]{:S(2)}) copy-start(bf16[128,2048]{1,0:T(8,128)(2,1)} %copy-done.3) | copy-start | bytes 1572868
  43.7 23.3 %collective-permute-start.10 = (bf16[128,2048]{1,0:T(8,128)(2,1)}, bf16[128,2048]{1,0:T(8,128)(2,1)S(1)}, u32[]{:S(2)}, u32[]{:S(2)}) collective-permute-start(bf16[128,2048]{1,0:T(8,128)(2,1)} %copy-done.3), channel_id=1, source_target_pairs={{0,2},{2,4},{4,6},{6,7},{7,5},{5,3},{3,1},{1,0},{8,10},{10,12},{12... | collective-permute-start | bytes 1572872 | tf_op jit(solution)/shard_map/ppermute | solution.py:95
  44.0 24.6 %collective-permute-start.12 = (bf16[128,2048]{1,0:T(8,128)(2,1)}, bf16[128,2048]{1,0:T(8,128)(2,1)S(1)}, u32[]{:S(2)}, u32[]{:S(2)}) collective-permute-start(bf16[128,2048]{1,0:T(8,128)(2,1)} %copy-done.3), channel_id=1, source_target_pairs={{0,1},{2,0},{4,2},{6,4},{7,6},{5,7},{3,5},{1,3},{8,9},{10,8},{12,1... | collective-permute-start | bytes 1572872 | tf_op jit(solution)/shard_map/ppermute | solution.py:95
  45.7 23.8 %collective-permute-start.5 = (bf16[128,2048]{1,0:T(8,128)(2,1)}, bf16[128,2048]{1,0:T(8,128)(2,1)S(1)}, u32[]{:S(2)}, u32[]{:S(2)}) collective-permute-start(bf16[128,2048]{1,0:T(8,128)(2,1)} %shard_map.96), channel_id=1, source_target_pairs={{0,1},{2,0},{4,2},{6,4},{7,6},{5,7},{3,5},{1,3},{8,9},{10,8},{12,1... | collective-permute-start | bytes 1572872 | tf_op jit(solution)/shard_map/ppermute | solution.py:95
  47.7 41.4 %copy-start.8 = (bf16[96,2048]{1,0:T(8,128)(2,1)S(1)}, bf16[96,2048]{1,0:T(8,128)(2,1)}, u32[]{:S(2)}) copy-start(bf16[96,2048]{1,0:T(8,128)(2,1)} %convolution_convert_fusion.19.refs_0_) | copy-start | bytes 1179652
  47.7 41.4 %copy-start.9 = (bf16[96,2048]{1,0:T(8,128)(2,1)S(1)}, bf16[96,2048]{1,0:T(8,128)(2,1)}, u32[]{:S(2)}) copy-start(bf16[96,2048]{1,0:T(8,128)(2,1)} %convolution_convert_fusion.12.refs_7_) | copy-start | bytes 1179652
  47.8 41.4 %copy-start.10 = (bf16[96,2048]{1,0:T(8,128)(2,1)S(1)}, bf16[96,2048]{1,0:T(8,128)(2,1)}, u32[]{:S(2)}) copy-start(bf16[96,2048]{1,0:T(8,128)(2,1)} %convolution_convert_fusion.18.refs_1_) | copy-start | bytes 1179652
  55.7 33.1 %collective-permute-start.9 = (bf16[128,2048]{1,0:T(8,128)(2,1)S(1)}, bf16[128,2048]{1,0:T(8,128)(2,1)S(1)}, u32[]{:S(2)}, u32[]{:S(2)}) collective-permute-start(bf16[128,2048]{1,0:T(8,128)(2,1)S(1)} %collective-permute-done.8), channel_id=1, source_target_pairs={{0,2},{2,4},{4,6},{6,7},{7,5},{5,3},{3,1},{1,0},{8,10},{10,12},{12... | collective-permute-start | bytes 1572872 | tf_op jit(solution)/shard_map/ppermute | solution.py:95
  67.0 19.7 %collective-permute-start.11 = (bf16[128,2048]{1,0:T(8,128)(2,1)S(1)}, bf16[128,2048]{1,0:T(8,128)(2,1)S(1)}, u32[]{:S(2)}, u32[]{:S(2)}) collective-permute-start(bf16[128,2048]{1,0:T(8,128)(2,1)S(1)} %collective-permute-done.10), channel_id=1, source_target_pairs={{0,2},{2,4},{4,6},{6,7},{7,5},{5,3},{3,1},{1,0},{8,10},{10,12},{12... | collective-permute-start | bytes 1572872 | tf_op jit(solution)/shard_map/ppermute | solution.py:95
  68.6 11.6 %collective-permute-start.13 = (bf16[128,2048]{1,0:T(8,128)(2,1)S(1)}, bf16[128,2048]{1,0:T(8,128)(2,1)S(1)}, u32[]{:S(2)}, u32[]{:S(2)}) collective-permute-start(bf16[128,2048]{1,0:T(8,128)(2,1)S(1)} %collective-permute-done.12), channel_id=1, source_target_pairs={{0,1},{2,0},{4,2},{6,4},{7,6},{5,7},{3,5},{1,3},{8,9},{10,8},{12,1... | collective-permute-start | bytes 1572872 | tf_op jit(solution)/shard_map/ppermute | solution.py:95
  80.2 19.5 %collective-permute-start.15 = (bf16[128,2048]{1,0:T(8,128)(2,1)S(1)}, bf16[128,2048]{1,0:T(8,128)(2,1)S(1)}, u32[]{:S(2)}, u32[]{:S(2)}) collective-permute-start(bf16[128,2048]{1,0:T(8,128)(2,1)S(1)} %collective-permute-done.13.refs_13_), channel_id=1, source_target_pairs={{0,1},{2,0},{4,2},{6,4},{7,6},{5,7},{3,5},{1,3},{8,9},{10,8},{12,1... | collective-permute-start | bytes 1572872 | tf_op jit(solution)/shard_map/ppermute | solution.py:95
  86.7 13.0 %collective-permute-start.14 = (bf16[128,2048]{1,0:T(8,128)(2,1)S(1)}, bf16[128,2048]{1,0:T(8,128)(2,1)S(1)}, u32[]{:S(2)}, u32[]{:S(2)}) collective-permute-start(bf16[128,2048]{1,0:T(8,128)(2,1)S(1)} %collective-permute-done.11.refs_12_), channel_id=1, source_target_pairs={{0,2},{2,4},{4,6},{6,7},{7,5},{5,3},{3,1},{1,0},{8,10},{10,12},{12... | collective-permute-start | bytes 1572872 | tf_op jit(solution)/shard_map/ppermute | solution.py:95
  104.4 43.5 %copy-start.1 = (bf16[8,96,2048]{2,1,0:T(8,128)(2,1)}, bf16[8,96,2048]{2,1,0:T(8,128)(2,1)S(1)}, u32[]{:S(2)}) copy-start(bf16[8,96,2048]{2,1,0:T(8,128)(2,1)S(1)} %shard_map.101.refs_9_) | copy-start | bytes 9437188
  104.7 14.9 %collective-permute-start.17 = (bf16[128,2048]{1,0:T(8,128)(2,1)S(1)}, bf16[128,2048]{1,0:T(8,128)(2,1)S(1)}, u32[]{:S(2)}, u32[]{:S(2)}) collective-permute-start(bf16[128,2048]{1,0:T(8,128)(2,1)S(1)} %collective-permute-done.15.refs_4_), channel_id=1, source_target_pairs={{0,1},{2,0},{4,2},{6,4},{7,6},{5,7},{3,5},{1,3},{8,9},{10,8},{12,1... | collective-permute-start | bytes 1572872 | tf_op jit(solution)/shard_map/ppermute | solution.py:95
  105.5 26.0 %collective-permute-start.16 = (bf16[128,2048]{1,0:T(8,128)(2,1)S(1)}, bf16[128,2048]{1,0:T(8,128)(2,1)S(1)}, u32[]{:S(2)}, u32[]{:S(2)}) collective-permute-start(bf16[128,2048]{1,0:T(8,128)(2,1)S(1)} %convolution_convert_fusion.3), channel_id=1, source_target_pairs={{0,2},{2,4},{4,6},{6,7},{7,5},{5,3},{3,1},{1,0},{8,10},{10,12},{12... | collective-permute-start | bytes 1572872 | tf_op jit(solution)/shard_map/ppermute | solution.py:95
  107.2 23.5 %collective-permute-start.21 = (bf16[128,2048]{1,0:T(8,128)(2,1)S(1)}, bf16[128,2048]{1,0:T(8,128)(2,1)S(1)}, u32[]{:S(2)}, u32[]{:S(2)}) collective-permute-start(bf16[128,2048]{1,0:T(8,128)(2,1)S(1)} %convolution_convert_fusion.2), channel_id=1, source_target_pairs={{0,1},{2,0},{4,2},{6,4},{7,6},{5,7},{3,5},{1,3},{8,9},{10,8},{12,1... | collective-permute-start | bytes 1572872 | tf_op jit(solution)/shard_map/ppermute | solution.py:95
  131.0 12.7 %collective-permute-start.22 = (bf16[128,2048]{1,0:T(8,128)(2,1)S(1)}, bf16[128,2048]{1,0:T(8,128)(2,1)S(1)}, u32[]{:S(2)}, u32[]{:S(2)}) collective-permute-start(bf16[128,2048]{1,0:T(8,128)(2,1)S(1)} %fusion.19), channel_id=1, source_target_pairs={{0,1},{2,0},{4,2},{6,4},{7,6},{5,7},{3,5},{1,3},{8,9},{10,8},{12,1... | collective-permute-start | bytes 1572872 | tf_op jit(solution)/shard_map/ppermute | solution.py:95
  131.8 16.1 %collective-permute-start.18 = (bf16[128,2048]{1,0:T(8,128)(2,1)S(1)}, bf16[128,2048]{1,0:T(8,128)(2,1)S(1)}, u32[]{:S(2)}, u32[]{:S(2)}) collective-permute-start(bf16[128,2048]{1,0:T(8,128)(2,1)S(1)} %fusion.20), channel_id=1, source_target_pairs={{0,2},{2,4},{4,6},{6,7},{7,5},{5,3},{3,1},{1,0},{8,10},{10,12},{12... | collective-permute-start | bytes 1572872 | tf_op jit(solution)/shard_map/ppermute | solution.py:95
  144.1 13.9 %collective-permute-start.23 = (bf16[128,2048]{1,0:T(8,128)(2,1)S(1)}, bf16[128,2048]{1,0:T(8,128)(2,1)S(1)}, u32[]{:S(2)}, u32[]{:S(2)}) collective-permute-start(bf16[128,2048]{1,0:T(8,128)(2,1)S(1)} %fusion.6), channel_id=1, source_target_pairs={{0,1},{2,0},{4,2},{6,4},{7,6},{5,7},{3,5},{1,3},{8,9},{10,8},{12,1... | collective-permute-start | bytes 1572872 | tf_op jit(solution)/shard_map/ppermute | solution.py:95
  147.0 20.0 %collective-permute-start.24 = (bf16[128,2048]{1,0:T(8,128)(2,1)S(1)}, bf16[128,2048]{1,0:T(8,128)(2,1)S(1)}, u32[]{:S(2)}, u32[]{:S(2)}) collective-permute-start(bf16[128,2048]{1,0:T(8,128)(2,1)S(1)} %fusion.14), channel_id=1, source_target_pairs={{0,1},{2,0},{4,2},{6,4},{7,6},{5,7},{3,5},{1,3},{8,9},{10,8},{12,1... | collective-permute-start | bytes 1572872 | tf_op jit(solution)/shard_map/ppermute | solution.py:95
  148.2 7.6 %copy-start.11 = (bf16[8,96,2048]{2,1,0:T(8,128)(2,1)S(1)}, bf16[8,96,2048]{2,1,0:T(8,128)(2,1)}, u32[]{:S(2)}) copy-start(bf16[8,96,2048]{2,1,0:T(8,128)(2,1)} %shard_map.103) | copy-start | bytes 9437188
  148.2 19.6 %collective-permute-start.19 = (bf16[128,2048]{1,0:T(8,128)(2,1)S(1)}, bf16[128,2048]{1,0:T(8,128)(2,1)S(1)}, u32[]{:S(2)}, u32[]{:S(2)}) collective-permute-start(bf16[128,2048]{1,0:T(8,128)(2,1)S(1)} %fusion.4), channel_id=1, source_target_pairs={{0,2},{2,4},{4,6},{6,7},{7,5},{5,3},{3,1},{1,0},{8,10},{10,12},{12... | collective-permute-start | bytes 1572872 | tf_op jit(solution)/shard_map/ppermute | solution.py:95
  156.2 16.5 %collective-permute-start.28 = (bf16[128,2048]{1,0:T(8,128)(2,1)S(1)}, bf16[128,2048]{1,0:T(8,128)(2,1)S(1)}, u32[]{:S(2)}, u32[]{:S(2)}) collective-permute-start(bf16[128,2048]{1,0:T(8,128)(2,1)S(1)} %fusion.15), channel_id=1, source_target_pairs={{0,2},{2,4},{4,6},{6,7},{7,5},{5,3},{3,1},{1,0},{8,10},{10,12},{12... | collective-permute-start | bytes 1572872 | tf_op jit(solution)/shard_map/ppermute | solution.py:95
  157.9 22.9 %copy-start.12 = (bf16[128,2048]{1,0:T(8,128)(2,1)}, bf16[128,2048]{1,0:T(8,128)(2,1)S(1)}, u32[]{:S(2)}) copy-start(bf16[128,2048]{1,0:T(8,128)(2,1)S(1)} %collective-permute-done.23) | copy-start | bytes 1572868
  167.4 13.4 %collective-permute-start.25 = (bf16[128,2048]{1,0:T(8,128)(2,1)S(1)}, bf16[128,2048]{1,0:T(8,128)(2,1)S(1)}, u32[]{:S(2)}, u32[]{:S(2)}) collective-permute-start(bf16[128,2048]{1,0:T(8,128)(2,1)S(1)} %fusion.21), channel_id=1, source_target_pairs={{0,1},{2,0},{4,2},{6,4},{7,6},{5,7},{3,5},{1,3},{8,9},{10,8},{12,1... | collective-permute-start | bytes 1572872 | tf_op jit(solution)/shard_map/ppermute | solution.py:95
  171.1 37.3 %copy-start.13 = (s32[128,4]{0,1:T(4,128)S(1)}, s32[128,4]{0,1:T(4,128)}, u32[]{:S(2)}) copy-start(s32[128,4]{0,1:T(4,128)} %param.9) | copy-start | bytes 6148
  171.1 11.7 %collective-permute-start.20 = (bf16[128,2048]{1,0:T(8,128)(2,1)}, bf16[128,2048]{1,0:T(8,128)(2,1)}, u32[]{:S(2)}, u32[]{:S(2)}) collective-permute-start(bf16[128,2048]{1,0:T(8,128)(2,1)} %fusion.3), channel_id=1, source_target_pairs={{0,2},{2,4},{4,6},{6,7},{7,5},{5,3},{3,1},{1,0},{8,10},{10,12},{12... | collective-permute-start | bytes 1572872 | tf_op jit(solution)/shard_map/ppermute | solution.py:95
  173.9 18.3 %collective-permute-start.29 = (bf16[128,2048]{1,0:T(8,128)(2,1)}, bf16[128,2048]{1,0:T(8,128)(2,1)}, u32[]{:S(2)}, u32[]{:S(2)}) collective-permute-start(bf16[128,2048]{1,0:T(8,128)(2,1)} %fusion.16), channel_id=1, source_target_pairs={{0,2},{2,4},{4,6},{6,7},{7,5},{5,3},{3,1},{1,0},{8,10},{10,12},{12... | collective-permute-start | bytes 1572872 | tf_op jit(solution)/shard_map/ppermute | solution.py:95
  181.9 14.2 %collective-permute-start.26 = (bf16[128,2048]{1,0:T(8,128)(2,1)}, bf16[128,2048]{1,0:T(8,128)(2,1)}, u32[]{:S(2)}, u32[]{:S(2)}) collective-permute-start(bf16[128,2048]{1,0:T(8,128)(2,1)} %fusion.10), channel_id=1, source_target_pairs={{0,1},{2,0},{4,2},{6,4},{7,6},{5,7},{3,5},{1,3},{8,9},{10,8},{12,1... | collective-permute-start | bytes 1572872 | tf_op jit(solution)/shard_map/ppermute | solution.py:95
  194.4 17.1 %collective-permute-start.30 = (bf16[128,2048]{1,0:T(8,128)(2,1)}, bf16[128,2048]{1,0:T(8,128)(2,1)}, u32[]{:S(2)}, u32[]{:S(2)}) collective-permute-start(bf16[128,2048]{1,0:T(8,128)(2,1)} %fusion.17), channel_id=1, source_target_pairs={{0,2},{2,4},{4,6},{6,7},{7,5},{5,3},{3,1},{1,0},{8,10},{10,12},{12... | collective-permute-start | bytes 1572872 | tf_op jit(solution)/shard_map/ppermute | solution.py:95
  198.2 13.3 %collective-permute-start.27 = (bf16[128,2048]{1,0:T(8,128)(2,1)}, bf16[128,2048]{1,0:T(8,128)(2,1)}, u32[]{:S(2)}, u32[]{:S(2)}) collective-permute-start(bf16[128,2048]{1,0:T(8,128)(2,1)} %fusion.9), channel_id=1, source_target_pairs={{0,1},{2,0},{4,2},{6,4},{7,6},{5,7},{3,5},{1,3},{8,9},{10,8},{12,1... | collective-permute-start | bytes 1572872 | tf_op jit(solution)/shard_map/ppermute | solution.py:95
  198.6 9.8 %all-to-all-start.1 = ((f32[8,2,128]{2,1,0:T(2,128)}), f32[8,2,128]{2,1,0:T(2,128)S(1)}, u32[]{:S(2)}, u32[]{:S(2)}) async-start(f32[8,2,128]{2,1,0:T(2,128)} %shard_map.104), calls=%async_computation.1 | async-start | bytes 16384 | tf_op jit(solution)/shard_map/all_to_all | solution.py:507

commit v10 on v9

--- a/solution.py
+++ b/solution.py
@@ -157,7 +157,7 @@
 
 
 def call_kernel(kernel, operands, kinds, outs, scratch, flops, behind=()):
-    spaces = {"any": pltpu.HBM, "vmem": pltpu.VMEM, "smem": pltpu.SMEM}
+    spaces = {"any": pl.ANY, "vmem": pltpu.VMEM, "smem": pltpu.SMEM}
     count = len(operands)
     operands = [*operands, *behind]
     kinds = [*kinds, *["any" for _ in behind]]
@@ -497,7 +497,7 @@
     outputs = run_down(hidden, down_mats, chips, [grad_hops[step][2] for step in (1, -1)])
     rows_grad = gather_rows(grad_shards)
     d_pre_gate, d_pre_up = run_d_hidden(rows_grad, slope, activated, down_mats)
-    behind = {(step, 1): (d_pre_gate,) for step in (1, -1)}
+    behind = {(-1, 0): (grad_hops[-1][-1],), (-1, 1): (d_pre_gate,)}
     mixed, mixed_hops = ring_reduce(scatter_rows(outputs), chips, 1, behind)
     d_copies = run_d_copy(
         d_pre_gate, d_pre_up, gate_mats, up_mats, chips, [mixed_hops[step][0] for step in (1, -1)]

time: 215 us -> 209 us (0.972)
  waiting for transfers between devices: 88.2 us -> 79.5 us
    ppermute x28, waiting for transfers between devices: 72.4 us -> 63.7 us  [ring_shift(): return lax.ppermute(array, 'ep', pairs)]
    slice x7 -> x8, local copies, waits for them, and re-layouts: 4.95 us -> 5.46 us  [after(): other[(slice(0, 1),) * other.ndim].reshape((1,) * array.ndim)]
  transfers between devices with their start and end apart: 33 -> 33, of which waited for: 12 -> 13; matrix products, arithmetic and copies ran while one was open for 16% -> 17% of each run, Pallas kernels for 16% -> 19%
where the time goes in v10:
time: 209 us; the launch traced here: 208 us
  waiting for transfers between devices  79.5 us (38%)
  starting transfers between devices  41 us (20%)
  Pallas kernels  39.4 us (19%)
  matrix products  29.1 us (14%)
  local copies, waits for them, and re-layouts  10.8 us (5%)
  between operations  6.33 us (3%)
  other arithmetic  2.13 us (1%)
    ppermute x28, waiting for transfers between devices, ring_shift(): return lax.ppermute(array, 'ep', pairs)  63.7 us
    pallas_call x7, Pallas kernels, call_kernel(): pl.pallas_call(body, out_shape=outs, in_specs=[pl.BlockSpec(memory_space=...  39.3 us
    ppermute x28, starting transfers between devices, ring_shift(): return lax.ppermute(array, 'ep', pairs)  30.2 us
    dot_general x16, matrix products, share_of(): lax.dot_general(spread[s], blocks[s], (((0,), (0,)), ((), ())), preferred...  17.4 us
    dot_general x16, matrix products, gather_rows(): jnp.dot(pick[s], shards[s], preferred_element_type=f32).astype(bf16)  11.7 us
    all_to_all x1, waiting for transfers between devices, body_ring(): lax.all_to_all(copies, 'ep', split_axis=0, concat_axis=0, tiled=True)  9.31 us
    all_to_all x1, waiting for transfers between devices, body_ring(): lax.all_to_all(per_token, 'ep', split_axis=0, concat_axis=0, tiled=True)  6.51 us
    all_to_all x1, starting transfers between devices, body_ring(): lax.all_to_all(copies, 'ep', split_axis=0, concat_axis=0, tiled=True)  6.25 us
  transfers between devices with their start and end apart: 33, of which 13 were waited for; matrix products, arithmetic and copies ran while one was open for 17% of the time, Pallas kernels for 19%

profile of v10, /device:TPU:0, one launch (start us, length us, event | category | flops | bytes accessed | tf_op | source)
XLA Modules:
  0.0 208.2 jit_solution(16576334388185478477)
XLA Ops:
  1.7 2.6 %collective-permute-start = (bf16[128,2048]{1,0:T(8,128)(2,1)}, bf16[128,2048]{1,0:T(8,128)(2,1)}, u32[]{:S(2)}, u32[]{:S(2)}) collective-permute-start(bf16[128,2048]{1,0:T(8,128)(2,1)} %param.7), channel_id=1, source_target_pairs={{0,1},{2,0},{4,2},{6,4},{7,6},{5,7},{3,5},{1,3},{8,9},{10,8},{12,1... | collective-permute-start | bytes 1572872 | tf_op jit(solution)/shard_map/ppermute | solution.py:95
  6.3 6.3 %all-to-all-start = ((f32[8,8,128]{2,1,0:T(8,128)}), f32[8,8,128]{2,1,0:T(8,128)S(1)}, u32[]{:S(2)}, u32[]{:S(2)}) async-start(f32[8,8,128]{2,1,0:T(8,128)} %broadcast_in_dim.10), calls=%async_computation | async-start | bytes 65536 | tf_op jit(solution)/shard_map/all_to_all | solution.py:460
  12.6 9.3 %all-to-all-done.refs_1_ = f32[8,8,128]{2,1,0:T(8,128)S(1)} async-done(((f32[8,8,128]{2,1,0:T(8,128)}), f32[8,8,128]{2,1,0:T(8,128)S(1)}, u32[]{:S(2)}, u32[]{:S(2)}) %all-to-all-start) | async-done | bytes 32800 | tf_op jit(solution)/shard_map/all_to_all | solution.py:460
  24.7 1.6 collective-permute-start.7
  26.2 2.1 convolution_convert_fusion.19.refs_0_
  28.3 2.0 convolution_convert_fusion.12.refs_7_
  30.3 2.1 %convolution_convert_fusion.18.refs_1_ = bf16[96,2048]{1,0:T(8,128)(2,1)} fusion(bf16[128,2048]{1,0:T(8,128)(2,1)} %shard_map.95, bf16[8,96,128]{2,1,0:T(8,128)(2,1)S(1)} %get-tuple-element.11.refs_10_), kind=kOutput, calls=%fused_computation.44 | convolution fusion | flops 50528256 | bytes 942080 | tf_op jit(solution)/shard_map/dot_general | solution.py:476
  32.4 4.9 %collective-permute-done.1.refs_0_.refs_2_ = bf16[128,2048]{1,0:T(8,128)(2,1)} collective-permute-done((bf16[128,2048]{1,0:T(8,128)(2,1)}, bf16[128,2048]{1,0:T(8,128)(2,1)}, u32[]{:S(2)}, u32[]{:S(2)}) %collective-permute-start.1) | collective-permute-done | bytes 524320 | tf_op jit(solution)/shard_map/ppermute | solution.py:95
  37.4 1.7 copy-done
  40.7 1.6 collective-permute-start.8
  42.3 1.3 convolution_convert_fusion.13.refs_6_
  44.0 1.7 collective-permute-start.12
  46.1 1.3 convolution_convert_fusion.17.refs_2_
  47.8 8.0 %collective-permute-done.8 = bf16[128,2048]{1,0:T(8,128)(2,1)S(1)} collective-permute-done((bf16[128,2048]{1,0:T(8,128)(2,1)}, bf16[128,2048]{1,0:T(8,128)(2,1)S(1)}, u32[]{:S(2)}, u32[]{:S(2)}) %collective-permute-start.8) | collective-permute-done | bytes 524320 | tf_op jit(solution)/shard_map/ppermute | solution.py:95
  55.7 1.6 collective-permute-start.9
  57.6 9.3 %collective-permute-done.10 = bf16[128,2048]{1,0:T(8,128)(2,1)S(1)} collective-permute-done((bf16[128,2048]{1,0:T(8,128)(2,1)}, bf16[128,2048]{1,0:T(8,128)(2,1)S(1)}, u32[]{:S(2)}, u32[]{:S(2)}) %collective-permute-start.10) | collective-permute-done | bytes 524320 | tf_op jit(solution)/shard_map/ppermute | solution.py:95
  67.0 1.6 collective-permute-start.11
  69.8 10.4 %collective-permute-done.13.refs_13_ = bf16[128,2048]{1,0:T(8,128)(2,1)S(1)} collective-permute-done((bf16[128,2048]{1,0:T(8,128)(2,1)S(1)}, bf16[128,2048]{1,0:T(8,128)(2,1)S(1)}, u32[]{:S(2)}, u32[]{:S(2)}) %collective-permute-start.13) | collective-permute-done | bytes 524320 | tf_op jit(solution)/shard_map/ppermute | solution.py:95
  81.1 5.6 %collective-permute-done.11.refs_12_ = bf16[128,2048]{1,0:T(8,128)(2,1)S(1)} collective-permute-done((bf16[128,2048]{1,0:T(8,128)(2,1)S(1)}, bf16[128,2048]{1,0:T(8,128)(2,1)S(1)}, u32[]{:S(2)}, u32[]{:S(2)}) %collective-permute-start.11) | collective-permute-done | bytes 524320 | tf_op jit(solution)/shard_map/ppermute | solution.py:95
  86.7 1.6 collective-permute-start.14
  89.1 10.5 %shard_map.100 = (bf16[2,384,768]{2,1,0:T(8,128)(2,1)S(1)}, f32[2,384,768]{2,1,0:T(8,128)}, f32[2,384,768]{2,1,0:T(8,128)}) custom-call(bf16[96,2048]{1,0:T(8,128)(2,1)S(1)} %copy-done.8, bf16[96,2048]{1,0:T(8,128)(2,1)S(1)} %copy-done.10, bf16[96,2048]{1,0:T(8,128)(2,1)S(1)} %convolution_convert_fusion.17.refs_2_, ...), custom_call_target="tpu_custom_call" | custom-call | flops 4831838208 | bytes 1048576 | tf_op jit(solution)/shard_map/pallas_call | solution.py:168
  100.1 4.7 %shard_map.101.refs_9_ = bf16[8,96,2048]{2,1,0:T(8,128)(2,1)S(1)} custom-call(bf16[2,384,768]{2,1,0:T(8,128)(2,1)S(1)} %get-tuple-element.12.refs_0_, bf16[768,2048]{1,0:T(8,128)(2,1)} %bitcast.166, bf16[768,2048]{1,0:T(8,128)(2,1)} %collective-permute-done.4.refs_3_.refs_5_.refs_2_.refs_11_, bf16[128,2048]{1,0:T(8,128)(2,1)S(1)} %collective-permute-done.14.refs_3_, ...), custom_call_target="tpu_custom_call" | custom-call | flops 2415919104 | bytes 1048576 | tf_op jit(solution)/shard_map/pallas_call | solution.py:168
  105.1 1.7 collective-permute-start.16
  107.1 3.0 %collective-permute-done.20 = bf16[128,2048]{1,0:T(8,128)(2,1)S(1)} collective-permute-done((bf16[128,2048]{1,0:T(8,128)(2,1)S(1)}, bf16[128,2048]{1,0:T(8,128)(2,1)S(1)}, u32[]{:S(2)}, u32[]{:S(2)}) %collective-permute-start.20) | collective-permute-done | bytes 524320 | tf_op jit(solution)/shard_map/ppermute | solution.py:95
  112.9 9.6 %shard_map.102 = (bf16[2,384,768]{2,1,0:T(8,128)(2,1)S(1)}, bf16[2,384,768]{2,1,0:T(8,128)(2,1)S(1)}) custom-call(bf16[96,2048]{1,0:T(8,128)(2,1)S(1)} %convolution_convert_fusion.11.refs_0_.refs_1_, bf16[96,2048]{1,0:T(8,128)(2,1)S(1)} %convolution_convert_fusion.10.refs_1_.refs_2_, bf16[96,2048]{1,0:T(8,128)(2,1)S(1)} %convolution_convert_fusion.9.refs_2_.refs_3_, ...), custom_call_target="tpu_custom_call" | custom-call | flops 2415919104 | bytes 1048576 | tf_op jit(solution)/shard_map/pallas_call | solution.py:168
  125.0 1.4 collective-permute-start.17
  126.5 10.2 %shard_map.103 = bf16[8,96,2048]{2,1,0:T(8,128)(2,1)} custom-call(bf16[2,384,768]{2,1,0:T(8,128)(2,1)S(1)} %get-tuple-element.15.refs_0_.refs_11_, bf16[2,384,768]{2,1,0:T(8,128)(2,1)S(1)} %get-tuple-element.16.refs_1_, bf16[2048,768]{1,0:T(8,128)(2,1)} %bitcast.170, bf16[2048,768]{1,0:T(8,128)(2,1)} %copy-done, bf16[2048,768]{1,0:T(8,128)(2,1)} %bitcast.173, ...), custom_call_target="tpu_custom_call" | custom-call | flops 4831838208 | bytes 1048576 | tf_op jit(solution)/shard_map/pallas_call | solution.py:168
  138.9 1.3 fusion.14
  142.7 3.5 %shard_map.104 = f32[8,2,128]{2,1,0:T(2,128)} custom-call(s32[2]{0:T(128)S(1)} %pad_add_fusion.1.refs_0_, bf16[96,2048]{1,0:T(8,128)(2,1)S(1)} %convolution_convert_fusion.11.refs_0_.refs_1_, bf16[96,2048]{1,0:T(8,128)(2,1)S(1)} %convolution_convert_fusion.10.refs_1_.refs_2_, bf16[96,2048]{1,0:T(8,128)(2,1)S(1)} %convolution_convert_fusion.9.refs_2_.refs_3_, ...), custom_call_target="tpu_custom_call" | custom-call | flops 1048576 | bytes 1048576 | tf_op jit(solution)/shard_map/pallas_call | solution.py:168
  146.2 1.2 slice.193
  149.5 1.4 collective-permute-start.28
  151.0 1.7 collective-permute-done.23
  153.8 7.3 %collective-permute-done.24 = bf16[128,2048]{1,0:T(8,128)(2,1)S(1)} collective-permute-done((bf16[128,2048]{1,0:T(8,128)(2,1)S(1)}, bf16[128,2048]{1,0:T(8,128)(2,1)S(1)}, u32[]{:S(2)}, u32[]{:S(2)}) %collective-permute-start.24) | collective-permute-done | bytes 524320 | tf_op jit(solution)/shard_map/ppermute | solution.py:95
  163.1 2.1 %fusion.3 = bf16[128,2048]{1,0:T(8,128)(2,1)} fusion(bf16[128,2048]{1,0:T(8,128)(2,1)S(1)} %collective-permute-done.18, bf16[8,96,2048]{2,1,0:T(8,128)(2,1)} %copy-done.1, bf16[8,96,128]{2,1,0:T(8,128)(2,1)S(1)} %get-tuple-element.10), kind=kOutput, calls=%fused_computation.15 | convolution fusion | flops 51118080 | bytes 1466368 | tf_op jit(solution)/shard_map/dot_general | solution.py:482
  165.2 1.7 collective-permute-start.19
  166.9 1.1 fusion.16
  168.1 1.5 collective-permute-start.29
  169.5 4.0 %collective-permute-done.25 = bf16[128,2048]{1,0:T(8,128)(2,1)S(1)} collective-permute-done((bf16[128,2048]{1,0:T(8,128)(2,1)S(1)}, bf16[128,2048]{1,0:T(8,128)(2,1)S(1)}, u32[]{:S(2)}, u32[]{:S(2)}) %collective-permute-start.25) | collective-permute-done | bytes 524320 | tf_op jit(solution)/shard_map/ppermute | solution.py:95
  175.0 4.0 %collective-permute-done.19 = bf16[128,2048]{1,0:T(8,128)(2,1)} collective-permute-done((bf16[128,2048]{1,0:T(8,128)(2,1)}, bf16[128,2048]{1,0:T(8,128)(2,1)}, u32[]{:S(2)}, u32[]{:S(2)}) %collective-permute-start.19) | collective-permute-done | bytes 524320 | tf_op jit(solution)/shard_map/ppermute | solution.py:95
  179.0 1.2 slice.199
  180.8 5.5 %collective-permute-done.29 = bf16[128,2048]{1,0:T(8,128)(2,1)} collective-permute-done((bf16[128,2048]{1,0:T(8,128)(2,1)}, bf16[128,2048]{1,0:T(8,128)(2,1)}, u32[]{:S(2)}, u32[]{:S(2)}) %collective-permute-start.29) | collective-permute-done | bytes 524320 | tf_op jit(solution)/shard_map/ppermute | solution.py:95
  186.3 2.2 %fusion.17 = bf16[128,2048]{1,0:T(8,128)(2,1)} fusion(bf16[128,2048]{1,0:T(8,128)(2,1)} %collective-permute-done.29, bf16[8,96,2048]{2,1,0:T(8,128)(2,1)S(1)} %copy-done.11, bf16[]{:T(256)} %bitcast.45, bf16[8,96,128]{2,1,0:T(8,128)(2,1)S(1)} %get-tuple-element.10), kind=kOutput, calls=%fused_computation.49 | convolution fusion | flops 51380224 | bytes 1466370 | tf_op jit(solution)/shard_map/dot_general | solution.py:482
  188.5 1.7 collective-permute-start.30
  190.2 2.2 %fusion.9 = bf16[128,2048]{1,0:T(8,128)(2,1)} fusion(bf16[128,2048]{1,0:T(8,128)(2,1)} %collective-permute-done.26, bf16[8,96,2048]{2,1,0:T(8,128)(2,1)S(1)} %copy-done.11, bf16[8,96,128]{2,1,0:T(8,128)(2,1)S(1)} %get-tuple-element.10), kind=kOutput, calls=%fused_computation.21 | convolution fusion | flops 51118080 | bytes 1466368 | tf_op jit(solution)/shard_map/dot_general | solution.py:482
  192.7 3.5 %all-to-all-start.1 = ((f32[8,2,128]{2,1,0:T(2,128)}), f32[8,2,128]{2,1,0:T(2,128)S(1)}, u32[]{:S(2)}, u32[]{:S(2)}) async-start(f32[8,2,128]{2,1,0:T(2,128)} %shard_map.104), calls=%async_computation.1 | async-start | bytes 16384 | tf_op jit(solution)/shard_map/all_to_all | solution.py:507
  196.2 6.5 %all-to-all-done.1 = f32[8,2,128]{2,1,0:T(2,128)S(1)} async-done(((f32[8,2,128]{2,1,0:T(2,128)}), f32[8,2,128]{2,1,0:T(2,128)S(1)}, u32[]{:S(2)}, u32[]{:S(2)}) %all-to-all-start.1) | async-done | bytes 8224 | tf_op jit(solution)/shard_map/all_to_all | solution.py:507
  203.4 2.5 %fusion.2 = bf16[128,2048]{1,0:T(8,128)(2,1)} fusion(bf16[128,2048]{1,0:T(8,128)(2,1)} %copy-done.12, bf16[128,2048]{1,0:T(8,128)(2,1)} %collective-permute-done.19, bf16[8,96,2048]{2,1,0:T(8,128)(2,1)} %copy-done.1, bf16[8,96,128]{2,1,0:T(8,128)(2,1)S(1)} %get-tuple-element.10), kind=kOutput, calls=%fused_computation.14 | convolution fusion | flops 51642368 | bytes 1990656 | tf_op jit(solution)/shard_map/dot_general | solution.py:482
  205.9 2.3 %fusion.8 = bf16[128,2048]{1,0:T(8,128)(2,1)} fusion(bf16[128,2048]{1,0:T(8,128)(2,1)} %collective-permute-done.30, bf16[128,2048]{1,0:T(8,128)(2,1)} %collective-permute-done.27, bf16[8,96,2048]{2,1,0:T(8,128)(2,1)S(1)} %copy-done.11, bf16[8,96,128]{2,1,0:T(8,128)(2,1)S(1)} %get-tuple-element.10), kind=kOutput, calls=%fused_computation.20 | convolution fusion | flops 51642368 | bytes 1990656 | tf_op jit(solution)/shard_map/dot_general | solution.py:482
  (106 shorter events, 25.6 us)
Async XLA Ops:
  0.6 36.7 %collective-permute-start.2 = (bf16[2048,768]{1,0:T(8,128)(2,1)}, bf16[2048,768]{1,0:T(8,128)(2,1)S(1)}, u32[]{:S(2)}, u32[]{:S(2)}) collective-permute-start(bf16[2048,768]{1,0:T(8,128)(2,1)} %bitcast.168), channel_id=1, source_target_pairs={{0,8},{8,0},{1,9},{9,1},{2,10},{10,2},{3,11},{11,3},{4,12},{12,4},... | collective-permute-start | bytes 9437192 | tf_op jit(solution)/shard_map/ppermute | solution.py:443
  1.1 36.2 %collective-permute-start.3 = (bf16[2048,768]{1,0:T(8,128)(2,1)}, bf16[2048,768]{1,0:T(8,128)(2,1)}, u32[]{:S(2)}, u32[]{:S(2)}) collective-permute-start(bf16[2048,768]{1,0:T(8,128)(2,1)} %bitcast.171), channel_id=1, source_target_pairs={{0,8},{8,0},{1,9},{9,1},{2,10},{10,2},{3,11},{11,3},{4,12},{12,4},... | collective-permute-start | bytes 9437192 | tf_op jit(solution)/shard_map/ppermute | solution.py:443
  1.2 36.1 %collective-permute-start.4 = (bf16[768,2048]{1,0:T(8,128)(2,1)}, bf16[768,2048]{1,0:T(8,128)(2,1)}, u32[]{:S(2)}, u32[]{:S(2)}) collective-permute-start(bf16[768,2048]{1,0:T(8,128)(2,1)} %bitcast.165), channel_id=1, source_target_pairs={{0,8},{8,0},{1,9},{9,1},{2,10},{10,2},{3,11},{11,3},{4,12},{12,4},... | collective-permute-start | bytes 9437192 | tf_op jit(solution)/shard_map/ppermute | solution.py:443
  1.7 22.4 %collective-permute-start = (bf16[128,2048]{1,0:T(8,128)(2,1)}, bf16[128,2048]{1,0:T(8,128)(2,1)}, u32[]{:S(2)}, u32[]{:S(2)}) collective-permute-start(bf16[128,2048]{1,0:T(8,128)(2,1)} %param.7), channel_id=1, source_target_pairs={{0,1},{2,0},{4,2},{6,4},{7,6},{5,7},{3,5},{1,3},{8,9},{10,8},{12,1... | collective-permute-start | bytes 1572872 | tf_op jit(solution)/shard_map/ppermute | solution.py:95
  4.2 20.4 %collective-permute-start.6 = (bf16[128,2048]{1,0:T(8,128)(2,1)}, bf16[128,2048]{1,0:T(8,128)(2,1)}, u32[]{:S(2)}, u32[]{:S(2)}) collective-permute-start(bf16[128,2048]{1,0:T(8,128)(2,1)} %param.7), channel_id=1, source_target_pairs={{0,2},{2,4},{4,6},{6,7},{7,5},{5,3},{3,1},{1,0},{8,10},{10,12},{12... | collective-permute-start | bytes 1572872 | tf_op jit(solution)/shard_map/ppermute | solution.py:95
  6.3 15.6 %all-to-all-start = ((f32[8,8,128]{2,1,0:T(8,128)}), f32[8,8,128]{2,1,0:T(8,128)S(1)}, u32[]{:S(2)}, u32[]{:S(2)}) async-start(f32[8,8,128]{2,1,0:T(8,128)} %broadcast_in_dim.10), calls=%async_computation | async-start | bytes 65536 | tf_op jit(solution)/shard_map/all_to_all | solution.py:460
  21.9 0.6 copy-start.6
  22.6 0.8 copy-start.7
  24.1 13.2 %collective-permute-start.1 = (bf16[128,2048]{1,0:T(8,128)(2,1)}, bf16[128,2048]{1,0:T(8,128)(2,1)}, u32[]{:S(2)}, u32[]{:S(2)}) collective-permute-start(bf16[128,2048]{1,0:T(8,128)(2,1)} %shard_map.95), channel_id=1, source_target_pairs={{0,1},{2,0},{4,2},{6,4},{7,6},{5,7},{3,5},{1,3},{8,9},{10,8},{12,1... | collective-permute-start | bytes 1572872 | tf_op jit(solution)/shard_map/ppermute | solution.py:95
  24.7 12.7 %copy-start.5 = (bf16[128,2048]{1,0:T(8,128)(2,1)S(1)}, bf16[128,2048]{1,0:T(8,128)(2,1)}, u32[]{:S(2)}) copy-start(bf16[128,2048]{1,0:T(8,128)(2,1)} %refs_0_.1) | copy-start | bytes 1572868
  24.7 12.7 %collective-permute-start.7 = (bf16[128,2048]{1,0:T(8,128)(2,1)}, bf16[128,2048]{1,0:T(8,128)(2,1)S(1)}, u32[]{:S(2)}, u32[]{:S(2)}) collective-permute-start(bf16[128,2048]{1,0:T(8,128)(2,1)} %shard_map.97), channel_id=1, source_target_pairs={{0,2},{2,4},{4,6},{6,7},{7,5},{5,3},{3,1},{1,0},{8,10},{10,12},{12... | collective-permute-start | bytes 1572872 | tf_op jit(solution)/shard_map/ppermute | solution.py:95
  37.3 1.7 copy-start
  39.1 0.8 copy-start.2
  39.9 0.8 copy-start.3
  40.7 15.1 %collective-permute-start.8 = (bf16[128,2048]{1,0:T(8,128)(2,1)}, bf16[128,2048]{1,0:T(8,128)(2,1)S(1)}, u32[]{:S(2)}, u32[]{:S(2)}) collective-permute-start(bf16[128,2048]{1,0:T(8,128)(2,1)} %shard_map.98), channel_id=1, source_target_pairs={{0,2},{2,4},{4,6},{6,7},{7,5},{5,3},{3,1},{1,0},{8,10},{10,12},{12... | collective-permute-start | bytes 1572872 | tf_op jit(solution)/shard_map/ppermute | solution.py:95
  43.6 3.8 %copy-start.4 = (bf16[128,2048]{1,0:T(8,128)(2,1)S(1)}, bf16[128,2048]{1,0:T(8,128)(2,1)}, u32[]{:S(2)}) copy-start(bf16[128,2048]{1,0:T(8,128)(2,1)} %copy-done.3) | copy-start | bytes 1572868
  43.7 23.3 %collective-permute-start.10 = (bf16[128,2048]{1,0:T(8,128)(2,1)}, bf16[128,2048]{1,0:T(8,128)(2,1)S(1)}, u32[]{:S(2)}, u32[]{:S(2)}) collective-permute-start(bf16[128,2048]{1,0:T(8,128)(2,1)} %copy-done.3), channel_id=1, source_target_pairs={{0,2},{2,4},{4,6},{6,7},{7,5},{5,3},{3,1},{1,0},{8,10},{10,12},{12... | collective-permute-start | bytes 1572872 | tf_op jit(solution)/shard_map/ppermute | solution.py:95
  44.0 24.6 %collective-permute-start.12 = (bf16[128,2048]{1,0:T(8,128)(2,1)}, bf16[128,2048]{1,0:T(8,128)(2,1)S(1)}, u32[]{:S(2)}, u32[]{:S(2)}) collective-permute-start(bf16[128,2048]{1,0:T(8,128)(2,1)} %copy-done.3), channel_id=1, source_target_pairs={{0,1},{2,0},{4,2},{6,4},{7,6},{5,7},{3,5},{1,3},{8,9},{10,8},{12,1... | collective-permute-start | bytes 1572872 | tf_op jit(solution)/shard_map/ppermute | solution.py:95
  45.7 23.8 %collective-permute-start.5 = (bf16[128,2048]{1,0:T(8,128)(2,1)}, bf16[128,2048]{1,0:T(8,128)(2,1)S(1)}, u32[]{:S(2)}, u32[]{:S(2)}) collective-permute-start(bf16[128,2048]{1,0:T(8,128)(2,1)} %shard_map.96), channel_id=1, source_target_pairs={{0,1},{2,0},{4,2},{6,4},{7,6},{5,7},{3,5},{1,3},{8,9},{10,8},{12,1... | collective-permute-start | bytes 1572872 | tf_op jit(solution)/shard_map/ppermute | solution.py:95
  47.7 41.4 %copy-start.8 = (bf16[96,2048]{1,0:T(8,128)(2,1)S(1)}, bf16[96,2048]{1,0:T(8,128)(2,1)}, u32[]{:S(2)}) copy-start(bf16[96,2048]{1,0:T(8,128)(2,1)} %convolution_convert_fusion.19.refs_0_) | copy-start | bytes 1179652
  47.7 41.4 %copy-start.9 = (bf16[96,2048]{1,0:T(8,128)(2,1)S(1)}, bf16[96,2048]{1,0:T(8,128)(2,1)}, u32[]{:S(2)}) copy-start(bf16[96,2048]{1,0:T(8,128)(2,1)} %convolution_convert_fusion.12.refs_7_) | copy-start | bytes 1179652
  47.8 41.4 %copy-start.10 = (bf16[96,2048]{1,0:T(8,128)(2,1)S(1)}, bf16[96,2048]{1,0:T(8,128)(2,1)}, u32[]{:S(2)}) copy-start(bf16[96,2048]{1,0:T(8,128)(2,1)} %convolution_convert_fusion.18.refs_1_) | copy-start | bytes 1179652
  55.7 33.1 %collective-permute-start.9 = (bf16[128,2048]{1,0:T(8,128)(2,1)S(1)}, bf16[128,2048]{1,0:T(8,128)(2,1)S(1)}, u32[]{:S(2)}, u32[]{:S(2)}) collective-permute-start(bf16[128,2048]{1,0:T(8,128)(2,1)S(1)} %collective-permute-done.8), channel_id=1, source_target_pairs={{0,2},{2,4},{4,6},{6,7},{7,5},{5,3},{3,1},{1,0},{8,10},{10,12},{12... | collective-permute-start | bytes 1572872 | tf_op jit(solution)/shard_map/ppermute | solution.py:95
  67.0 19.7 %collective-permute-start.11 = (bf16[128,2048]{1,0:T(8,128)(2,1)S(1)}, bf16[128,2048]{1,0:T(8,128)(2,1)S(1)}, u32[]{:S(2)}, u32[]{:S(2)}) collective-permute-start(bf16[128,2048]{1,0:T(8,128)(2,1)S(1)} %collective-permute-done.10), channel_id=1, source_target_pairs={{0,2},{2,4},{4,6},{6,7},{7,5},{5,3},{3,1},{1,0},{8,10},{10,12},{12... | collective-permute-start | bytes 1572872 | tf_op jit(solution)/shard_map/ppermute | solution.py:95
  68.6 11.6 %collective-permute-start.13 = (bf16[128,2048]{1,0:T(8,128)(2,1)S(1)}, bf16[128,2048]{1,0:T(8,128)(2,1)S(1)}, u32[]{:S(2)}, u32[]{:S(2)}) collective-permute-start(bf16[128,2048]{1,0:T(8,128)(2,1)S(1)} %collective-permute-done.12), channel_id=1, source_target_pairs={{0,1},{2,0},{4,2},{6,4},{7,6},{5,7},{3,5},{1,3},{8,9},{10,8},{12,1... | collective-permute-start | bytes 1572872 | tf_op jit(solution)/shard_map/ppermute | solution.py:95
  80.2 19.4 %collective-permute-start.15 = (bf16[128,2048]{1,0:T(8,128)(2,1)S(1)}, bf16[128,2048]{1,0:T(8,128)(2,1)S(1)}, u32[]{:S(2)}, u32[]{:S(2)}) collective-permute-start(bf16[128,2048]{1,0:T(8,128)(2,1)S(1)} %collective-permute-done.13.refs_13_), channel_id=1, source_target_pairs={{0,1},{2,0},{4,2},{6,4},{7,6},{5,7},{3,5},{1,3},{8,9},{10,8},{12,1... | collective-permute-start | bytes 1572872 | tf_op jit(solution)/shard_map/ppermute | solution.py:95
  86.7 13.4 %collective-permute-start.14 = (bf16[128,2048]{1,0:T(8,128)(2,1)S(1)}, bf16[128,2048]{1,0:T(8,128)(2,1)S(1)}, u32[]{:S(2)}, u32[]{:S(2)}) collective-permute-start(bf16[128,2048]{1,0:T(8,128)(2,1)S(1)} %collective-permute-done.11.refs_12_), channel_id=1, source_target_pairs={{0,2},{2,4},{4,6},{6,7},{7,5},{5,3},{3,1},{1,0},{8,10},{10,12},{12... | collective-permute-start | bytes 1572872 | tf_op jit(solution)/shard_map/ppermute | solution.py:95
  99.6 10.4 %collective-permute-start.20 = (bf16[128,2048]{1,0:T(8,128)(2,1)S(1)}, bf16[128,2048]{1,0:T(8,128)(2,1)S(1)}, u32[]{:S(2)}, u32[]{:S(2)}) collective-permute-start(bf16[128,2048]{1,0:T(8,128)(2,1)S(1)} %collective-permute-done.15.refs_4_), channel_id=1, source_target_pairs={{0,1},{2,0},{4,2},{6,4},{7,6},{5,7},{3,5},{1,3},{8,9},{10,8},{12,1... | collective-permute-start | bytes 1572872 | tf_op jit(solution)/shard_map/ppermute | solution.py:95
  104.8 36.4 %copy-start.1 = (bf16[8,96,2048]{2,1,0:T(8,128)(2,1)}, bf16[8,96,2048]{2,1,0:T(8,128)(2,1)S(1)}, u32[]{:S(2)}) copy-start(bf16[8,96,2048]{2,1,0:T(8,128)(2,1)S(1)} %shard_map.101.refs_9_) | copy-start | bytes 9437188
  105.1 19.6 %collective-permute-start.16 = (bf16[128,2048]{1,0:T(8,128)(2,1)S(1)}, bf16[128,2048]{1,0:T(8,128)(2,1)S(1)}, u32[]{:S(2)}, u32[]{:S(2)}) collective-permute-start(bf16[128,2048]{1,0:T(8,128)(2,1)S(1)} %convolution_convert_fusion.3), channel_id=1, source_target_pairs={{0,2},{2,4},{4,6},{6,7},{7,5},{5,3},{3,1},{1,0},{8,10},{10,12},{12... | collective-permute-start | bytes 1572872 | tf_op jit(solution)/shard_map/ppermute | solution.py:95
  111.6 12.1 %collective-permute-start.21 = (bf16[128,2048]{1,0:T(8,128)(2,1)S(1)}, bf16[128,2048]{1,0:T(8,128)(2,1)S(1)}, u32[]{:S(2)}, u32[]{:S(2)}) collective-permute-start(bf16[128,2048]{1,0:T(8,128)(2,1)S(1)} %broadcast_add_fusion), channel_id=1, source_target_pairs={{0,1},{2,0},{4,2},{6,4},{7,6},{5,7},{3,5},{1,3},{8,9},{10,8},{12,1... | collective-permute-start | bytes 1572872 | tf_op jit(solution)/shard_map/ppermute | solution.py:95
  124.0 12.7 %collective-permute-start.22 = (bf16[128,2048]{1,0:T(8,128)(2,1)S(1)}, bf16[128,2048]{1,0:T(8,128)(2,1)S(1)}, u32[]{:S(2)}, u32[]{:S(2)}) collective-permute-start(bf16[128,2048]{1,0:T(8,128)(2,1)S(1)} %fusion.19), channel_id=1, source_target_pairs={{0,1},{2,0},{4,2},{6,4},{7,6},{5,7},{3,5},{1,3},{8,9},{10,8},{12,1... | collective-permute-start | bytes 1572872 | tf_op jit(solution)/shard_map/ppermute | solution.py:95
  125.0 16.2 %collective-permute-start.17 = (bf16[128,2048]{1,0:T(8,128)(2,1)S(1)}, bf16[128,2048]{1,0:T(8,128)(2,1)S(1)}, u32[]{:S(2)}, u32[]{:S(2)}) collective-permute-start(bf16[128,2048]{1,0:T(8,128)(2,1)S(1)} %fusion.5), channel_id=1, source_target_pairs={{0,2},{2,4},{4,6},{6,7},{7,5},{5,3},{3,1},{1,0},{8,10},{10,12},{12... | collective-permute-start | bytes 1572872 | tf_op jit(solution)/shard_map/ppermute | solution.py:95
  138.2 14.4 %collective-permute-start.23 = (bf16[128,2048]{1,0:T(8,128)(2,1)S(1)}, bf16[128,2048]{1,0:T(8,128)(2,1)S(1)}, u32[]{:S(2)}, u32[]{:S(2)}) collective-permute-start(bf16[128,2048]{1,0:T(8,128)(2,1)S(1)} %fusion.6), channel_id=1, source_target_pairs={{0,1},{2,0},{4,2},{6,4},{7,6},{5,7},{3,5},{1,3},{8,9},{10,8},{12,1... | collective-permute-start | bytes 1572872 | tf_op jit(solution)/shard_map/ppermute | solution.py:95
  140.2 21.0 %collective-permute-start.24 = (bf16[128,2048]{1,0:T(8,128)(2,1)S(1)}, bf16[128,2048]{1,0:T(8,128)(2,1)S(1)}, u32[]{:S(2)}, u32[]{:S(2)}) collective-permute-start(bf16[128,2048]{1,0:T(8,128)(2,1)S(1)} %fusion.14), channel_id=1, source_target_pairs={{0,1},{2,0},{4,2},{6,4},{7,6},{5,7},{3,5},{1,3},{8,9},{10,8},{12,1... | collective-permute-start | bytes 1572872 | tf_op jit(solution)/shard_map/ppermute | solution.py:95
  141.6 7.6 %copy-start.11 = (bf16[8,96,2048]{2,1,0:T(8,128)(2,1)S(1)}, bf16[8,96,2048]{2,1,0:T(8,128)(2,1)}, u32[]{:S(2)}) copy-start(bf16[8,96,2048]{2,1,0:T(8,128)(2,1)} %shard_map.103) | copy-start | bytes 9437188
  141.6 20.3 %collective-permute-start.18 = (bf16[128,2048]{1,0:T(8,128)(2,1)S(1)}, bf16[128,2048]{1,0:T(8,128)(2,1)S(1)}, u32[]{:S(2)}, u32[]{:S(2)}) collective-permute-start(bf16[128,2048]{1,0:T(8,128)(2,1)S(1)} %fusion.4), channel_id=1, source_target_pairs={{0,2},{2,4},{4,6},{6,7},{7,5},{5,3},{3,1},{1,0},{8,10},{10,12},{12... | collective-permute-start | bytes 1572872 | tf_op jit(solution)/shard_map/ppermute | solution.py:95
  149.5 17.4 %collective-permute-start.28 = (bf16[128,2048]{1,0:T(8,128)(2,1)S(1)}, bf16[128,2048]{1,0:T(8,128)(2,1)S(1)}, u32[]{:S(2)}, u32[]{:S(2)}) collective-permute-start(bf16[128,2048]{1,0:T(8,128)(2,1)S(1)} %fusion.15), channel_id=1, source_target_pairs={{0,2},{2,4},{4,6},{6,7},{7,5},{5,3},{3,1},{1,0},{8,10},{10,12},{12... | collective-permute-start | bytes 1572872 | tf_op jit(solution)/shard_map/ppermute | solution.py:95
  152.6 20.9 %copy-start.12 = (bf16[128,2048]{1,0:T(8,128)(2,1)}, bf16[128,2048]{1,0:T(8,128)(2,1)S(1)}, u32[]{:S(2)}) copy-start(bf16[128,2048]{1,0:T(8,128)(2,1)S(1)} %collective-permute-done.23) | copy-start | bytes 1572868
  161.5 12.0 %collective-permute-start.25 = (bf16[128,2048]{1,0:T(8,128)(2,1)S(1)}, bf16[128,2048]{1,0:T(8,128)(2,1)S(1)}, u32[]{:S(2)}, u32[]{:S(2)}) collective-permute-start(bf16[128,2048]{1,0:T(8,128)(2,1)S(1)} %fusion.20), channel_id=1, source_target_pairs={{0,1},{2,0},{4,2},{6,4},{7,6},{5,7},{3,5},{1,3},{8,9},{10,8},{12,1... | collective-permute-start | bytes 1572872 | tf_op jit(solution)/shard_map/ppermute | solution.py:95
  165.2 37.6 %copy-start.13 = (s32[128,4]{0,1:T(4,128)S(1)}, s32[128,4]{0,1:T(4,128)}, u32[]{:S(2)}) copy-start(s32[128,4]{0,1:T(4,128)} %param.9) | copy-start | bytes 6148
  165.2 13.8 %collective-permute-start.19 = (bf16[128,2048]{1,0:T(8,128)(2,1)}, bf16[128,2048]{1,0:T(8,128)(2,1)}, u32[]{:S(2)}, u32[]{:S(2)}) collective-permute-start(bf16[128,2048]{1,0:T(8,128)(2,1)} %fusion.3), channel_id=1, source_target_pairs={{0,2},{2,4},{4,6},{6,7},{7,5},{5,3},{3,1},{1,0},{8,10},{10,12},{12... | collective-permute-start | bytes 1572872 | tf_op jit(solution)/shard_map/ppermute | solution.py:95
  168.1 18.3 %collective-permute-start.29 = (bf16[128,2048]{1,0:T(8,128)(2,1)}, bf16[128,2048]{1,0:T(8,128)(2,1)}, u32[]{:S(2)}, u32[]{:S(2)}) collective-permute-start(bf16[128,2048]{1,0:T(8,128)(2,1)} %fusion.16), channel_id=1, source_target_pairs={{0,2},{2,4},{4,6},{6,7},{7,5},{5,3},{3,1},{1,0},{8,10},{10,12},{12... | collective-permute-start | bytes 1572872 | tf_op jit(solution)/shard_map/ppermute | solution.py:95
  174.7 15.6 %collective-permute-start.26 = (bf16[128,2048]{1,0:T(8,128)(2,1)}, bf16[128,2048]{1,0:T(8,128)(2,1)}, u32[]{:S(2)}, u32[]{:S(2)}) collective-permute-start(bf16[128,2048]{1,0:T(8,128)(2,1)} %fusion.10), channel_id=1, source_target_pairs={{0,1},{2,0},{4,2},{6,4},{7,6},{5,7},{3,5},{1,3},{8,9},{10,8},{12,1... | collective-permute-start | bytes 1572872 | tf_op jit(solution)/shard_map/ppermute | solution.py:95
  188.5 17.4 %collective-permute-start.30 = (bf16[128,2048]{1,0:T(8,128)(2,1)}, bf16[128,2048]{1,0:T(8,128)(2,1)}, u32[]{:S(2)}, u32[]{:S(2)}) collective-permute-start(bf16[128,2048]{1,0:T(8,128)(2,1)} %fusion.17), channel_id=1, source_target_pairs={{0,2},{2,4},{4,6},{6,7},{7,5},{5,3},{3,1},{1,0},{8,10},{10,12},{12... | collective-permute-start | bytes 1572872 | tf_op jit(solution)/shard_map/ppermute | solution.py:95
  192.4 13.5 %collective-permute-start.27 = (bf16[128,2048]{1,0:T(8,128)(2,1)}, bf16[128,2048]{1,0:T(8,128)(2,1)}, u32[]{:S(2)}, u32[]{:S(2)}) collective-permute-start(bf16[128,2048]{1,0:T(8,128)(2,1)} %fusion.9), channel_id=1, source_target_pairs={{0,1},{2,0},{4,2},{6,4},{7,6},{5,7},{3,5},{1,3},{8,9},{10,8},{12,1... | collective-permute-start | bytes 1572872 | tf_op jit(solution)/shard_map/ppermute | solution.py:95
  192.7 10.0 %all-to-all-start.1 = ((f32[8,2,128]{2,1,0:T(2,128)}), f32[8,2,128]{2,1,0:T(2,128)S(1)}, u32[]{:S(2)}, u32[]{:S(2)}) async-start(f32[8,2,128]{2,1,0:T(2,128)} %shard_map.104), calls=%async_computation.1 | async-start | bytes 16384 | tf_op jit(solution)/shard_map/all_to_all | solution.py:507

commit v11 on v10

--- a/solution.py
+++ b/solution.py
@@ -197,7 +197,7 @@
     return call_kernel(kernel, [array], ["vmem"], [shape], [], 1, behind)[0]
 
 
-def run_routing(ids, tables, top_count, capacity):
+def run_routing(ids, tables, top_count, capacity, behind):
     count, _, tokens = tables.shape
     f32, bf16 = jnp.float32, jnp.bfloat16
 
@@ -229,7 +229,7 @@
                 spread_ref[s, span, :] = (chosen * weights[i]).astype(bf16)
 
     shape = jax.ShapeDtypeStruct((count, 2 * capacity, tokens), bf16)
-    return call_kernel(kernel, [ids, tables], ["smem", "vmem"], [shape, shape], [], 1 << 20)
+    return call_kernel(kernel, [ids, tables], ["smem", "vmem"], [shape, shape], [], 1 << 20, behind)
 
 
 def run_hidden(parts, gate_mats, up_mats, behind):
@@ -458,12 +458,12 @@
     table = jnp.concatenate([routes.astype(f32), gates.astype(f32)], axis=1).T
     copies = jnp.broadcast_to(table[None], (chips,) + table.shape)
     tables = lax.all_to_all(copies, "ep", split_axis=0, concat_axis=0, tiled=True)
-    pick, spread = run_routing(ids, tables, top_count, capacity)
-
     gate_mats = (w_gate[0], swap_cores(w_gate[0]))
     up_mats = (w_up[0], swap_cores(w_up[0]))
     down_mats = (w_down[0], swap_cores(w_down[0]))
-    swapped = (gate_mats[1], up_mats[1], down_mats[1])
+    pick, spread = run_routing(ids, tables, top_count, capacity, (gate_mats[1], up_mats[1]))
+
+    swapped = (down_mats[1],)
 
     behind = {(step, 2): (tables,) for step in (1, -1)}
     behind.update({(step, 3): swapped for step in (1, -1)})
@@ -492,9 +492,9 @@
 
     rows_in = gather_rows(in_shards)
     hidden, slope, activated = run_hidden(
-        rows_in, gate_mats, up_mats, [grad_hops[step][1] for step in (1, -1)]
-    )
-    outputs = run_down(hidden, down_mats, chips, [grad_hops[step][2] for step in (1, -1)])
+        rows_in, gate_mats, up_mats, [grad_hops[-1][1]]
+    )
+    outputs = run_down(hidden, down_mats, chips, [grad_hops[-1][2]])
     rows_grad = gather_rows(grad_shards)
     d_pre_gate, d_pre_up = run_d_hidden(rows_grad, slope, activated, down_mats)
     behind = {(-1, 0): (grad_hops[-1][-1],), (-1, 1): (d_pre_gate,)}
@@ -510,7 +510,7 @@
         for step in (1, -1)
         for hop in range(len(mixed_hops[step]) - 1)
     }
-    behind[-1, 1] += (per_token,)
+    behind[-1, 2] = (per_token,)
     d_tokens, _ = ring_reduce(scatter_rows(d_copies), chips, -1, behind)
     chip_ids = jnp.arange(chips, dtype=jnp.int32)
     served = jnp.stack([core * chips + chip_ids, (1 - core) * chips + chip_ids], axis=1)

time: 209 us -> 211 us (level)
  blocking collectives: 0 us -> 16.4 us
  matrix products: 29.1 us -> 21.3 us
  starting transfers between devices: 41 us -> 37.5 us
  local copies, waits for them, and re-layouts: 10.8 us -> 8.41 us
    all_to_all x0 -> x1, blocking collectives: none -> 16.4 us  [body_ring(): lax.all_to_all(copies, 'ep', split_axis=0, concat_axis=0, tiled=True)]
    all_to_all x1 -> x0, waiting for transfers between devices: 9.31 us -> none  [body_ring(): lax.all_to_all(copies, 'ep', split_axis=0, concat_axis=0, tiled=True)]
    ppermute x28, waiting for transfers between devices: 63.7 us -> 72.2 us  [ring_shift(): return lax.ppermute(array, 'ep', pairs)]
    all_to_all x1 -> x0, starting transfers between devices: 6.25 us -> none  [body_ring(): lax.all_to_all(copies, 'ep', split_axis=0, concat_axis=0, tiled=True)]
    dot_general x16, matrix products: 17.4 us -> 12.9 us  [share_of(): lax.dot_general(spread[s], blocks[s], (((0,), (0,)), ((), ())), preferred...]
    dot_general x16, matrix products: 11.7 us -> 8.35 us  [gather_rows(): jnp.dot(pick[s], shards[s], preferred_element_type=f32).astype(bf16)]
    unnamed x28 -> x22, local copies, waits for them, and re-layouts: 4.67 us -> 3.53 us
  transfers between devices with their start and end apart: 33 -> 32, of which waited for: 13 -> 14; matrix products, arithmetic and copies ran while one was open for 17% -> 12% of each run, Pallas kernels for 19% -> 19%
where the time goes in v11:
time: 211 us; the launch traced here: 210 us
  waiting for transfers between devices  78.7 us (37%)
  Pallas kernels  39.3 us (19%)
  starting transfers between devices  37.5 us (18%)
  matrix products  21.3 us (10%)
  blocking collectives  16.4 us (8%)
  local copies, waits for them, and re-layouts  8.41 us (4%)
  between operations  6.56 us (3%)
  other arithmetic  2.13 us (1%)
    ppermute x28, waiting for transfers between devices, ring_shift(): return lax.ppermute(array, 'ep', pairs)  72.2 us
    pallas_call x7, Pallas kernels, call_kernel(): pl.pallas_call(body, out_shape=outs, in_specs=[pl.BlockSpec(memory_space=...  39.2 us
    ppermute x28, starting transfers between devices, ring_shift(): return lax.ppermute(array, 'ep', pairs)  30.9 us
    all_to_all x1, blocking collectives, body_ring(): lax.all_to_all(copies, 'ep', split_axis=0, concat_axis=0, tiled=True)  16.4 us
    dot_general x16, matrix products, share_of(): lax.dot_general(spread[s], blocks[s], (((0,), (0,)), ((), ())), preferred...  12.9 us
    dot_general x16, matrix products, gather_rows(): jnp.dot(pick[s], shards[s], preferred_element_type=f32).astype(bf16)  8.35 us
    all_to_all x1, waiting for transfers between devices, body_ring(): lax.all_to_all(per_token, 'ep', split_axis=0, concat_axis=0, tiled=True)  6.51 us
    all_to_all x1, starting transfers between devices, body_ring(): lax.all_to_all(per_token, 'ep', split_axis=0, concat_axis=0, tiled=True)  5.49 us
  transfers between devices with their start and end apart: 32, of which 14 were waited for; matrix products, arithmetic and copies ran while one was open for 12% of the time, Pallas kernels for 19%

profile of v11, /device:TPU:0, one launch (start us, length us, event | category | flops | bytes accessed | tf_op | source)
XLA Modules:
  0.0 210.1 jit_solution(11376686275112372864)
XLA Ops:
  1.7 2.6 %collective-permute-start.2 = (bf16[128,2048]{1,0:T(8,128)(2,1)}, bf16[128,2048]{1,0:T(8,128)(2,1)}, u32[]{:S(2)}, u32[]{:S(2)}) collective-permute-start(bf16[128,2048]{1,0:T(8,128)(2,1)} %param.7), channel_id=1, source_target_pairs={{0,1},{2,0},{4,2},{6,4},{7,6},{5,7},{3,5},{1,3},{8,9},{10,8},{12,1... | collective-permute-start | bytes 1572872 | tf_op jit(solution)/shard_map/ppermute | solution.py:95
  5.7 16.4 %all_to_all.10.refs_1_ = f32[8,8,128]{2,1,0:T(8,128)} all-to-all(f32[8,8,128]{2,1,0:T(8,128)S(1)} %broadcast_in_dim.10), channel_id=1, replica_groups=mesh['rep'=2,'grp'=2,'ep'=8] {'ep'}, dimensions={0} | all-to-all | bytes 65536 | tf_op jit(solution)/shard_map/all_to_all | solution.py:460
  22.5 1.6 collective-permute-start.7
  24.2 11.0 %collective-permute-done.3.refs_0_.refs_2_ = bf16[128,2048]{1,0:T(8,128)(2,1)} collective-permute-done((bf16[128,2048]{1,0:T(8,128)(2,1)}, bf16[128,2048]{1,0:T(8,128)(2,1)}, u32[]{:S(2)}, u32[]{:S(2)}) %collective-permute-start.3) | collective-permute-done | bytes 524320 | tf_op jit(solution)/shard_map/ppermute | solution.py:95
  35.3 1.0 copy-done.5
  36.4 1.7 copy-done
  38.9 1.6 collective-permute-start.8
  41.7 1.4 convolution_convert_fusion.13.refs_6_
  43.1 1.3 convolution_convert_fusion.17.refs_2_
  44.4 1.3 convolution_convert_fusion.12.refs_7_
  45.7 1.3 convolution_convert_fusion.18.refs_1_
  47.0 0.9 collective-permute-start.10
  47.9 1.2 collective-permute-start.19
  49.6 4.3 %collective-permute-done.8 = bf16[128,2048]{1,0:T(8,128)(2,1)S(1)} collective-permute-done((bf16[128,2048]{1,0:T(8,128)(2,1)}, bf16[128,2048]{1,0:T(8,128)(2,1)S(1)}, u32[]{:S(2)}, u32[]{:S(2)}) %collective-permute-start.8) | collective-permute-done | bytes 524320 | tf_op jit(solution)/shard_map/ppermute | solution.py:95
  53.9 1.6 collective-permute-start.9
  55.8 8.2 %collective-permute-done.10 = bf16[128,2048]{1,0:T(8,128)(2,1)S(1)} collective-permute-done((bf16[128,2048]{1,0:T(8,128)(2,1)S(1)}, bf16[128,2048]{1,0:T(8,128)(2,1)S(1)}, u32[]{:S(2)}, u32[]{:S(2)}) %collective-permute-start.10) | collective-permute-done | bytes 524320 | tf_op jit(solution)/shard_map/ppermute | solution.py:95
  65.2 1.6 collective-permute-start.20
  67.6 8.5 %collective-permute-done.11.refs_12_ = bf16[128,2048]{1,0:T(8,128)(2,1)S(1)} collective-permute-done((bf16[128,2048]{1,0:T(8,128)(2,1)S(1)}, bf16[128,2048]{1,0:T(8,128)(2,1)S(1)}, u32[]{:S(2)}, u32[]{:S(2)}) %collective-permute-start.11) | collective-permute-done | bytes 524320 | tf_op jit(solution)/shard_map/ppermute | solution.py:95
  76.5 8.4 %collective-permute-done.20 = bf16[128,2048]{1,0:T(8,128)(2,1)S(1)} collective-permute-done((bf16[128,2048]{1,0:T(8,128)(2,1)S(1)}, bf16[128,2048]{1,0:T(8,128)(2,1)S(1)}, u32[]{:S(2)}, u32[]{:S(2)}) %collective-permute-start.20) | collective-permute-done | bytes 524320 | tf_op jit(solution)/shard_map/ppermute | solution.py:95
  84.9 1.6 collective-permute-start.21
  87.3 10.5 %shard_map.100 = (bf16[2,384,768]{2,1,0:T(8,128)(2,1)S(1)}, f32[2,384,768]{2,1,0:T(8,128)}, f32[2,384,768]{2,1,0:T(8,128)}) custom-call(bf16[96,2048]{1,0:T(8,128)(2,1)S(1)} %convolution_convert_fusion.19.refs_0_, bf16[96,2048]{1,0:T(8,128)(2,1)S(1)} %convolution_convert_fusion.18.refs_1_, bf16[96,2048]{1,0:T(8,128)(2,1)S(1)} %convolution_convert_fusion.17.refs_2_, ...), custom_call_target="tpu_custom_call" | custom-call | flops 4831838208 | bytes 1048576 | tf_op jit(solution)/shard_map/pallas_call | solution.py:168
  98.2 4.7 %shard_map.101.refs_9_ = bf16[8,96,2048]{2,1,0:T(8,128)(2,1)S(1)} custom-call(bf16[2,384,768]{2,1,0:T(8,128)(2,1)S(1)} %get-tuple-element.12.refs_0_, bf16[768,2048]{1,0:T(8,128)(2,1)} %bitcast.166, bf16[768,2048]{1,0:T(8,128)(2,1)} %copy-done, bf16[128,2048]{1,0:T(8,128)(2,1)S(1)} %collective-permute-done.12.refs_3_), custom_call_target="tpu_custom_call" | custom-call | flops 2415919104 | bytes 1048576 | tf_op jit(solution)/shard_map/pallas_call | solution.py:168
  103.3 1.7 collective-permute-start.13
  105.2 2.6 %collective-permute-done.17 = bf16[128,2048]{1,0:T(8,128)(2,1)S(1)} collective-permute-done((bf16[128,2048]{1,0:T(8,128)(2,1)S(1)}, bf16[128,2048]{1,0:T(8,128)(2,1)S(1)}, u32[]{:S(2)}, u32[]{:S(2)}) %collective-permute-start.17) | collective-permute-done | bytes 524320 | tf_op jit(solution)/shard_map/ppermute | solution.py:95
  109.3 1.0 collective-permute-start.18
  110.9 9.6 %shard_map.102 = (bf16[2,384,768]{2,1,0:T(8,128)(2,1)S(1)}, bf16[2,384,768]{2,1,0:T(8,128)(2,1)S(1)}) custom-call(bf16[96,2048]{1,0:T(8,128)(2,1)S(1)} %convolution_convert_fusion.11.refs_0_.refs_1_, bf16[96,2048]{1,0:T(8,128)(2,1)S(1)} %convolution_convert_fusion.10.refs_1_.refs_2_, bf16[96,2048]{1,0:T(8,128)(2,1)S(1)} %convolution_convert_fusion.9.refs_2_.refs_3_, ...), custom_call_target="tpu_custom_call" | custom-call | flops 2415919104 | bytes 1048576 | tf_op jit(solution)/shard_map/pallas_call | solution.py:168
  123.2 1.3 collective-permute-start.14
  124.5 10.3 %shard_map.103 = bf16[8,96,2048]{2,1,0:T(8,128)(2,1)} custom-call(bf16[2,384,768]{2,1,0:T(8,128)(2,1)S(1)} %get-tuple-element.15.refs_0_.refs_11_, bf16[2,384,768]{2,1,0:T(8,128)(2,1)S(1)} %get-tuple-element.16.refs_1_, bf16[2048,768]{1,0:T(8,128)(2,1)} %bitcast.170, bf16[2048,768]{1,0:T(8,128)(2,1)} %collective-permute-done.refs_2_.refs_9_.refs_3_, ...), custom_call_target="tpu_custom_call" | custom-call | flops 4831838208 | bytes 1048576 | tf_op jit(solution)/shard_map/pallas_call | solution.py:168
  137.4 1.3 fusion.14
  139.7 1.5 collective-permute-start.15
  142.7 1.3 collective-permute-start.28
  143.9 6.7 %collective-permute-done.23 = bf16[128,2048]{1,0:T(8,128)(2,1)S(1)} collective-permute-done((bf16[128,2048]{1,0:T(8,128)(2,1)S(1)}, bf16[128,2048]{1,0:T(8,128)(2,1)S(1)}, u32[]{:S(2)}, u32[]{:S(2)}) %collective-permute-start.23) | collective-permute-done | bytes 524320 | tf_op jit(solution)/shard_map/ppermute | solution.py:95
  151.9 7.2 %collective-permute-done.24 = bf16[128,2048]{1,0:T(8,128)(2,1)S(1)} collective-permute-done((bf16[128,2048]{1,0:T(8,128)(2,1)S(1)}, bf16[128,2048]{1,0:T(8,128)(2,1)S(1)}, u32[]{:S(2)}, u32[]{:S(2)}) %collective-permute-start.24) | collective-permute-done | bytes 524320 | tf_op jit(solution)/shard_map/ppermute | solution.py:95
  160.2 3.4 %shard_map.104 = f32[8,2,128]{2,1,0:T(2,128)} custom-call(s32[2]{0:T(128)S(1)} %pad_add_fusion.1.refs_0_, bf16[96,2048]{1,0:T(8,128)(2,1)S(1)} %convolution_convert_fusion.11.refs_0_.refs_1_, bf16[96,2048]{1,0:T(8,128)(2,1)S(1)} %convolution_convert_fusion.10.refs_1_.refs_2_, bf16[96,2048]{1,0:T(8,128)(2,1)S(1)} %convolution_convert_fusion.9.refs_2_.refs_3_, ...), custom_call_target="tpu_custom_call" | custom-call | flops 1048576 | bytes 1048576 | tf_op jit(solution)/shard_map/pallas_call | solution.py:168
  163.6 1.3 slice.193
  166.0 1.3 fusion.3
  167.4 1.3 collective-permute-start.16
  169.0 1.3 collective-permute-start.29
  171.9 1.3 collective-permute-start.26
  173.3 4.4 %collective-permute-done.16 = bf16[128,2048]{1,0:T(8,128)(2,1)S(1)} collective-permute-done((bf16[128,2048]{1,0:T(8,128)(2,1)S(1)}, bf16[128,2048]{1,0:T(8,128)(2,1)S(1)}, u32[]{:S(2)}, u32[]{:S(2)}) %collective-permute-start.16) | collective-permute-done | bytes 524320 | tf_op jit(solution)/shard_map/ppermute | solution.py:95
  178.8 9.4 %collective-permute-done.29 = bf16[128,2048]{1,0:T(8,128)(2,1)S(1)} collective-permute-done((bf16[128,2048]{1,0:T(8,128)(2,1)S(1)}, bf16[128,2048]{1,0:T(8,128)(2,1)S(1)}, u32[]{:S(2)}, u32[]{:S(2)}) %collective-permute-start.29) | collective-permute-done | bytes 524320 | tf_op jit(solution)/shard_map/ppermute | solution.py:95
  188.2 1.3 fusion.17
  189.5 1.9 collective-permute-start.30
  191.4 1.5 fusion.9
  193.1 5.5 %all-to-all-start.1 = ((f32[8,2,128]{2,1,0:T(2,128)}), f32[8,2,128]{2,1,0:T(2,128)S(1)}, u32[]{:S(2)}, u32[]{:S(2)}) async-start(f32[8,2,128]{2,1,0:T(2,128)} %shard_map.104), calls=%async_computation.1 | async-start | bytes 16384 | tf_op jit(solution)/shard_map/all_to_all | solution.py:507
  198.6 6.5 %all-to-all-done.1 = f32[8,2,128]{2,1,0:T(2,128)S(1)} async-done(((f32[8,2,128]{2,1,0:T(2,128)}), f32[8,2,128]{2,1,0:T(2,128)S(1)}, u32[]{:S(2)}, u32[]{:S(2)}) %all-to-all-start.1) | async-done | bytes 8224 | tf_op jit(solution)/shard_map/all_to_all | solution.py:507
  205.8 2.1 %fusion.2 = bf16[128,2048]{1,0:T(8,128)(2,1)} fusion(bf16[128,2048]{1,0:T(8,128)(2,1)S(1)} %copy-done.9, bf16[128,2048]{1,0:T(8,128)(2,1)S(1)} %collective-permute-done.16, bf16[8,96,2048]{2,1,0:T(8,128)(2,1)} %copy-done.1, bf16[8,96,128]{2,1,0:T(8,128)(2,1)S(1)} %get-tuple-element.10), kind=kOutput, calls=%fused_computation.14 | convolution fusion | flops 51642368 | bytes 1990656 | tf_op jit(solution)/shard_map/dot_general | solution.py:482
  208.0 2.1 %fusion.8 = bf16[128,2048]{1,0:T(8,128)(2,1)} fusion(bf16[128,2048]{1,0:T(8,128)(2,1)S(1)} %collective-permute-done.30, bf16[128,2048]{1,0:T(8,128)(2,1)S(1)} %collective-permute-done.27, bf16[8,96,2048]{2,1,0:T(8,128)(2,1)} %shard_map.103, bf16[8,96,128]{2,1,0:T(8,128)(2,1)S(1)} %get-tuple-element.10), kind=kOutput, calls=%fused_computation.20 | convolution fusion | flops 51642368 | bytes 1990656 | tf_op jit(solution)/shard_map/dot_general | solution.py:482
  (99 shorter events, 21.9 us)
Async XLA Ops:
  0.6 34.7 %collective-permute-start.4 = (bf16[768,2048]{1,0:T(8,128)(2,1)}, bf16[768,2048]{1,0:T(8,128)(2,1)S(1)}, u32[]{:S(2)}, u32[]{:S(2)}) collective-permute-start(bf16[768,2048]{1,0:T(8,128)(2,1)} %bitcast.165), channel_id=1, source_target_pairs={{0,8},{8,0},{1,9},{9,1},{2,10},{10,2},{3,11},{11,3},{4,12},{12,4},... | collective-permute-start | bytes 9437192 | tf_op jit(solution)/shard_map/ppermute | solution.py:443
  1.1 39.7 %collective-permute-start = (bf16[2048,768]{1,0:T(8,128)(2,1)}, bf16[2048,768]{1,0:T(8,128)(2,1)}, u32[]{:S(2)}, u32[]{:S(2)}) collective-permute-start(bf16[2048,768]{1,0:T(8,128)(2,1)} %bitcast.168), channel_id=1, source_target_pairs={{0,8},{8,0},{1,9},{9,1},{2,10},{10,2},{3,11},{11,3},{4,12},{12,4},... | collective-permute-start | bytes 9437192 | tf_op jit(solution)/shard_map/ppermute | solution.py:443
  1.2 39.7 %collective-permute-start.1 = (bf16[2048,768]{1,0:T(8,128)(2,1)}, bf16[2048,768]{1,0:T(8,128)(2,1)}, u32[]{:S(2)}, u32[]{:S(2)}) collective-permute-start(bf16[2048,768]{1,0:T(8,128)(2,1)} %bitcast.171), channel_id=1, source_target_pairs={{0,8},{8,0},{1,9},{9,1},{2,10},{10,2},{3,11},{11,3},{4,12},{12,4},... | collective-permute-start | bytes 9437192 | tf_op jit(solution)/shard_map/ppermute | solution.py:443
  1.7 20.4 %collective-permute-start.2 = (bf16[128,2048]{1,0:T(8,128)(2,1)}, bf16[128,2048]{1,0:T(8,128)(2,1)}, u32[]{:S(2)}, u32[]{:S(2)}) collective-permute-start(bf16[128,2048]{1,0:T(8,128)(2,1)} %param.7), channel_id=1, source_target_pairs={{0,1},{2,0},{4,2},{6,4},{7,6},{5,7},{3,5},{1,3},{8,9},{10,8},{12,1... | collective-permute-start | bytes 1572872 | tf_op jit(solution)/shard_map/ppermute | solution.py:95
  4.2 18.3 %collective-permute-start.6 = (bf16[128,2048]{1,0:T(8,128)(2,1)}, bf16[128,2048]{1,0:T(8,128)(2,1)}, u32[]{:S(2)}, u32[]{:S(2)}) collective-permute-start(bf16[128,2048]{1,0:T(8,128)(2,1)} %param.7), channel_id=1, source_target_pairs={{0,2},{2,4},{4,6},{6,7},{7,5},{5,3},{3,1},{1,0},{8,10},{10,12},{12... | collective-permute-start | bytes 1572872 | tf_op jit(solution)/shard_map/ppermute | solution.py:95
  22.1 13.1 %collective-permute-start.3 = (bf16[128,2048]{1,0:T(8,128)(2,1)}, bf16[128,2048]{1,0:T(8,128)(2,1)}, u32[]{:S(2)}, u32[]{:S(2)}) collective-permute-start(bf16[128,2048]{1,0:T(8,128)(2,1)} %shard_map.95), channel_id=1, source_target_pairs={{0,1},{2,0},{4,2},{6,4},{7,6},{5,7},{3,5},{1,3},{8,9},{10,8},{12,1... | collective-permute-start | bytes 1572872 | tf_op jit(solution)/shard_map/ppermute | solution.py:95
  22.5 12.8 %collective-permute-start.7 = (bf16[128,2048]{1,0:T(8,128)(2,1)}, bf16[128,2048]{1,0:T(8,128)(2,1)}, u32[]{:S(2)}, u32[]{:S(2)}) collective-permute-start(bf16[128,2048]{1,0:T(8,128)(2,1)} %shard_map.97), channel_id=1, source_target_pairs={{0,2},{2,4},{4,6},{6,7},{7,5},{5,3},{3,1},{1,0},{8,10},{10,12},{12... | collective-permute-start | bytes 1572872 | tf_op jit(solution)/shard_map/ppermute | solution.py:95
  35.3 1.0 copy-start.5
  36.4 1.7 copy-start
  38.1 0.8 copy-start.2
  38.8 2.0 copy-start.4
  38.9 15.1 %collective-permute-start.8 = (bf16[128,2048]{1,0:T(8,128)(2,1)}, bf16[128,2048]{1,0:T(8,128)(2,1)S(1)}, u32[]{:S(2)}, u32[]{:S(2)}) collective-permute-start(bf16[128,2048]{1,0:T(8,128)(2,1)} %shard_map.98), channel_id=1, source_target_pairs={{0,2},{2,4},{4,6},{6,7},{7,5},{5,3},{3,1},{1,0},{8,10},{10,12},{12... | collective-permute-start | bytes 1572872 | tf_op jit(solution)/shard_map/ppermute | solution.py:95
  40.5 26.8 %collective-permute-start.5 = (bf16[128,2048]{1,0:T(8,128)(2,1)}, bf16[128,2048]{1,0:T(8,128)(2,1)S(1)}, u32[]{:S(2)}, u32[]{:S(2)}) collective-permute-start(bf16[128,2048]{1,0:T(8,128)(2,1)} %shard_map.96), channel_id=1, source_target_pairs={{0,1},{2,0},{4,2},{6,4},{7,6},{5,7},{3,5},{1,3},{8,9},{10,8},{12,1... | collective-permute-start | bytes 1572872 | tf_op jit(solution)/shard_map/ppermute | solution.py:95
  41.7 5.3 %copy-start.3 = (bf16[128,2048]{1,0:T(8,128)(2,1)S(1)}, bf16[128,2048]{1,0:T(8,128)(2,1)}, u32[]{:S(2)}) copy-start(bf16[128,2048]{1,0:T(8,128)(2,1)} %copy-done.2) | copy-start | bytes 1572868
  41.7 7.4 %copy-start.7 = (bf16[128,2048]{1,0:T(8,128)(2,1)S(1)}, bf16[128,2048]{1,0:T(8,128)(2,1)}, u32[]{:S(2)}) copy-start(bf16[128,2048]{1,0:T(8,128)(2,1)} %param.7) | copy-start | bytes 1572868
  47.0 17.0 %collective-permute-start.10 = (bf16[128,2048]{1,0:T(8,128)(2,1)S(1)}, bf16[128,2048]{1,0:T(8,128)(2,1)S(1)}, u32[]{:S(2)}, u32[]{:S(2)}) collective-permute-start(bf16[128,2048]{1,0:T(8,128)(2,1)S(1)} %copy-done.3), channel_id=1, source_target_pairs={{0,1},{2,0},{4,2},{6,4},{7,6},{5,7},{3,5},{1,3},{8,9},{10,8},{12,1... | collective-permute-start | bytes 1572872 | tf_op jit(solution)/shard_map/ppermute | solution.py:95
  47.9 17.3 %collective-permute-start.19 = (bf16[128,2048]{1,0:T(8,128)(2,1)S(1)}, bf16[128,2048]{1,0:T(8,128)(2,1)S(1)}, u32[]{:S(2)}, u32[]{:S(2)}) collective-permute-start(bf16[128,2048]{1,0:T(8,128)(2,1)S(1)} %copy-done.3), channel_id=1, source_target_pairs={{0,2},{2,4},{4,6},{6,7},{7,5},{5,3},{3,1},{1,0},{8,10},{10,12},{12... | collective-permute-start | bytes 1572872 | tf_op jit(solution)/shard_map/ppermute | solution.py:95
  53.9 33.1 %collective-permute-start.9 = (bf16[128,2048]{1,0:T(8,128)(2,1)S(1)}, bf16[128,2048]{1,0:T(8,128)(2,1)S(1)}, u32[]{:S(2)}, u32[]{:S(2)}) collective-permute-start(bf16[128,2048]{1,0:T(8,128)(2,1)S(1)} %collective-permute-done.8), channel_id=1, source_target_pairs={{0,2},{2,4},{4,6},{6,7},{7,5},{5,3},{3,1},{1,0},{8,10},{10,12},{12... | collective-permute-start | bytes 1572872 | tf_op jit(solution)/shard_map/ppermute | solution.py:95
  64.0 12.1 %collective-permute-start.11 = (bf16[128,2048]{1,0:T(8,128)(2,1)S(1)}, bf16[128,2048]{1,0:T(8,128)(2,1)S(1)}, u32[]{:S(2)}, u32[]{:S(2)}) collective-permute-start(bf16[128,2048]{1,0:T(8,128)(2,1)S(1)} %collective-permute-done.10), channel_id=1, source_target_pairs={{0,1},{2,0},{4,2},{6,4},{7,6},{5,7},{3,5},{1,3},{8,9},{10,8},{12,1... | collective-permute-start | bytes 1572872 | tf_op jit(solution)/shard_map/ppermute | solution.py:95
  65.2 19.7 %collective-permute-start.20 = (bf16[128,2048]{1,0:T(8,128)(2,1)S(1)}, bf16[128,2048]{1,0:T(8,128)(2,1)S(1)}, u32[]{:S(2)}, u32[]{:S(2)}) collective-permute-start(bf16[128,2048]{1,0:T(8,128)(2,1)S(1)} %collective-permute-done.19), channel_id=1, source_target_pairs={{0,2},{2,4},{4,6},{6,7},{7,5},{5,3},{3,1},{1,0},{8,10},{10,12},{12... | collective-permute-start | bytes 1572872 | tf_op jit(solution)/shard_map/ppermute | solution.py:95
  76.1 21.7 %collective-permute-start.12 = (bf16[128,2048]{1,0:T(8,128)(2,1)S(1)}, bf16[128,2048]{1,0:T(8,128)(2,1)S(1)}, u32[]{:S(2)}, u32[]{:S(2)}) collective-permute-start(bf16[128,2048]{1,0:T(8,128)(2,1)S(1)} %collective-permute-done.11.refs_12_), channel_id=1, source_target_pairs={{0,1},{2,0},{4,2},{6,4},{7,6},{5,7},{3,5},{1,3},{8,9},{10,8},{12,1... | collective-permute-start | bytes 1572872 | tf_op jit(solution)/shard_map/ppermute | solution.py:95
  84.9 25.5 %collective-permute-start.21 = (bf16[128,2048]{1,0:T(8,128)(2,1)S(1)}, bf16[128,2048]{1,0:T(8,128)(2,1)S(1)}, u32[]{:S(2)}, u32[]{:S(2)}) collective-permute-start(bf16[128,2048]{1,0:T(8,128)(2,1)S(1)} %collective-permute-done.20), channel_id=1, source_target_pairs={{0,2},{2,4},{4,6},{6,7},{7,5},{5,3},{3,1},{1,0},{8,10},{10,12},{12... | collective-permute-start | bytes 1572872 | tf_op jit(solution)/shard_map/ppermute | solution.py:95
  97.8 10.0 %collective-permute-start.17 = (bf16[128,2048]{1,0:T(8,128)(2,1)S(1)}, bf16[128,2048]{1,0:T(8,128)(2,1)S(1)}, u32[]{:S(2)}, u32[]{:S(2)}) collective-permute-start(bf16[128,2048]{1,0:T(8,128)(2,1)S(1)} %collective-permute-done.12.refs_3_), channel_id=1, source_target_pairs={{0,1},{2,0},{4,2},{6,4},{7,6},{5,7},{3,5},{1,3},{8,9},{10,8},{12,1... | collective-permute-start | bytes 1572872 | tf_op jit(solution)/shard_map/ppermute | solution.py:95
  102.9 36.4 %copy-start.1 = (bf16[8,96,2048]{2,1,0:T(8,128)(2,1)}, bf16[8,96,2048]{2,1,0:T(8,128)(2,1)S(1)}, u32[]{:S(2)}) copy-start(bf16[8,96,2048]{2,1,0:T(8,128)(2,1)S(1)} %shard_map.101.refs_9_) | copy-start | bytes 9437188
  103.3 19.6 %collective-permute-start.13 = (bf16[128,2048]{1,0:T(8,128)(2,1)S(1)}, bf16[128,2048]{1,0:T(8,128)(2,1)S(1)}, u32[]{:S(2)}, u32[]{:S(2)}) collective-permute-start(bf16[128,2048]{1,0:T(8,128)(2,1)S(1)} %convolution_convert_fusion.3), channel_id=1, source_target_pairs={{0,2},{2,4},{4,6},{6,7},{7,5},{5,3},{3,1},{1,0},{8,10},{10,12},{12... | collective-permute-start | bytes 1572872 | tf_op jit(solution)/shard_map/ppermute | solution.py:95
  109.3 12.4 %collective-permute-start.18 = (bf16[128,2048]{1,0:T(8,128)(2,1)S(1)}, bf16[128,2048]{1,0:T(8,128)(2,1)S(1)}, u32[]{:S(2)}, u32[]{:S(2)}) collective-permute-start(bf16[128,2048]{1,0:T(8,128)(2,1)S(1)} %broadcast_add_fusion), channel_id=1, source_target_pairs={{0,1},{2,0},{4,2},{6,4},{7,6},{5,7},{3,5},{1,3},{8,9},{10,8},{12,1... | collective-permute-start | bytes 1572872 | tf_op jit(solution)/shard_map/ppermute | solution.py:95
  122.0 12.7 %collective-permute-start.22 = (bf16[128,2048]{1,0:T(8,128)(2,1)S(1)}, bf16[128,2048]{1,0:T(8,128)(2,1)S(1)}, u32[]{:S(2)}, u32[]{:S(2)}) collective-permute-start(bf16[128,2048]{1,0:T(8,128)(2,1)S(1)} %fusion.20), channel_id=1, source_target_pairs={{0,1},{2,0},{4,2},{6,4},{7,6},{5,7},{3,5},{1,3},{8,9},{10,8},{12,1... | collective-permute-start | bytes 1572872 | tf_op jit(solution)/shard_map/ppermute | solution.py:95
  123.2 16.1 %collective-permute-start.14 = (bf16[128,2048]{1,0:T(8,128)(2,1)S(1)}, bf16[128,2048]{1,0:T(8,128)(2,1)S(1)}, u32[]{:S(2)}, u32[]{:S(2)}) collective-permute-start(bf16[128,2048]{1,0:T(8,128)(2,1)S(1)} %fusion.5), channel_id=1, source_target_pairs={{0,2},{2,4},{4,6},{6,7},{7,5},{5,3},{3,1},{1,0},{8,10},{10,12},{12... | collective-permute-start | bytes 1572872 | tf_op jit(solution)/shard_map/ppermute | solution.py:95
  134.7 7.6 %copy-start.6 = (bf16[8,96,2048]{2,1,0:T(8,128)(2,1)S(1)}, bf16[8,96,2048]{2,1,0:T(8,128)(2,1)}, u32[]{:S(2)}) copy-start(bf16[8,96,2048]{2,1,0:T(8,128)(2,1)} %shard_map.103) | copy-start | bytes 9437188
  136.5 14.1 %collective-permute-start.23 = (bf16[128,2048]{1,0:T(8,128)(2,1)S(1)}, bf16[128,2048]{1,0:T(8,128)(2,1)S(1)}, u32[]{:S(2)}, u32[]{:S(2)}) collective-permute-start(bf16[128,2048]{1,0:T(8,128)(2,1)S(1)} %fusion.6), channel_id=1, source_target_pairs={{0,1},{2,0},{4,2},{6,4},{7,6},{5,7},{3,5},{1,3},{8,9},{10,8},{12,1... | collective-permute-start | bytes 1572872 | tf_op jit(solution)/shard_map/ppermute | solution.py:95
  138.7 20.3 %collective-permute-start.24 = (bf16[128,2048]{1,0:T(8,128)(2,1)S(1)}, bf16[128,2048]{1,0:T(8,128)(2,1)S(1)}, u32[]{:S(2)}, u32[]{:S(2)}) collective-permute-start(bf16[128,2048]{1,0:T(8,128)(2,1)S(1)} %fusion.14), channel_id=1, source_target_pairs={{0,1},{2,0},{4,2},{6,4},{7,6},{5,7},{3,5},{1,3},{8,9},{10,8},{12,1... | collective-permute-start | bytes 1572872 | tf_op jit(solution)/shard_map/ppermute | solution.py:95
  139.7 25.2 %collective-permute-start.15 = (bf16[128,2048]{1,0:T(8,128)(2,1)S(1)}, bf16[128,2048]{1,0:T(8,128)(2,1)S(1)}, u32[]{:S(2)}, u32[]{:S(2)}) collective-permute-start(bf16[128,2048]{1,0:T(8,128)(2,1)S(1)} %fusion.4), channel_id=1, source_target_pairs={{0,2},{2,4},{4,6},{6,7},{7,5},{5,3},{3,1},{1,0},{8,10},{10,12},{12... | collective-permute-start | bytes 1572872 | tf_op jit(solution)/shard_map/ppermute | solution.py:95
  142.7 26.0 %collective-permute-start.28 = (bf16[128,2048]{1,0:T(8,128)(2,1)S(1)}, bf16[128,2048]{1,0:T(8,128)(2,1)S(1)}, u32[]{:S(2)}, u32[]{:S(2)}) collective-permute-start(bf16[128,2048]{1,0:T(8,128)(2,1)S(1)} %fusion.15), channel_id=1, source_target_pairs={{0,2},{2,4},{4,6},{6,7},{7,5},{5,3},{3,1},{1,0},{8,10},{10,12},{12... | collective-permute-start | bytes 1572872 | tf_op jit(solution)/shard_map/ppermute | solution.py:95
  150.7 8.4 %copy-start.8 = (bf16[128,2048]{1,0:T(8,128)(2,1)}, bf16[128,2048]{1,0:T(8,128)(2,1)S(1)}, u32[]{:S(2)}) copy-start(bf16[128,2048]{1,0:T(8,128)(2,1)S(1)} %collective-permute-done.23) | copy-start | bytes 1572868
  159.4 12.3 %collective-permute-start.25 = (bf16[128,2048]{1,0:T(8,128)(2,1)S(1)}, bf16[128,2048]{1,0:T(8,128)(2,1)S(1)}, u32[]{:S(2)}, u32[]{:S(2)}) collective-permute-start(bf16[128,2048]{1,0:T(8,128)(2,1)S(1)} %fusion.18), channel_id=1, source_target_pairs={{0,1},{2,0},{4,2},{6,4},{7,6},{5,7},{3,5},{1,3},{8,9},{10,8},{12,1... | collective-permute-start | bytes 1572872 | tf_op jit(solution)/shard_map/ppermute | solution.py:95
  167.4 37.8 %copy-start.10 = (s32[128,4]{0,1:T(4,128)S(1)}, s32[128,4]{0,1:T(4,128)}, u32[]{:S(2)}) copy-start(s32[128,4]{0,1:T(4,128)} %param.9) | copy-start | bytes 6148
  167.4 38.4 %copy-start.9 = (bf16[128,2048]{1,0:T(8,128)(2,1)S(1)}, bf16[128,2048]{1,0:T(8,128)(2,1)}, u32[]{:S(2)}) copy-start(bf16[128,2048]{1,0:T(8,128)(2,1)} %copy-done.8) | copy-start | bytes 1572868
  167.4 10.2 %collective-permute-start.16 = (bf16[128,2048]{1,0:T(8,128)(2,1)S(1)}, bf16[128,2048]{1,0:T(8,128)(2,1)S(1)}, u32[]{:S(2)}, u32[]{:S(2)}) collective-permute-start(bf16[128,2048]{1,0:T(8,128)(2,1)S(1)} %fusion.3), channel_id=1, source_target_pairs={{0,2},{2,4},{4,6},{6,7},{7,5},{5,3},{3,1},{1,0},{8,10},{10,12},{12... | collective-permute-start | bytes 1572872 | tf_op jit(solution)/shard_map/ppermute | solution.py:95
  169.0 19.1 %collective-permute-start.29 = (bf16[128,2048]{1,0:T(8,128)(2,1)S(1)}, bf16[128,2048]{1,0:T(8,128)(2,1)S(1)}, u32[]{:S(2)}, u32[]{:S(2)}) collective-permute-start(bf16[128,2048]{1,0:T(8,128)(2,1)S(1)} %fusion.16), channel_id=1, source_target_pairs={{0,2},{2,4},{4,6},{6,7},{7,5},{5,3},{3,1},{1,0},{8,10},{10,12},{12... | collective-permute-start | bytes 1572872 | tf_op jit(solution)/shard_map/ppermute | solution.py:95
  171.9 19.4 %collective-permute-start.26 = (bf16[128,2048]{1,0:T(8,128)(2,1)S(1)}, bf16[128,2048]{1,0:T(8,128)(2,1)}, u32[]{:S(2)}, u32[]{:S(2)}) collective-permute-start(bf16[128,2048]{1,0:T(8,128)(2,1)S(1)} %fusion.19), channel_id=1, source_target_pairs={{0,1},{2,0},{4,2},{6,4},{7,6},{5,7},{3,5},{1,3},{8,9},{10,8},{12,1... | collective-permute-start | bytes 1572872 | tf_op jit(solution)/shard_map/ppermute | solution.py:95
  189.5 18.5 %collective-permute-start.30 = (bf16[128,2048]{1,0:T(8,128)(2,1)S(1)}, bf16[128,2048]{1,0:T(8,128)(2,1)S(1)}, u32[]{:S(2)}, u32[]{:S(2)}) collective-permute-start(bf16[128,2048]{1,0:T(8,128)(2,1)S(1)} %fusion.17), channel_id=1, source_target_pairs={{0,2},{2,4},{4,6},{6,7},{7,5},{5,3},{3,1},{1,0},{8,10},{10,12},{12... | collective-permute-start | bytes 1572872 | tf_op jit(solution)/shard_map/ppermute | solution.py:95
  192.8 15.1 %collective-permute-start.27 = (bf16[128,2048]{1,0:T(8,128)(2,1)S(1)}, bf16[128,2048]{1,0:T(8,128)(2,1)S(1)}, u32[]{:S(2)}, u32[]{:S(2)}) collective-permute-start(bf16[128,2048]{1,0:T(8,128)(2,1)S(1)} %fusion.9), channel_id=1, source_target_pairs={{0,1},{2,0},{4,2},{6,4},{7,6},{5,7},{3,5},{1,3},{8,9},{10,8},{12,1... | collective-permute-start | bytes 1572872 | tf_op jit(solution)/shard_map/ppermute | solution.py:95
  193.1 12.0 %all-to-all-start.1 = ((f32[8,2,128]{2,1,0:T(2,128)}), f32[8,2,128]{2,1,0:T(2,128)S(1)}, u32[]{:S(2)}, u32[]{:S(2)}) async-start(f32[8,2,128]{2,1,0:T(2,128)} %shard_map.104), calls=%async_computation.1 | async-start | bytes 16384 | tf_op jit(solution)/shard_map/all_to_all | solution.py:507

commit v12 on v11

--- a/solution.py
+++ b/solution.py
@@ -510,7 +510,8 @@
         for step in (1, -1)
         for hop in range(len(mixed_hops[step]) - 1)
     }
-    behind[-1, 2] = (per_token,)
+    behind[-1, 1] += (per_token,)
+    behind[-1, 3] = (returned,)
     d_tokens, _ = ring_reduce(scatter_rows(d_copies), chips, -1, behind)
     chip_ids = jnp.arange(chips, dtype=jnp.int32)
     served = jnp.stack([core * chips + chip_ids, (1 - core) * chips + chip_ids], axis=1)

time: 211 us -> 202 us (0.957)
  waiting for transfers between devices: 78.7 us -> 68.4 us
    ppermute x28, waiting for transfers between devices: 72.2 us -> 61.2 us  [ring_shift(): return lax.ppermute(array, 'ep', pairs)]
    slice x8 -> x9, local copies, waits for them, and re-layouts: 4.87 us -> 5.94 us  [after(): other[(slice(0, 1),) * other.ndim].reshape((1,) * array.ndim)]
  transfers between devices with their start and end apart: 32 -> 32, of which waited for: 14 -> 14; matrix products, arithmetic and copies ran while one was open for 12% -> 15% of each run, Pallas kernels for 19% -> 20%
where the time goes in v12:
time: 202 us; the launch traced here: 201 us
  waiting for transfers between devices  68.4 us (34%)
  Pallas kernels  39.3 us (19%)
  starting transfers between devices  35.5 us (18%)
  matrix products  22.8 us (11%)
  blocking collectives  16.4 us (8%)
  local copies, waits for them, and re-layouts  9.49 us (5%)
  between operations  6.98 us (3%)
  other arithmetic  2.13 us (1%)
    ppermute x28, waiting for transfers between devices, ring_shift(): return lax.ppermute(array, 'ep', pairs)  61.2 us
    pallas_call x7, Pallas kernels, call_kernel(): pl.pallas_call(body, out_shape=outs, in_specs=[pl.BlockSpec(memory_space=...  39.3 us
    ppermute x28, starting transfers between devices, ring_shift(): return lax.ppermute(array, 'ep', pairs)  30.7 us
    all_to_all x1, blocking collectives, body_ring(): lax.all_to_all(copies, 'ep', split_axis=0, concat_axis=0, tiled=True)  16.4 us
    dot_general x16, matrix products, share_of(): lax.dot_general(spread[s], blocks[s], (((0,), (0,)), ((), ())), preferred...  14.5 us
    dot_general x16, matrix products, gather_rows(): jnp.dot(pick[s], shards[s], preferred_element_type=f32).astype(bf16)  8.36 us
    all_to_all x1, waiting for transfers between devices, body_ring(): lax.all_to_all(per_token, 'ep', split_axis=0, concat_axis=0, tiled=True)  7.19 us
    slice x9, local copies, waits for them, and re-layouts, after(): other[(slice(0, 1),) * other.ndim].reshape((1,) * array.ndim)  5.94 us
  transfers between devices with their start and end apart: 32, of which 14 were waited for; matrix products, arithmetic and copies ran while one was open for 15% of the time, Pallas kernels for 20%

profile of v12, /device:TPU:0, one launch (start us, length us, event | category | flops | bytes accessed | tf_op | source)
XLA Modules:
  0.0 201.0 jit_solution(9067876244756360855)
XLA Ops:
  1.7 2.6 %collective-permute-start.2 = (bf16[128,2048]{1,0:T(8,128)(2,1)}, bf16[128,2048]{1,0:T(8,128)(2,1)}, u32[]{:S(2)}, u32[]{:S(2)}) collective-permute-start(bf16[128,2048]{1,0:T(8,128)(2,1)} %param.7), channel_id=1, source_target_pairs={{0,1},{2,0},{4,2},{6,4},{7,6},{5,7},{3,5},{1,3},{8,9},{10,8},{12,1... | collective-permute-start | bytes 1572872 | tf_op jit(solution)/shard_map/ppermute | solution.py:95
  5.7 16.4 %all_to_all.10.refs_1_ = f32[8,8,128]{2,1,0:T(8,128)} all-to-all(f32[8,8,128]{2,1,0:T(8,128)S(1)} %broadcast_in_dim.10), channel_id=1, replica_groups=mesh['rep'=2,'grp'=2,'ep'=8] {'ep'}, dimensions={0} | all-to-all | bytes 65536 | tf_op jit(solution)/shard_map/all_to_all | solution.py:460
  22.5 1.6 collective-permute-start.7
  24.2 11.0 %collective-permute-done.3.refs_0_.refs_2_ = bf16[128,2048]{1,0:T(8,128)(2,1)} collective-permute-done((bf16[128,2048]{1,0:T(8,128)(2,1)}, bf16[128,2048]{1,0:T(8,128)(2,1)}, u32[]{:S(2)}, u32[]{:S(2)}) %collective-permute-start.3) | collective-permute-done | bytes 524320 | tf_op jit(solution)/shard_map/ppermute | solution.py:95
  36.4 1.7 copy-done
  38.9 1.6 collective-permute-start.8
  41.7 1.4 convolution_convert_fusion.13.refs_6_
  43.1 1.3 convolution_convert_fusion.17.refs_2_
  44.4 1.3 convolution_convert_fusion.12.refs_7_
  45.7 1.3 convolution_convert_fusion.18.refs_1_
  47.9 1.2 collective-permute-start.19
  49.7 4.3 %collective-permute-done.8 = bf16[128,2048]{1,0:T(8,128)(2,1)S(1)} collective-permute-done((bf16[128,2048]{1,0:T(8,128)(2,1)}, bf16[128,2048]{1,0:T(8,128)(2,1)S(1)}, u32[]{:S(2)}, u32[]{:S(2)}) %collective-permute-start.8) | collective-permute-done | bytes 524320 | tf_op jit(solution)/shard_map/ppermute | solution.py:95
  53.9 1.6 collective-permute-start.9
  55.8 8.2 %collective-permute-done.10 = bf16[128,2048]{1,0:T(8,128)(2,1)S(1)} collective-permute-done((bf16[128,2048]{1,0:T(8,128)(2,1)S(1)}, bf16[128,2048]{1,0:T(8,128)(2,1)S(1)}, u32[]{:S(2)}, u32[]{:S(2)}) %collective-permute-start.10) | collective-permute-done | bytes 524320 | tf_op jit(solution)/shard_map/ppermute | solution.py:95
  65.2 1.6 collective-permute-start.20
  67.6 8.5 %collective-permute-done.11.refs_12_ = bf16[128,2048]{1,0:T(8,128)(2,1)S(1)} collective-permute-done((bf16[128,2048]{1,0:T(8,128)(2,1)S(1)}, bf16[128,2048]{1,0:T(8,128)(2,1)S(1)}, u32[]{:S(2)}, u32[]{:S(2)}) %collective-permute-start.11) | collective-permute-done | bytes 524320 | tf_op jit(solution)/shard_map/ppermute | solution.py:95
  76.5 8.4 %collective-permute-done.20 = bf16[128,2048]{1,0:T(8,128)(2,1)S(1)} collective-permute-done((bf16[128,2048]{1,0:T(8,128)(2,1)S(1)}, bf16[128,2048]{1,0:T(8,128)(2,1)S(1)}, u32[]{:S(2)}, u32[]{:S(2)}) %collective-permute-start.20) | collective-permute-done | bytes 524320 | tf_op jit(solution)/shard_map/ppermute | solution.py:95
  84.9 1.6 collective-permute-start.21
  87.3 10.5 %shard_map.100 = (bf16[2,384,768]{2,1,0:T(8,128)(2,1)S(1)}, f32[2,384,768]{2,1,0:T(8,128)}, f32[2,384,768]{2,1,0:T(8,128)}) custom-call(bf16[96,2048]{1,0:T(8,128)(2,1)S(1)} %convolution_convert_fusion.19.refs_0_, bf16[96,2048]{1,0:T(8,128)(2,1)S(1)} %convolution_convert_fusion.18.refs_1_, bf16[96,2048]{1,0:T(8,128)(2,1)S(1)} %convolution_convert_fusion.17.refs_2_, ...), custom_call_target="tpu_custom_call" | custom-call | flops 4831838208 | bytes 1048576 | tf_op jit(solution)/shard_map/pallas_call | solution.py:168
  98.3 4.7 %shard_map.101.refs_9_ = bf16[8,96,2048]{2,1,0:T(8,128)(2,1)S(1)} custom-call(bf16[2,384,768]{2,1,0:T(8,128)(2,1)S(1)} %get-tuple-element.12.refs_0_, bf16[768,2048]{1,0:T(8,128)(2,1)} %bitcast.167, bf16[768,2048]{1,0:T(8,128)(2,1)} %copy-done, bf16[128,2048]{1,0:T(8,128)(2,1)S(1)} %collective-permute-done.12.refs_3_), custom_call_target="tpu_custom_call" | custom-call | flops 2415919104 | bytes 1048576 | tf_op jit(solution)/shard_map/pallas_call | solution.py:168
  103.3 1.7 collective-permute-start.13
  105.2 2.6 %collective-permute-done.17 = bf16[128,2048]{1,0:T(8,128)(2,1)S(1)} collective-permute-done((bf16[128,2048]{1,0:T(8,128)(2,1)S(1)}, bf16[128,2048]{1,0:T(8,128)(2,1)S(1)}, u32[]{:S(2)}, u32[]{:S(2)}) %collective-permute-start.17) | collective-permute-done | bytes 524320 | tf_op jit(solution)/shard_map/ppermute | solution.py:95
  110.9 9.6 %shard_map.102 = (bf16[2,384,768]{2,1,0:T(8,128)(2,1)S(1)}, bf16[2,384,768]{2,1,0:T(8,128)(2,1)S(1)}) custom-call(bf16[96,2048]{1,0:T(8,128)(2,1)S(1)} %convolution_convert_fusion.11.refs_0_.refs_1_, bf16[96,2048]{1,0:T(8,128)(2,1)S(1)} %convolution_convert_fusion.10.refs_1_.refs_2_, bf16[96,2048]{1,0:T(8,128)(2,1)S(1)} %convolution_convert_fusion.9.refs_2_.refs_3_, ...), custom_call_target="tpu_custom_call" | custom-call | flops 2415919104 | bytes 1048576 | tf_op jit(solution)/shard_map/pallas_call | solution.py:168
  123.2 1.3 collective-permute-start.14
  124.5 10.3 %shard_map.103 = bf16[8,96,2048]{2,1,0:T(8,128)(2,1)} custom-call(bf16[2,384,768]{2,1,0:T(8,128)(2,1)S(1)} %get-tuple-element.15.refs_0_.refs_11_, bf16[2,384,768]{2,1,0:T(8,128)(2,1)S(1)} %get-tuple-element.16.refs_1_, bf16[2048,768]{1,0:T(8,128)(2,1)} %bitcast.171, bf16[2048,768]{1,0:T(8,128)(2,1)} %collective-permute-done.refs_2_.refs_9_.refs_3_, ...), custom_call_target="tpu_custom_call" | custom-call | flops 4831838208 | bytes 1048576 | tf_op jit(solution)/shard_map/pallas_call | solution.py:168
  137.2 1.3 fusion.14
  139.4 1.5 collective-permute-start.15
  140.9 3.4 %shard_map.104 = f32[8,2,128]{2,1,0:T(2,128)} custom-call(s32[2]{0:T(128)S(1)} %pad_add_fusion.1.refs_0_, bf16[96,2048]{1,0:T(8,128)(2,1)S(1)} %convolution_convert_fusion.11.refs_0_.refs_1_, bf16[96,2048]{1,0:T(8,128)(2,1)S(1)} %convolution_convert_fusion.10.refs_1_.refs_2_, bf16[96,2048]{1,0:T(8,128)(2,1)S(1)} %convolution_convert_fusion.9.refs_2_.refs_3_, ...), custom_call_target="tpu_custom_call" | custom-call | flops 1048576 | bytes 1048576 | tf_op jit(solution)/shard_map/pallas_call | solution.py:168
  144.4 1.1 slice.198
  147.7 1.3 collective-permute-start.28
  148.9 1.5 collective-permute-done.23
  151.6 7.1 %collective-permute-done.24 = bf16[128,2048]{1,0:T(8,128)(2,1)S(1)} collective-permute-done((bf16[128,2048]{1,0:T(8,128)(2,1)S(1)}, bf16[128,2048]{1,0:T(8,128)(2,1)S(1)}, u32[]{:S(2)}, u32[]{:S(2)}) %collective-permute-start.24) | collective-permute-done | bytes 524320 | tf_op jit(solution)/shard_map/ppermute | solution.py:95
  161.1 2.1 %fusion.3 = bf16[128,2048]{1,0:T(8,128)(2,1)} fusion(bf16[128,2048]{1,0:T(8,128)(2,1)S(1)} %collective-permute-done.15, bf16[8,96,2048]{2,1,0:T(8,128)(2,1)} %copy-done.1, bf16[8,96,128]{2,1,0:T(8,128)(2,1)S(1)} %get-tuple-element.10), kind=kOutput, calls=%fused_computation.15 | convolution fusion | flops 51118080 | bytes 1466368 | tf_op jit(solution)/shard_map/dot_general | solution.py:482
  163.2 1.3 collective-permute-start.16
  164.5 1.2 fusion.16
  165.7 1.2 collective-permute-start.29
  166.9 4.0 %collective-permute-done.25 = bf16[128,2048]{1,0:T(8,128)(2,1)S(1)} collective-permute-done((bf16[128,2048]{1,0:T(8,128)(2,1)S(1)}, bf16[128,2048]{1,0:T(8,128)(2,1)S(1)}, u32[]{:S(2)}, u32[]{:S(2)}) %collective-permute-start.25) | collective-permute-done | bytes 524320 | tf_op jit(solution)/shard_map/ppermute | solution.py:95
  172.1 1.2 collective-permute-start.26
  173.3 3.7 %all-to-all-start.1 = ((f32[8,2,128]{2,1,0:T(2,128)}), f32[8,2,128]{2,1,0:T(2,128)S(1)}, u32[]{:S(2)}, u32[]{:S(2)}) async-start(f32[8,2,128]{2,1,0:T(2,128)} %shard_map.104), calls=%async_computation.1 | async-start | bytes 16384 | tf_op jit(solution)/shard_map/all_to_all | solution.py:507
  177.0 7.2 %all-to-all-done.1 = f32[8,2,128]{2,1,0:T(2,128)S(1)} async-done(((f32[8,2,128]{2,1,0:T(2,128)}), f32[8,2,128]{2,1,0:T(2,128)S(1)}, u32[]{:S(2)}, u32[]{:S(2)}) %all-to-all-start.1) | async-done | bytes 8224 | tf_op jit(solution)/shard_map/all_to_all | solution.py:507
  185.4 1.2 slice.205
  187.3 1.4 fusion.17
  189.2 1.4 fusion.19
  190.6 1.6 collective-permute-start.27
  192.8 2.3 %fusion.2 = bf16[128,2048]{1,0:T(8,128)(2,1)} fusion(bf16[128,2048]{1,0:T(8,128)(2,1)S(1)} %copy-done.9, bf16[128,2048]{1,0:T(8,128)(2,1)} %collective-permute-done.16, bf16[8,96,2048]{2,1,0:T(8,128)(2,1)} %copy-done.1, bf16[8,96,128]{2,1,0:T(8,128)(2,1)S(1)} %get-tuple-element.10), kind=kOutput, calls=%fused_computation.14 | convolution fusion | flops 51642368 | bytes 1990656 | tf_op jit(solution)/shard_map/dot_general | solution.py:482
  195.1 2.7 %collective-permute-done.30 = bf16[128,2048]{1,0:T(8,128)(2,1)S(1)} collective-permute-done((bf16[128,2048]{1,0:T(8,128)(2,1)S(1)}, bf16[128,2048]{1,0:T(8,128)(2,1)S(1)}, u32[]{:S(2)}, u32[]{:S(2)}) %collective-permute-start.30) | collective-permute-done | bytes 524320 | tf_op jit(solution)/shard_map/ppermute | solution.py:95
  197.9 2.0 collective-permute-done.27
  199.8 1.1 fusion.8
  (100 shorter events, 25.0 us)
Async XLA Ops:
  0.6 34.7 %collective-permute-start.4 = (bf16[768,2048]{1,0:T(8,128)(2,1)}, bf16[768,2048]{1,0:T(8,128)(2,1)S(1)}, u32[]{:S(2)}, u32[]{:S(2)}) collective-permute-start(bf16[768,2048]{1,0:T(8,128)(2,1)} %bitcast.166), channel_id=1, source_target_pairs={{0,8},{8,0},{1,9},{9,1},{2,10},{10,2},{3,11},{11,3},{4,12},{12,4},... | collective-permute-start | bytes 9437192 | tf_op jit(solution)/shard_map/ppermute | solution.py:443
  1.1 39.8 %collective-permute-start = (bf16[2048,768]{1,0:T(8,128)(2,1)}, bf16[2048,768]{1,0:T(8,128)(2,1)}, u32[]{:S(2)}, u32[]{:S(2)}) collective-permute-start(bf16[2048,768]{1,0:T(8,128)(2,1)} %bitcast.169), channel_id=1, source_target_pairs={{0,8},{8,0},{1,9},{9,1},{2,10},{10,2},{3,11},{11,3},{4,12},{12,4},... | collective-permute-start | bytes 9437192 | tf_op jit(solution)/shard_map/ppermute | solution.py:443
  1.2 39.7 %collective-permute-start.1 = (bf16[2048,768]{1,0:T(8,128)(2,1)}, bf16[2048,768]{1,0:T(8,128)(2,1)}, u32[]{:S(2)}, u32[]{:S(2)}) collective-permute-start(bf16[2048,768]{1,0:T(8,128)(2,1)} %bitcast.172), channel_id=1, source_target_pairs={{0,8},{8,0},{1,9},{9,1},{2,10},{10,2},{3,11},{11,3},{4,12},{12,4},... | collective-permute-start | bytes 9437192 | tf_op jit(solution)/shard_map/ppermute | solution.py:443
  1.7 20.4 %collective-permute-start.2 = (bf16[128,2048]{1,0:T(8,128)(2,1)}, bf16[128,2048]{1,0:T(8,128)(2,1)}, u32[]{:S(2)}, u32[]{:S(2)}) collective-permute-start(bf16[128,2048]{1,0:T(8,128)(2,1)} %param.7), channel_id=1, source_target_pairs={{0,1},{2,0},{4,2},{6,4},{7,6},{5,7},{3,5},{1,3},{8,9},{10,8},{12,1... | collective-permute-start | bytes 1572872 | tf_op jit(solution)/shard_map/ppermute | solution.py:95
  4.2 18.3 %collective-permute-start.6 = (bf16[128,2048]{1,0:T(8,128)(2,1)}, bf16[128,2048]{1,0:T(8,128)(2,1)}, u32[]{:S(2)}, u32[]{:S(2)}) collective-permute-start(bf16[128,2048]{1,0:T(8,128)(2,1)} %param.7), channel_id=1, source_target_pairs={{0,2},{2,4},{4,6},{6,7},{7,5},{5,3},{3,1},{1,0},{8,10},{10,12},{12... | collective-permute-start | bytes 1572872 | tf_op jit(solution)/shard_map/ppermute | solution.py:95
  22.1 13.1 %collective-permute-start.3 = (bf16[128,2048]{1,0:T(8,128)(2,1)}, bf16[128,2048]{1,0:T(8,128)(2,1)}, u32[]{:S(2)}, u32[]{:S(2)}) collective-permute-start(bf16[128,2048]{1,0:T(8,128)(2,1)} %shard_map.95), channel_id=1, source_target_pairs={{0,1},{2,0},{4,2},{6,4},{7,6},{5,7},{3,5},{1,3},{8,9},{10,8},{12,1... | collective-permute-start | bytes 1572872 | tf_op jit(solution)/shard_map/ppermute | solution.py:95
  22.5 12.8 %collective-permute-start.7 = (bf16[128,2048]{1,0:T(8,128)(2,1)}, bf16[128,2048]{1,0:T(8,128)(2,1)}, u32[]{:S(2)}, u32[]{:S(2)}) collective-permute-start(bf16[128,2048]{1,0:T(8,128)(2,1)} %shard_map.97), channel_id=1, source_target_pairs={{0,2},{2,4},{4,6},{6,7},{7,5},{5,3},{3,1},{1,0},{8,10},{10,12},{12... | collective-permute-start | bytes 1572872 | tf_op jit(solution)/shard_map/ppermute | solution.py:95
  35.3 1.0 copy-start.5
  36.4 1.7 copy-start
  38.1 0.8 copy-start.2
  38.9 2.0 %copy-start.4 = (f32[8,8,128]{2,1,0:T(8,128)S(1)}, f32[8,8,128]{2,1,0:T(8,128)}, u32[]{:S(2)}) copy-start(f32[8,8,128]{2,1,0:T(8,128)} %all_to_all.10.refs_1_) | copy-start | bytes 98308
  38.9 15.1 %collective-permute-start.8 = (bf16[128,2048]{1,0:T(8,128)(2,1)}, bf16[128,2048]{1,0:T(8,128)(2,1)S(1)}, u32[]{:S(2)}, u32[]{:S(2)}) collective-permute-start(bf16[128,2048]{1,0:T(8,128)(2,1)} %shard_map.98), channel_id=1, source_target_pairs={{0,2},{2,4},{4,6},{6,7},{7,5},{5,3},{3,1},{1,0},{8,10},{10,12},{12... | collective-permute-start | bytes 1572872 | tf_op jit(solution)/shard_map/ppermute | solution.py:95
  40.5 26.8 %collective-permute-start.5 = (bf16[128,2048]{1,0:T(8,128)(2,1)}, bf16[128,2048]{1,0:T(8,128)(2,1)S(1)}, u32[]{:S(2)}, u32[]{:S(2)}) collective-permute-start(bf16[128,2048]{1,0:T(8,128)(2,1)} %shard_map.96), channel_id=1, source_target_pairs={{0,1},{2,0},{4,2},{6,4},{7,6},{5,7},{3,5},{1,3},{8,9},{10,8},{12,1... | collective-permute-start | bytes 1572872 | tf_op jit(solution)/shard_map/ppermute | solution.py:95
  41.7 5.3 %copy-start.3 = (bf16[128,2048]{1,0:T(8,128)(2,1)S(1)}, bf16[128,2048]{1,0:T(8,128)(2,1)}, u32[]{:S(2)}) copy-start(bf16[128,2048]{1,0:T(8,128)(2,1)} %copy-done.2) | copy-start | bytes 1572868
  41.7 7.4 %copy-start.7 = (bf16[128,2048]{1,0:T(8,128)(2,1)S(1)}, bf16[128,2048]{1,0:T(8,128)(2,1)}, u32[]{:S(2)}) copy-start(bf16[128,2048]{1,0:T(8,128)(2,1)} %param.7) | copy-start | bytes 1572868
  47.0 17.0 %collective-permute-start.10 = (bf16[128,2048]{1,0:T(8,128)(2,1)S(1)}, bf16[128,2048]{1,0:T(8,128)(2,1)S(1)}, u32[]{:S(2)}, u32[]{:S(2)}) collective-permute-start(bf16[128,2048]{1,0:T(8,128)(2,1)S(1)} %copy-done.3), channel_id=1, source_target_pairs={{0,1},{2,0},{4,2},{6,4},{7,6},{5,7},{3,5},{1,3},{8,9},{10,8},{12,1... | collective-permute-start | bytes 1572872 | tf_op jit(solution)/shard_map/ppermute | solution.py:95
  47.9 17.3 %collective-permute-start.19 = (bf16[128,2048]{1,0:T(8,128)(2,1)S(1)}, bf16[128,2048]{1,0:T(8,128)(2,1)S(1)}, u32[]{:S(2)}, u32[]{:S(2)}) collective-permute-start(bf16[128,2048]{1,0:T(8,128)(2,1)S(1)} %copy-done.3), channel_id=1, source_target_pairs={{0,2},{2,4},{4,6},{6,7},{7,5},{5,3},{3,1},{1,0},{8,10},{10,12},{12... | collective-permute-start | bytes 1572872 | tf_op jit(solution)/shard_map/ppermute | solution.py:95
  53.9 33.1 %collective-permute-start.9 = (bf16[128,2048]{1,0:T(8,128)(2,1)S(1)}, bf16[128,2048]{1,0:T(8,128)(2,1)S(1)}, u32[]{:S(2)}, u32[]{:S(2)}) collective-permute-start(bf16[128,2048]{1,0:T(8,128)(2,1)S(1)} %collective-permute-done.8), channel_id=1, source_target_pairs={{0,2},{2,4},{4,6},{6,7},{7,5},{5,3},{3,1},{1,0},{8,10},{10,12},{12... | collective-permute-start | bytes 1572872 | tf_op jit(solution)/shard_map/ppermute | solution.py:95
  64.0 12.1 %collective-permute-start.11 = (bf16[128,2048]{1,0:T(8,128)(2,1)S(1)}, bf16[128,2048]{1,0:T(8,128)(2,1)S(1)}, u32[]{:S(2)}, u32[]{:S(2)}) collective-permute-start(bf16[128,2048]{1,0:T(8,128)(2,1)S(1)} %collective-permute-done.10), channel_id=1, source_target_pairs={{0,1},{2,0},{4,2},{6,4},{7,6},{5,7},{3,5},{1,3},{8,9},{10,8},{12,1... | collective-permute-start | bytes 1572872 | tf_op jit(solution)/shard_map/ppermute | solution.py:95
  65.2 19.7 %collective-permute-start.20 = (bf16[128,2048]{1,0:T(8,128)(2,1)S(1)}, bf16[128,2048]{1,0:T(8,128)(2,1)S(1)}, u32[]{:S(2)}, u32[]{:S(2)}) collective-permute-start(bf16[128,2048]{1,0:T(8,128)(2,1)S(1)} %collective-permute-done.19), channel_id=1, source_target_pairs={{0,2},{2,4},{4,6},{6,7},{7,5},{5,3},{3,1},{1,0},{8,10},{10,12},{12... | collective-permute-start | bytes 1572872 | tf_op jit(solution)/shard_map/ppermute | solution.py:95
  76.1 21.7 %collective-permute-start.12 = (bf16[128,2048]{1,0:T(8,128)(2,1)S(1)}, bf16[128,2048]{1,0:T(8,128)(2,1)S(1)}, u32[]{:S(2)}, u32[]{:S(2)}) collective-permute-start(bf16[128,2048]{1,0:T(8,128)(2,1)S(1)} %collective-permute-done.11.refs_12_), channel_id=1, source_target_pairs={{0,1},{2,0},{4,2},{6,4},{7,6},{5,7},{3,5},{1,3},{8,9},{10,8},{12,1... | collective-permute-start | bytes 1572872 | tf_op jit(solution)/shard_map/ppermute | solution.py:95
  84.9 25.5 %collective-permute-start.21 = (bf16[128,2048]{1,0:T(8,128)(2,1)S(1)}, bf16[128,2048]{1,0:T(8,128)(2,1)S(1)}, u32[]{:S(2)}, u32[]{:S(2)}) collective-permute-start(bf16[128,2048]{1,0:T(8,128)(2,1)S(1)} %collective-permute-done.20), channel_id=1, source_target_pairs={{0,2},{2,4},{4,6},{6,7},{7,5},{5,3},{3,1},{1,0},{8,10},{10,12},{12... | collective-permute-start | bytes 1572872 | tf_op jit(solution)/shard_map/ppermute | solution.py:95
  97.8 10.0 %collective-permute-start.17 = (bf16[128,2048]{1,0:T(8,128)(2,1)S(1)}, bf16[128,2048]{1,0:T(8,128)(2,1)S(1)}, u32[]{:S(2)}, u32[]{:S(2)}) collective-permute-start(bf16[128,2048]{1,0:T(8,128)(2,1)S(1)} %collective-permute-done.12.refs_3_), channel_id=1, source_target_pairs={{0,1},{2,0},{4,2},{6,4},{7,6},{5,7},{3,5},{1,3},{8,9},{10,8},{12,1... | collective-permute-start | bytes 1572872 | tf_op jit(solution)/shard_map/ppermute | solution.py:95
  103.0 36.2 %copy-start.1 = (bf16[8,96,2048]{2,1,0:T(8,128)(2,1)}, bf16[8,96,2048]{2,1,0:T(8,128)(2,1)S(1)}, u32[]{:S(2)}) copy-start(bf16[8,96,2048]{2,1,0:T(8,128)(2,1)S(1)} %shard_map.101.refs_9_) | copy-start | bytes 9437188
  103.3 19.6 %collective-permute-start.13 = (bf16[128,2048]{1,0:T(8,128)(2,1)S(1)}, bf16[128,2048]{1,0:T(8,128)(2,1)S(1)}, u32[]{:S(2)}, u32[]{:S(2)}) collective-permute-start(bf16[128,2048]{1,0:T(8,128)(2,1)S(1)} %convolution_convert_fusion.3), channel_id=1, source_target_pairs={{0,2},{2,4},{4,6},{6,7},{7,5},{5,3},{3,1},{1,0},{8,10},{10,12},{12... | collective-permute-start | bytes 1572872 | tf_op jit(solution)/shard_map/ppermute | solution.py:95
  109.3 12.4 %collective-permute-start.18 = (bf16[128,2048]{1,0:T(8,128)(2,1)S(1)}, bf16[128,2048]{1,0:T(8,128)(2,1)S(1)}, u32[]{:S(2)}, u32[]{:S(2)}) collective-permute-start(bf16[128,2048]{1,0:T(8,128)(2,1)S(1)} %broadcast_add_fusion), channel_id=1, source_target_pairs={{0,1},{2,0},{4,2},{6,4},{7,6},{5,7},{3,5},{1,3},{8,9},{10,8},{12,1... | collective-permute-start | bytes 1572872 | tf_op jit(solution)/shard_map/ppermute | solution.py:95
  122.0 12.8 %collective-permute-start.22 = (bf16[128,2048]{1,0:T(8,128)(2,1)S(1)}, bf16[128,2048]{1,0:T(8,128)(2,1)S(1)}, u32[]{:S(2)}, u32[]{:S(2)}) collective-permute-start(bf16[128,2048]{1,0:T(8,128)(2,1)S(1)} %fusion.20), channel_id=1, source_target_pairs={{0,1},{2,0},{4,2},{6,4},{7,6},{5,7},{3,5},{1,3},{8,9},{10,8},{12,1... | collective-permute-start | bytes 1572872 | tf_op jit(solution)/shard_map/ppermute | solution.py:95
  123.2 15.9 %collective-permute-start.14 = (bf16[128,2048]{1,0:T(8,128)(2,1)S(1)}, bf16[128,2048]{1,0:T(8,128)(2,1)S(1)}, u32[]{:S(2)}, u32[]{:S(2)}) collective-permute-start(bf16[128,2048]{1,0:T(8,128)(2,1)S(1)} %fusion.5), channel_id=1, source_target_pairs={{0,2},{2,4},{4,6},{6,7},{7,5},{5,3},{3,1},{1,0},{8,10},{10,12},{12... | collective-permute-start | bytes 1572872 | tf_op jit(solution)/shard_map/ppermute | solution.py:95
  136.3 14.2 %collective-permute-start.23 = (bf16[128,2048]{1,0:T(8,128)(2,1)S(1)}, bf16[128,2048]{1,0:T(8,128)(2,1)S(1)}, u32[]{:S(2)}, u32[]{:S(2)}) collective-permute-start(bf16[128,2048]{1,0:T(8,128)(2,1)S(1)} %fusion.6), channel_id=1, source_target_pairs={{0,1},{2,0},{4,2},{6,4},{7,6},{5,7},{3,5},{1,3},{8,9},{10,8},{12,1... | collective-permute-start | bytes 1572872 | tf_op jit(solution)/shard_map/ppermute | solution.py:95
  138.5 20.3 %collective-permute-start.24 = (bf16[128,2048]{1,0:T(8,128)(2,1)S(1)}, bf16[128,2048]{1,0:T(8,128)(2,1)S(1)}, u32[]{:S(2)}, u32[]{:S(2)}) collective-permute-start(bf16[128,2048]{1,0:T(8,128)(2,1)S(1)} %fusion.14), channel_id=1, source_target_pairs={{0,1},{2,0},{4,2},{6,4},{7,6},{5,7},{3,5},{1,3},{8,9},{10,8},{12,1... | collective-permute-start | bytes 1572872 | tf_op jit(solution)/shard_map/ppermute | solution.py:95
  139.4 7.9 %copy-start.6 = (bf16[8,96,2048]{2,1,0:T(8,128)(2,1)S(1)}, bf16[8,96,2048]{2,1,0:T(8,128)(2,1)}, u32[]{:S(2)}) copy-start(bf16[8,96,2048]{2,1,0:T(8,128)(2,1)} %shard_map.103) | copy-start | bytes 9437188
  139.4 20.5 %collective-permute-start.15 = (bf16[128,2048]{1,0:T(8,128)(2,1)S(1)}, bf16[128,2048]{1,0:T(8,128)(2,1)S(1)}, u32[]{:S(2)}, u32[]{:S(2)}) collective-permute-start(bf16[128,2048]{1,0:T(8,128)(2,1)S(1)} %fusion.4), channel_id=1, source_target_pairs={{0,2},{2,4},{4,6},{6,7},{7,5},{5,3},{3,1},{1,0},{8,10},{10,12},{12... | collective-permute-start | bytes 1572872 | tf_op jit(solution)/shard_map/ppermute | solution.py:95
  147.7 16.8 %collective-permute-start.28 = (bf16[128,2048]{1,0:T(8,128)(2,1)S(1)}, bf16[128,2048]{1,0:T(8,128)(2,1)S(1)}, u32[]{:S(2)}, u32[]{:S(2)}) collective-permute-start(bf16[128,2048]{1,0:T(8,128)(2,1)S(1)} %fusion.15), channel_id=1, source_target_pairs={{0,2},{2,4},{4,6},{6,7},{7,5},{5,3},{3,1},{1,0},{8,10},{10,12},{12... | collective-permute-start | bytes 1572872 | tf_op jit(solution)/shard_map/ppermute | solution.py:95
  150.4 8.3 %copy-start.8 = (bf16[128,2048]{1,0:T(8,128)(2,1)}, bf16[128,2048]{1,0:T(8,128)(2,1)S(1)}, u32[]{:S(2)}) copy-start(bf16[128,2048]{1,0:T(8,128)(2,1)S(1)} %collective-permute-done.23) | copy-start | bytes 1572868
  159.1 11.8 %collective-permute-start.25 = (bf16[128,2048]{1,0:T(8,128)(2,1)S(1)}, bf16[128,2048]{1,0:T(8,128)(2,1)S(1)}, u32[]{:S(2)}, u32[]{:S(2)}) collective-permute-start(bf16[128,2048]{1,0:T(8,128)(2,1)S(1)} %fusion.21), channel_id=1, source_target_pairs={{0,1},{2,0},{4,2},{6,4},{7,6},{5,7},{3,5},{1,3},{8,9},{10,8},{12,1... | collective-permute-start | bytes 1572872 | tf_op jit(solution)/shard_map/ppermute | solution.py:95
  163.2 28.9 %copy-start.10 = (s32[128,4]{0,1:T(4,128)S(1)}, s32[128,4]{0,1:T(4,128)}, u32[]{:S(2)}) copy-start(s32[128,4]{0,1:T(4,128)} %param.9) | copy-start | bytes 6148
  163.2 22.2 %collective-permute-start.16 = (bf16[128,2048]{1,0:T(8,128)(2,1)}, bf16[128,2048]{1,0:T(8,128)(2,1)}, u32[]{:S(2)}, u32[]{:S(2)}) collective-permute-start(bf16[128,2048]{1,0:T(8,128)(2,1)} %fusion.3), channel_id=1, source_target_pairs={{0,2},{2,4},{4,6},{6,7},{7,5},{5,3},{3,1},{1,0},{8,10},{10,12},{12... | collective-permute-start | bytes 1572872 | tf_op jit(solution)/shard_map/ppermute | solution.py:95
  165.7 21.6 %collective-permute-start.29 = (bf16[128,2048]{1,0:T(8,128)(2,1)}, bf16[128,2048]{1,0:T(8,128)(2,1)}, u32[]{:S(2)}, u32[]{:S(2)}) collective-permute-start(bf16[128,2048]{1,0:T(8,128)(2,1)} %fusion.16), channel_id=1, source_target_pairs={{0,2},{2,4},{4,6},{6,7},{7,5},{5,3},{3,1},{1,0},{8,10},{10,12},{12... | collective-permute-start | bytes 1572872 | tf_op jit(solution)/shard_map/ppermute | solution.py:95
  172.1 17.1 %collective-permute-start.26 = (bf16[128,2048]{1,0:T(8,128)(2,1)}, bf16[128,2048]{1,0:T(8,128)(2,1)}, u32[]{:S(2)}, u32[]{:S(2)}) collective-permute-start(bf16[128,2048]{1,0:T(8,128)(2,1)} %fusion.10), channel_id=1, source_target_pairs={{0,1},{2,0},{4,2},{6,4},{7,6},{5,7},{3,5},{1,3},{8,9},{10,8},{12,1... | collective-permute-start | bytes 1572872 | tf_op jit(solution)/shard_map/ppermute | solution.py:95
  173.3 10.9 %all-to-all-start.1 = ((f32[8,2,128]{2,1,0:T(2,128)}), f32[8,2,128]{2,1,0:T(2,128)S(1)}, u32[]{:S(2)}, u32[]{:S(2)}) async-start(f32[8,2,128]{2,1,0:T(2,128)} %shard_map.104), calls=%async_computation.1 | async-start | bytes 16384 | tf_op jit(solution)/shard_map/all_to_all | solution.py:507
  184.2 8.6 %copy-start.9 = (bf16[128,2048]{1,0:T(8,128)(2,1)S(1)}, bf16[128,2048]{1,0:T(8,128)(2,1)}, u32[]{:S(2)}) copy-start(bf16[128,2048]{1,0:T(8,128)(2,1)} %copy-done.8) | copy-start | bytes 1572868
  188.6 9.2 %collective-permute-start.30 = (bf16[128,2048]{1,0:T(8,128)(2,1)S(1)}, bf16[128,2048]{1,0:T(8,128)(2,1)S(1)}, u32[]{:S(2)}, u32[]{:S(2)}) collective-permute-start(bf16[128,2048]{1,0:T(8,128)(2,1)S(1)} %fusion.17), channel_id=1, source_target_pairs={{0,2},{2,4},{4,6},{6,7},{7,5},{5,3},{3,1},{1,0},{8,10},{10,12},{12... | collective-permute-start | bytes 1572872 | tf_op jit(solution)/shard_map/ppermute | solution.py:95
  190.6 9.2 %collective-permute-start.27 = (bf16[128,2048]{1,0:T(8,128)(2,1)S(1)}, bf16[128,2048]{1,0:T(8,128)(2,1)S(1)}, u32[]{:S(2)}, u32[]{:S(2)}) collective-permute-start(bf16[128,2048]{1,0:T(8,128)(2,1)S(1)} %fusion.19), channel_id=1, source_target_pairs={{0,1},{2,0},{4,2},{6,4},{7,6},{5,7},{3,5},{1,3},{8,9},{10,8},{12,1... | collective-permute-start | bytes 1572872 | tf_op jit(solution)/shard_map/ppermute | solution.py:95

commit v13 on v12

--- a/solution.py
+++ b/solution.py
@@ -511,7 +511,7 @@
         for hop in range(len(mixed_hops[step]) - 1)
     }
     behind[-1, 1] += (per_token,)
-    behind[-1, 3] = (returned,)
+    behind[-1, 2] = (returned,)
     d_tokens, _ = ring_reduce(scatter_rows(d_copies), chips, -1, behind)
     chip_ids = jnp.arange(chips, dtype=jnp.int32)
     served = jnp.stack([core * chips + chip_ids, (1 - core) * chips + chip_ids], axis=1)

time: 202 us -> 204 us (level)
  waiting for transfers between devices: 68.4 us -> 60.8 us
  matrix products: 22.8 us -> 30.3 us
    dot_general x16, matrix products: 14.5 us -> 21.9 us  [share_of(): lax.dot_general(spread[s], blocks[s], (((0,), (0,)), ((), ())), preferred...]
    all_to_all x1, waiting for transfers between devices: 7.19 us -> 0.01 us  [body_ring(): lax.all_to_all(per_token, 'ep', split_axis=0, concat_axis=0, tiled=True)]
  transfers between devices with their start and end apart: 32 -> 32, of which waited for: 14 -> 12; matrix products, arithmetic and copies ran while one was open for 15% -> 19% of each run, Pallas kernels for 20% -> 19%
where the time goes in v13:
time: 204 us; the launch traced here: 203 us
  waiting for transfers between devices  60.8 us (30%)
  Pallas kernels  39.3 us (19%)
  starting transfers between devices  36 us (18%)
  matrix products  30.3 us (15%)
  blocking collectives  16.4 us (8%)
  local copies, waits for them, and re-layouts  11.5 us (6%)
  between operations  6.94 us (3%)
  other arithmetic  2.13 us (1%)
    ppermute x28, waiting for transfers between devices, ring_shift(): return lax.ppermute(array, 'ep', pairs)  60.8 us
    pallas_call x7, Pallas kernels, call_kernel(): pl.pallas_call(body, out_shape=outs, in_specs=[pl.BlockSpec(memory_space=...  39.3 us
    ppermute x28, starting transfers between devices, ring_shift(): return lax.ppermute(array, 'ep', pairs)  31.1 us
    dot_general x16, matrix products, share_of(): lax.dot_general(spread[s], blocks[s], (((0,), (0,)), ((), ())), preferred...  21.9 us
    all_to_all x1, blocking collectives, body_ring(): lax.all_to_all(copies, 'ep', split_axis=0, concat_axis=0, tiled=True)  16.4 us
    dot_general x16, matrix products, gather_rows(): jnp.dot(pick[s], shards[s], preferred_element_type=f32).astype(bf16)  8.36 us
    slice x9, local copies, waits for them, and re-layouts, after(): other[(slice(0, 1),) * other.ndim].reshape((1,) * array.ndim)  7.95 us
  transfers between devices with their start and end apart: 32, of which 12 were waited for; matrix products, arithmetic and copies ran while one was open for 19% of the time, Pallas kernels for 19%

profile of v13, /device:TPU:0, one launch (start us, length us, event | category | flops | bytes accessed | tf_op | source)
XLA Modules:
  0.0 203.3 jit_solution(565688189151261302)
XLA Ops:
  1.7 2.6 %collective-permute-start.2 = (bf16[128,2048]{1,0:T(8,128)(2,1)}, bf16[128,2048]{1,0:T(8,128)(2,1)}, u32[]{:S(2)}, u32[]{:S(2)}) collective-permute-start(bf16[128,2048]{1,0:T(8,128)(2,1)} %param.7), channel_id=1, source_target_pairs={{0,1},{2,0},{4,2},{6,4},{7,6},{5,7},{3,5},{1,3},{8,9},{10,8},{12,1... | collective-permute-start | bytes 1572872 | tf_op jit(solution)/shard_map/ppermute | solution.py:95
  5.7 16.4 %all_to_all.10.refs_1_ = f32[8,8,128]{2,1,0:T(8,128)} all-to-all(f32[8,8,128]{2,1,0:T(8,128)S(1)} %broadcast_in_dim.10), channel_id=1, replica_groups=mesh['rep'=2,'grp'=2,'ep'=8] {'ep'}, dimensions={0} | all-to-all | bytes 65536 | tf_op jit(solution)/shard_map/all_to_all | solution.py:460
  22.5 1.6 collective-permute-start.7
  24.2 11.0 %collective-permute-done.3.refs_0_.refs_2_ = bf16[128,2048]{1,0:T(8,128)(2,1)} collective-permute-done((bf16[128,2048]{1,0:T(8,128)(2,1)}, bf16[128,2048]{1,0:T(8,128)(2,1)}, u32[]{:S(2)}, u32[]{:S(2)}) %collective-permute-start.3) | collective-permute-done | bytes 524320 | tf_op jit(solution)/shard_map/ppermute | solution.py:95
  36.4 1.7 copy-done
  38.9 1.6 collective-permute-start.8
  41.7 1.4 convolution_convert_fusion.13.refs_6_
  43.1 1.3 convolution_convert_fusion.17.refs_2_
  44.4 1.3 convolution_convert_fusion.12.refs_7_
  45.7 1.3 convolution_convert_fusion.18.refs_1_
  47.9 1.2 collective-permute-start.19
  49.6 4.3 %collective-permute-done.8 = bf16[128,2048]{1,0:T(8,128)(2,1)S(1)} collective-permute-done((bf16[128,2048]{1,0:T(8,128)(2,1)}, bf16[128,2048]{1,0:T(8,128)(2,1)S(1)}, u32[]{:S(2)}, u32[]{:S(2)}) %collective-permute-start.8) | collective-permute-done | bytes 524320 | tf_op jit(solution)/shard_map/ppermute | solution.py:95
  53.9 1.6 collective-permute-start.9
  55.8 8.2 %collective-permute-done.10 = bf16[128,2048]{1,0:T(8,128)(2,1)S(1)} collective-permute-done((bf16[128,2048]{1,0:T(8,128)(2,1)S(1)}, bf16[128,2048]{1,0:T(8,128)(2,1)S(1)}, u32[]{:S(2)}, u32[]{:S(2)}) %collective-permute-start.10) | collective-permute-done | bytes 524320 | tf_op jit(solution)/shard_map/ppermute | solution.py:95
  65.2 1.6 collective-permute-start.20
  67.6 8.5 %collective-permute-done.11.refs_12_ = bf16[128,2048]{1,0:T(8,128)(2,1)S(1)} collective-permute-done((bf16[128,2048]{1,0:T(8,128)(2,1)S(1)}, bf16[128,2048]{1,0:T(8,128)(2,1)S(1)}, u32[]{:S(2)}, u32[]{:S(2)}) %collective-permute-start.11) | collective-permute-done | bytes 524320 | tf_op jit(solution)/shard_map/ppermute | solution.py:95
  76.5 8.4 %collective-permute-done.20 = bf16[128,2048]{1,0:T(8,128)(2,1)S(1)} collective-permute-done((bf16[128,2048]{1,0:T(8,128)(2,1)S(1)}, bf16[128,2048]{1,0:T(8,128)(2,1)S(1)}, u32[]{:S(2)}, u32[]{:S(2)}) %collective-permute-start.20) | collective-permute-done | bytes 524320 | tf_op jit(solution)/shard_map/ppermute | solution.py:95
  84.9 1.6 collective-permute-start.21
  87.3 10.5 %shard_map.100 = (bf16[2,384,768]{2,1,0:T(8,128)(2,1)S(1)}, f32[2,384,768]{2,1,0:T(8,128)}, f32[2,384,768]{2,1,0:T(8,128)}) custom-call(bf16[96,2048]{1,0:T(8,128)(2,1)S(1)} %convolution_convert_fusion.19.refs_0_, bf16[96,2048]{1,0:T(8,128)(2,1)S(1)} %convolution_convert_fusion.18.refs_1_, bf16[96,2048]{1,0:T(8,128)(2,1)S(1)} %convolution_convert_fusion.17.refs_2_, ...), custom_call_target="tpu_custom_call" | custom-call | flops 4831838208 | bytes 1048576 | tf_op jit(solution)/shard_map/pallas_call | solution.py:168
  98.3 4.7 %shard_map.101.refs_9_ = bf16[8,96,2048]{2,1,0:T(8,128)(2,1)S(1)} custom-call(bf16[2,384,768]{2,1,0:T(8,128)(2,1)S(1)} %get-tuple-element.12.refs_0_, bf16[768,2048]{1,0:T(8,128)(2,1)} %bitcast.167, bf16[768,2048]{1,0:T(8,128)(2,1)} %copy-done, bf16[128,2048]{1,0:T(8,128)(2,1)S(1)} %collective-permute-done.12.refs_3_), custom_call_target="tpu_custom_call" | custom-call | flops 2415919104 | bytes 1048576 | tf_op jit(solution)/shard_map/pallas_call | solution.py:168
  103.3 1.7 collective-permute-start.13
  105.2 2.6 %collective-permute-done.17 = bf16[128,2048]{1,0:T(8,128)(2,1)S(1)} collective-permute-done((bf16[128,2048]{1,0:T(8,128)(2,1)S(1)}, bf16[128,2048]{1,0:T(8,128)(2,1)S(1)}, u32[]{:S(2)}, u32[]{:S(2)}) %collective-permute-start.17) | collective-permute-done | bytes 524320 | tf_op jit(solution)/shard_map/ppermute | solution.py:95
  110.9 9.6 %shard_map.102 = (bf16[2,384,768]{2,1,0:T(8,128)(2,1)S(1)}, bf16[2,384,768]{2,1,0:T(8,128)(2,1)S(1)}) custom-call(bf16[96,2048]{1,0:T(8,128)(2,1)S(1)} %convolution_convert_fusion.11.refs_0_.refs_1_, bf16[96,2048]{1,0:T(8,128)(2,1)S(1)} %convolution_convert_fusion.10.refs_1_.refs_2_, bf16[96,2048]{1,0:T(8,128)(2,1)S(1)} %convolution_convert_fusion.9.refs_2_.refs_3_, ...), custom_call_target="tpu_custom_call" | custom-call | flops 2415919104 | bytes 1048576 | tf_op jit(solution)/shard_map/pallas_call | solution.py:168
  123.2 1.3 collective-permute-start.14
  124.5 10.3 %shard_map.103 = bf16[8,96,2048]{2,1,0:T(8,128)(2,1)} custom-call(bf16[2,384,768]{2,1,0:T(8,128)(2,1)S(1)} %get-tuple-element.15.refs_0_.refs_11_, bf16[2,384,768]{2,1,0:T(8,128)(2,1)S(1)} %get-tuple-element.16.refs_1_, bf16[2048,768]{1,0:T(8,128)(2,1)} %bitcast.171, bf16[2048,768]{1,0:T(8,128)(2,1)} %collective-permute-done.refs_2_.refs_9_.refs_3_, ...), custom_call_target="tpu_custom_call" | custom-call | flops 4831838208 | bytes 1048576 | tf_op jit(solution)/shard_map/pallas_call | solution.py:168
  137.9 2.1 %fusion.14 = bf16[128,2048]{1,0:T(8,128)(2,1)} fusion(bf16[8,96,2048]{2,1,0:T(8,128)(2,1)} %shard_map.103, bf16[]{:T(256)} %bitcast.37, bf16[8,96,128]{2,1,0:T(8,128)(2,1)S(1)} %get-tuple-element.10), kind=kOutput, calls=%fused_computation.46 | convolution fusion | flops 50855936 | bytes 942592 | tf_op jit(solution)/shard_map/dot_general | solution.py:482
  141.7 1.4 collective-permute-start.15
  143.1 3.4 %shard_map.104 = f32[8,2,128]{2,1,0:T(2,128)} custom-call(s32[2]{0:T(128)S(1)} %pad_add_fusion.1.refs_0_, bf16[96,2048]{1,0:T(8,128)(2,1)S(1)} %convolution_convert_fusion.11.refs_0_.refs_1_, bf16[96,2048]{1,0:T(8,128)(2,1)S(1)} %convolution_convert_fusion.10.refs_1_.refs_2_, bf16[96,2048]{1,0:T(8,128)(2,1)S(1)} %convolution_convert_fusion.9.refs_2_.refs_3_, ...), custom_call_target="tpu_custom_call" | custom-call | flops 1048576 | bytes 1048576 | tf_op jit(solution)/shard_map/pallas_call | solution.py:168
  147.7 3.9 %all-to-all-start.1 = ((f32[8,2,128]{2,1,0:T(2,128)}), f32[8,2,128]{2,1,0:T(2,128)S(1)}, u32[]{:S(2)}, u32[]{:S(2)}) async-start(f32[8,2,128]{2,1,0:T(2,128)} %shard_map.104), calls=%async_computation.1 | async-start | bytes 16384 | tf_op jit(solution)/shard_map/all_to_all | solution.py:507
  152.2 1.2 slice.203
  155.2 2.0 collective-permute-start.28
  157.3 1.2 slice.197
  159.1 2.2 %fusion.21 = bf16[128,2048]{1,0:T(8,128)(2,1)} fusion(bf16[128,2048]{1,0:T(8,128)(2,1)} %collective-permute-done.24, bf16[8,96,2048]{2,1,0:T(8,128)(2,1)S(1)} %copy-done.6, bf16[]{:T(256)} %bitcast.39, bf16[]{:T(256)} %bitcast.38, bf16[8,96,128]{2,1,0:T(8,128)(2,1)S(1)} %get-tuple-element.10), kind=kOutput, calls=%fused_computation.53 | convolution fusion | flops 51642368 | bytes 1466372 | tf_op jit(solution)/shard_map/dot_general | solution.py:482
  161.8 1.2 slice.204
  163.7 2.3 %fusion.3 = bf16[128,2048]{1,0:T(8,128)(2,1)} fusion(bf16[128,2048]{1,0:T(8,128)(2,1)} %collective-permute-done.15, bf16[8,96,2048]{2,1,0:T(8,128)(2,1)} %copy-done.1, bf16[8,96,128]{2,1,0:T(8,128)(2,1)S(1)} %get-tuple-element.10), kind=kOutput, calls=%fused_computation.15 | convolution fusion | flops 51118080 | bytes 1466368 | tf_op jit(solution)/shard_map/dot_general | solution.py:482
  166.0 2.0 collective-permute-start.16
  168.0 2.2 %fusion.16 = bf16[128,2048]{1,0:T(8,128)(2,1)} fusion(bf16[128,2048]{1,0:T(8,128)(2,1)} %collective-permute-done.28, bf16[8,96,2048]{2,1,0:T(8,128)(2,1)S(1)} %copy-done.6, bf16[]{:T(256)} %bitcast.45, bf16[8,96,128]{2,1,0:T(8,128)(2,1)S(1)} %get-tuple-element.10), kind=kOutput, calls=%fused_computation.48 | convolution fusion | flops 51380224 | bytes 1466370 | tf_op jit(solution)/shard_map/dot_general | solution.py:482
  170.2 1.5 collective-permute-start.29
  172.3 2.2 %fusion.19 = bf16[128,2048]{1,0:T(8,128)(2,1)} fusion(bf16[128,2048]{1,0:T(8,128)(2,1)} %collective-permute-done.25, bf16[8,96,2048]{2,1,0:T(8,128)(2,1)S(1)} %copy-done.6, bf16[]{:T(256)} %bitcast.40, bf16[8,96,128]{2,1,0:T(8,128)(2,1)S(1)} %get-tuple-element.10), kind=kOutput, calls=%fused_computation.51 | convolution fusion | flops 51380224 | bytes 1466370 | tf_op jit(solution)/shard_map/dot_general | solution.py:482
  175.0 6.1 %collective-permute-done.16 = bf16[128,2048]{1,0:T(8,128)(2,1)} collective-permute-done((bf16[128,2048]{1,0:T(8,128)(2,1)}, bf16[128,2048]{1,0:T(8,128)(2,1)}, u32[]{:S(2)}, u32[]{:S(2)}) %collective-permute-start.16) | collective-permute-done | bytes 524320 | tf_op jit(solution)/shard_map/ppermute | solution.py:95
  181.1 1.2 slice.205
  183.0 4.8 %collective-permute-done.29 = bf16[128,2048]{1,0:T(8,128)(2,1)} collective-permute-done((bf16[128,2048]{1,0:T(8,128)(2,1)}, bf16[128,2048]{1,0:T(8,128)(2,1)}, u32[]{:S(2)}, u32[]{:S(2)}) %collective-permute-start.29) | collective-permute-done | bytes 524320 | tf_op jit(solution)/shard_map/ppermute | solution.py:95
  187.8 1.4 fusion.17
  189.2 2.4 %collective-permute-start.30 = (bf16[128,2048]{1,0:T(8,128)(2,1)S(1)}, bf16[128,2048]{1,0:T(8,128)(2,1)S(1)}, u32[]{:S(2)}, u32[]{:S(2)}) collective-permute-start(bf16[128,2048]{1,0:T(8,128)(2,1)S(1)} %fusion.17), channel_id=1, source_target_pairs={{0,2},{2,4},{4,6},{6,7},{7,5},{5,3},{3,1},{1,0},{8,10},{10,12},{12... | collective-permute-start | bytes 1572872 | tf_op jit(solution)/shard_map/ppermute | solution.py:95
  191.5 1.4 fusion.9
  193.7 2.5 %fusion.2 = bf16[128,2048]{1,0:T(8,128)(2,1)} fusion(bf16[128,2048]{1,0:T(8,128)(2,1)} %collective-permute-done.23, bf16[128,2048]{1,0:T(8,128)(2,1)} %collective-permute-done.16, bf16[8,96,2048]{2,1,0:T(8,128)(2,1)} %copy-done.1, bf16[8,96,128]{2,1,0:T(8,128)(2,1)S(1)} %get-tuple-element.10), kind=kOutput, calls=%fused_computation.14 | convolution fusion | flops 51642368 | bytes 1990656 | tf_op jit(solution)/shard_map/dot_general | solution.py:482
  196.1 2.5 %collective-permute-done.30 = bf16[128,2048]{1,0:T(8,128)(2,1)S(1)} collective-permute-done((bf16[128,2048]{1,0:T(8,128)(2,1)S(1)}, bf16[128,2048]{1,0:T(8,128)(2,1)S(1)}, u32[]{:S(2)}, u32[]{:S(2)}) %collective-permute-start.30) | collective-permute-done | bytes 524320 | tf_op jit(solution)/shard_map/ppermute | solution.py:95
  198.7 3.4 %collective-permute-done.27 = bf16[128,2048]{1,0:T(8,128)(2,1)S(1)} collective-permute-done((bf16[128,2048]{1,0:T(8,128)(2,1)S(1)}, bf16[128,2048]{1,0:T(8,128)(2,1)S(1)}, u32[]{:S(2)}, u32[]{:S(2)}) %collective-permute-start.27) | collective-permute-done | bytes 524320 | tf_op jit(solution)/shard_map/ppermute | solution.py:95
  (98 shorter events, 25.9 us)
Async XLA Ops:
  0.6 34.7 %collective-permute-start.4 = (bf16[768,2048]{1,0:T(8,128)(2,1)}, bf16[768,2048]{1,0:T(8,128)(2,1)S(1)}, u32[]{:S(2)}, u32[]{:S(2)}) collective-permute-start(bf16[768,2048]{1,0:T(8,128)(2,1)} %bitcast.166), channel_id=1, source_target_pairs={{0,8},{8,0},{1,9},{9,1},{2,10},{10,2},{3,11},{11,3},{4,12},{12,4},... | collective-permute-start | bytes 9437192 | tf_op jit(solution)/shard_map/ppermute | solution.py:443
  1.1 39.7 %collective-permute-start = (bf16[2048,768]{1,0:T(8,128)(2,1)}, bf16[2048,768]{1,0:T(8,128)(2,1)}, u32[]{:S(2)}, u32[]{:S(2)}) collective-permute-start(bf16[2048,768]{1,0:T(8,128)(2,1)} %bitcast.169), channel_id=1, source_target_pairs={{0,8},{8,0},{1,9},{9,1},{2,10},{10,2},{3,11},{11,3},{4,12},{12,4},... | collective-permute-start | bytes 9437192 | tf_op jit(solution)/shard_map/ppermute | solution.py:443
  1.2 39.7 %collective-permute-start.1 = (bf16[2048,768]{1,0:T(8,128)(2,1)}, bf16[2048,768]{1,0:T(8,128)(2,1)}, u32[]{:S(2)}, u32[]{:S(2)}) collective-permute-start(bf16[2048,768]{1,0:T(8,128)(2,1)} %bitcast.172), channel_id=1, source_target_pairs={{0,8},{8,0},{1,9},{9,1},{2,10},{10,2},{3,11},{11,3},{4,12},{12,4},... | collective-permute-start | bytes 9437192 | tf_op jit(solution)/shard_map/ppermute | solution.py:443
  1.7 20.4 %collective-permute-start.2 = (bf16[128,2048]{1,0:T(8,128)(2,1)}, bf16[128,2048]{1,0:T(8,128)(2,1)}, u32[]{:S(2)}, u32[]{:S(2)}) collective-permute-start(bf16[128,2048]{1,0:T(8,128)(2,1)} %param.7), channel_id=1, source_target_pairs={{0,1},{2,0},{4,2},{6,4},{7,6},{5,7},{3,5},{1,3},{8,9},{10,8},{12,1... | collective-permute-start | bytes 1572872 | tf_op jit(solution)/shard_map/ppermute | solution.py:95
  4.2 18.3 %collective-permute-start.6 = (bf16[128,2048]{1,0:T(8,128)(2,1)}, bf16[128,2048]{1,0:T(8,128)(2,1)}, u32[]{:S(2)}, u32[]{:S(2)}) collective-permute-start(bf16[128,2048]{1,0:T(8,128)(2,1)} %param.7), channel_id=1, source_target_pairs={{0,2},{2,4},{4,6},{6,7},{7,5},{5,3},{3,1},{1,0},{8,10},{10,12},{12... | collective-permute-start | bytes 1572872 | tf_op jit(solution)/shard_map/ppermute | solution.py:95
  22.1 13.1 %collective-permute-start.3 = (bf16[128,2048]{1,0:T(8,128)(2,1)}, bf16[128,2048]{1,0:T(8,128)(2,1)}, u32[]{:S(2)}, u32[]{:S(2)}) collective-permute-start(bf16[128,2048]{1,0:T(8,128)(2,1)} %shard_map.95), channel_id=1, source_target_pairs={{0,1},{2,0},{4,2},{6,4},{7,6},{5,7},{3,5},{1,3},{8,9},{10,8},{12,1... | collective-permute-start | bytes 1572872 | tf_op jit(solution)/shard_map/ppermute | solution.py:95
  22.5 12.8 %collective-permute-start.7 = (bf16[128,2048]{1,0:T(8,128)(2,1)}, bf16[128,2048]{1,0:T(8,128)(2,1)}, u32[]{:S(2)}, u32[]{:S(2)}) collective-permute-start(bf16[128,2048]{1,0:T(8,128)(2,1)} %shard_map.97), channel_id=1, source_target_pairs={{0,2},{2,4},{4,6},{6,7},{7,5},{5,3},{3,1},{1,0},{8,10},{10,12},{12... | collective-permute-start | bytes 1572872 | tf_op jit(solution)/shard_map/ppermute | solution.py:95
  35.3 1.0 copy-start.5
  36.4 1.7 copy-start
  38.1 0.8 copy-start.2
  38.9 2.0 %copy-start.4 = (f32[8,8,128]{2,1,0:T(8,128)S(1)}, f32[8,8,128]{2,1,0:T(8,128)}, u32[]{:S(2)}) copy-start(f32[8,8,128]{2,1,0:T(8,128)} %all_to_all.10.refs_1_) | copy-start | bytes 98308
  38.9 15.1 %collective-permute-start.8 = (bf16[128,2048]{1,0:T(8,128)(2,1)}, bf16[128,2048]{1,0:T(8,128)(2,1)S(1)}, u32[]{:S(2)}, u32[]{:S(2)}) collective-permute-start(bf16[128,2048]{1,0:T(8,128)(2,1)} %shard_map.98), channel_id=1, source_target_pairs={{0,2},{2,4},{4,6},{6,7},{7,5},{5,3},{3,1},{1,0},{8,10},{10,12},{12... | collective-permute-start | bytes 1572872 | tf_op jit(solution)/shard_map/ppermute | solution.py:95
  40.5 26.8 %collective-permute-start.5 = (bf16[128,2048]{1,0:T(8,128)(2,1)}, bf16[128,2048]{1,0:T(8,128)(2,1)S(1)}, u32[]{:S(2)}, u32[]{:S(2)}) collective-permute-start(bf16[128,2048]{1,0:T(8,128)(2,1)} %shard_map.96), channel_id=1, source_target_pairs={{0,1},{2,0},{4,2},{6,4},{7,6},{5,7},{3,5},{1,3},{8,9},{10,8},{12,1... | collective-permute-start | bytes 1572872 | tf_op jit(solution)/shard_map/ppermute | solution.py:95
  41.7 5.3 %copy-start.3 = (bf16[128,2048]{1,0:T(8,128)(2,1)S(1)}, bf16[128,2048]{1,0:T(8,128)(2,1)}, u32[]{:S(2)}) copy-start(bf16[128,2048]{1,0:T(8,128)(2,1)} %copy-done.2) | copy-start | bytes 1572868
  41.7 7.4 %copy-start.7 = (bf16[128,2048]{1,0:T(8,128)(2,1)S(1)}, bf16[128,2048]{1,0:T(8,128)(2,1)}, u32[]{:S(2)}) copy-start(bf16[128,2048]{1,0:T(8,128)(2,1)} %param.7) | copy-start | bytes 1572868
  47.0 17.0 %collective-permute-start.10 = (bf16[128,2048]{1,0:T(8,128)(2,1)S(1)}, bf16[128,2048]{1,0:T(8,128)(2,1)S(1)}, u32[]{:S(2)}, u32[]{:S(2)}) collective-permute-start(bf16[128,2048]{1,0:T(8,128)(2,1)S(1)} %copy-done.3), channel_id=1, source_target_pairs={{0,1},{2,0},{4,2},{6,4},{7,6},{5,7},{3,5},{1,3},{8,9},{10,8},{12,1... | collective-permute-start | bytes 1572872 | tf_op jit(solution)/shard_map/ppermute | solution.py:95
  47.9 17.3 %collective-permute-start.19 = (bf16[128,2048]{1,0:T(8,128)(2,1)S(1)}, bf16[128,2048]{1,0:T(8,128)(2,1)S(1)}, u32[]{:S(2)}, u32[]{:S(2)}) collective-permute-start(bf16[128,2048]{1,0:T(8,128)(2,1)S(1)} %copy-done.3), channel_id=1, source_target_pairs={{0,2},{2,4},{4,6},{6,7},{7,5},{5,3},{3,1},{1,0},{8,10},{10,12},{12... | collective-permute-start | bytes 1572872 | tf_op jit(solution)/shard_map/ppermute | solution.py:95
  53.9 33.1 %collective-permute-start.9 = (bf16[128,2048]{1,0:T(8,128)(2,1)S(1)}, bf16[128,2048]{1,0:T(8,128)(2,1)S(1)}, u32[]{:S(2)}, u32[]{:S(2)}) collective-permute-start(bf16[128,2048]{1,0:T(8,128)(2,1)S(1)} %collective-permute-done.8), channel_id=1, source_target_pairs={{0,2},{2,4},{4,6},{6,7},{7,5},{5,3},{3,1},{1,0},{8,10},{10,12},{12... | collective-permute-start | bytes 1572872 | tf_op jit(solution)/shard_map/ppermute | solution.py:95
  64.0 12.1 %collective-permute-start.11 = (bf16[128,2048]{1,0:T(8,128)(2,1)S(1)}, bf16[128,2048]{1,0:T(8,128)(2,1)S(1)}, u32[]{:S(2)}, u32[]{:S(2)}) collective-permute-start(bf16[128,2048]{1,0:T(8,128)(2,1)S(1)} %collective-permute-done.10), channel_id=1, source_target_pairs={{0,1},{2,0},{4,2},{6,4},{7,6},{5,7},{3,5},{1,3},{8,9},{10,8},{12,1... | collective-permute-start | bytes 1572872 | tf_op jit(solution)/shard_map/ppermute | solution.py:95
  65.2 19.7 %collective-permute-start.20 = (bf16[128,2048]{1,0:T(8,128)(2,1)S(1)}, bf16[128,2048]{1,0:T(8,128)(2,1)S(1)}, u32[]{:S(2)}, u32[]{:S(2)}) collective-permute-start(bf16[128,2048]{1,0:T(8,128)(2,1)S(1)} %collective-permute-done.19), channel_id=1, source_target_pairs={{0,2},{2,4},{4,6},{6,7},{7,5},{5,3},{3,1},{1,0},{8,10},{10,12},{12... | collective-permute-start | bytes 1572872 | tf_op jit(solution)/shard_map/ppermute | solution.py:95
  76.1 21.7 %collective-permute-start.12 = (bf16[128,2048]{1,0:T(8,128)(2,1)S(1)}, bf16[128,2048]{1,0:T(8,128)(2,1)S(1)}, u32[]{:S(2)}, u32[]{:S(2)}) collective-permute-start(bf16[128,2048]{1,0:T(8,128)(2,1)S(1)} %collective-permute-done.11.refs_12_), channel_id=1, source_target_pairs={{0,1},{2,0},{4,2},{6,4},{7,6},{5,7},{3,5},{1,3},{8,9},{10,8},{12,1... | collective-permute-start | bytes 1572872 | tf_op jit(solution)/shard_map/ppermute | solution.py:95
  84.9 25.5 %collective-permute-start.21 = (bf16[128,2048]{1,0:T(8,128)(2,1)S(1)}, bf16[128,2048]{1,0:T(8,128)(2,1)S(1)}, u32[]{:S(2)}, u32[]{:S(2)}) collective-permute-start(bf16[128,2048]{1,0:T(8,128)(2,1)S(1)} %collective-permute-done.20), channel_id=1, source_target_pairs={{0,2},{2,4},{4,6},{6,7},{7,5},{5,3},{3,1},{1,0},{8,10},{10,12},{12... | collective-permute-start | bytes 1572872 | tf_op jit(solution)/shard_map/ppermute | solution.py:95
  97.8 10.0 %collective-permute-start.17 = (bf16[128,2048]{1,0:T(8,128)(2,1)S(1)}, bf16[128,2048]{1,0:T(8,128)(2,1)S(1)}, u32[]{:S(2)}, u32[]{:S(2)}) collective-permute-start(bf16[128,2048]{1,0:T(8,128)(2,1)S(1)} %collective-permute-done.12.refs_3_), channel_id=1, source_target_pairs={{0,1},{2,0},{4,2},{6,4},{7,6},{5,7},{3,5},{1,3},{8,9},{10,8},{12,1... | collective-permute-start | bytes 1572872 | tf_op jit(solution)/shard_map/ppermute | solution.py:95
  102.9 37.6 %copy-start.1 = (bf16[8,96,2048]{2,1,0:T(8,128)(2,1)}, bf16[8,96,2048]{2,1,0:T(8,128)(2,1)S(1)}, u32[]{:S(2)}) copy-start(bf16[8,96,2048]{2,1,0:T(8,128)(2,1)S(1)} %shard_map.101.refs_9_) | copy-start | bytes 9437188
  103.3 19.6 %collective-permute-start.13 = (bf16[128,2048]{1,0:T(8,128)(2,1)S(1)}, bf16[128,2048]{1,0:T(8,128)(2,1)S(1)}, u32[]{:S(2)}, u32[]{:S(2)}) collective-permute-start(bf16[128,2048]{1,0:T(8,128)(2,1)S(1)} %convolution_convert_fusion.3), channel_id=1, source_target_pairs={{0,2},{2,4},{4,6},{6,7},{7,5},{5,3},{3,1},{1,0},{8,10},{10,12},{12... | collective-permute-start | bytes 1572872 | tf_op jit(solution)/shard_map/ppermute | solution.py:95
  109.3 12.4 %collective-permute-start.18 = (bf16[128,2048]{1,0:T(8,128)(2,1)S(1)}, bf16[128,2048]{1,0:T(8,128)(2,1)S(1)}, u32[]{:S(2)}, u32[]{:S(2)}) collective-permute-start(bf16[128,2048]{1,0:T(8,128)(2,1)S(1)} %broadcast_add_fusion), channel_id=1, source_target_pairs={{0,1},{2,0},{4,2},{6,4},{7,6},{5,7},{3,5},{1,3},{8,9},{10,8},{12,1... | collective-permute-start | bytes 1572872 | tf_op jit(solution)/shard_map/ppermute | solution.py:95
  122.0 12.7 %collective-permute-start.22 = (bf16[128,2048]{1,0:T(8,128)(2,1)S(1)}, bf16[128,2048]{1,0:T(8,128)(2,1)S(1)}, u32[]{:S(2)}, u32[]{:S(2)}) collective-permute-start(bf16[128,2048]{1,0:T(8,128)(2,1)S(1)} %fusion.20), channel_id=1, source_target_pairs={{0,1},{2,0},{4,2},{6,4},{7,6},{5,7},{3,5},{1,3},{8,9},{10,8},{12,1... | collective-permute-start | bytes 1572872 | tf_op jit(solution)/shard_map/ppermute | solution.py:95
  123.2 17.4 %collective-permute-start.14 = (bf16[128,2048]{1,0:T(8,128)(2,1)S(1)}, bf16[128,2048]{1,0:T(8,128)(2,1)S(1)}, u32[]{:S(2)}, u32[]{:S(2)}) collective-permute-start(bf16[128,2048]{1,0:T(8,128)(2,1)S(1)} %fusion.5), channel_id=1, source_target_pairs={{0,2},{2,4},{4,6},{6,7},{7,5},{5,3},{3,1},{1,0},{8,10},{10,12},{12... | collective-permute-start | bytes 1572872 | tf_op jit(solution)/shard_map/ppermute | solution.py:95
  137.1 20.2 %collective-permute-start.23 = (bf16[128,2048]{1,0:T(8,128)(2,1)}, bf16[128,2048]{1,0:T(8,128)(2,1)}, u32[]{:S(2)}, u32[]{:S(2)}) collective-permute-start(bf16[128,2048]{1,0:T(8,128)(2,1)} %fusion.6), channel_id=1, source_target_pairs={{0,1},{2,0},{4,2},{6,4},{7,6},{5,7},{3,5},{1,3},{8,9},{10,8},{12,1... | collective-permute-start | bytes 1572872 | tf_op jit(solution)/shard_map/ppermute | solution.py:95
  140.0 19.1 %collective-permute-start.24 = (bf16[128,2048]{1,0:T(8,128)(2,1)}, bf16[128,2048]{1,0:T(8,128)(2,1)}, u32[]{:S(2)}, u32[]{:S(2)}) collective-permute-start(bf16[128,2048]{1,0:T(8,128)(2,1)} %fusion.14), channel_id=1, source_target_pairs={{0,1},{2,0},{4,2},{6,4},{7,6},{5,7},{3,5},{1,3},{8,9},{10,8},{12,1... | collective-permute-start | bytes 1572872 | tf_op jit(solution)/shard_map/ppermute | solution.py:95
  140.6 5.9 %copy-start.8 = (bf16[128,2048]{1,0:T(8,128)(2,1)}, bf16[128,2048]{1,0:T(8,128)(2,1)S(1)}, u32[]{:S(2)}) copy-start(bf16[128,2048]{1,0:T(8,128)(2,1)S(1)} %collective-permute-done.14) | copy-start | bytes 1572868
  141.7 12.3 %copy-start.6 = (bf16[8,96,2048]{2,1,0:T(8,128)(2,1)S(1)}, bf16[8,96,2048]{2,1,0:T(8,128)(2,1)}, u32[]{:S(2)}) copy-start(bf16[8,96,2048]{2,1,0:T(8,128)(2,1)} %shard_map.103) | copy-start | bytes 9437188
  141.7 20.1 %collective-permute-start.15 = (bf16[128,2048]{1,0:T(8,128)(2,1)}, bf16[128,2048]{1,0:T(8,128)(2,1)}, u32[]{:S(2)}, u32[]{:S(2)}) collective-permute-start(bf16[128,2048]{1,0:T(8,128)(2,1)} %fusion.4), channel_id=1, source_target_pairs={{0,2},{2,4},{4,6},{6,7},{7,5},{5,3},{3,1},{1,0},{8,10},{10,12},{12... | collective-permute-start | bytes 1572872 | tf_op jit(solution)/shard_map/ppermute | solution.py:95
  147.7 13.6 %all-to-all-start.1 = ((f32[8,2,128]{2,1,0:T(2,128)}), f32[8,2,128]{2,1,0:T(2,128)S(1)}, u32[]{:S(2)}, u32[]{:S(2)}) async-start(f32[8,2,128]{2,1,0:T(2,128)} %shard_map.104), calls=%async_computation.1 | async-start | bytes 16384 | tf_op jit(solution)/shard_map/all_to_all | solution.py:507
  155.2 12.8 %collective-permute-start.28 = (bf16[128,2048]{1,0:T(8,128)(2,1)}, bf16[128,2048]{1,0:T(8,128)(2,1)}, u32[]{:S(2)}, u32[]{:S(2)}) collective-permute-start(bf16[128,2048]{1,0:T(8,128)(2,1)} %fusion.15), channel_id=1, source_target_pairs={{0,2},{2,4},{4,6},{6,7},{7,5},{5,3},{3,1},{1,0},{8,10},{10,12},{12... | collective-permute-start | bytes 1572872 | tf_op jit(solution)/shard_map/ppermute | solution.py:95
  161.3 11.0 %collective-permute-start.25 = (bf16[128,2048]{1,0:T(8,128)(2,1)}, bf16[128,2048]{1,0:T(8,128)(2,1)}, u32[]{:S(2)}, u32[]{:S(2)}) collective-permute-start(bf16[128,2048]{1,0:T(8,128)(2,1)} %fusion.21), channel_id=1, source_target_pairs={{0,1},{2,0},{4,2},{6,4},{7,6},{5,7},{3,5},{1,3},{8,9},{10,8},{12,1... | collective-permute-start | bytes 1572872 | tf_op jit(solution)/shard_map/ppermute | solution.py:95
  166.0 27.0 %copy-start.9 = (s32[128,4]{0,1:T(4,128)S(1)}, s32[128,4]{0,1:T(4,128)}, u32[]{:S(2)}) copy-start(s32[128,4]{0,1:T(4,128)} %param.9) | copy-start | bytes 6148
  166.0 15.2 %collective-permute-start.16 = (bf16[128,2048]{1,0:T(8,128)(2,1)}, bf16[128,2048]{1,0:T(8,128)(2,1)}, u32[]{:S(2)}, u32[]{:S(2)}) collective-permute-start(bf16[128,2048]{1,0:T(8,128)(2,1)} %fusion.3), channel_id=1, source_target_pairs={{0,2},{2,4},{4,6},{6,7},{7,5},{5,3},{3,1},{1,0},{8,10},{10,12},{12... | collective-permute-start | bytes 1572872 | tf_op jit(solution)/shard_map/ppermute | solution.py:95
  170.2 17.6 %collective-permute-start.29 = (bf16[128,2048]{1,0:T(8,128)(2,1)}, bf16[128,2048]{1,0:T(8,128)(2,1)}, u32[]{:S(2)}, u32[]{:S(2)}) collective-permute-start(bf16[128,2048]{1,0:T(8,128)(2,1)} %fusion.16), channel_id=1, source_target_pairs={{0,2},{2,4},{4,6},{6,7},{7,5},{5,3},{3,1},{1,0},{8,10},{10,12},{12... | collective-permute-start | bytes 1572872 | tf_op jit(solution)/shard_map/ppermute | solution.py:95
  174.4 17.1 %collective-permute-start.26 = (bf16[128,2048]{1,0:T(8,128)(2,1)}, bf16[128,2048]{1,0:T(8,128)(2,1)}, u32[]{:S(2)}, u32[]{:S(2)}) collective-permute-start(bf16[128,2048]{1,0:T(8,128)(2,1)} %fusion.19), channel_id=1, source_target_pairs={{0,1},{2,0},{4,2},{6,4},{7,6},{5,7},{3,5},{1,3},{8,9},{10,8},{12,1... | collective-permute-start | bytes 1572872 | tf_op jit(solution)/shard_map/ppermute | solution.py:95
  189.2 9.5 %collective-permute-start.30 = (bf16[128,2048]{1,0:T(8,128)(2,1)S(1)}, bf16[128,2048]{1,0:T(8,128)(2,1)S(1)}, u32[]{:S(2)}, u32[]{:S(2)}) collective-permute-start(bf16[128,2048]{1,0:T(8,128)(2,1)S(1)} %fusion.17), channel_id=1, source_target_pairs={{0,2},{2,4},{4,6},{6,7},{7,5},{5,3},{3,1},{1,0},{8,10},{10,12},{12... | collective-permute-start | bytes 1572872 | tf_op jit(solution)/shard_map/ppermute | solution.py:95
  192.9 9.2 %collective-permute-start.27 = (bf16[128,2048]{1,0:T(8,128)(2,1)S(1)}, bf16[128,2048]{1,0:T(8,128)(2,1)S(1)}, u32[]{:S(2)}, u32[]{:S(2)}) collective-permute-start(bf16[128,2048]{1,0:T(8,128)(2,1)S(1)} %fusion.9), channel_id=1, source_target_pairs={{0,1},{2,0},{4,2},{6,4},{7,6},{5,7},{3,5},{1,3},{8,9},{10,8},{12,1... | collective-permute-start | bytes 1572872 | tf_op jit(solution)/shard_map/ppermute | solution.py:95
